TPU v7x, 32 devices: a whole 2x2x4 slice. The times are simulated.
32 devices in a mesh: group: 1, row: 32 (over z, y, x, core).
Axes of the slice: x: 2, y: 2, z: 4, core: 2. Of those that a mesh axis runs over, the one named last changes fastest.
Arguments:
- alignment_tensor: bfloat16 [64, 512, 256], P(('group', 'row')), may hold values from -6 to 6
- pairwise_tensor: bfloat16 [512, 512, 128], P('group', 'row'), may hold values from -6 to 6
- standardize_factor: float32 [256], replicated, may hold values from 0.1 to 1.9
- standardize_shift: float32 [256], replicated, may hold values from -3 to 3
- first_matrix: bfloat16 [256, 32], replicated, may hold values from -0.375 to 0.375
- first_shift: float32 [32], replicated, may hold values from -3 to 3
- second_matrix: bfloat16 [256, 32], replicated, may hold values from -0.375 to 0.375
- second_shift: float32 [32], replicated, may hold values from -3 to 3
- final_matrix: bfloat16 [1024, 128], replicated, may hold values from -3 to 3
- final_shift: float32 [128], replicated, may hold values from -3 to 3
Outputs:
- pair_out: bfloat16 [512, 512, 128], P('group', 'row')
All inputs are finite; a program needn't handle non-finite values.
Results may differ from a plain program's by a relative error of at most 0.0061.
Values may be sent and summed in bfloat16 or wider, within the bound.
No kernel may reach another device: no remote copies, remote signals or barrier semaphores. Data moves between devices by JAX's collectives and lax.ppermute only.
A program may use at most 192 MiB of HBM per device.

v0:
```python
import functools

import jax
import jax.numpy as jnp
from jax import lax
from jax.experimental import pallas as pl
from jax.experimental.pallas import tpu as pltpu
from jax.sharding import PartitionSpec as P

LANES = 128


def _stacked(weights, copies):
    q, c = weights.shape
    rows = []
    for k in range(copies):
        left = [jnp.zeros((q, k * c), weights.dtype)] if k else []
        right = [jnp.zeros((q, (copies - 1 - k) * c), weights.dtype)] if k < copies - 1 else []
        rows.append(jnp.concatenate(left + [weights] + right, axis=1))
    return jnp.concatenate(rows, axis=0)


def _project_kernel(x_ref, gain_ref, bias_ref, w1_ref, b1_ref, w2_ref, b2_ref, left_ref, right_ref):
    band_half = left_ref.shape[0]
    n = right_ref.shape[0]
    feats = x_ref.shape[2]
    odd = lax.axis_index("row") % 2
    normed = []
    for s in range(2):
        x = x_ref[s].astype(jnp.float32)
        center = jnp.mean(x, axis=-1, keepdims=True)
        off = x - center
        spread = jnp.mean(off * off, axis=-1, keepdims=True)
        normed.append(off * lax.rsqrt(spread + 1e-05) * gain_ref[...] + bias_ref[...])
    low = [v[:band_half].astype(jnp.bfloat16) for v in normed]
    high = [v[band_half : 2 * band_half].astype(jnp.bfloat16) for v in normed]
    stack1 = _stacked(w1_ref[...], 4)
    shift1 = jnp.concatenate([b1_ref[...]] * 4, axis=1)
    left = jnp.dot(jnp.concatenate(low + high, axis=1), stack1, preferred_element_type=jnp.float32) + shift1
    swapped = pltpu.roll(left, 64, 1)
    left_ref[...] = jnp.where(odd == 1, swapped, left).astype(jnp.bfloat16)

    split = [v.reshape(n, 2, 8, feats) for v in normed]
    parts = [split[s][:, jh].reshape(n * 8, feats).astype(jnp.bfloat16) for jh in range(2) for s in range(2)]
    stack2 = _stacked(w2_ref[...], 4)
    shift2 = jnp.concatenate([b2_ref[...]] * 4, axis=1)
    right = jnp.dot(jnp.concatenate(parts, axis=1), stack2, preferred_element_type=jnp.float32) + shift2
    right_ref[...] = right.reshape(n, 8, LANES).astype(jnp.bfloat16)


def _fold_kernel(right_ref, final_ref, out_ref, scratch):
    d = right_ref.shape[0]
    chans = 32
    block = right_ref[...].astype(jnp.float32).reshape(d * 8, LANES)
    lane = lax.broadcasted_iota(jnp.int32, block.shape, 1) // chans
    lhs = jnp.concatenate([jnp.where(lane == q, block, 0.0) for q in range(4)], axis=0).astype(jnp.bfloat16)
    for c in range(0, chans, 2):
        pair = []
        for k in range(2):
            w = final_ref[pl.ds((c + k) * chans, chans), :]
            pair.append(jnp.concatenate([w] * 4, axis=0))
        rhs = jnp.concatenate(pair, axis=1)
        res = jnp.dot(lhs, rhs, preferred_element_type=jnp.float32)
        for k in range(2):
            scratch[pl.ds(c + k, 4 * d * 8, stride=chans), :] = res[:, k * LANES : (k + 1) * LANES]
    for q in range(4):
        jh, s = q // 2, q % 2
        for dd in range(d):
            for jr in range(8):
                row = ((q * d + dd) * 8 + jr) * chans
                j = jh * 8 + jr
                out_ref[pl.ds((dd * 2 + s) * chans, chans), pl.ds(j * LANES, LANES)] = scratch[
                    pl.ds(row, chans), :
                ].astype(jnp.bfloat16)


def _band_kernel(count, groups, *refs):
    own_refs, other_refs = refs[:groups], refs[groups : 2 * groups]
    t_ref, pair_ref, shift_ref, out_ref, l_ref, acc_ref = refs[2 * groups :]
    step = pl.program_id(0)
    steps = pl.num_programs(0)
    half = own_refs[0].shape[1]
    band, cols = pair_ref.shape[0], pair_ref.shape[1]
    me = lax.axis_index("row")

    @pl.when(step == 0)
    def _():
        lane = lax.broadcasted_iota(jnp.int32, (half, LANES), 1)
        first = (lane // 64) == (me % 2)
        for g in range(groups):
            for zi in range(own_refs[g].shape[0]):
                chip = (zi * groups + g) ^ (me // 2)
                a = own_refs[g][zi].astype(jnp.float32)
                b = other_refs[g][zi].astype(jnp.float32)
                at = pl.ds(pl.multiple_of(chip * LANES, LANES), LANES)
                l_ref[pl.ds(0, half), at] = jnp.where(first, a, b).astype(jnp.bfloat16)
                l_ref[pl.ds(half, half), at] = pltpu.roll(jnp.where(first, b, a), 64, 1).astype(jnp.bfloat16)

    res = jnp.dot(l_ref[...], t_ref[...], preferred_element_type=jnp.float32)
    width = t_ref.shape[1] // LANES
    for k in range(width):
        acc_ref[pl.ds(step * width + k, band, stride=cols), :] = res[:, k * LANES : (k + 1) * LANES]

    @pl.when(step == steps - 1)
    def _():
        shift = shift_ref[...].reshape(1, 1, LANES)
        rows = 32

        def body(r, _):
            at = pl.ds(pl.multiple_of(r * rows, rows), rows)
            flat = pl.ds(pl.multiple_of(r * rows * cols, rows * cols), rows * cols)
            total = acc_ref[flat, :].reshape(rows, cols, LANES) * (1.0 / count) + shift
            out_ref[at] = (pair_ref[at].astype(jnp.float32) + total).astype(jnp.bfloat16)
            return 0

        lax.fori_loop(0, band // rows, body, 0)


def _xor(x, mask, n):
    return lax.ppermute(x, "row", [(i, i ^ mask) for i in range(n)])


def shards(n, alignment, pair, gain, bias, w1, b1, w2, b2, final, shift):
    seqs, residues, feats = alignment.shape
    band, cols, zdim = pair.shape
    chans = w1.shape[1]
    half = band // 2
    count = float(seqs * n)
    vmem = pltpu.CompilerParams(vmem_limit_bytes=48 * 1024 * 1024)

    left, right = pl.pallas_call(
        _project_kernel,
        out_shape=(
            jax.ShapeDtypeStruct((half, LANES), jnp.bfloat16),
            jax.ShapeDtypeStruct((n, 8, LANES), jnp.bfloat16),
        ),
        compiler_params=vmem,
        cost_estimate=pl.CostEstimate(
            flops=4 * seqs * residues * feats * chans, bytes_accessed=2 * seqs * residues * feats, transcendentals=0
        ),
    )(alignment, gain.reshape(1, -1), bias.reshape(1, -1), w1, b1.reshape(1, -1), w2, b2.reshape(1, -1))

    right = lax.all_to_all(right, "row", split_axis=0, concat_axis=0, tiled=True)

    line = [left] + [_xor(left, m, n) for m in range(8, n, 8)]
    line = jnp.stack(line)
    own = [line] + [_xor(line, m, n) for m in (2, 4, 6)]
    other = [_xor(o, 1, n) for o in own]
    groups = 4

    step_d = 4
    folded = pl.pallas_call(
        _fold_kernel,
        grid=(n // step_d,),
        in_specs=[
            pl.BlockSpec((step_d, 8, LANES), lambda i: (i, 0, 0)),
            pl.BlockSpec(final.shape, lambda i: (0, 0)),
        ],
        out_specs=pl.BlockSpec((step_d * 2 * chans, cols * zdim), lambda i: (i, 0)),
        out_shape=jax.ShapeDtypeStruct((n * 2 * chans, cols * zdim), jnp.bfloat16),
        scratch_shapes=[pltpu.VMEM((step_d * 32 * chans, LANES), jnp.float32)],
        compiler_params=vmem,
        cost_estimate=pl.CostEstimate(
            flops=16 * n * 32 * 256 * chans * zdim, bytes_accessed=n * 4 * chans * cols * zdim, transcendentals=0
        ),
    )(right, final)

    k = n * 2 * chans
    tile = 256
    whole = lambda a: pl.BlockSpec(a.shape, lambda i: (0,) * a.ndim)
    return pl.pallas_call(
        functools.partial(_band_kernel, count, groups),
        grid=(cols * zdim // tile,),
        in_specs=[whole(a) for a in own + other]
        + [
            pl.BlockSpec((k, tile), lambda i: (0, i)),
            whole(pair),
            pl.BlockSpec((1, zdim), lambda i: (0, 0)),
        ],
        out_specs=whole(pair),
        out_shape=jax.ShapeDtypeStruct(pair.shape, jnp.bfloat16),
        scratch_shapes=[pltpu.VMEM((band, k), jnp.bfloat16), pltpu.VMEM((band * cols, zdim), jnp.float32)],
        compiler_params=vmem,
        cost_estimate=pl.CostEstimate(
            flops=2 * band * k * cols * zdim, bytes_accessed=2 * k * cols * zdim, transcendentals=0
        ),
    )(*own, *other, folded, pair, shift.reshape(1, -1))


def solution(mesh):
    placed = (P(("group", "row"), None, None), P("group", "row", None)) + (P(),) * 8
    return jax.shard_map(
        functools.partial(shards, mesh.shape["row"]),
        mesh=mesh,
        in_specs=placed,
        out_specs=P("group", "row", None),
        check_vma=False,
    )
```

profile of v0, /device:TPU:0, one launch (start us, length us, event | category | flops | bytes accessed | tf_op | source)
XLA Modules:
  0.0 61.2 jit_solution(9460837351503392473)
XLA Ops:
  0.0 0.8 %copy.11.w1_ref = bf16[256,32]{1,0:T(8,128)(2,1)S(1)} copy(bf16[256,32]{0,1:T(8,128)(2,1)} %param.14) | data formatting | bytes 32768 | tf_op args[4]
  0.8 0.8 %copy.12.w2_ref = bf16[256,32]{1,0:T(8,128)(2,1)S(1)} copy(bf16[256,32]{0,1:T(8,128)(2,1)} %param.16) | data formatting | bytes 32768 | tf_op args[6]
  1.7 1.0 %copy-done = bf16[2,512,256]{2,1,0:T(8,128)(2,1)S(1)} copy-done((bf16[2,512,256]{2,1,0:T(8,128)(2,1)S(1)}, bf16[2,512,256]{2,1,0:T(8,128)(2,1)}, u32[]{:S(2)}) %copy-start) | copy-done | bytes 524312
  2.7 0.7 %copy-done.1 = f32[256]{0:T(256)S(1)} copy-done((f32[256]{0:T(256)S(1)}, f32[256]{0:T(256)}, u32[]{:S(2)}) %copy-start.1) | copy-done | bytes 1048
  3.4 0.7 %copy-done.2 = f32[256]{0:T(256)S(1)} copy-done((f32[256]{0:T(256)S(1)}, f32[256]{0:T(256)}, u32[]{:S(2)}) %copy-start.2) | copy-done | bytes 1048
  4.1 0.7 %copy-done.3 = f32[32]{0:T(128)S(1)} copy-done((f32[32]{0:T(128)S(1)}, f32[32]{0:T(128)}, u32[]{:S(2)}) %copy-start.3) | copy-done | bytes 152
  4.7 0.7 %copy-done.4 = f32[32]{0:T(128)S(1)} copy-done((f32[32]{0:T(128)S(1)}, f32[32]{0:T(128)}, u32[]{:S(2)}) %copy-start.4) | copy-done | bytes 152
  5.4 1.7 %shard_map.100 = (bf16[256,128]{1,0:T(8,128)(2,1)S(1)}, bf16[32,8,128]{2,1,0:T(8,128)(2,1)}) custom-call(bf16[2,512,256]{2,1,0:T(8,128)(2,1)S(1)} %copy-done, f32[1,256]{1,0:T(1,128)S(1)} %bitcast.10, f32[1,256]{1,0:T(1,128)S(1)} %bitcast.11, bf16[256,32]{1,0:T(8,128)(2,1)S(1)} %copy.11.w1_ref, f32[1,32]{1,0:T(1,128)S(1)} %bitcast.12, ...), custom_call_target="tpu_custom_call" | custom-call | flops 33554432 | bytes 524288 | tf_op jit(solution)/shard_map/pallas_call | solution.py:131
  7.1 5.0 %collective-permute-start.2 = (bf16[256,128]{1,0:T(8,128)(2,1)S(1)}, bf16[256,128]{1,0:T(8,128)(2,1)S(1)}, u32[]{:S(2)}, u32[]{:S(2)}) collective-permute-start(bf16[256,128]{1,0:T(8,128)(2,1)S(1)} %get-tuple-element.7), channel_id=1, source_target_pairs={{0,24},{1,25},{2,26},{3,27},{4,28},{5,29},{6,30},{7,31},{8,16},{9,... | collective-permute-start | bytes 196616 | tf_op jit(solution)/shard_map/ppermute | solution.py:120
  12.2 0.0 collective-permute-start.1
  12.2 0.6 collective-permute-start
  12.7 2.0 %collective-permute-done.2 = bf16[256,128]{1,0:T(8,128)(2,1)S(1)} collective-permute-done((bf16[256,128]{1,0:T(8,128)(2,1)S(1)}, bf16[256,128]{1,0:T(8,128)(2,1)S(1)}, u32[]{:S(2)}, u32[]{:S(2)}) %collective-permute-start.2) | collective-permute-done | bytes 65568 | tf_op jit(solution)/shard_map/ppermute | solution.py:120
  14.7 3.0 %collective-permute-done.1 = bf16[256,128]{1,0:T(8,128)(2,1)S(1)} collective-permute-done((bf16[256,128]{1,0:T(8,128)(2,1)S(1)}, bf16[256,128]{1,0:T(8,128)(2,1)S(1)}, u32[]{:S(2)}, u32[]{:S(2)}) %collective-permute-start.1) | collective-permute-done | bytes 65568 | tf_op jit(solution)/shard_map/ppermute | solution.py:120
  17.8 0.0 collective-permute-done
  17.8 2.5 %collective-permute-start.5 = (bf16[4,256,128]{2,1,0:T(8,128)(2,1)S(1)}, bf16[4,256,128]{2,1,0:T(8,128)(2,1)S(1)}, u32[]{:S(2)}, u32[]{:S(2)}) collective-permute-start(bf16[4,256,128]{2,1,0:T(8,128)(2,1)S(1)} %pad_maximum_fusion.refs_0_), channel_id=1, source_target_pairs={{0,6},{1,7},{2,4},{3,5},{4,2},{5,3},{6,0},{7,1},{8,14},{9,15},{10,... | collective-permute-start | bytes 786440 | tf_op jit(solution)/shard_map/ppermute | solution.py:120
  20.3 0.5 collective-permute-start.4
  20.8 0.5 collective-permute-start.3
  21.4 4.9 %all-to-all-start = ((bf16[32,8,128]{2,1,0:T(8,128)(2,1)}), bf16[32,8,128]{2,1,0:T(8,128)(2,1)S(1)}, u32[]{:S(2)}, u32[]{:S(2)}) async-start(bf16[32,8,128]{2,1,0:T(8,128)(2,1)} %get-tuple-element.8), calls=%async_computation | async-start | bytes 131072 | tf_op jit(solution)/shard_map/all_to_all | solution.py:143
  26.3 0.0 copy-start.5
  26.3 0.3 collective-permute-start.6
  26.6 1.4 %collective-permute-done.5.refs_3_ = bf16[4,256,128]{2,1,0:T(8,128)(2,1)S(1)} collective-permute-done((bf16[4,256,128]{2,1,0:T(8,128)(2,1)S(1)}, bf16[4,256,128]{2,1,0:T(8,128)(2,1)S(1)}, u32[]{:S(2)}, u32[]{:S(2)}) %collective-permute-start.5) | collective-permute-done | bytes 262176 | tf_op jit(solution)/shard_map/ppermute | solution.py:120
  28.0 0.0 collective-permute-start.9
  28.0 4.8 %collective-permute-done.4.refs_2_ = bf16[4,256,128]{2,1,0:T(8,128)(2,1)S(1)} collective-permute-done((bf16[4,256,128]{2,1,0:T(8,128)(2,1)S(1)}, bf16[4,256,128]{2,1,0:T(8,128)(2,1)S(1)}, u32[]{:S(2)}, u32[]{:S(2)}) %collective-permute-start.4) | collective-permute-done | bytes 262176 | tf_op jit(solution)/shard_map/ppermute | solution.py:120
  32.8 0.0 collective-permute-start.8
  32.8 0.4 collective-permute-done.3.refs_1_
  33.1 0.2 collective-permute-start.7
  33.3 0.4 all-to-all-done.right_ref
  33.7 0.9 %copy-done.6 = bf16[1024,128]{1,0:T(8,128)(2,1)S(1)} copy-done((bf16[1024,128]{1,0:T(8,128)(2,1)S(1)}, bf16[1024,128]{1,0:T(8,128)(2,1)}, u32[]{:S(2)}) %copy-start.6) | copy-done | bytes 262168
  34.6 14.3 %shard_map.101.refs_8_ = bf16[2048,2048]{1,0:T(8,128)(2,1)} custom-call(bf16[32,8,128]{2,1,0:T(8,128)(2,1)S(1)} %all-to-all-done.right_ref, bf16[1024,128]{1,0:T(8,128)(2,1)S(1)} %copy-done.6), custom_call_target="tpu_custom_call" | custom-call | flops 17179869184 | bytes 8388608 | tf_op jit(solution)/shard_map/pallas_call | solution.py:152
  48.9 0.0 collective-permute-done.8.refs_6_
  48.9 0.0 collective-permute-done.7.refs_5_
  48.9 12.2 %shard_map.102 = bf16[512,16,128]{2,1,0:T(8,128)(2,1)} custom-call(bf16[4,256,128]{2,1,0:T(8,128)(2,1)S(1)} %pad_maximum_fusion.refs_0_, bf16[4,256,128]{2,1,0:T(8,128)(2,1)S(1)} %collective-permute-done.3.refs_1_, bf16[4,256,128]{2,1,0:T(8,128)(2,1)S(1)} %collective-permute-done.4.refs_2_, bf16[4,256,128]{2,1,0:T(8,128)(2,1)S(1)} %collective-permute-done.5.refs_3_, ...), custom_call_target="tpu_custom_call" | custom-call | flops 4294967296 | bytes 8388608 | tf_op jit(solution)/shard_map/pallas_call | solution.py:171
  (12 shorter events, 0.1 us)
Async XLA Ops:
  1.7 1.0 %copy-start = (bf16[2,512,256]{2,1,0:T(8,128)(2,1)S(1)}, bf16[2,512,256]{2,1,0:T(8,128)(2,1)}, u32[]{:S(2)}) copy-start(bf16[2,512,256]{2,1,0:T(8,128)(2,1)} %x_ref.1) | copy-start | bytes 1572868
  2.7 0.7 %copy-start.1 = (f32[256]{0:T(256)S(1)}, f32[256]{0:T(256)}, u32[]{:S(2)}) copy-start(f32[256]{0:T(256)} %param.12) | copy-start | bytes 3076
  3.4 0.7 %copy-start.2 = (f32[256]{0:T(256)S(1)}, f32[256]{0:T(256)}, u32[]{:S(2)}) copy-start(f32[256]{0:T(256)} %param.13) | copy-start | bytes 3076
  4.1 0.7 %copy-start.3 = (f32[32]{0:T(128)S(1)}, f32[32]{0:T(128)}, u32[]{:S(2)}) copy-start(f32[32]{0:T(128)} %param.15) | copy-start | bytes 388
  4.7 0.7 %copy-start.4 = (f32[32]{0:T(128)S(1)}, f32[32]{0:T(128)}, u32[]{:S(2)}) copy-start(f32[32]{0:T(128)} %param.17) | copy-start | bytes 388
  7.1 7.6 %collective-permute-start.2 = (bf16[256,128]{1,0:T(8,128)(2,1)S(1)}, bf16[256,128]{1,0:T(8,128)(2,1)S(1)}, u32[]{:S(2)}, u32[]{:S(2)}) collective-permute-start(bf16[256,128]{1,0:T(8,128)(2,1)S(1)} %get-tuple-element.7), channel_id=1, source_target_pairs={{0,24},{1,25},{2,26},{3,27},{4,28},{5,29},{6,30},{7,31},{8,16},{9,... | collective-permute-start | bytes 196616 | tf_op jit(solution)/shard_map/ppermute | solution.py:120
  12.2 5.6 %collective-permute-start.1 = (bf16[256,128]{1,0:T(8,128)(2,1)S(1)}, bf16[256,128]{1,0:T(8,128)(2,1)S(1)}, u32[]{:S(2)}, u32[]{:S(2)}) collective-permute-start(bf16[256,128]{1,0:T(8,128)(2,1)S(1)} %get-tuple-element.7), channel_id=1, source_target_pairs={{0,16},{1,17},{2,18},{3,19},{4,20},{5,21},{6,22},{7,23},{8,24},{9,... | collective-permute-start | bytes 196616 | tf_op jit(solution)/shard_map/ppermute | solution.py:120
  12.2 5.6 %collective-permute-start = (bf16[256,128]{1,0:T(8,128)(2,1)S(1)}, bf16[256,128]{1,0:T(8,128)(2,1)S(1)}, u32[]{:S(2)}, u32[]{:S(2)}) collective-permute-start(bf16[256,128]{1,0:T(8,128)(2,1)S(1)} %get-tuple-element.7), channel_id=1, source_target_pairs={{0,8},{1,9},{2,10},{3,11},{4,12},{5,13},{6,14},{7,15},{8,0},{9,1},... | collective-permute-start | bytes 196616 | tf_op jit(solution)/shard_map/ppermute | solution.py:120
  17.8 10.2 %collective-permute-start.5 = (bf16[4,256,128]{2,1,0:T(8,128)(2,1)S(1)}, bf16[4,256,128]{2,1,0:T(8,128)(2,1)S(1)}, u32[]{:S(2)}, u32[]{:S(2)}) collective-permute-start(bf16[4,256,128]{2,1,0:T(8,128)(2,1)S(1)} %pad_maximum_fusion.refs_0_), channel_id=1, source_target_pairs={{0,6},{1,7},{2,4},{3,5},{4,2},{5,3},{6,0},{7,1},{8,14},{9,15},{10,... | collective-permute-start | bytes 786440 | tf_op jit(solution)/shard_map/ppermute | solution.py:120
  20.3 12.5 %collective-permute-start.4 = (bf16[4,256,128]{2,1,0:T(8,128)(2,1)S(1)}, bf16[4,256,128]{2,1,0:T(8,128)(2,1)S(1)}, u32[]{:S(2)}, u32[]{:S(2)}) collective-permute-start(bf16[4,256,128]{2,1,0:T(8,128)(2,1)S(1)} %pad_maximum_fusion.refs_0_), channel_id=1, source_target_pairs={{0,4},{1,5},{2,6},{3,7},{4,0},{5,1},{6,2},{7,3},{8,12},{9,13},{10,... | collective-permute-start | bytes 786440 | tf_op jit(solution)/shard_map/ppermute | solution.py:120
  20.8 12.3 %collective-permute-start.3 = (bf16[4,256,128]{2,1,0:T(8,128)(2,1)S(1)}, bf16[4,256,128]{2,1,0:T(8,128)(2,1)S(1)}, u32[]{:S(2)}, u32[]{:S(2)}) collective-permute-start(bf16[4,256,128]{2,1,0:T(8,128)(2,1)S(1)} %pad_maximum_fusion.refs_0_), channel_id=1, source_target_pairs={{0,2},{1,3},{2,0},{3,1},{4,6},{5,7},{6,4},{7,5},{8,10},{9,11},{10,... | collective-permute-start | bytes 786440 | tf_op jit(solution)/shard_map/ppermute | solution.py:120
  21.3 27.6 %copy-start.7 = (f32[128]{0:T(128)S(1)}, f32[128]{0:T(128)}, u32[]{:S(2)}) copy-start(f32[128]{0:T(128)} %param.19) | copy-start | bytes 1540
  21.4 12.3 %all-to-all-start = ((bf16[32,8,128]{2,1,0:T(8,128)(2,1)}), bf16[32,8,128]{2,1,0:T(8,128)(2,1)S(1)}, u32[]{:S(2)}, u32[]{:S(2)}) async-start(bf16[32,8,128]{2,1,0:T(8,128)(2,1)} %get-tuple-element.8), calls=%async_computation | async-start | bytes 131072 | tf_op jit(solution)/shard_map/all_to_all | solution.py:143
  26.3 22.7 %copy-start.5 = (bf16[512,16,128]{2,1,0:T(8,128)(2,1)S(1)}, bf16[512,16,128]{2,1,0:T(8,128)(2,1)}, u32[]{:S(2)}) copy-start(bf16[512,16,128]{2,1,0:T(8,128)(2,1)} %refs_9_.1) | copy-start | bytes 6291460
  26.3 22.6 %collective-permute-start.6 = (bf16[4,256,128]{2,1,0:T(8,128)(2,1)S(1)}, bf16[4,256,128]{2,1,0:T(8,128)(2,1)S(1)}, u32[]{:S(2)}, u32[]{:S(2)}) collective-permute-start(bf16[4,256,128]{2,1,0:T(8,128)(2,1)S(1)} %pad_maximum_fusion.refs_0_), channel_id=1, source_target_pairs={{0,1},{1,0},{2,3},{3,2},{4,5},{5,4},{6,7},{7,6},{8,9},{9,8},{10,11... | collective-permute-start | bytes 786440 | tf_op jit(solution)/shard_map/ppermute | solution.py:120
  28.0 20.9 %collective-permute-start.9 = (bf16[4,256,128]{2,1,0:T(8,128)(2,1)S(1)}, bf16[4,256,128]{2,1,0:T(8,128)(2,1)}, u32[]{:S(2)}, u32[]{:S(2)}) collective-permute-start(bf16[4,256,128]{2,1,0:T(8,128)(2,1)S(1)} %collective-permute-done.5.refs_3_), channel_id=1, source_target_pairs={{0,1},{1,0},{2,3},{3,2},{4,5},{5,4},{6,7},{7,6},{8,9},{9,8},{10,11... | collective-permute-start | bytes 786440 | tf_op jit(solution)/shard_map/ppermute | solution.py:120
  32.8 16.1 %collective-permute-start.8 = (bf16[4,256,128]{2,1,0:T(8,128)(2,1)S(1)}, bf16[4,256,128]{2,1,0:T(8,128)(2,1)}, u32[]{:S(2)}, u32[]{:S(2)}) collective-permute-start(bf16[4,256,128]{2,1,0:T(8,128)(2,1)S(1)} %collective-permute-done.4.refs_2_), channel_id=1, source_target_pairs={{0,1},{1,0},{2,3},{3,2},{4,5},{5,4},{6,7},{7,6},{8,9},{9,8},{10,11... | collective-permute-start | bytes 786440 | tf_op jit(solution)/shard_map/ppermute | solution.py:120
  33.1 15.8 %collective-permute-start.7 = (bf16[4,256,128]{2,1,0:T(8,128)(2,1)S(1)}, bf16[4,256,128]{2,1,0:T(8,128)(2,1)}, u32[]{:S(2)}, u32[]{:S(2)}) collective-permute-start(bf16[4,256,128]{2,1,0:T(8,128)(2,1)S(1)} %collective-permute-done.3.refs_1_), channel_id=1, source_target_pairs={{0,1},{1,0},{2,3},{3,2},{4,5},{5,4},{6,7},{7,6},{8,9},{9,8},{10,11... | collective-permute-start | bytes 786440 | tf_op jit(solution)/shard_map/ppermute | solution.py:120
  33.7 1.0 %copy-start.6 = (bf16[1024,128]{1,0:T(8,128)(2,1)S(1)}, bf16[1024,128]{1,0:T(8,128)(2,1)}, u32[]{:S(2)}) copy-start(bf16[1024,128]{1,0:T(8,128)(2,1)} %final_ref.1) | copy-start | bytes 786436
where the time goes:
time: 61.7 us; the launch traced here: 61.2 us
  Pallas kernels  28.2 us (46%)
  starting transfers between devices  14.5 us (24%)
  waiting for transfers between devices  12 us (19%)
  local copies, waits for them, and re-layouts  6.34 us (10%)
    pallas_call x1, Pallas kernels, shards(): pl.pallas_call(_fold_kernel, grid=(n // step_d,), in_specs=[pl.BlockSpec(...  14.3 us
    pallas_call x1, Pallas kernels, shards(): pl.pallas_call(functools.partial(_band_kernel, count, groups), grid=(cols...  12.2 us
    ppermute x10, waiting for transfers between devices, _xor(): return lax.ppermute(x, 'row', [(i, i ^ mask) for i in range(n)])  11.6 us
    ppermute x10, starting transfers between devices, _xor(): return lax.ppermute(x, 'row', [(i, i ^ mask) for i in range(n)])  9.64 us
    unnamed x18, local copies, waits for them, and re-layouts  6.34 us
    all_to_all x1, starting transfers between devices, shards(): lax.all_to_all(right, 'row', split_axis=0, concat_axis=0, tiled=True)  4.89 us
    pallas_call x1, Pallas kernels, shards(): pl.pallas_call(_project_kernel, out_shape=(jax.ShapeDtypeStruct((half, LA...  1.71 us
  transfers between devices with their start and end apart: 11, of which 6 were waited for; matrix products, arithmetic and copies ran while one was open for 0% of the time, Pallas kernels for 23%

commit v1 on v0

v1 whole, which is shorter than its diff:
```python
import functools

import jax
import jax.numpy as jnp
from jax import lax
from jax.experimental import pallas as pl
from jax.experimental.pallas import tpu as pltpu
from jax.sharding import PartitionSpec as P

LANES = 128
CHANS = 32
NT = (((1,), (1,)), ((), ()))


def _stacked(weights, copies):
    c, q = weights.shape
    rows = []
    for k in range(copies):
        left = [jnp.zeros((c, k * q), weights.dtype)] if k else []
        right = [jnp.zeros((c, (copies - 1 - k) * q), weights.dtype)] if k < copies - 1 else []
        rows.append(jnp.concatenate(left + [weights] + right, axis=1))
    return jnp.concatenate(rows, axis=0)


def _project_kernel(*refs):
    sources, (left_ref, right_ref), held = refs[:7], refs[7:9], refs[9:16]
    sems = refs[16]
    copies = [pltpu.make_async_copy(a, b, sems.at[i]) for i, (a, b) in enumerate(zip(sources, held))]
    for copy in copies:
        copy.start()
    for copy in copies:
        copy.wait()
    x_ref, gain_ref, bias_ref, w1_ref, b1_ref, w2_ref, b2_ref = held
    band_half = left_ref.shape[0]
    n = right_ref.shape[0]
    feats = x_ref.shape[2]
    normed = []
    for s in range(2):
        x = x_ref[s].astype(jnp.float32)
        center = jnp.mean(x, axis=-1, keepdims=True)
        off = x - center
        spread = jnp.mean(off * off, axis=-1, keepdims=True)
        normed.append(off * lax.rsqrt(spread + 1e-05) * gain_ref[...] + bias_ref[...])
    low = [v[:band_half].astype(jnp.bfloat16) for v in normed]
    high = [v[band_half : 2 * band_half].astype(jnp.bfloat16) for v in normed]
    shift1 = jnp.concatenate([b1_ref[...]] * 4, axis=1)
    left = lax.dot_general(
        jnp.concatenate(low + high, axis=1), _stacked(w1_ref[...], 4), NT, preferred_element_type=jnp.float32
    )
    left_ref[...] = (left + shift1).astype(jnp.bfloat16)

    split = [v.reshape(n, 2, 8, feats) for v in normed]
    parts = [split[s][:, jh].reshape(n * 8, feats).astype(jnp.bfloat16) for jh in range(2) for s in range(2)]
    shift2 = jnp.concatenate([b2_ref[...]] * 4, axis=1)
    right = lax.dot_general(
        jnp.concatenate(parts, axis=1), _stacked(w2_ref[...], 4), NT, preferred_element_type=jnp.float32
    )
    right_ref[...] = (right + shift2).reshape(n, 8, LANES).astype(jnp.bfloat16)


def _order(me, half):
    row = lax.broadcasted_iota(jnp.int32, (4 * LANES, 8 * CHANS), 0)
    col = lax.broadcasted_iota(jnp.int32, (4 * LANES, 8 * CHANS), 1)
    device = (row // LANES) ^ (me % 4)
    wanted = (row % CHANS) * 8 + ((row // CHANS) % 2) * 4 + device
    hit = (wanted == col) & ((row // (2 * CHANS)) % 2 == half)
    return jnp.where(hit, 1.0, 0.0).astype(jnp.bfloat16)


def _fold_kernel(right_ref, final_ref, out_ref, order_ref):
    me = lax.axis_index("row")
    for h in range(2):
        order_ref[h] = _order(me, h)
    devices = right_ref.shape[0]
    groups = devices // 4
    rows = devices * 8
    block = right_ref[...].astype(jnp.float32).reshape(rows, LANES)
    row = lax.broadcasted_iota(jnp.int32, (2 * rows, 2 * rows), 0)
    col = lax.broadcasted_iota(jnp.int32, (2 * rows, 2 * rows), 1)
    device = (row // 8) % groups * 4 + row % 4
    wanted = ((row // 4) % 2) * rows + device * 8 + row // (8 * groups)
    spread = jnp.where(wanted == col, 1.0, 0.0).astype(jnp.bfloat16)
    lane = lax.broadcasted_iota(jnp.int32, block.shape, 1) // CHANS
    lhs = []
    for jh in range(2):
        both = jnp.concatenate([jnp.where(lane == jh * 2 + s, block, 0.0) for s in range(2)], axis=0)
        moved = jnp.dot(spread, both.astype(jnp.bfloat16), preferred_element_type=jnp.float32)
        lhs.append(moved.astype(jnp.bfloat16))
    lhs = jnp.concatenate(lhs, axis=0)

    def body(pair, _):
        rhs = []
        for k in range(2):
            at = pl.multiple_of(pair * 2 * CHANS + k * CHANS, CHANS)
            rhs.append(jnp.concatenate([final_ref[pl.ds(at, CHANS), :]] * 4, axis=0))
        res = jnp.dot(lhs, jnp.concatenate(rhs, axis=1), preferred_element_type=jnp.float32)
        for j in range(16):
            for g in range(groups):
                r = (j * groups + g) * 8
                tile = jnp.concatenate([res[r : r + 8, :LANES], res[r : r + 8, LANES:]], axis=0)
                at = pl.multiple_of(g * 8 * CHANS + pair * 16, 16)
                out_ref[pl.ds(at, 16), pl.ds(j * LANES, LANES)] = tile.astype(jnp.bfloat16)
        return 0

    lax.fori_loop(0, CHANS // 2, body, 0)


def _band_kernel(count, *refs):
    own_refs, other_refs = refs[:4], refs[4:8]
    t_ref, order_ref, pair_ref, shift_ref, out_ref, l_ref, acc_ref, done_ref, sems = refs[8:17]
    fetched = refs[17:]
    half = own_refs[0].shape[1]
    band, cols = pair_ref.shape[0], pair_ref.shape[1]
    me = lax.axis_index("row")
    wide = 8 * CHANS

    for zi in range(own_refs[0].shape[0]):
        for y in range(2):
            lhs = jnp.concatenate(
                [own_refs[2 * y][zi], other_refs[2 * y][zi], own_refs[2 * y + 1][zi], other_refs[2 * y + 1][zi]],
                axis=1,
            )
            group = (zi * 2 + y) ^ (me // 4)
            at = pl.ds(pl.multiple_of(group * wide, wide), wide)
            for h in range(2):
                moved = jnp.dot(lhs, order_ref[h], preferred_element_type=jnp.float32)
                l_ref[pl.ds(h * half, half), at] = moved.astype(jnp.bfloat16)

    tile = 256
    pitch = cols + 1

    def column(step, _):
        at = pl.ds(pl.multiple_of(step * tile, tile), tile)
        if fetched:
            pltpu.sync_copy(t_ref.at[:, at], fetched[0])
            rhs = fetched[0][...]
        else:
            rhs = t_ref[:, at]
        res = jnp.dot(l_ref[...], rhs, preferred_element_type=jnp.float32)
        for k in range(tile // LANES):
            acc_ref[pl.ds(step * (tile // LANES) + k, band, stride=pitch), :] = res[:, k * LANES : (k + 1) * LANES]
        return 0

    lax.fori_loop(0, cols * LANES // tile, column, 0)

    rows = 32
    shift = shift_ref[...]

    def finish(r, _):
        for k in range(rows):
            i = r * rows + k
            total = acc_ref[pl.ds(i * pitch, cols), :] * (1.0 / count) + shift
            done_ref[i] = (pair_ref[i].astype(jnp.float32) + total).astype(jnp.bfloat16)
        at = pl.ds(pl.multiple_of(r * rows, rows), rows)
        pltpu.make_async_copy(done_ref.at[at], out_ref.at[at], sems.at[r]).start()
        return 0

    lax.fori_loop(0, band // rows, finish, 0)

    def drain(r, _):
        at = pl.ds(pl.multiple_of(r * rows, rows), rows)
        pltpu.make_async_copy(done_ref.at[at], out_ref.at[at], sems.at[r]).wait()
        return 0

    lax.fori_loop(0, band // rows, drain, 0)


def _xor(x, mask, n):
    return lax.ppermute(x, "row", [(i, i ^ mask) for i in range(n)])


def shards(n, alignment, pair, gain, bias, w1, b1, w2, b2, final, shift):
    seqs, residues, feats = alignment.shape
    band, cols, zdim = pair.shape
    half = band // 2
    count = float(seqs * n)
    small = n <= 32
    params = pltpu.CompilerParams(vmem_limit_bytes=(24 if small else 48) * 1024 * 1024)
    anywhere = pl.BlockSpec(memory_space=pl.ANY)
    vmem = pl.BlockSpec(memory_space=pltpu.VMEM)

    sources = [
        alignment, gain.reshape(1, -1), bias.reshape(1, -1), w1.T, b1.reshape(1, -1), w2.T, b2.reshape(1, -1)
    ]
    left, right = pl.pallas_call(
        _project_kernel,
        in_specs=[pl.BlockSpec(memory_space=pltpu.HBM)] * 7,
        out_specs=(vmem, vmem),
        out_shape=(
            jax.ShapeDtypeStruct((half, LANES), jnp.bfloat16),
            jax.ShapeDtypeStruct((n, 8, LANES), jnp.bfloat16),
        ),
        scratch_shapes=[pltpu.VMEM(a.shape, a.dtype) for a in sources] + [pltpu.SemaphoreType.DMA((7,))],
        compiler_params=pltpu.CompilerParams(vmem_limit_bytes=60 * 1024 * 1024),
        cost_estimate=pl.CostEstimate(
            flops=4 * seqs * residues * feats * CHANS, bytes_accessed=2 * seqs * residues * feats, transcendentals=0
        ),
    )(*sources)

    right = lax.all_to_all(right, "row", split_axis=0, concat_axis=0, tiled=True)

    line = [left] + [_xor(left, m, n) for m in range(8, n, 8)]
    line, right = lax.optimization_barrier((jnp.stack(line), right))
    plane = [_xor(line, m, n) for m in (2, 4, 6)]

    k = n * 2 * CHANS
    part = 32
    fold_cost = pl.CostEstimate(
        flops=2 * n * 32 * 256 * CHANS * zdim, bytes_accessed=2 * n * 2 * CHANS * cols * zdim, transcendentals=0
    )
    fold_out = (
        jax.ShapeDtypeStruct((k, cols * zdim), jnp.bfloat16),
        jax.ShapeDtypeStruct((2, 4 * LANES, 8 * CHANS), jnp.bfloat16),
    )
    if small:
        folded, order = pl.pallas_call(
            _fold_kernel,
            in_specs=[vmem, vmem],
            out_specs=(vmem, vmem),
            out_shape=fold_out,
            compiler_params=params,
            cost_estimate=fold_cost,
        )(right, final)
    else:
        folded, order = pl.pallas_call(
            _fold_kernel,
            grid=(n // part,),
            in_specs=[
                pl.BlockSpec((part, 8, LANES), lambda i: (i, 0, 0)),
                pl.BlockSpec(final.shape, lambda i: (0, 0)),
            ],
            out_specs=(
                pl.BlockSpec((part * 2 * CHANS, cols * zdim), lambda i: (i, 0)),
                pl.BlockSpec((2, 4 * LANES, 8 * CHANS), lambda i: (0, 0, 0)),
            ),
            out_shape=fold_out,
            compiler_params=params,
            cost_estimate=fold_cost,
        )(right, final)

    plane, folded = lax.optimization_barrier((plane, folded))
    own = [line] + plane
    other = [_xor(o, 1, n) for o in own]

    return pl.pallas_call(
        functools.partial(_band_kernel, count),
        in_specs=[vmem] * 8 + [vmem if small else anywhere] + [vmem] * 3,
        out_specs=anywhere,
        out_shape=jax.ShapeDtypeStruct(pair.shape, jnp.bfloat16),
        scratch_shapes=[
            pltpu.VMEM((band, k), jnp.bfloat16),
            pltpu.VMEM((band * (cols + 1), zdim), jnp.float32),
            pltpu.VMEM(pair.shape, jnp.bfloat16),
            pltpu.SemaphoreType.DMA((band // 32,)),
        ]
        + ([] if small else [pltpu.VMEM((k, 256), jnp.bfloat16)]),
        compiler_params=params,
        cost_estimate=pl.CostEstimate(
            flops=2 * band * k * cols * zdim, bytes_accessed=2 * k * cols * zdim, transcendentals=0
        ),
    )(*own, *other, folded, order, pair, shift.reshape(1, -1))


def solution(mesh):
    placed = (P(("group", "row"), None, None), P("group", "row", None)) + (P(),) * 8
    return jax.shard_map(
        functools.partial(shards, mesh.shape["row"]),
        mesh=mesh,
        in_specs=placed,
        out_specs=P("group", "row", None),
        check_vma=False,
    )
```

time: 61.7 us -> 47.2 us (0.76)
  Pallas kernels: 28.2 us -> 17.1 us
  local copies, waits for them, and re-layouts: 6.34 us -> 0.96 us
  starting transfers between devices: 14.5 us -> 15.8 us
  other arithmetic: 0.04 us -> 0.88 us
    pallas_call x3, Pallas kernels: 28.2 us -> 17.1 us  [the longest x1 8.75 us: shards(): pl.pallas_call(functools.partial(_band_kernel, count), in_specs=[vmem] *...]
    all_to_all x1, waiting for transfers between devices: 0.37 us -> 6.47 us  [shards(): lax.all_to_all(right, 'row', split_axis=0, concat_axis=0, tiled=True)]
    ppermute x10, waiting for transfers between devices: 11.6 us -> 5.66 us  [_xor(): return lax.ppermute(x, 'row', [(i, i ^ mask) for i in range(n)])]
    unnamed x18 -> x6, local copies, waits for them, and re-layouts: 6.34 us -> 0.96 us
    all_to_all x1, starting transfers between devices: 4.89 us -> 5.99 us  [shards(): lax.all_to_all(right, 'row', split_axis=0, concat_axis=0, tiled=True)]
    another operation x1, other arithmetic: 0.04 us -> 0.88 us  [shards(): line, right = lax.optimization_barrier((jnp.stack(line), right))]
  transfers between devices with their start and end apart: 11 -> 11, of which waited for: 6 -> 5; matrix products, arithmetic and copies ran while one was open for 0% -> 2% of each run, Pallas kernels for 23% -> 13%
where the time goes in v1:
time: 47.2 us; the launch traced here: 47 us
  Pallas kernels  17.1 us (36%)
  starting transfers between devices  15.8 us (33%)
  waiting for transfers between devices  12.1 us (26%)
  local copies, waits for them, and re-layouts  0.96 us (2%)
  other arithmetic  0.88 us (2%)
    ppermute x10, starting transfers between devices, _xor(): return lax.ppermute(x, 'row', [(i, i ^ mask) for i in range(n)])  9.76 us
    pallas_call x1, Pallas kernels, shards(): pl.pallas_call(functools.partial(_band_kernel, count), in_specs=[vmem] *...  8.75 us
    all_to_all x1, waiting for transfers between devices, shards(): lax.all_to_all(right, 'row', split_axis=0, concat_axis=0, tiled=True)  6.47 us
    all_to_all x1, starting transfers between devices, shards(): lax.all_to_all(right, 'row', split_axis=0, concat_axis=0, tiled=True)  5.99 us
    pallas_call x1, Pallas kernels, shards(): pl.pallas_call(_fold_kernel, in_specs=[vmem, vmem], out_specs=(vmem, vmem...  5.92 us
    ppermute x10, waiting for transfers between devices, _xor(): return lax.ppermute(x, 'row', [(i, i ^ mask) for i in range(n)])  5.66 us
    pallas_call x1, Pallas kernels, shards(): pl.pallas_call(_project_kernel, in_specs=[pl.BlockSpec(memory_space=pltpu...  2.48 us
    unnamed x6, local copies, waits for them, and re-layouts  0.96 us
  transfers between devices with their start and end apart: 11, of which 5 were waited for; matrix products, arithmetic and copies ran while one was open for 2% of the time, Pallas kernels for 13%

profile of v1, /device:TPU:0, one launch (start us, length us, event | category | flops | bytes accessed | tf_op | source)
XLA Modules:
  0.0 47.0 jit_solution(13460852436325536165)
XLA Ops:
  0.0 2.5 %shard_map.100 = (bf16[256,128]{1,0:T(8,128)(2,1)}, bf16[32,8,128]{2,1,0:T(8,128)(2,1)}) custom-call(bf16[2,512,256]{2,1,0:T(8,128)(2,1)} %refs_0_.1, f32[1,256]{1,0:T(1,128)} %bitcast.18, f32[1,256]{1,0:T(1,128)} %bitcast.19, bf16[32,256]{1,0:T(8,128)(2,1)} %bitcast.16, f32[1,32]{1,0:T(1,128)} %bitcast.20, bf16[32,256]{1,0:T(8,128)(2,1)} %bitcast.17, ...), custom_call_target="tpu_custom_call" | custom-call | flops 33554432 | bytes 524288 | tf_op jit(solution)/shard_map/pallas_call | solution.py:185
  2.5 5.1 %collective-permute-start.2 = (bf16[256,128]{1,0:T(8,128)(2,1)}, bf16[256,128]{1,0:T(8,128)(2,1)S(1)}, u32[]{:S(2)}, u32[]{:S(2)}) collective-permute-start(bf16[256,128]{1,0:T(8,128)(2,1)} %get-tuple-element.15), channel_id=1, source_target_pairs={{0,24},{1,25},{2,26},{3,27},{4,28},{5,29},{6,30},{7,31},{8,16},{9,... | collective-permute-start | bytes 196616 | tf_op jit(solution)/shard_map/ppermute | solution.py:169
  7.6 0.0 collective-permute-start.1
  7.6 0.6 %collective-permute-start = (bf16[256,128]{1,0:T(8,128)(2,1)}, bf16[256,128]{1,0:T(8,128)(2,1)S(1)}, u32[]{:S(2)}, u32[]{:S(2)}) collective-permute-start(bf16[256,128]{1,0:T(8,128)(2,1)} %get-tuple-element.15), channel_id=1, source_target_pairs={{0,8},{1,9},{2,10},{3,11},{4,12},{5,13},{6,14},{7,15},{8,0},{9,1},... | collective-permute-start | bytes 196616 | tf_op jit(solution)/shard_map/ppermute | solution.py:169
  8.2 6.0 %all-to-all-start = ((bf16[32,8,128]{2,1,0:T(8,128)(2,1)}), bf16[32,8,128]{2,1,0:T(8,128)(2,1)S(1)}, u32[]{:S(2)}, u32[]{:S(2)}) async-start(bf16[32,8,128]{2,1,0:T(8,128)(2,1)} %get-tuple-element.16), calls=%async_computation | async-start | bytes 131072 | tf_op jit(solution)/shard_map/all_to_all | solution.py:200
  14.2 0.0 collective-permute-done.2
  14.3 0.0 collective-permute-done.1
  14.3 0.0 collective-permute-done
  14.3 0.0 copy-start.2
  14.3 0.9 %pad_maximum_fusion.refs_0_ = bf16[4,256,128]{2,1,0:T(8,128)(2,1)S(1)} fusion(bf16[1,256,128]{2,1,0:T(8,128)(2,1)S(1)} %bitcast.13, bf16[1,256,128]{2,1,0:T(8,128)(2,1)S(1)} %bitcast.14, bf16[1,256,128]{2,1,0:T(8,128)(2,1)S(1)} %bitcast.15, bf16[1,256,128]{2,1,0:T(8,128)(2,1)} %bitcast.12), kind=kLoop, calls=%fused_computation | loop fusion | flops 393216 | bytes 524288 | tf_op jit(solution)/shard_map/stack | solution.py:203
  15.2 0.0 copy-start
  15.2 6.5 %all-to-all-done.right_ref = bf16[32,8,128]{2,1,0:T(8,128)(2,1)S(1)} async-done(((bf16[32,8,128]{2,1,0:T(8,128)(2,1)}), bf16[32,8,128]{2,1,0:T(8,128)(2,1)S(1)}, u32[]{:S(2)}, u32[]{:S(2)}) %all-to-all-start) | async-done | bytes 65568 | tf_op jit(solution)/shard_map/all_to_all | solution.py:200
  21.7 0.7 %collective-permute-start.5 = (bf16[4,256,128]{2,1,0:T(8,128)(2,1)S(1)}, bf16[4,256,128]{2,1,0:T(8,128)(2,1)S(1)}, u32[]{:S(2)}, u32[]{:S(2)}) collective-permute-start(bf16[4,256,128]{2,1,0:T(8,128)(2,1)S(1)} %pad_maximum_fusion.refs_0_), channel_id=1, source_target_pairs={{0,6},{1,7},{2,4},{3,5},{4,2},{5,3},{6,0},{7,1},{8,14},{9,15},{10,... | collective-permute-start | bytes 786440 | tf_op jit(solution)/shard_map/ppermute | solution.py:169
  22.4 1.2 %collective-permute-start.4 = (bf16[4,256,128]{2,1,0:T(8,128)(2,1)S(1)}, bf16[4,256,128]{2,1,0:T(8,128)(2,1)S(1)}, u32[]{:S(2)}, u32[]{:S(2)}) collective-permute-start(bf16[4,256,128]{2,1,0:T(8,128)(2,1)S(1)} %pad_maximum_fusion.refs_0_), channel_id=1, source_target_pairs={{0,4},{1,5},{2,6},{3,7},{4,0},{5,1},{6,2},{7,3},{8,12},{9,13},{10,... | collective-permute-start | bytes 786440 | tf_op jit(solution)/shard_map/ppermute | solution.py:169
  23.6 1.6 %collective-permute-start.3 = (bf16[4,256,128]{2,1,0:T(8,128)(2,1)S(1)}, bf16[4,256,128]{2,1,0:T(8,128)(2,1)S(1)}, u32[]{:S(2)}, u32[]{:S(2)}) collective-permute-start(bf16[4,256,128]{2,1,0:T(8,128)(2,1)S(1)} %pad_maximum_fusion.refs_0_), channel_id=1, source_target_pairs={{0,2},{1,3},{2,0},{3,1},{4,6},{5,7},{6,4},{7,5},{8,10},{9,11},{10,... | collective-permute-start | bytes 786440 | tf_op jit(solution)/shard_map/ppermute | solution.py:169
  25.1 0.0 collective-permute-start.6
  25.1 0.0 copy-start.1
  25.2 0.9 %copy-done.1 = bf16[1024,128]{1,0:T(8,128)(2,1)S(1)} copy-done((bf16[1024,128]{1,0:T(8,128)(2,1)S(1)}, bf16[1024,128]{1,0:T(8,128)(2,1)}, u32[]{:S(2)}) %copy-start.1) | copy-done | bytes 262168
  26.1 5.9 %shard_map.101 = (bf16[2048,2048]{1,0:T(8,128)(2,1)S(1)}, bf16[2,512,256]{2,1,0:T(8,128)(2,1)S(1)}) custom-call(bf16[32,8,128]{2,1,0:T(8,128)(2,1)S(1)} %all-to-all-done.right_ref, bf16[1024,128]{1,0:T(8,128)(2,1)S(1)} %copy-done.1), custom_call_target="tpu_custom_call" | custom-call | flops 2147483648 | bytes 8388608 | tf_op jit(solution)/shard_map/pallas_call | solution.py:216
  32.0 0.0 collective-permute-done.5.refs_3_
  32.0 3.9 %collective-permute-done.4.refs_2_ = bf16[4,256,128]{2,1,0:T(8,128)(2,1)S(1)} collective-permute-done((bf16[4,256,128]{2,1,0:T(8,128)(2,1)S(1)}, bf16[4,256,128]{2,1,0:T(8,128)(2,1)S(1)}, u32[]{:S(2)}, u32[]{:S(2)}) %collective-permute-start.4) | collective-permute-done | bytes 262176 | tf_op jit(solution)/shard_map/ppermute | solution.py:169
  35.9 0.0 collective-permute-done.3.refs_1_
  35.9 0.0 collective-permute-start.7
  35.9 0.5 %collective-permute-start.8 = (bf16[4,256,128]{2,1,0:T(8,128)(2,1)S(1)}, bf16[4,256,128]{2,1,0:T(8,128)(2,1)S(1)}, u32[]{:S(2)}, u32[]{:S(2)}) collective-permute-start(bf16[4,256,128]{2,1,0:T(8,128)(2,1)S(1)} %collective-permute-done.4.refs_2_), channel_id=1, source_target_pairs={{0,1},{1,0},{2,3},{3,2},{4,5},{5,4},{6,7},{7,6},{8,9},{9,8},{10,11... | collective-permute-start | bytes 786440 | tf_op jit(solution)/shard_map/ppermute | solution.py:169
  36.4 0.0 collective-permute-start.9
  36.4 0.0 collective-permute-done.6.refs_4_
  36.4 1.0 %collective-permute-done.7.refs_5_ = bf16[4,256,128]{2,1,0:T(8,128)(2,1)S(1)} collective-permute-done((bf16[4,256,128]{2,1,0:T(8,128)(2,1)S(1)}, bf16[4,256,128]{2,1,0:T(8,128)(2,1)S(1)}, u32[]{:S(2)}, u32[]{:S(2)}) %collective-permute-start.7) | collective-permute-done | bytes 262176 | tf_op jit(solution)/shard_map/ppermute | solution.py:169
  37.5 0.4 collective-permute-done.8.refs_6_
  37.8 0.4 collective-permute-done.9.refs_7_
  38.2 0.0 copy-done.2
  38.2 0.0 copy-done
  38.2 8.7 %shard_map.102 = bf16[512,16,128]{2,1,0:T(8,128)(2,1)} custom-call(bf16[4,256,128]{2,1,0:T(8,128)(2,1)S(1)} %pad_maximum_fusion.refs_0_, bf16[4,256,128]{2,1,0:T(8,128)(2,1)S(1)} %collective-permute-done.3.refs_1_, bf16[4,256,128]{2,1,0:T(8,128)(2,1)S(1)} %collective-permute-done.4.refs_2_, bf16[4,256,128]{2,1,0:T(8,128)(2,1)S(1)} %collective-permute-done.5.refs_3_, ...), custom_call_target="tpu_custom_call" | custom-call | flops 4294967296 | bytes 8388608 | tf_op jit(solution)/shard_map/pallas_call | solution.py:245
Async XLA Ops:
  2.5 11.8 %collective-permute-start.2 = (bf16[256,128]{1,0:T(8,128)(2,1)}, bf16[256,128]{1,0:T(8,128)(2,1)S(1)}, u32[]{:S(2)}, u32[]{:S(2)}) collective-permute-start(bf16[256,128]{1,0:T(8,128)(2,1)} %get-tuple-element.15), channel_id=1, source_target_pairs={{0,24},{1,25},{2,26},{3,27},{4,28},{5,29},{6,30},{7,31},{8,16},{9,... | collective-permute-start | bytes 196616 | tf_op jit(solution)/shard_map/ppermute | solution.py:169
  7.6 6.7 %collective-permute-start.1 = (bf16[256,128]{1,0:T(8,128)(2,1)}, bf16[256,128]{1,0:T(8,128)(2,1)S(1)}, u32[]{:S(2)}, u32[]{:S(2)}) collective-permute-start(bf16[256,128]{1,0:T(8,128)(2,1)} %get-tuple-element.15), channel_id=1, source_target_pairs={{0,16},{1,17},{2,18},{3,19},{4,20},{5,21},{6,22},{7,23},{8,24},{9,... | collective-permute-start | bytes 196616 | tf_op jit(solution)/shard_map/ppermute | solution.py:169
  7.6 6.7 %collective-permute-start = (bf16[256,128]{1,0:T(8,128)(2,1)}, bf16[256,128]{1,0:T(8,128)(2,1)S(1)}, u32[]{:S(2)}, u32[]{:S(2)}) collective-permute-start(bf16[256,128]{1,0:T(8,128)(2,1)} %get-tuple-element.15), channel_id=1, source_target_pairs={{0,8},{1,9},{2,10},{3,11},{4,12},{5,13},{6,14},{7,15},{8,0},{9,1},... | collective-permute-start | bytes 196616 | tf_op jit(solution)/shard_map/ppermute | solution.py:169
  8.2 13.4 %all-to-all-start = ((bf16[32,8,128]{2,1,0:T(8,128)(2,1)}), bf16[32,8,128]{2,1,0:T(8,128)(2,1)S(1)}, u32[]{:S(2)}, u32[]{:S(2)}) async-start(bf16[32,8,128]{2,1,0:T(8,128)(2,1)} %get-tuple-element.16), calls=%async_computation | async-start | bytes 131072 | tf_op jit(solution)/shard_map/all_to_all | solution.py:200
  14.3 23.9 %copy-start.2 = (f32[128]{0:T(128)S(1)}, f32[128]{0:T(128)}, u32[]{:S(2)}) copy-start(f32[128]{0:T(128)} %param.19) | copy-start | bytes 1540
  15.2 23.0 %copy-start = (bf16[512,16,128]{2,1,0:T(8,128)(2,1)S(1)}, bf16[512,16,128]{2,1,0:T(8,128)(2,1)}, u32[]{:S(2)}) copy-start(bf16[512,16,128]{2,1,0:T(8,128)(2,1)} %refs_10_.1) | copy-start | bytes 6291460
  21.7 10.4 %collective-permute-start.5 = (bf16[4,256,128]{2,1,0:T(8,128)(2,1)S(1)}, bf16[4,256,128]{2,1,0:T(8,128)(2,1)S(1)}, u32[]{:S(2)}, u32[]{:S(2)}) collective-permute-start(bf16[4,256,128]{2,1,0:T(8,128)(2,1)S(1)} %pad_maximum_fusion.refs_0_), channel_id=1, source_target_pairs={{0,6},{1,7},{2,4},{3,5},{4,2},{5,3},{6,0},{7,1},{8,14},{9,15},{10,... | collective-permute-start | bytes 786440 | tf_op jit(solution)/shard_map/ppermute | solution.py:169
  22.4 13.5 %collective-permute-start.4 = (bf16[4,256,128]{2,1,0:T(8,128)(2,1)S(1)}, bf16[4,256,128]{2,1,0:T(8,128)(2,1)S(1)}, u32[]{:S(2)}, u32[]{:S(2)}) collective-permute-start(bf16[4,256,128]{2,1,0:T(8,128)(2,1)S(1)} %pad_maximum_fusion.refs_0_), channel_id=1, source_target_pairs={{0,4},{1,5},{2,6},{3,7},{4,0},{5,1},{6,2},{7,3},{8,12},{9,13},{10,... | collective-permute-start | bytes 786440 | tf_op jit(solution)/shard_map/ppermute | solution.py:169
  23.6 12.4 %collective-permute-start.3 = (bf16[4,256,128]{2,1,0:T(8,128)(2,1)S(1)}, bf16[4,256,128]{2,1,0:T(8,128)(2,1)S(1)}, u32[]{:S(2)}, u32[]{:S(2)}) collective-permute-start(bf16[4,256,128]{2,1,0:T(8,128)(2,1)S(1)} %pad_maximum_fusion.refs_0_), channel_id=1, source_target_pairs={{0,2},{1,3},{2,0},{3,1},{4,6},{5,7},{6,4},{7,5},{8,10},{9,11},{10,... | collective-permute-start | bytes 786440 | tf_op jit(solution)/shard_map/ppermute | solution.py:169
  25.1 11.3 %collective-permute-start.6 = (bf16[4,256,128]{2,1,0:T(8,128)(2,1)S(1)}, bf16[4,256,128]{2,1,0:T(8,128)(2,1)S(1)}, u32[]{:S(2)}, u32[]{:S(2)}) collective-permute-start(bf16[4,256,128]{2,1,0:T(8,128)(2,1)S(1)} %pad_maximum_fusion.refs_0_), channel_id=1, source_target_pairs={{0,1},{1,0},{2,3},{3,2},{4,5},{5,4},{6,7},{7,6},{8,9},{9,8},{10,11... | collective-permute-start | bytes 786440 | tf_op jit(solution)/shard_map/ppermute | solution.py:169
  25.1 1.0 %copy-start.1 = (bf16[1024,128]{1,0:T(8,128)(2,1)S(1)}, bf16[1024,128]{1,0:T(8,128)(2,1)}, u32[]{:S(2)}) copy-start(bf16[1024,128]{1,0:T(8,128)(2,1)} %final_ref.1) | copy-start | bytes 786436
  35.9 1.5 %collective-permute-start.7 = (bf16[4,256,128]{2,1,0:T(8,128)(2,1)S(1)}, bf16[4,256,128]{2,1,0:T(8,128)(2,1)S(1)}, u32[]{:S(2)}, u32[]{:S(2)}) collective-permute-start(bf16[4,256,128]{2,1,0:T(8,128)(2,1)S(1)} %collective-permute-done.3.refs_1_), channel_id=1, source_target_pairs={{0,1},{1,0},{2,3},{3,2},{4,5},{5,4},{6,7},{7,6},{8,9},{9,8},{10,11... | collective-permute-start | bytes 786440 | tf_op jit(solution)/shard_map/ppermute | solution.py:169
  35.9 1.9 %collective-permute-start.8 = (bf16[4,256,128]{2,1,0:T(8,128)(2,1)S(1)}, bf16[4,256,128]{2,1,0:T(8,128)(2,1)S(1)}, u32[]{:S(2)}, u32[]{:S(2)}) collective-permute-start(bf16[4,256,128]{2,1,0:T(8,128)(2,1)S(1)} %collective-permute-done.4.refs_2_), channel_id=1, source_target_pairs={{0,1},{1,0},{2,3},{3,2},{4,5},{5,4},{6,7},{7,6},{8,9},{9,8},{10,11... | collective-permute-start | bytes 786440 | tf_op jit(solution)/shard_map/ppermute | solution.py:169
  36.4 1.8 %collective-permute-start.9 = (bf16[4,256,128]{2,1,0:T(8,128)(2,1)S(1)}, bf16[4,256,128]{2,1,0:T(8,128)(2,1)S(1)}, u32[]{:S(2)}, u32[]{:S(2)}) collective-permute-start(bf16[4,256,128]{2,1,0:T(8,128)(2,1)S(1)} %collective-permute-done.5.refs_3_), channel_id=1, source_target_pairs={{0,1},{1,0},{2,3},{3,2},{4,5},{5,4},{6,7},{7,6},{8,9},{9,8},{10,11... | collective-permute-start | bytes 786440 | tf_op jit(solution)/shard_map/ppermute | solution.py:169

commit v2 on v1

--- a/solution.py
+++ b/solution.py
@@ -130,7 +130,7 @@
     pitch = cols + 1
 
     def column(step, _):
-        at = pl.ds(pl.multiple_of(step * tile, tile), tile)
+        at = pl.ds(step * tile if isinstance(step, int) else pl.multiple_of(step * tile, tile), tile)
         if fetched:
             pltpu.sync_copy(t_ref.at[:, at], fetched[0])
             rhs = fetched[0][...]
@@ -141,7 +141,11 @@
             acc_ref[pl.ds(step * (tile // LANES) + k, band, stride=pitch), :] = res[:, k * LANES : (k + 1) * LANES]
         return 0
 
-    lax.fori_loop(0, cols * LANES // tile, column, 0)
+    if fetched:
+        lax.fori_loop(0, cols * LANES // tile, column, 0)
+    else:
+        for step in range(cols * LANES // tile):
+            column(step, 0)
 
     rows = 32
     shift = shift_ref[...]
@@ -200,7 +204,7 @@
     right = lax.all_to_all(right, "row", split_axis=0, concat_axis=0, tiled=True)
 
     line = [left] + [_xor(left, m, n) for m in range(8, n, 8)]
-    line, right = lax.optimization_barrier((jnp.stack(line), right))
+    line = jnp.stack(line)
     plane = [_xor(line, m, n) for m in (2, 4, 6)]
 
     k = n * 2 * CHANS

time: 47.2 us -> 40.6 us (0.86)
  waiting for transfers between devices: 12.1 us -> 6.85 us
  Pallas kernels: 17.1 us -> 15.7 us
    all_to_all x1, waiting for transfers between devices: 6.47 us -> 2.97 us  [shards(): lax.all_to_all(right, 'row', split_axis=0, concat_axis=0, tiled=True)]
    ppermute x10, waiting for transfers between devices: 5.66 us -> 3.88 us  [_xor(): return lax.ppermute(x, 'row', [(i, i ^ mask) for i in range(n)])]
    pallas_call x1, Pallas kernels: 8.75 us -> 7.32 us  [shards(): pl.pallas_call(functools.partial(_band_kernel, count), in_specs=[vmem] *...]
  transfers between devices with their start and end apart: 11 -> 11, of which waited for: 5 -> 5; matrix products, arithmetic and copies ran while one was open for 2% -> 2% of each run, Pallas kernels for 13% -> 15%
where the time goes in v2:
time: 40.6 us; the launch traced here: 40.3 us
  starting transfers between devices  15.8 us (39%)
  Pallas kernels  15.7 us (39%)
  waiting for transfers between devices  6.85 us (17%)
  local copies, waits for them, and re-layouts  0.96 us (2%)
  other arithmetic  0.88 us (2%)
    ppermute x10, starting transfers between devices, _xor(): return lax.ppermute(x, 'row', [(i, i ^ mask) for i in range(n)])  9.83 us
    pallas_call x1, Pallas kernels, shards(): pl.pallas_call(functools.partial(_band_kernel, count), in_specs=[vmem] *...  7.32 us
    all_to_all x1, starting transfers between devices, shards(): lax.all_to_all(right, 'row', split_axis=0, concat_axis=0, tiled=True)  5.99 us
    pallas_call x1, Pallas kernels, shards(): pl.pallas_call(_fold_kernel, in_specs=[vmem, vmem], out_specs=(vmem, vmem...  5.92 us
    ppermute x10, waiting for transfers between devices, _xor(): return lax.ppermute(x, 'row', [(i, i ^ mask) for i in range(n)])  3.88 us
    all_to_all x1, waiting for transfers between devices, shards(): lax.all_to_all(right, 'row', split_axis=0, concat_axis=0, tiled=True)  2.97 us
    pallas_call x1, Pallas kernels, shards(): pl.pallas_call(_project_kernel, in_specs=[pl.BlockSpec(memory_space=pltpu...  2.48 us
    unnamed x6, local copies, waits for them, and re-layouts  0.96 us
  transfers between devices with their start and end apart: 11, of which 5 were waited for; matrix products, arithmetic and copies ran while one was open for 2% of the time, Pallas kernels for 15%

profile of v2, /device:TPU:0, one launch (start us, length us, event | category | flops | bytes accessed | tf_op | source)
XLA Modules:
  0.0 40.3 jit_solution(12553932070630861087)
XLA Ops:
  0.0 2.5 %shard_map.100 = (bf16[256,128]{1,0:T(8,128)(2,1)}, bf16[32,8,128]{2,1,0:T(8,128)(2,1)}) custom-call(bf16[2,512,256]{2,1,0:T(8,128)(2,1)} %refs_0_.1, f32[1,256]{1,0:T(1,128)} %bitcast.18, f32[1,256]{1,0:T(1,128)} %bitcast.19, bf16[32,256]{1,0:T(8,128)(2,1)} %bitcast.16, f32[1,32]{1,0:T(1,128)} %bitcast.20, bf16[32,256]{1,0:T(8,128)(2,1)} %bitcast.17, ...), custom_call_target="tpu_custom_call" | custom-call | flops 33554432 | bytes 524288 | tf_op jit(solution)/shard_map/pallas_call | solution.py:189
  2.5 5.1 %collective-permute-start.2 = (bf16[256,128]{1,0:T(8,128)(2,1)}, bf16[256,128]{1,0:T(8,128)(2,1)S(1)}, u32[]{:S(2)}, u32[]{:S(2)}) collective-permute-start(bf16[256,128]{1,0:T(8,128)(2,1)} %get-tuple-element.13), channel_id=1, source_target_pairs={{0,24},{1,25},{2,26},{3,27},{4,28},{5,29},{6,30},{7,31},{8,16},{9,... | collective-permute-start | bytes 196616 | tf_op jit(solution)/shard_map/ppermute | solution.py:173
  7.6 0.0 collective-permute-start.1
  7.6 0.6 %collective-permute-start = (bf16[256,128]{1,0:T(8,128)(2,1)}, bf16[256,128]{1,0:T(8,128)(2,1)S(1)}, u32[]{:S(2)}, u32[]{:S(2)}) collective-permute-start(bf16[256,128]{1,0:T(8,128)(2,1)} %get-tuple-element.13), channel_id=1, source_target_pairs={{0,8},{1,9},{2,10},{3,11},{4,12},{5,13},{6,14},{7,15},{8,0},{9,1},... | collective-permute-start | bytes 196616 | tf_op jit(solution)/shard_map/ppermute | solution.py:173
  8.2 6.0 %all-to-all-start = ((bf16[32,8,128]{2,1,0:T(8,128)(2,1)}), bf16[32,8,128]{2,1,0:T(8,128)(2,1)S(1)}, u32[]{:S(2)}, u32[]{:S(2)}) async-start(bf16[32,8,128]{2,1,0:T(8,128)(2,1)} %get-tuple-element.14), calls=%async_computation | async-start | bytes 131072 | tf_op jit(solution)/shard_map/all_to_all | solution.py:204
  14.2 0.0 collective-permute-done.2
  14.3 0.0 collective-permute-done.1
  14.3 0.0 collective-permute-done
  14.3 0.0 copy-start.2
  14.3 0.9 %pad_maximum_fusion.refs_0_ = bf16[4,256,128]{2,1,0:T(8,128)(2,1)S(1)} fusion(bf16[1,256,128]{2,1,0:T(8,128)(2,1)S(1)} %bitcast.13, bf16[1,256,128]{2,1,0:T(8,128)(2,1)S(1)} %bitcast.14, bf16[1,256,128]{2,1,0:T(8,128)(2,1)S(1)} %bitcast.15, bf16[1,256,128]{2,1,0:T(8,128)(2,1)} %bitcast.12), kind=kLoop, calls=%fused_computation | loop fusion | flops 393216 | bytes 524288 | tf_op jit(solution)/shard_map/stack | solution.py:207
  15.2 0.0 copy-start
  15.2 2.7 %collective-permute-start.5 = (bf16[4,256,128]{2,1,0:T(8,128)(2,1)S(1)}, bf16[4,256,128]{2,1,0:T(8,128)(2,1)S(1)}, u32[]{:S(2)}, u32[]{:S(2)}) collective-permute-start(bf16[4,256,128]{2,1,0:T(8,128)(2,1)S(1)} %pad_maximum_fusion.refs_0_), channel_id=1, source_target_pairs={{0,6},{1,7},{2,4},{3,5},{4,2},{5,3},{6,0},{7,1},{8,14},{9,15},{10,... | collective-permute-start | bytes 786440 | tf_op jit(solution)/shard_map/ppermute | solution.py:173
  17.9 0.6 %collective-permute-start.4 = (bf16[4,256,128]{2,1,0:T(8,128)(2,1)S(1)}, bf16[4,256,128]{2,1,0:T(8,128)(2,1)S(1)}, u32[]{:S(2)}, u32[]{:S(2)}) collective-permute-start(bf16[4,256,128]{2,1,0:T(8,128)(2,1)S(1)} %pad_maximum_fusion.refs_0_), channel_id=1, source_target_pairs={{0,4},{1,5},{2,6},{3,7},{4,0},{5,1},{6,2},{7,3},{8,12},{9,13},{10,... | collective-permute-start | bytes 786440 | tf_op jit(solution)/shard_map/ppermute | solution.py:173
  18.5 0.3 collective-permute-start.3
  18.7 0.0 collective-permute-start.6
  18.7 3.0 %all-to-all-done.right_ref = bf16[32,8,128]{2,1,0:T(8,128)(2,1)S(1)} async-done(((bf16[32,8,128]{2,1,0:T(8,128)(2,1)}), bf16[32,8,128]{2,1,0:T(8,128)(2,1)S(1)}, u32[]{:S(2)}, u32[]{:S(2)}) %all-to-all-start) | async-done | bytes 65568 | tf_op jit(solution)/shard_map/all_to_all | solution.py:204
  21.7 0.0 copy-start.1
  21.7 0.9 %copy-done.1 = bf16[1024,128]{1,0:T(8,128)(2,1)S(1)} copy-done((bf16[1024,128]{1,0:T(8,128)(2,1)S(1)}, bf16[1024,128]{1,0:T(8,128)(2,1)}, u32[]{:S(2)}) %copy-start.1) | copy-done | bytes 262168
  22.7 5.9 %shard_map.101 = (bf16[2048,2048]{1,0:T(8,128)(2,1)S(1)}, bf16[2,512,256]{2,1,0:T(8,128)(2,1)S(1)}) custom-call(bf16[32,8,128]{2,1,0:T(8,128)(2,1)S(1)} %all-to-all-done.right_ref, bf16[1024,128]{1,0:T(8,128)(2,1)S(1)} %copy-done.1), custom_call_target="tpu_custom_call" | custom-call | flops 2147483648 | bytes 8388608 | tf_op jit(solution)/shard_map/pallas_call | solution.py:220
  28.6 0.0 collective-permute-done.5.refs_3_
  28.6 2.1 %collective-permute-done.4.refs_2_ = bf16[4,256,128]{2,1,0:T(8,128)(2,1)S(1)} collective-permute-done((bf16[4,256,128]{2,1,0:T(8,128)(2,1)S(1)}, bf16[4,256,128]{2,1,0:T(8,128)(2,1)S(1)}, u32[]{:S(2)}, u32[]{:S(2)}) %collective-permute-start.4) | collective-permute-done | bytes 262176 | tf_op jit(solution)/shard_map/ppermute | solution.py:173
  30.7 0.0 collective-permute-done.3.refs_1_
  30.7 0.0 collective-permute-start.7
  30.7 0.5 %collective-permute-start.8 = (bf16[4,256,128]{2,1,0:T(8,128)(2,1)S(1)}, bf16[4,256,128]{2,1,0:T(8,128)(2,1)S(1)}, u32[]{:S(2)}, u32[]{:S(2)}) collective-permute-start(bf16[4,256,128]{2,1,0:T(8,128)(2,1)S(1)} %collective-permute-done.4.refs_2_), channel_id=1, source_target_pairs={{0,1},{1,0},{2,3},{3,2},{4,5},{5,4},{6,7},{7,6},{8,9},{9,8},{10,11... | collective-permute-start | bytes 786440 | tf_op jit(solution)/shard_map/ppermute | solution.py:173
  31.2 0.0 collective-permute-start.9
  31.2 0.0 collective-permute-done.6.refs_4_
  31.2 1.0 %collective-permute-done.7.refs_5_ = bf16[4,256,128]{2,1,0:T(8,128)(2,1)S(1)} collective-permute-done((bf16[4,256,128]{2,1,0:T(8,128)(2,1)S(1)}, bf16[4,256,128]{2,1,0:T(8,128)(2,1)S(1)}, u32[]{:S(2)}, u32[]{:S(2)}) %collective-permute-start.7) | collective-permute-done | bytes 262176 | tf_op jit(solution)/shard_map/ppermute | solution.py:173
  32.2 0.4 collective-permute-done.8.refs_6_
  32.6 0.4 collective-permute-done.9.refs_7_
  33.0 0.0 copy-done.2
  33.0 0.0 copy-done
  33.0 7.3 %shard_map.102 = bf16[512,16,128]{2,1,0:T(8,128)(2,1)} custom-call(bf16[4,256,128]{2,1,0:T(8,128)(2,1)S(1)} %pad_maximum_fusion.refs_0_, bf16[4,256,128]{2,1,0:T(8,128)(2,1)S(1)} %collective-permute-done.3.refs_1_, bf16[4,256,128]{2,1,0:T(8,128)(2,1)S(1)} %collective-permute-done.4.refs_2_, bf16[4,256,128]{2,1,0:T(8,128)(2,1)S(1)} %collective-permute-done.5.refs_3_, ...), custom_call_target="tpu_custom_call" | custom-call | flops 4294967296 | bytes 8388608 | tf_op jit(solution)/shard_map/pallas_call | solution.py:249
Async XLA Ops:
  2.5 11.8 %collective-permute-start.2 = (bf16[256,128]{1,0:T(8,128)(2,1)}, bf16[256,128]{1,0:T(8,128)(2,1)S(1)}, u32[]{:S(2)}, u32[]{:S(2)}) collective-permute-start(bf16[256,128]{1,0:T(8,128)(2,1)} %get-tuple-element.13), channel_id=1, source_target_pairs={{0,24},{1,25},{2,26},{3,27},{4,28},{5,29},{6,30},{7,31},{8,16},{9,... | collective-permute-start | bytes 196616 | tf_op jit(solution)/shard_map/ppermute | solution.py:173
  7.6 6.7 %collective-permute-start.1 = (bf16[256,128]{1,0:T(8,128)(2,1)}, bf16[256,128]{1,0:T(8,128)(2,1)S(1)}, u32[]{:S(2)}, u32[]{:S(2)}) collective-permute-start(bf16[256,128]{1,0:T(8,128)(2,1)} %get-tuple-element.13), channel_id=1, source_target_pairs={{0,16},{1,17},{2,18},{3,19},{4,20},{5,21},{6,22},{7,23},{8,24},{9,... | collective-permute-start | bytes 196616 | tf_op jit(solution)/shard_map/ppermute | solution.py:173
  7.6 6.7 %collective-permute-start = (bf16[256,128]{1,0:T(8,128)(2,1)}, bf16[256,128]{1,0:T(8,128)(2,1)S(1)}, u32[]{:S(2)}, u32[]{:S(2)}) collective-permute-start(bf16[256,128]{1,0:T(8,128)(2,1)} %get-tuple-element.13), channel_id=1, source_target_pairs={{0,8},{1,9},{2,10},{3,11},{4,12},{5,13},{6,14},{7,15},{8,0},{9,1},... | collective-permute-start | bytes 196616 | tf_op jit(solution)/shard_map/ppermute | solution.py:173
  8.2 13.5 %all-to-all-start = ((bf16[32,8,128]{2,1,0:T(8,128)(2,1)}), bf16[32,8,128]{2,1,0:T(8,128)(2,1)S(1)}, u32[]{:S(2)}, u32[]{:S(2)}) async-start(bf16[32,8,128]{2,1,0:T(8,128)(2,1)} %get-tuple-element.14), calls=%async_computation | async-start | bytes 131072 | tf_op jit(solution)/shard_map/all_to_all | solution.py:204
  14.3 18.7 %copy-start.2 = (f32[128]{0:T(128)S(1)}, f32[128]{0:T(128)}, u32[]{:S(2)}) copy-start(f32[128]{0:T(128)} %param.19) | copy-start | bytes 1540
  15.2 17.8 %copy-start = (bf16[512,16,128]{2,1,0:T(8,128)(2,1)S(1)}, bf16[512,16,128]{2,1,0:T(8,128)(2,1)}, u32[]{:S(2)}) copy-start(bf16[512,16,128]{2,1,0:T(8,128)(2,1)} %refs_10_.1) | copy-start | bytes 6291460
  15.2 13.4 %collective-permute-start.5 = (bf16[4,256,128]{2,1,0:T(8,128)(2,1)S(1)}, bf16[4,256,128]{2,1,0:T(8,128)(2,1)S(1)}, u32[]{:S(2)}, u32[]{:S(2)}) collective-permute-start(bf16[4,256,128]{2,1,0:T(8,128)(2,1)S(1)} %pad_maximum_fusion.refs_0_), channel_id=1, source_target_pairs={{0,6},{1,7},{2,4},{3,5},{4,2},{5,3},{6,0},{7,1},{8,14},{9,15},{10,... | collective-permute-start | bytes 786440 | tf_op jit(solution)/shard_map/ppermute | solution.py:173
  17.9 12.8 %collective-permute-start.4 = (bf16[4,256,128]{2,1,0:T(8,128)(2,1)S(1)}, bf16[4,256,128]{2,1,0:T(8,128)(2,1)S(1)}, u32[]{:S(2)}, u32[]{:S(2)}) collective-permute-start(bf16[4,256,128]{2,1,0:T(8,128)(2,1)S(1)} %pad_maximum_fusion.refs_0_), channel_id=1, source_target_pairs={{0,4},{1,5},{2,6},{3,7},{4,0},{5,1},{6,2},{7,3},{8,12},{9,13},{10,... | collective-permute-start | bytes 786440 | tf_op jit(solution)/shard_map/ppermute | solution.py:173
  18.5 12.2 %collective-permute-start.3 = (bf16[4,256,128]{2,1,0:T(8,128)(2,1)S(1)}, bf16[4,256,128]{2,1,0:T(8,128)(2,1)S(1)}, u32[]{:S(2)}, u32[]{:S(2)}) collective-permute-start(bf16[4,256,128]{2,1,0:T(8,128)(2,1)S(1)} %pad_maximum_fusion.refs_0_), channel_id=1, source_target_pairs={{0,2},{1,3},{2,0},{3,1},{4,6},{5,7},{6,4},{7,5},{8,10},{9,11},{10,... | collective-permute-start | bytes 786440 | tf_op jit(solution)/shard_map/ppermute | solution.py:173
  18.7 12.5 %collective-permute-start.6 = (bf16[4,256,128]{2,1,0:T(8,128)(2,1)S(1)}, bf16[4,256,128]{2,1,0:T(8,128)(2,1)S(1)}, u32[]{:S(2)}, u32[]{:S(2)}) collective-permute-start(bf16[4,256,128]{2,1,0:T(8,128)(2,1)S(1)} %pad_maximum_fusion.refs_0_), channel_id=1, source_target_pairs={{0,1},{1,0},{2,3},{3,2},{4,5},{5,4},{6,7},{7,6},{8,9},{9,8},{10,11... | collective-permute-start | bytes 786440 | tf_op jit(solution)/shard_map/ppermute | solution.py:173
  21.7 1.0 %copy-start.1 = (bf16[1024,128]{1,0:T(8,128)(2,1)S(1)}, bf16[1024,128]{1,0:T(8,128)(2,1)}, u32[]{:S(2)}) copy-start(bf16[1024,128]{1,0:T(8,128)(2,1)} %final_ref.1) | copy-start | bytes 786436
  30.7 1.5 %collective-permute-start.7 = (bf16[4,256,128]{2,1,0:T(8,128)(2,1)S(1)}, bf16[4,256,128]{2,1,0:T(8,128)(2,1)S(1)}, u32[]{:S(2)}, u32[]{:S(2)}) collective-permute-start(bf16[4,256,128]{2,1,0:T(8,128)(2,1)S(1)} %collective-permute-done.3.refs_1_), channel_id=1, source_target_pairs={{0,1},{1,0},{2,3},{3,2},{4,5},{5,4},{6,7},{7,6},{8,9},{9,8},{10,11... | collective-permute-start | bytes 786440 | tf_op jit(solution)/shard_map/ppermute | solution.py:173
  30.7 1.9 %collective-permute-start.8 = (bf16[4,256,128]{2,1,0:T(8,128)(2,1)S(1)}, bf16[4,256,128]{2,1,0:T(8,128)(2,1)S(1)}, u32[]{:S(2)}, u32[]{:S(2)}) collective-permute-start(bf16[4,256,128]{2,1,0:T(8,128)(2,1)S(1)} %collective-permute-done.4.refs_2_), channel_id=1, source_target_pairs={{0,1},{1,0},{2,3},{3,2},{4,5},{5,4},{6,7},{7,6},{8,9},{9,8},{10,11... | collective-permute-start | bytes 786440 | tf_op jit(solution)/shard_map/ppermute | solution.py:173
  31.2 1.8 %collective-permute-start.9 = (bf16[4,256,128]{2,1,0:T(8,128)(2,1)S(1)}, bf16[4,256,128]{2,1,0:T(8,128)(2,1)S(1)}, u32[]{:S(2)}, u32[]{:S(2)}) collective-permute-start(bf16[4,256,128]{2,1,0:T(8,128)(2,1)S(1)} %collective-permute-done.5.refs_3_), channel_id=1, source_target_pairs={{0,1},{1,0},{2,3},{3,2},{4,5},{5,4},{6,7},{7,6},{8,9},{9,8},{10,11... | collective-permute-start | bytes 786440 | tf_op jit(solution)/shard_map/ppermute | solution.py:173

commit v3 on v1

--- a/solution.py
+++ b/solution.py
@@ -61,7 +61,7 @@
 def _order(me, half):
     row = lax.broadcasted_iota(jnp.int32, (4 * LANES, 8 * CHANS), 0)
     col = lax.broadcasted_iota(jnp.int32, (4 * LANES, 8 * CHANS), 1)
-    device = (row // LANES) ^ (me % 4)
+    device = (row // LANES) ^ (me // 8 % 4)
     wanted = (row % CHANS) * 8 + ((row // CHANS) % 2) * 4 + device
     hit = (wanted == col) & ((row // (2 * CHANS)) % 2 == half)
     return jnp.where(hit, 1.0, 0.0).astype(jnp.bfloat16)
@@ -77,7 +77,7 @@
     block = right_ref[...].astype(jnp.float32).reshape(rows, LANES)
     row = lax.broadcasted_iota(jnp.int32, (2 * rows, 2 * rows), 0)
     col = lax.broadcasted_iota(jnp.int32, (2 * rows, 2 * rows), 1)
-    device = (row // 8) % groups * 4 + row % 4
+    device = (row // 8) % groups + row % 4 * groups
     wanted = ((row // 4) % 2) * rows + device * 8 + row // (8 * groups)
     spread = jnp.where(wanted == col, 1.0, 0.0).astype(jnp.bfloat16)
     lane = lax.broadcasted_iota(jnp.int32, block.shape, 1) // CHANS
@@ -88,60 +88,70 @@
         lhs.append(moved.astype(jnp.bfloat16))
     lhs = jnp.concatenate(lhs, axis=0)
 
-    def body(pair, _):
+    for pair in range(CHANS // 2):
         rhs = []
         for k in range(2):
-            at = pl.multiple_of(pair * 2 * CHANS + k * CHANS, CHANS)
+            at = pair * 2 * CHANS + k * CHANS
             rhs.append(jnp.concatenate([final_ref[pl.ds(at, CHANS), :]] * 4, axis=0))
         res = jnp.dot(lhs, jnp.concatenate(rhs, axis=1), preferred_element_type=jnp.float32)
         for j in range(16):
             for g in range(groups):
                 r = (j * groups + g) * 8
                 tile = jnp.concatenate([res[r : r + 8, :LANES], res[r : r + 8, LANES:]], axis=0)
-                at = pl.multiple_of(g * 8 * CHANS + pair * 16, 16)
-                out_ref[pl.ds(at, 16), pl.ds(j * LANES, LANES)] = tile.astype(jnp.bfloat16)
-        return 0
-
-    lax.fori_loop(0, CHANS // 2, body, 0)
-
-
-def _band_kernel(count, *refs):
-    own_refs, other_refs = refs[:4], refs[4:8]
-    t_ref, order_ref, pair_ref, shift_ref, out_ref, l_ref, acc_ref, done_ref, sems = refs[8:17]
-    fetched = refs[17:]
-    half = own_refs[0].shape[1]
-    band, cols = pair_ref.shape[0], pair_ref.shape[1]
+                out_ref[g, 0, pl.ds(pair * 16, 16), pl.ds(j * LANES, LANES)] = tile.astype(jnp.bfloat16)
+
+
+def _band_kernel(masks, begins, count, held, *refs):
+    refs = list(refs)
+    take = lambda k: [refs.pop(0) for _ in range(k)]
+    lines = take(len(masks))
+    t_ref, order_ref = take(2)
+    (sum_ref,) = (None,) if begins else take(1)
+    pair_ref, shift_ref = (None, None) if count is None else take(2)
+    (out_ref,) = take(1)
+    (l_ref,) = take(1)
     me = lax.axis_index("row")
     wide = 8 * CHANS
-
-    for zi in range(own_refs[0].shape[0]):
-        for y in range(2):
-            lhs = jnp.concatenate(
-                [own_refs[2 * y][zi], other_refs[2 * y][zi], own_refs[2 * y + 1][zi], other_refs[2 * y + 1][zi]],
-                axis=1,
-            )
-            group = (zi * 2 + y) ^ (me // 4)
-            at = pl.ds(pl.multiple_of(group * wide, wide), wide)
+    places, half, _ = lines[0].shape
+    chunks = []
+    for line, mask in zip(lines, masks):
+        for q in range(places // 4):
+            lhs = jnp.concatenate([line[q * 4 + u] for u in range(4)], axis=1)
+            at = pl.ds(len(chunks) * wide, wide)
             for h in range(2):
                 moved = jnp.dot(lhs, order_ref[h], preferred_element_type=jnp.float32)
                 l_ref[pl.ds(h * half, half), at] = moved.astype(jnp.bfloat16)
+            chunks.append(((me % 8) ^ mask, q ^ (me // 32)))
 
     tile = 256
-    pitch = cols + 1
-
-    def column(step, _):
-        at = pl.ds(pl.multiple_of(step * tile, tile), tile)
-        if fetched:
-            pltpu.sync_copy(t_ref.at[:, at], fetched[0])
-            rhs = fetched[0][...]
+    band = 2 * half
+    if count is not None:
+        acc_ref, done_ref, sems = take(3)
+        cols = pair_ref.shape[1]
+        pitch = cols + 1
+
+    def column(step):
+        at = pl.ds(step * tile, tile)
+        if held:
+            rhs = jnp.concatenate([t_ref[g, q, :, at] for g, q in chunks], axis=0)
         else:
-            rhs = t_ref[:, at]
+            for i, (g, q) in enumerate(chunks):
+                pltpu.sync_copy(t_ref.at[g, q, :, at], refs[0].at[pl.ds(i * wide, wide)])
+            rhs = refs[0][...]
         res = jnp.dot(l_ref[...], rhs, preferred_element_type=jnp.float32)
-        for k in range(tile // LANES):
-            acc_ref[pl.ds(step * (tile // LANES) + k, band, stride=pitch), :] = res[:, k * LANES : (k + 1) * LANES]
-        return 0
-
-    lax.fori_loop(0, cols * LANES // tile, column, 0)
+        if sum_ref is not None:
+            res = res + sum_ref[:, at]
+        if count is None:
+            out_ref[:, at] = res
+        else:
+            for k in range(tile // LANES):
+                j = step * (tile // LANES) + k
+                acc_ref[pl.ds(j, band, stride=pitch), :] = res[:, k * LANES : (k + 1) * LANES]
+
+    for step in range(t_ref.shape[3] // tile):
+        column(step)
+    if count is None:
+        return
 
     rows = 32
     shift = shift_ref[...]
@@ -200,65 +210,71 @@
     right = lax.all_to_all(right, "row", split_axis=0, concat_axis=0, tiled=True)
 
     line = [left] + [_xor(left, m, n) for m in range(8, n, 8)]
-    line, right = lax.optimization_barrier((jnp.stack(line), right))
+    line = jnp.stack(line)
     plane = [_xor(line, m, n) for m in (2, 4, 6)]
 
-    k = n * 2 * CHANS
     part = 32
+    parts = n // part
     fold_cost = pl.CostEstimate(
-        flops=2 * n * 32 * 256 * CHANS * zdim, bytes_accessed=2 * n * 2 * CHANS * cols * zdim, transcendentals=0
+        flops=2 * n * 32 * 256 * CHANS * zdim, bytes_accessed=4 * n * CHANS * cols * zdim, transcendentals=0
     )
     fold_out = (
-        jax.ShapeDtypeStruct((k, cols * zdim), jnp.bfloat16),
+        jax.ShapeDtypeStruct((8, parts, 8 * CHANS, cols * zdim), jnp.bfloat16),
         jax.ShapeDtypeStruct((2, 4 * LANES, 8 * CHANS), jnp.bfloat16),
     )
     if small:
-        folded, order = pl.pallas_call(
-            _fold_kernel,
-            in_specs=[vmem, vmem],
-            out_specs=(vmem, vmem),
-            out_shape=fold_out,
-            compiler_params=params,
-            cost_estimate=fold_cost,
-        )(right, final)
+        specs = dict(in_specs=[vmem, vmem], out_specs=(vmem, vmem))
     else:
-        folded, order = pl.pallas_call(
-            _fold_kernel,
-            grid=(n // part,),
+        specs = dict(
+            grid=(parts,),
             in_specs=[
                 pl.BlockSpec((part, 8, LANES), lambda i: (i, 0, 0)),
                 pl.BlockSpec(final.shape, lambda i: (0, 0)),
             ],
             out_specs=(
-                pl.BlockSpec((part * 2 * CHANS, cols * zdim), lambda i: (i, 0)),
+                pl.BlockSpec((8, 1, 8 * CHANS, cols * zdim), lambda i: (0, i, 0, 0)),
                 pl.BlockSpec((2, 4 * LANES, 8 * CHANS), lambda i: (0, 0, 0)),
             ),
-            out_shape=fold_out,
+        )
+    folded, order = pl.pallas_call(
+        _fold_kernel, out_shape=fold_out, compiler_params=params, cost_estimate=fold_cost, **specs
+    )(right, final)
+
+    def add(lines, masks, total, last):
+        depth = len(masks) * parts * 8 * CHANS
+        scratch = [pltpu.VMEM((band, depth), jnp.bfloat16)]
+        operands = [*lines, folded, order] + ([] if total is None else [total])
+        if last:
+            operands += [pair, shift.reshape(1, -1)]
+            scratch += [
+                pltpu.VMEM((band * (cols + 1), zdim), jnp.float32),
+                pltpu.VMEM(pair.shape, jnp.bfloat16),
+                pltpu.SemaphoreType.DMA((band // 32,)),
+            ]
+        if not small:
+            scratch.append(pltpu.VMEM((depth, 256), jnp.bfloat16))
+        in_specs = [vmem] * len(operands)
+        if not small:
+            in_specs[len(lines)] = anywhere
+        return pl.pallas_call(
+            functools.partial(_band_kernel, masks, total is None, count if last else None, small),
+            in_specs=in_specs,
+            out_specs=anywhere if last else vmem,
+            out_shape=jax.ShapeDtypeStruct(pair.shape, jnp.bfloat16)
+            if last
+            else jax.ShapeDtypeStruct((band, cols * zdim), jnp.float32),
+            scratch_shapes=scratch,
             compiler_params=params,
-            cost_estimate=fold_cost,
-        )(right, final)
-
-    plane, folded = lax.optimization_barrier((plane, folded))
-    own = [line] + plane
-    other = [_xor(o, 1, n) for o in own]
-
-    return pl.pallas_call(
-        functools.partial(_band_kernel, count),
-        in_specs=[vmem] * 8 + [vmem if small else anywhere] + [vmem] * 3,
-        out_specs=anywhere,
-        out_shape=jax.ShapeDtypeStruct(pair.shape, jnp.bfloat16),
-        scratch_shapes=[
-            pltpu.VMEM((band, k), jnp.bfloat16),
-            pltpu.VMEM((band * (cols + 1), zdim), jnp.float32),
-            pltpu.VMEM(pair.shape, jnp.bfloat16),
-            pltpu.SemaphoreType.DMA((band // 32,)),
-        ]
-        + ([] if small else [pltpu.VMEM((k, 256), jnp.bfloat16)]),
-        compiler_params=params,
-        cost_estimate=pl.CostEstimate(
-            flops=2 * band * k * cols * zdim, bytes_accessed=2 * k * cols * zdim, transcendentals=0
-        ),
-    )(*own, *other, folded, order, pair, shift.reshape(1, -1))
+            cost_estimate=pl.CostEstimate(
+                flops=2 * band * depth * cols * zdim, bytes_accessed=2 * depth * cols * zdim, transcendentals=0
+            ),
+        )(*operands)
+
+    total = add([line, _xor(line, 1, n)], (0, 1), None, False)
+    plane, total = lax.optimization_barrier((plane, total))
+    other = [_xor(o, 1, n) for o in plane]
+    total = add(plane, (2, 4, 6), total, False)
+    return add(other, (3, 5, 7), total, True)
 
 
 def solution(mesh):

time: 47.2 us -> 37.8 us (0.80)
  waiting for transfers between devices: 12.1 us -> 6.28 us
  Pallas kernels: 17.1 us -> 13.2 us
    pallas_call x2 -> x4, Pallas kernels: 14.7 us -> 10.7 us  [the longest x3 7.44 us: add(): pl.pallas_call(functools.partial(_band_kernel, masks, total is None, coun...]
    all_to_all x1, waiting for transfers between devices: 6.47 us -> 2.74 us  [shards(): lax.all_to_all(right, 'row', split_axis=0, concat_axis=0, tiled=True)]
    ppermute x10, waiting for transfers between devices: 5.66 us -> 3.54 us  [_xor(): return lax.ppermute(x, 'row', [(i, i ^ mask) for i in range(n)])]
  transfers between devices with their start and end apart: 11 -> 11, of which waited for: 5 -> 3; matrix products, arithmetic and copies ran while one was open for 2% -> 2% of each run, Pallas kernels for 13% -> 19%
where the time goes in v3:
time: 37.8 us; the launch traced here: 37.5 us
  starting transfers between devices  16.1 us (43%)
  Pallas kernels  13.2 us (35%)
  waiting for transfers between devices  6.28 us (17%)
  local copies, waits for them, and re-layouts  0.96 us (3%)
  other arithmetic  0.88 us (2%)
    ppermute x10, starting transfers between devices, _xor(): return lax.ppermute(x, 'row', [(i, i ^ mask) for i in range(n)])  10.1 us
    pallas_call x3, Pallas kernels, add(): pl.pallas_call(functools.partial(_band_kernel, masks, total is None, coun...  7.44 us
    all_to_all x1, starting transfers between devices, shards(): lax.all_to_all(right, 'row', split_axis=0, concat_axis=0, tiled=True)  5.99 us
    ppermute x10, waiting for transfers between devices, _xor(): return lax.ppermute(x, 'row', [(i, i ^ mask) for i in range(n)])  3.54 us
    pallas_call x1, Pallas kernels, shards(): pl.pallas_call(_fold_kernel, out_shape=fold_out, compiler_params=params,...  3.24 us
    all_to_all x1, waiting for transfers between devices, shards(): lax.all_to_all(right, 'row', split_axis=0, concat_axis=0, tiled=True)  2.74 us
    pallas_call x1, Pallas kernels, shards(): pl.pallas_call(_project_kernel, in_specs=[pl.BlockSpec(memory_space=pltpu...  2.48 us
    unnamed x6, local copies, waits for them, and re-layouts  0.96 us
  transfers between devices with their start and end apart: 11, of which 3 were waited for; matrix products, arithmetic and copies ran while one was open for 2% of the time, Pallas kernels for 19%

profile of v3, /device:TPU:0, one launch (start us, length us, event | category | flops | bytes accessed | tf_op | source)
XLA Modules:
  0.0 37.5 jit_solution(6924852318276270488)
XLA Ops:
  0.0 2.5 %shard_map.100 = (bf16[256,128]{1,0:T(8,128)(2,1)}, bf16[32,8,128]{2,1,0:T(8,128)(2,1)}) custom-call(bf16[2,512,256]{2,1,0:T(8,128)(2,1)} %refs_0_.1, f32[1,256]{1,0:T(1,128)} %bitcast.18, f32[1,256]{1,0:T(1,128)} %bitcast.19, bf16[32,256]{1,0:T(8,128)(2,1)} %bitcast.16, f32[1,32]{1,0:T(1,128)} %bitcast.20, bf16[32,256]{1,0:T(8,128)(2,1)} %bitcast.17, ...), custom_call_target="tpu_custom_call" | custom-call | flops 33554432 | bytes 524288 | tf_op jit(solution)/shard_map/pallas_call | solution.py:195
  2.5 5.1 %collective-permute-start.2 = (bf16[256,128]{1,0:T(8,128)(2,1)}, bf16[256,128]{1,0:T(8,128)(2,1)S(1)}, u32[]{:S(2)}, u32[]{:S(2)}) collective-permute-start(bf16[256,128]{1,0:T(8,128)(2,1)} %get-tuple-element.13), channel_id=1, source_target_pairs={{0,24},{1,25},{2,26},{3,27},{4,28},{5,29},{6,30},{7,31},{8,16},{9,... | collective-permute-start | bytes 196616 | tf_op jit(solution)/shard_map/ppermute | solution.py:179
  7.6 0.0 collective-permute-start.1
  7.6 0.6 %collective-permute-start = (bf16[256,128]{1,0:T(8,128)(2,1)}, bf16[256,128]{1,0:T(8,128)(2,1)S(1)}, u32[]{:S(2)}, u32[]{:S(2)}) collective-permute-start(bf16[256,128]{1,0:T(8,128)(2,1)} %get-tuple-element.13), channel_id=1, source_target_pairs={{0,8},{1,9},{2,10},{3,11},{4,12},{5,13},{6,14},{7,15},{8,0},{9,1},... | collective-permute-start | bytes 196616 | tf_op jit(solution)/shard_map/ppermute | solution.py:179
  8.2 6.0 %all-to-all-start = ((bf16[32,8,128]{2,1,0:T(8,128)(2,1)}), bf16[32,8,128]{2,1,0:T(8,128)(2,1)S(1)}, u32[]{:S(2)}, u32[]{:S(2)}) async-start(bf16[32,8,128]{2,1,0:T(8,128)(2,1)} %get-tuple-element.14), calls=%async_computation | async-start | bytes 131072 | tf_op jit(solution)/shard_map/all_to_all | solution.py:210
  14.2 0.0 collective-permute-done.2
  14.3 0.0 collective-permute-done.1
  14.3 0.0 collective-permute-done
  14.3 0.9 %pad_maximum_fusion.refs_0_ = bf16[4,256,128]{2,1,0:T(8,128)(2,1)S(1)} fusion(bf16[1,256,128]{2,1,0:T(8,128)(2,1)S(1)} %bitcast.13, bf16[1,256,128]{2,1,0:T(8,128)(2,1)S(1)} %bitcast.14, bf16[1,256,128]{2,1,0:T(8,128)(2,1)S(1)} %bitcast.15, bf16[1,256,128]{2,1,0:T(8,128)(2,1)} %bitcast.12), kind=kLoop, calls=%fused_computation | loop fusion | flops 393216 | bytes 524288 | tf_op jit(solution)/shard_map/stack | solution.py:213
  15.2 0.3 collective-permute-start.6
  15.5 2.6 %collective-permute-start.5 = (bf16[4,256,128]{2,1,0:T(8,128)(2,1)S(1)}, bf16[4,256,128]{2,1,0:T(8,128)(2,1)S(1)}, u32[]{:S(2)}, u32[]{:S(2)}) collective-permute-start(bf16[4,256,128]{2,1,0:T(8,128)(2,1)S(1)} %pad_maximum_fusion.refs_0_), channel_id=1, source_target_pairs={{0,6},{1,7},{2,4},{3,5},{4,2},{5,3},{6,0},{7,1},{8,14},{9,15},{10,... | collective-permute-start | bytes 786440 | tf_op jit(solution)/shard_map/ppermute | solution.py:179
  18.1 0.6 %collective-permute-start.4 = (bf16[4,256,128]{2,1,0:T(8,128)(2,1)S(1)}, bf16[4,256,128]{2,1,0:T(8,128)(2,1)S(1)}, u32[]{:S(2)}, u32[]{:S(2)}) collective-permute-start(bf16[4,256,128]{2,1,0:T(8,128)(2,1)S(1)} %pad_maximum_fusion.refs_0_), channel_id=1, source_target_pairs={{0,4},{1,5},{2,6},{3,7},{4,0},{5,1},{6,2},{7,3},{8,12},{9,13},{10,... | collective-permute-start | bytes 786440 | tf_op jit(solution)/shard_map/ppermute | solution.py:179
  18.6 0.3 collective-permute-start.3
  19.0 2.7 %all-to-all-done.right_ref = bf16[32,8,128]{2,1,0:T(8,128)(2,1)S(1)} async-done(((bf16[32,8,128]{2,1,0:T(8,128)(2,1)}), bf16[32,8,128]{2,1,0:T(8,128)(2,1)S(1)}, u32[]{:S(2)}, u32[]{:S(2)}) %all-to-all-start) | async-done | bytes 65568 | tf_op jit(solution)/shard_map/all_to_all | solution.py:210
  21.7 0.9 %copy-done.2 = bf16[1024,128]{1,0:T(8,128)(2,1)S(1)} copy-done((bf16[1024,128]{1,0:T(8,128)(2,1)S(1)}, bf16[1024,128]{1,0:T(8,128)(2,1)}, u32[]{:S(2)}) %copy-start.2) | copy-done | bytes 262168
  22.7 3.2 %shard_map.101 = (bf16[8,1,256,2048]{3,2,1,0:T(8,128)(2,1)S(1)}, bf16[2,512,256]{2,1,0:T(8,128)(2,1)S(1)}) custom-call(bf16[32,8,128]{2,1,0:T(8,128)(2,1)S(1)} %all-to-all-done.right_ref, bf16[1024,128]{1,0:T(8,128)(2,1)S(1)} %copy-done.2), custom_call_target="tpu_custom_call" | custom-call | flops 2147483648 | bytes 8388608 | tf_op jit(solution)/shard_map/pallas_call | solution.py:239
  25.9 0.0 collective-permute-done.6.refs_1_
  25.9 1.5 %shard_map.102.refs_5_ = f32[512,2048]{1,0:T(8,128)S(1)} custom-call(bf16[4,256,128]{2,1,0:T(8,128)(2,1)S(1)} %pad_maximum_fusion.refs_0_, bf16[4,256,128]{2,1,0:T(8,128)(2,1)S(1)} %collective-permute-done.6.refs_1_, bf16[8,1,256,2048]{3,2,1,0:T(8,128)(2,1)S(1)} %get-tuple-element.15.refs_2_.refs_3_, bf16[2,512,256]{2,1,0:T(8,128)(2,1)S(1)} %get-tuple-element.16.refs_3_.refs_4_), custom_call_target="tpu_custom_call" | custom-call | flops 1073741824 | bytes 2097152 | tf_op jit(solution)/shard_map/pallas_call | solution.py:259
  27.4 0.0 copy-start
  27.5 0.0 copy-start.1
  27.5 0.0 collective-permute-done.5.refs_2_
  27.5 3.4 %collective-permute-done.4.refs_1_ = bf16[4,256,128]{2,1,0:T(8,128)(2,1)S(1)} collective-permute-done((bf16[4,256,128]{2,1,0:T(8,128)(2,1)S(1)}, bf16[4,256,128]{2,1,0:T(8,128)(2,1)S(1)}, u32[]{:S(2)}, u32[]{:S(2)}) %collective-permute-start.4) | collective-permute-done | bytes 262176 | tf_op jit(solution)/shard_map/ppermute | solution.py:179
  30.9 0.1 collective-permute-done.3.refs_0_
  31.0 0.0 collective-permute-start.7
  31.0 0.5 %collective-permute-start.8 = (bf16[4,256,128]{2,1,0:T(8,128)(2,1)S(1)}, bf16[4,256,128]{2,1,0:T(8,128)(2,1)S(1)}, u32[]{:S(2)}, u32[]{:S(2)}) collective-permute-start(bf16[4,256,128]{2,1,0:T(8,128)(2,1)S(1)} %collective-permute-done.4.refs_1_), channel_id=1, source_target_pairs={{0,1},{1,0},{2,3},{3,2},{4,5},{5,4},{6,7},{7,6},{8,9},{9,8},{10,11... | collective-permute-start | bytes 786440 | tf_op jit(solution)/shard_map/ppermute | solution.py:179
  31.5 0.0 collective-permute-start.9
  31.5 2.2 %shard_map.103.refs_5_ = f32[512,2048]{1,0:T(8,128)S(1)} custom-call(bf16[4,256,128]{2,1,0:T(8,128)(2,1)S(1)} %collective-permute-done.3.refs_0_, bf16[4,256,128]{2,1,0:T(8,128)(2,1)S(1)} %collective-permute-done.4.refs_1_, bf16[4,256,128]{2,1,0:T(8,128)(2,1)S(1)} %collective-permute-done.5.refs_2_, ...), custom_call_target="tpu_custom_call" | custom-call | flops 1610612736 | bytes 3145728 | tf_op jit(solution)/shard_map/pallas_call | solution.py:259
  33.7 0.0 collective-permute-done.7.refs_0_
  33.7 0.0 collective-permute-done.8.refs_1_
  33.7 0.0 collective-permute-done.9.refs_2_
  33.8 0.0 copy-done
  33.8 3.7 %shard_map.104 = bf16[512,16,128]{2,1,0:T(8,128)(2,1)} custom-call(bf16[4,256,128]{2,1,0:T(8,128)(2,1)S(1)} %collective-permute-done.7.refs_0_, bf16[4,256,128]{2,1,0:T(8,128)(2,1)S(1)} %collective-permute-done.8.refs_1_, bf16[4,256,128]{2,1,0:T(8,128)(2,1)S(1)} %collective-permute-done.9.refs_2_, ...), custom_call_target="tpu_custom_call" | custom-call | flops 1610612736 | bytes 3145728 | tf_op jit(solution)/shard_map/pallas_call | solution.py:259
  (2 shorter events, 0.0 us)
Async XLA Ops:
  2.5 11.8 %collective-permute-start.2 = (bf16[256,128]{1,0:T(8,128)(2,1)}, bf16[256,128]{1,0:T(8,128)(2,1)S(1)}, u32[]{:S(2)}, u32[]{:S(2)}) collective-permute-start(bf16[256,128]{1,0:T(8,128)(2,1)} %get-tuple-element.13), channel_id=1, source_target_pairs={{0,24},{1,25},{2,26},{3,27},{4,28},{5,29},{6,30},{7,31},{8,16},{9,... | collective-permute-start | bytes 196616 | tf_op jit(solution)/shard_map/ppermute | solution.py:179
  7.6 6.7 %collective-permute-start.1 = (bf16[256,128]{1,0:T(8,128)(2,1)}, bf16[256,128]{1,0:T(8,128)(2,1)S(1)}, u32[]{:S(2)}, u32[]{:S(2)}) collective-permute-start(bf16[256,128]{1,0:T(8,128)(2,1)} %get-tuple-element.13), channel_id=1, source_target_pairs={{0,16},{1,17},{2,18},{3,19},{4,20},{5,21},{6,22},{7,23},{8,24},{9,... | collective-permute-start | bytes 196616 | tf_op jit(solution)/shard_map/ppermute | solution.py:179
  7.6 6.7 %collective-permute-start = (bf16[256,128]{1,0:T(8,128)(2,1)}, bf16[256,128]{1,0:T(8,128)(2,1)S(1)}, u32[]{:S(2)}, u32[]{:S(2)}) collective-permute-start(bf16[256,128]{1,0:T(8,128)(2,1)} %get-tuple-element.13), channel_id=1, source_target_pairs={{0,8},{1,9},{2,10},{3,11},{4,12},{5,13},{6,14},{7,15},{8,0},{9,1},... | collective-permute-start | bytes 196616 | tf_op jit(solution)/shard_map/ppermute | solution.py:179
  8.2 13.5 %all-to-all-start = ((bf16[32,8,128]{2,1,0:T(8,128)(2,1)}), bf16[32,8,128]{2,1,0:T(8,128)(2,1)S(1)}, u32[]{:S(2)}, u32[]{:S(2)}) async-start(bf16[32,8,128]{2,1,0:T(8,128)(2,1)} %get-tuple-element.14), calls=%async_computation | async-start | bytes 131072 | tf_op jit(solution)/shard_map/all_to_all | solution.py:210
  15.2 10.7 %collective-permute-start.6 = (bf16[4,256,128]{2,1,0:T(8,128)(2,1)S(1)}, bf16[4,256,128]{2,1,0:T(8,128)(2,1)S(1)}, u32[]{:S(2)}, u32[]{:S(2)}) collective-permute-start(bf16[4,256,128]{2,1,0:T(8,128)(2,1)S(1)} %pad_maximum_fusion.refs_0_), channel_id=1, source_target_pairs={{0,1},{1,0},{2,3},{3,2},{4,5},{5,4},{6,7},{7,6},{8,9},{9,8},{10,11... | collective-permute-start | bytes 786440 | tf_op jit(solution)/shard_map/ppermute | solution.py:179
  15.5 12.0 %collective-permute-start.5 = (bf16[4,256,128]{2,1,0:T(8,128)(2,1)S(1)}, bf16[4,256,128]{2,1,0:T(8,128)(2,1)S(1)}, u32[]{:S(2)}, u32[]{:S(2)}) collective-permute-start(bf16[4,256,128]{2,1,0:T(8,128)(2,1)S(1)} %pad_maximum_fusion.refs_0_), channel_id=1, source_target_pairs={{0,6},{1,7},{2,4},{3,5},{4,2},{5,3},{6,0},{7,1},{8,14},{9,15},{10,... | collective-permute-start | bytes 786440 | tf_op jit(solution)/shard_map/ppermute | solution.py:179
  18.1 12.8 %collective-permute-start.4 = (bf16[4,256,128]{2,1,0:T(8,128)(2,1)S(1)}, bf16[4,256,128]{2,1,0:T(8,128)(2,1)S(1)}, u32[]{:S(2)}, u32[]{:S(2)}) collective-permute-start(bf16[4,256,128]{2,1,0:T(8,128)(2,1)S(1)} %pad_maximum_fusion.refs_0_), channel_id=1, source_target_pairs={{0,4},{1,5},{2,6},{3,7},{4,0},{5,1},{6,2},{7,3},{8,12},{9,13},{10,... | collective-permute-start | bytes 786440 | tf_op jit(solution)/shard_map/ppermute | solution.py:179
  18.6 12.4 %collective-permute-start.3 = (bf16[4,256,128]{2,1,0:T(8,128)(2,1)S(1)}, bf16[4,256,128]{2,1,0:T(8,128)(2,1)S(1)}, u32[]{:S(2)}, u32[]{:S(2)}) collective-permute-start(bf16[4,256,128]{2,1,0:T(8,128)(2,1)S(1)} %pad_maximum_fusion.refs_0_), channel_id=1, source_target_pairs={{0,2},{1,3},{2,0},{3,1},{4,6},{5,7},{6,4},{7,5},{8,10},{9,11},{10,... | collective-permute-start | bytes 786440 | tf_op jit(solution)/shard_map/ppermute | solution.py:179
  21.7 1.0 %copy-start.2 = (bf16[1024,128]{1,0:T(8,128)(2,1)S(1)}, bf16[1024,128]{1,0:T(8,128)(2,1)}, u32[]{:S(2)}) copy-start(bf16[1024,128]{1,0:T(8,128)(2,1)} %final_ref.1) | copy-start | bytes 786436
  27.4 6.3 %copy-start = (bf16[512,16,128]{2,1,0:T(8,128)(2,1)S(1)}, bf16[512,16,128]{2,1,0:T(8,128)(2,1)}, u32[]{:S(2)}) copy-start(bf16[512,16,128]{2,1,0:T(8,128)(2,1)} %refs_6_.1) | copy-start | bytes 6291460
  27.5 6.3 %copy-start.1 = (f32[128]{0:T(128)S(1)}, f32[128]{0:T(128)}, u32[]{:S(2)}) copy-start(f32[128]{0:T(128)} %param.19) | copy-start | bytes 1540
  31.0 2.7 %collective-permute-start.7 = (bf16[4,256,128]{2,1,0:T(8,128)(2,1)S(1)}, bf16[4,256,128]{2,1,0:T(8,128)(2,1)S(1)}, u32[]{:S(2)}, u32[]{:S(2)}) collective-permute-start(bf16[4,256,128]{2,1,0:T(8,128)(2,1)S(1)} %collective-permute-done.3.refs_0_), channel_id=1, source_target_pairs={{0,1},{1,0},{2,3},{3,2},{4,5},{5,4},{6,7},{7,6},{8,9},{9,8},{10,11... | collective-permute-start | bytes 786440 | tf_op jit(solution)/shard_map/ppermute | solution.py:179
  31.0 2.7 %collective-permute-start.8 = (bf16[4,256,128]{2,1,0:T(8,128)(2,1)S(1)}, bf16[4,256,128]{2,1,0:T(8,128)(2,1)S(1)}, u32[]{:S(2)}, u32[]{:S(2)}) collective-permute-start(bf16[4,256,128]{2,1,0:T(8,128)(2,1)S(1)} %collective-permute-done.4.refs_1_), channel_id=1, source_target_pairs={{0,1},{1,0},{2,3},{3,2},{4,5},{5,4},{6,7},{7,6},{8,9},{9,8},{10,11... | collective-permute-start | bytes 786440 | tf_op jit(solution)/shard_map/ppermute | solution.py:179
  31.5 2.2 %collective-permute-start.9 = (bf16[4,256,128]{2,1,0:T(8,128)(2,1)S(1)}, bf16[4,256,128]{2,1,0:T(8,128)(2,1)S(1)}, u32[]{:S(2)}, u32[]{:S(2)}) collective-permute-start(bf16[4,256,128]{2,1,0:T(8,128)(2,1)S(1)} %collective-permute-done.5.refs_2_), channel_id=1, source_target_pairs={{0,1},{1,0},{2,3},{3,2},{4,5},{5,4},{6,7},{7,6},{8,9},{9,8},{10,11... | collective-permute-start | bytes 786440 | tf_op jit(solution)/shard_map/ppermute | solution.py:179

commit v4 on v3

--- a/solution.py
+++ b/solution.py
@@ -101,10 +101,10 @@
                 out_ref[g, 0, pl.ds(pair * 16, 16), pl.ds(j * LANES, LANES)] = tile.astype(jnp.bfloat16)
 
 
-def _band_kernel(masks, begins, count, held, *refs):
+def _band_kernel(lines, operands, begins, count, held, *refs):
     refs = list(refs)
     take = lambda k: [refs.pop(0) for _ in range(k)]
-    lines = take(len(masks))
+    blocks = take(operands)
     t_ref, order_ref = take(2)
     (sum_ref,) = (None,) if begins else take(1)
     pair_ref, shift_ref = (None, None) if count is None else take(2)
@@ -112,11 +112,12 @@
     (l_ref,) = take(1)
     me = lax.axis_index("row")
     wide = 8 * CHANS
-    places, half, _ = lines[0].shape
+    half = blocks[0].shape[-2]
     chunks = []
-    for line, mask in zip(lines, masks):
-        for q in range(places // 4):
-            lhs = jnp.concatenate([line[q * 4 + u] for u in range(4)], axis=1)
+    for mask, line in lines.items():
+        for q in range(len(line) // 4):
+            slots = [blocks[i][...] if k is None else blocks[i][k] for i, k in line[q * 4 : q * 4 + 4]]
+            lhs = jnp.concatenate(slots, axis=1)
             at = pl.ds(len(chunks) * wide, wide)
             for h in range(2):
                 moved = jnp.dot(lhs, order_ref[h], preferred_element_type=jnp.float32)
@@ -209,10 +210,11 @@
 
     right = lax.all_to_all(right, "row", split_axis=0, concat_axis=0, tiled=True)
 
-    line = [left] + [_xor(left, m, n) for m in range(8, n, 8)]
-    line = jnp.stack(line)
-    plane = [_xor(line, m, n) for m in (2, 4, 6)]
-
+    alone = [_xor(left, m, n) for m in range(8, n, 8)]
+    firsts = [_xor(left, m, n) for m in (2, 4, 6)]
+    partner = _xor(left, 1, n)
+    rest = jnp.stack(alone)
+    plane = [_xor(rest, m, n) for m in (2, 4, 6)]
     part = 32
     parts = n // part
     fold_cost = pl.CostEstimate(
@@ -240,10 +242,10 @@
         _fold_kernel, out_shape=fold_out, compiler_params=params, cost_estimate=fold_cost, **specs
     )(right, final)
 
-    def add(lines, masks, total, last):
-        depth = len(masks) * parts * 8 * CHANS
+    def add(blocks, lines, total, last):
+        depth = len(lines) * parts * 8 * CHANS
         scratch = [pltpu.VMEM((band, depth), jnp.bfloat16)]
-        operands = [*lines, folded, order] + ([] if total is None else [total])
+        operands = [*blocks, folded, order] + ([] if total is None else [total])
         if last:
             operands += [pair, shift.reshape(1, -1)]
             scratch += [
@@ -255,9 +257,9 @@
             scratch.append(pltpu.VMEM((depth, 256), jnp.bfloat16))
         in_specs = [vmem] * len(operands)
         if not small:
-            in_specs[len(lines)] = anywhere
+            in_specs[len(blocks)] = anywhere
         return pl.pallas_call(
-            functools.partial(_band_kernel, masks, total is None, count if last else None, small),
+            functools.partial(_band_kernel, lines, len(blocks), total is None, count if last else None, small),
             in_specs=in_specs,
             out_specs=anywhere if last else vmem,
             out_shape=jax.ShapeDtypeStruct(pair.shape, jnp.bfloat16)
@@ -270,11 +272,18 @@
             ),
         )(*operands)
 
-    total = add([line, _xor(line, 1, n)], (0, 1), None, False)
+    more = len(alone)
+    whole = lambda first, i: [first] + [(i, k) for k in range(more)]
+    alone, firsts, folded = lax.optimization_barrier((alone, firsts, folded))
+    across = _xor(jnp.stack(alone + firsts), 1, n)
+    total = add([left, rest], {0: whole((0, None), 1)}, None, False)
     plane, total = lax.optimization_barrier((plane, total))
-    other = [_xor(o, 1, n) for o in plane]
-    total = add(plane, (2, 4, 6), total, False)
-    return add(other, (3, 5, 7), total, True)
+    others = [_xor(o, 1, n) for o in plane]
+    lines = {2 * g + 2: whole((g, None), 3 + g) for g in range(3)}
+    lines[1] = whole((6, None), 7)
+    total = add(firsts + plane + [partner, across], lines, total, False)
+    lines = {2 * g + 3: whole((0, more + g), 1 + g) for g in range(3)}
+    return add([across] + others, lines, total, True)
 
 
 def solution(mesh):

time: 37.8 us -> 42.8 us (1.13)
  starting transfers between devices: 16.1 us -> 19.4 us
  waiting for transfers between devices: 6.28 us -> 8.66 us
  other arithmetic: 0.88 us -> 0.03 us
    ppermute x10 -> x14, waiting for transfers between devices: 3.54 us -> 8.65 us  [_xor(): return lax.ppermute(x, 'row', [(i, i ^ mask) for i in range(n)])]
    all_to_all x1, waiting for transfers between devices: 2.74 us -> 0.01 us  [shards(): lax.all_to_all(right, 'row', split_axis=0, concat_axis=0, tiled=True)]
    ppermute x10 -> x14, starting transfers between devices: 10.1 us -> 12.1 us  [_xor(): return lax.ppermute(x, 'row', [(i, i ^ mask) for i in range(n)])]
    all_to_all x1, starting transfers between devices: 5.99 us -> 7.3 us  [shards(): lax.all_to_all(right, 'row', split_axis=0, concat_axis=0, tiled=True)]
    another operation x1, other arithmetic: 0.88 us -> 0.03 us  [shards(): rest = jnp.stack(alone)]
    unnamed x6 -> x13, local copies, waits for them, and re-layouts: 0.96 us -> 1.03 us
  transfers between devices with their start and end apart: 11 -> 15, of which waited for: 3 -> 4; matrix products, arithmetic and copies ran while one was open for 2% -> 0% of each run, Pallas kernels for 19% -> 17%
where the time goes in v4:
time: 42.8 us; the launch traced here: 42.5 us
  starting transfers between devices  19.4 us (45%)
  Pallas kernels  13.3 us (31%)
  waiting for transfers between devices  8.66 us (20%)
  local copies, waits for them, and re-layouts  1.05 us (2%)
    ppermute x14, starting transfers between devices, _xor(): return lax.ppermute(x, 'row', [(i, i ^ mask) for i in range(n)])  12.1 us
    ppermute x14, waiting for transfers between devices, _xor(): return lax.ppermute(x, 'row', [(i, i ^ mask) for i in range(n)])  8.65 us
    pallas_call x3, Pallas kernels, add(): pl.pallas_call(functools.partial(_band_kernel, lines, len(blocks), total...  7.53 us
    all_to_all x1, starting transfers between devices, shards(): lax.all_to_all(right, 'row', split_axis=0, concat_axis=0, tiled=True)  7.3 us
    pallas_call x1, Pallas kernels, shards(): pl.pallas_call(_fold_kernel, out_shape=fold_out, compiler_params=params,...  3.24 us
    pallas_call x1, Pallas kernels, shards(): pl.pallas_call(_project_kernel, in_specs=[pl.BlockSpec(memory_space=pltpu...  2.48 us
    unnamed x13, local copies, waits for them, and re-layouts  1.03 us
  transfers between devices with their start and end apart: 15, of which 4 were waited for; matrix products, arithmetic and copies ran while one was open for 0% of the time, Pallas kernels for 17%

profile of v4, /device:TPU:0, one launch (start us, length us, event | category | flops | bytes accessed | tf_op | source)
XLA Modules:
  0.0 42.5 jit_solution(12170171046549663467)
XLA Ops:
  0.0 2.5 %shard_map.100 = (bf16[256,128]{1,0:T(8,128)(2,1)}, bf16[32,8,128]{2,1,0:T(8,128)(2,1)}) custom-call(bf16[2,512,256]{2,1,0:T(8,128)(2,1)} %refs_0_.1, f32[1,256]{1,0:T(1,128)} %bitcast.28, f32[1,256]{1,0:T(1,128)} %bitcast.29, bf16[32,256]{1,0:T(8,128)(2,1)} %bitcast.26, f32[1,32]{1,0:T(1,128)} %bitcast.30, bf16[32,256]{1,0:T(8,128)(2,1)} %bitcast.27, ...), custom_call_target="tpu_custom_call" | custom-call | flops 33554432 | bytes 524288 | tf_op jit(solution)/shard_map/pallas_call | solution.py:196
  2.5 7.3 %all-to-all-start = ((bf16[32,8,128]{2,1,0:T(8,128)(2,1)}), bf16[32,8,128]{2,1,0:T(8,128)(2,1)S(1)}, u32[]{:S(2)}, u32[]{:S(2)}) async-start(bf16[32,8,128]{2,1,0:T(8,128)(2,1)} %get-tuple-element.21), calls=%async_computation | async-start | bytes 131072 | tf_op jit(solution)/shard_map/all_to_all | solution.py:211
  9.8 0.0 copy-start.1
  9.8 2.7 %collective-permute-start.5 = (bf16[256,128]{1,0:T(8,128)(2,1)}, bf16[256,128]{1,0:T(8,128)(2,1)S(1)}, u32[]{:S(2)}, u32[]{:S(2)}) collective-permute-start(bf16[256,128]{1,0:T(8,128)(2,1)} %get-tuple-element.20.refs_0_), channel_id=1, source_target_pairs={{0,6},{1,7},{2,4},{3,5},{4,2},{5,3},{6,0},{7,1},{8,14},{9,15},{10,... | collective-permute-start | bytes 196616 | tf_op jit(solution)/shard_map/ppermute | solution.py:180
  12.5 0.6 %collective-permute-start.4 = (bf16[256,128]{1,0:T(8,128)(2,1)}, bf16[256,128]{1,0:T(8,128)(2,1)S(1)}, u32[]{:S(2)}, u32[]{:S(2)}) collective-permute-start(bf16[256,128]{1,0:T(8,128)(2,1)} %get-tuple-element.20.refs_0_), channel_id=1, source_target_pairs={{0,4},{1,5},{2,6},{3,7},{4,0},{5,1},{6,2},{7,3},{8,12},{9,13},{10,... | collective-permute-start | bytes 196616 | tf_op jit(solution)/shard_map/ppermute | solution.py:180
  13.1 0.3 collective-permute-start.3
  13.4 3.6 %collective-permute-start.2 = (bf16[256,128]{1,0:T(8,128)(2,1)}, bf16[256,128]{1,0:T(8,128)(2,1)S(1)}, u32[]{:S(2)}, u32[]{:S(2)}) collective-permute-start(bf16[256,128]{1,0:T(8,128)(2,1)} %get-tuple-element.20.refs_0_), channel_id=1, source_target_pairs={{0,24},{1,25},{2,26},{3,27},{4,28},{5,29},{6,30},{7,31},{8,16},{9,... | collective-permute-start | bytes 196616 | tf_op jit(solution)/shard_map/ppermute | solution.py:180
  17.0 0.0 collective-permute-start.1
  17.0 0.0 collective-permute-done.5.refs_2_
  17.0 0.8 %collective-permute-start = (bf16[256,128]{1,0:T(8,128)(2,1)}, bf16[256,128]{1,0:T(8,128)(2,1)S(1)}, u32[]{:S(2)}, u32[]{:S(2)}) collective-permute-start(bf16[256,128]{1,0:T(8,128)(2,1)} %get-tuple-element.20.refs_0_), channel_id=1, source_target_pairs={{0,8},{1,9},{2,10},{3,11},{4,12},{5,13},{6,14},{7,15},{8,0},{9,1},... | collective-permute-start | bytes 196616 | tf_op jit(solution)/shard_map/ppermute | solution.py:180
  17.8 0.0 all-to-all-done.right_ref
  17.8 0.9 %copy-done.3 = bf16[1024,128]{1,0:T(8,128)(2,1)S(1)} copy-done((bf16[1024,128]{1,0:T(8,128)(2,1)S(1)}, bf16[1024,128]{1,0:T(8,128)(2,1)}, u32[]{:S(2)}) %copy-start.3) | copy-done | bytes 262168
  18.7 3.2 %shard_map.101 = (bf16[8,1,256,2048]{3,2,1,0:T(8,128)(2,1)S(1)}, bf16[2,512,256]{2,1,0:T(8,128)(2,1)S(1)}) custom-call(bf16[32,8,128]{2,1,0:T(8,128)(2,1)S(1)} %all-to-all-done.right_ref, bf16[1024,128]{1,0:T(8,128)(2,1)S(1)} %copy-done.3), custom_call_target="tpu_custom_call" | custom-call | flops 2147483648 | bytes 8388608 | tf_op jit(solution)/shard_map/pallas_call | solution.py:241
  22.0 0.0 collective-permute-done.4.refs_1_
  22.0 0.6 %collective-permute-done.1 = bf16[256,128]{1,0:T(8,128)(2,1)S(1)} collective-permute-done((bf16[256,128]{1,0:T(8,128)(2,1)}, bf16[256,128]{1,0:T(8,128)(2,1)S(1)}, u32[]{:S(2)}, u32[]{:S(2)}) %collective-permute-start.1) | collective-permute-done | bytes 65568 | tf_op jit(solution)/shard_map/ppermute | solution.py:180
  22.7 0.1 collective-permute-start.6
  22.8 2.4 %collective-permute-start.9 = (bf16[3,256,128]{2,1,0:T(8,128)(2,1)S(1)}, bf16[3,256,128]{2,1,0:T(8,128)(2,1)S(1)}, u32[]{:S(2)}, u32[]{:S(2)}) collective-permute-start(bf16[3,256,128]{2,1,0:T(8,128)(2,1)S(1)} %pad_maximum_fusion.refs_1_), channel_id=1, source_target_pairs={{0,6},{1,7},{2,4},{3,5},{4,2},{5,3},{6,0},{7,1},{8,14},{9,15},{10,... | collective-permute-start | bytes 589832 | tf_op jit(solution)/shard_map/ppermute | solution.py:180
  25.3 0.6 %collective-permute-start.8 = (bf16[3,256,128]{2,1,0:T(8,128)(2,1)S(1)}, bf16[3,256,128]{2,1,0:T(8,128)(2,1)S(1)}, u32[]{:S(2)}, u32[]{:S(2)}) collective-permute-start(bf16[3,256,128]{2,1,0:T(8,128)(2,1)S(1)} %pad_maximum_fusion.refs_1_), channel_id=1, source_target_pairs={{0,4},{1,5},{2,6},{3,7},{4,0},{5,1},{6,2},{7,3},{8,12},{9,13},{10,... | collective-permute-start | bytes 589832 | tf_op jit(solution)/shard_map/ppermute | solution.py:180
  25.8 0.6 %collective-permute-start.7 = (bf16[3,256,128]{2,1,0:T(8,128)(2,1)S(1)}, bf16[3,256,128]{2,1,0:T(8,128)(2,1)S(1)}, u32[]{:S(2)}, u32[]{:S(2)}) collective-permute-start(bf16[3,256,128]{2,1,0:T(8,128)(2,1)S(1)} %pad_maximum_fusion.refs_1_), channel_id=1, source_target_pairs={{0,2},{1,3},{2,0},{3,1},{4,6},{5,7},{6,4},{7,5},{8,10},{9,11},{10,... | collective-permute-start | bytes 589832 | tf_op jit(solution)/shard_map/ppermute | solution.py:180
  26.4 0.0 collective-permute-start.13
  26.4 0.9 %shard_map.102.refs_10_ = f32[512,2048]{1,0:T(8,128)S(1)} custom-call(bf16[256,128]{1,0:T(8,128)(2,1)S(1)} %copy-done.1, bf16[3,256,128]{2,1,0:T(8,128)(2,1)S(1)} %pad_maximum_fusion.refs_1_, bf16[8,1,256,2048]{3,2,1,0:T(8,128)(2,1)S(1)} %get-tuple-element.29.refs_2_.refs_8_.refs_4_, bf16[2,512,256]{2,1,0:T(8,128)(2,1)S(1)} %get-tuple-element.30.refs_3_.refs_9_.refs_5_), custom_call_target="tpu_custom_call" | custom-call | flops 536870912 | bytes 1048576 | tf_op jit(solution)/shard_map/pallas_call | solution.py:261
  27.3 0.0 copy-start
  27.3 0.0 copy-start.2
  27.4 4.2 %collective-permute-done.9.refs_5_ = bf16[3,256,128]{2,1,0:T(8,128)(2,1)S(1)} collective-permute-done((bf16[3,256,128]{2,1,0:T(8,128)(2,1)S(1)}, bf16[3,256,128]{2,1,0:T(8,128)(2,1)S(1)}, u32[]{:S(2)}, u32[]{:S(2)}) %collective-permute-start.9) | collective-permute-done | bytes 196640 | tf_op jit(solution)/shard_map/ppermute | solution.py:180
  31.5 3.8 %collective-permute-done.8.refs_4_ = bf16[3,256,128]{2,1,0:T(8,128)(2,1)S(1)} collective-permute-done((bf16[3,256,128]{2,1,0:T(8,128)(2,1)S(1)}, bf16[3,256,128]{2,1,0:T(8,128)(2,1)S(1)}, u32[]{:S(2)}, u32[]{:S(2)}) %collective-permute-start.8) | collective-permute-done | bytes 196640 | tf_op jit(solution)/shard_map/ppermute | solution.py:180
  35.3 0.1 collective-permute-done.7.refs_3_
  35.4 0.5 %collective-permute-start.11 = (bf16[3,256,128]{2,1,0:T(8,128)(2,1)S(1)}, bf16[3,256,128]{2,1,0:T(8,128)(2,1)S(1)}, u32[]{:S(2)}, u32[]{:S(2)}) collective-permute-start(bf16[3,256,128]{2,1,0:T(8,128)(2,1)S(1)} %collective-permute-done.8.refs_4_), channel_id=1, source_target_pairs={{0,1},{1,0},{2,3},{3,2},{4,5},{5,4},{6,7},{7,6},{8,9},{9,8},{10,11... | collective-permute-start | bytes 589832 | tf_op jit(solution)/shard_map/ppermute | solution.py:180
  35.9 0.0 collective-permute-start.12
  35.9 0.0 collective-permute-done.13.refs_6_
  35.9 0.0 collective-permute-done.6.refs_7_.refs_0_
  35.9 2.9 %shard_map.103.refs_6_ = f32[512,2048]{1,0:T(8,128)S(1)} custom-call(bf16[256,128]{1,0:T(8,128)(2,1)S(1)} %collective-permute-done.3.refs_0_, bf16[256,128]{1,0:T(8,128)(2,1)S(1)} %collective-permute-done.4.refs_1_, bf16[256,128]{1,0:T(8,128)(2,1)S(1)} %collective-permute-done.5.refs_2_, bf16[3,256,128]{2,1,0:T(8,128)(2,1)S(1)} %collective-permute-done.7.refs_3_, ...), custom_call_target="tpu_custom_call" | custom-call | flops 2147483648 | bytes 4194304 | tf_op jit(solution)/shard_map/pallas_call | solution.py:261
  38.8 3.7 %shard_map.104 = bf16[512,16,128]{2,1,0:T(8,128)(2,1)} custom-call(bf16[6,256,128]{2,1,0:T(8,128)(2,1)S(1)} %collective-permute-done.6.refs_7_.refs_0_, bf16[3,256,128]{2,1,0:T(8,128)(2,1)S(1)} %collective-permute-done.10.refs_1_, bf16[3,256,128]{2,1,0:T(8,128)(2,1)S(1)} %collective-permute-done.11.refs_2_, ...), custom_call_target="tpu_custom_call" | custom-call | flops 1610612736 | bytes 3145728 | tf_op jit(solution)/shard_map/pallas_call | solution.py:261
  (18 shorter events, 0.1 us)
Async XLA Ops:
  2.5 15.3 %all-to-all-start = ((bf16[32,8,128]{2,1,0:T(8,128)(2,1)}), bf16[32,8,128]{2,1,0:T(8,128)(2,1)S(1)}, u32[]{:S(2)}, u32[]{:S(2)}) async-start(bf16[32,8,128]{2,1,0:T(8,128)(2,1)} %get-tuple-element.21), calls=%async_computation | async-start | bytes 131072 | tf_op jit(solution)/shard_map/all_to_all | solution.py:211
  9.8 16.6 %copy-start.1 = (bf16[256,128]{1,0:T(8,128)(2,1)S(1)}, bf16[256,128]{1,0:T(8,128)(2,1)}, u32[]{:S(2)}) copy-start(bf16[256,128]{1,0:T(8,128)(2,1)} %get-tuple-element.20.refs_0_) | copy-start | bytes 196612
  9.8 7.2 %collective-permute-start.5 = (bf16[256,128]{1,0:T(8,128)(2,1)}, bf16[256,128]{1,0:T(8,128)(2,1)S(1)}, u32[]{:S(2)}, u32[]{:S(2)}) collective-permute-start(bf16[256,128]{1,0:T(8,128)(2,1)} %get-tuple-element.20.refs_0_), channel_id=1, source_target_pairs={{0,6},{1,7},{2,4},{3,5},{4,2},{5,3},{6,0},{7,1},{8,14},{9,15},{10,... | collective-permute-start | bytes 196616 | tf_op jit(solution)/shard_map/ppermute | solution.py:180
  12.5 9.4 %collective-permute-start.4 = (bf16[256,128]{1,0:T(8,128)(2,1)}, bf16[256,128]{1,0:T(8,128)(2,1)S(1)}, u32[]{:S(2)}, u32[]{:S(2)}) collective-permute-start(bf16[256,128]{1,0:T(8,128)(2,1)} %get-tuple-element.20.refs_0_), channel_id=1, source_target_pairs={{0,4},{1,5},{2,6},{3,7},{4,0},{5,1},{6,2},{7,3},{8,12},{9,13},{10,... | collective-permute-start | bytes 196616 | tf_op jit(solution)/shard_map/ppermute | solution.py:180
  13.1 8.9 %collective-permute-start.3 = (bf16[256,128]{1,0:T(8,128)(2,1)}, bf16[256,128]{1,0:T(8,128)(2,1)S(1)}, u32[]{:S(2)}, u32[]{:S(2)}) collective-permute-start(bf16[256,128]{1,0:T(8,128)(2,1)} %get-tuple-element.20.refs_0_), channel_id=1, source_target_pairs={{0,2},{1,3},{2,0},{3,1},{4,6},{5,7},{6,4},{7,5},{8,10},{9,11},{10,... | collective-permute-start | bytes 196616 | tf_op jit(solution)/shard_map/ppermute | solution.py:180
  13.4 8.6 %collective-permute-start.2 = (bf16[256,128]{1,0:T(8,128)(2,1)}, bf16[256,128]{1,0:T(8,128)(2,1)S(1)}, u32[]{:S(2)}, u32[]{:S(2)}) collective-permute-start(bf16[256,128]{1,0:T(8,128)(2,1)} %get-tuple-element.20.refs_0_), channel_id=1, source_target_pairs={{0,24},{1,25},{2,26},{3,27},{4,28},{5,29},{6,30},{7,31},{8,16},{9,... | collective-permute-start | bytes 196616 | tf_op jit(solution)/shard_map/ppermute | solution.py:180
  17.0 5.6 %collective-permute-start.1 = (bf16[256,128]{1,0:T(8,128)(2,1)}, bf16[256,128]{1,0:T(8,128)(2,1)S(1)}, u32[]{:S(2)}, u32[]{:S(2)}) collective-permute-start(bf16[256,128]{1,0:T(8,128)(2,1)} %get-tuple-element.20.refs_0_), channel_id=1, source_target_pairs={{0,16},{1,17},{2,18},{3,19},{4,20},{5,21},{6,22},{7,23},{8,24},{9,... | collective-permute-start | bytes 196616 | tf_op jit(solution)/shard_map/ppermute | solution.py:180
  17.0 5.6 %collective-permute-start = (bf16[256,128]{1,0:T(8,128)(2,1)}, bf16[256,128]{1,0:T(8,128)(2,1)S(1)}, u32[]{:S(2)}, u32[]{:S(2)}) collective-permute-start(bf16[256,128]{1,0:T(8,128)(2,1)} %get-tuple-element.20.refs_0_), channel_id=1, source_target_pairs={{0,8},{1,9},{2,10},{3,11},{4,12},{5,13},{6,14},{7,15},{8,0},{9,1},... | collective-permute-start | bytes 196616 | tf_op jit(solution)/shard_map/ppermute | solution.py:180
  17.8 1.0 %copy-start.3 = (bf16[1024,128]{1,0:T(8,128)(2,1)S(1)}, bf16[1024,128]{1,0:T(8,128)(2,1)}, u32[]{:S(2)}) copy-start(bf16[1024,128]{1,0:T(8,128)(2,1)} %final_ref.1) | copy-start | bytes 786436
  22.7 13.2 %collective-permute-start.6 = (bf16[6,256,128]{2,1,0:T(8,128)(2,1)S(1)}, bf16[6,256,128]{2,1,0:T(8,128)(2,1)S(1)}, u32[]{:S(2)}, u32[]{:S(2)}) collective-permute-start(bf16[6,256,128]{2,1,0:T(8,128)(2,1)S(1)} %bitcast_dynamic-update-slice_fusion), channel_id=1, source_target_pairs={{0,1},{1,0},{2,3},{3,2},{4,5},{5,4},{6,7},{7,6},{8,9},{9,8},{10,11... | collective-permute-start | bytes 1179656 | tf_op jit(solution)/shard_map/ppermute | solution.py:180
  22.8 8.7 %collective-permute-start.9 = (bf16[3,256,128]{2,1,0:T(8,128)(2,1)S(1)}, bf16[3,256,128]{2,1,0:T(8,128)(2,1)S(1)}, u32[]{:S(2)}, u32[]{:S(2)}) collective-permute-start(bf16[3,256,128]{2,1,0:T(8,128)(2,1)S(1)} %pad_maximum_fusion.refs_1_), channel_id=1, source_target_pairs={{0,6},{1,7},{2,4},{3,5},{4,2},{5,3},{6,0},{7,1},{8,14},{9,15},{10,... | collective-permute-start | bytes 589832 | tf_op jit(solution)/shard_map/ppermute | solution.py:180
  25.3 10.0 %collective-permute-start.8 = (bf16[3,256,128]{2,1,0:T(8,128)(2,1)S(1)}, bf16[3,256,128]{2,1,0:T(8,128)(2,1)S(1)}, u32[]{:S(2)}, u32[]{:S(2)}) collective-permute-start(bf16[3,256,128]{2,1,0:T(8,128)(2,1)S(1)} %pad_maximum_fusion.refs_1_), channel_id=1, source_target_pairs={{0,4},{1,5},{2,6},{3,7},{4,0},{5,1},{6,2},{7,3},{8,12},{9,13},{10,... | collective-permute-start | bytes 589832 | tf_op jit(solution)/shard_map/ppermute | solution.py:180
  25.8 9.5 %collective-permute-start.7 = (bf16[3,256,128]{2,1,0:T(8,128)(2,1)S(1)}, bf16[3,256,128]{2,1,0:T(8,128)(2,1)S(1)}, u32[]{:S(2)}, u32[]{:S(2)}) collective-permute-start(bf16[3,256,128]{2,1,0:T(8,128)(2,1)S(1)} %pad_maximum_fusion.refs_1_), channel_id=1, source_target_pairs={{0,2},{1,3},{2,0},{3,1},{4,6},{5,7},{6,4},{7,5},{8,10},{9,11},{10,... | collective-permute-start | bytes 589832 | tf_op jit(solution)/shard_map/ppermute | solution.py:180
  26.4 9.5 %collective-permute-start.13 = (bf16[256,128]{1,0:T(8,128)(2,1)S(1)}, bf16[256,128]{1,0:T(8,128)(2,1)S(1)}, u32[]{:S(2)}, u32[]{:S(2)}) collective-permute-start(bf16[256,128]{1,0:T(8,128)(2,1)S(1)} %copy-done.1), channel_id=1, source_target_pairs={{0,1},{1,0},{2,3},{3,2},{4,5},{5,4},{6,7},{7,6},{8,9},{9,8},{10,11... | collective-permute-start | bytes 196616 | tf_op jit(solution)/shard_map/ppermute | solution.py:180
  27.3 11.5 %copy-start = (bf16[512,16,128]{2,1,0:T(8,128)(2,1)S(1)}, bf16[512,16,128]{2,1,0:T(8,128)(2,1)}, u32[]{:S(2)}) copy-start(bf16[512,16,128]{2,1,0:T(8,128)(2,1)} %refs_7_.1) | copy-start | bytes 6291460
  27.3 11.5 %copy-start.2 = (f32[128]{0:T(128)S(1)}, f32[128]{0:T(128)}, u32[]{:S(2)}) copy-start(f32[128]{0:T(128)} %param.19) | copy-start | bytes 1540
  35.4 3.4 %collective-permute-start.10 = (bf16[3,256,128]{2,1,0:T(8,128)(2,1)S(1)}, bf16[3,256,128]{2,1,0:T(8,128)(2,1)S(1)}, u32[]{:S(2)}, u32[]{:S(2)}) collective-permute-start(bf16[3,256,128]{2,1,0:T(8,128)(2,1)S(1)} %collective-permute-done.7.refs_3_), channel_id=1, source_target_pairs={{0,1},{1,0},{2,3},{3,2},{4,5},{5,4},{6,7},{7,6},{8,9},{9,8},{10,11... | collective-permute-start | bytes 589832 | tf_op jit(solution)/shard_map/ppermute | solution.py:180
  35.4 3.4 %collective-permute-start.11 = (bf16[3,256,128]{2,1,0:T(8,128)(2,1)S(1)}, bf16[3,256,128]{2,1,0:T(8,128)(2,1)S(1)}, u32[]{:S(2)}, u32[]{:S(2)}) collective-permute-start(bf16[3,256,128]{2,1,0:T(8,128)(2,1)S(1)} %collective-permute-done.8.refs_4_), channel_id=1, source_target_pairs={{0,1},{1,0},{2,3},{3,2},{4,5},{5,4},{6,7},{7,6},{8,9},{9,8},{10,11... | collective-permute-start | bytes 589832 | tf_op jit(solution)/shard_map/ppermute | solution.py:180
  35.9 2.9 %collective-permute-start.12 = (bf16[3,256,128]{2,1,0:T(8,128)(2,1)S(1)}, bf16[3,256,128]{2,1,0:T(8,128)(2,1)S(1)}, u32[]{:S(2)}, u32[]{:S(2)}) collective-permute-start(bf16[3,256,128]{2,1,0:T(8,128)(2,1)S(1)} %collective-permute-done.9.refs_5_), channel_id=1, source_target_pairs={{0,1},{1,0},{2,3},{3,2},{4,5},{5,4},{6,7},{7,6},{8,9},{9,8},{10,11... | collective-permute-start | bytes 589832 | tf_op jit(solution)/shard_map/ppermute | solution.py:180

commit v5 on v4

--- a/solution.py
+++ b/solution.py
@@ -31,7 +31,7 @@
     for copy in copies:
         copy.wait()
     x_ref, gain_ref, bias_ref, w1_ref, b1_ref, w2_ref, b2_ref = held
-    band_half = left_ref.shape[0]
+    band_half = left_ref.shape[1]
     n = right_ref.shape[0]
     feats = x_ref.shape[2]
     normed = []
@@ -47,7 +47,9 @@
     left = lax.dot_general(
         jnp.concatenate(low + high, axis=1), _stacked(w1_ref[...], 4), NT, preferred_element_type=jnp.float32
     )
-    left_ref[...] = (left + shift1).astype(jnp.bfloat16)
+    left = (left + shift1).astype(jnp.bfloat16)
+    for k in range(left_ref.shape[0]):
+        left_ref[k] = left
 
     split = [v.reshape(n, 2, 8, feats) for v in normed]
     parts = [split[s][:, jh].reshape(n * 8, feats).astype(jnp.bfloat16) for jh in range(2) for s in range(2)]
@@ -58,19 +60,17 @@
     right_ref[...] = (right + shift2).reshape(n, 8, LANES).astype(jnp.bfloat16)
 
 
-def _order(me, half):
+def _order(half):
     row = lax.broadcasted_iota(jnp.int32, (4 * LANES, 8 * CHANS), 0)
     col = lax.broadcasted_iota(jnp.int32, (4 * LANES, 8 * CHANS), 1)
-    device = (row // LANES) ^ (me // 8 % 4)
-    wanted = (row % CHANS) * 8 + ((row // CHANS) % 2) * 4 + device
+    wanted = (row % CHANS) * 8 + ((row // CHANS) % 2) * 4 + row // LANES
     hit = (wanted == col) & ((row // (2 * CHANS)) % 2 == half)
     return jnp.where(hit, 1.0, 0.0).astype(jnp.bfloat16)
 
 
 def _fold_kernel(right_ref, final_ref, out_ref, order_ref):
-    me = lax.axis_index("row")
     for h in range(2):
-        order_ref[h] = _order(me, h)
+        order_ref[h] = _order(h)
     devices = right_ref.shape[0]
     groups = devices // 4
     rows = devices * 8
@@ -112,17 +112,17 @@
     (l_ref,) = take(1)
     me = lax.axis_index("row")
     wide = 8 * CHANS
-    half = blocks[0].shape[-2]
+    places, half, _ = blocks[0].shape[-3:]
     chunks = []
-    for mask, line in lines.items():
-        for q in range(len(line) // 4):
-            slots = [blocks[i][...] if k is None else blocks[i][k] for i, k in line[q * 4 : q * 4 + 4]]
-            lhs = jnp.concatenate(slots, axis=1)
+    for mask, operand, plane in lines:
+        block = blocks[operand].at[(me // 2 % 4) ^ (mask // 2)] if plane else blocks[operand]
+        for q in range(places // 4):
+            lhs = jnp.concatenate([block[q * 4 + u] for u in range(4)], axis=1)
             at = pl.ds(len(chunks) * wide, wide)
             for h in range(2):
                 moved = jnp.dot(lhs, order_ref[h], preferred_element_type=jnp.float32)
                 l_ref[pl.ds(h * half, half), at] = moved.astype(jnp.bfloat16)
-            chunks.append(((me % 8) ^ mask, q ^ (me // 32)))
+            chunks.append(((me % 8) ^ mask, q))
 
     tile = 256
     band = 2 * half
@@ -198,7 +198,7 @@
         in_specs=[pl.BlockSpec(memory_space=pltpu.HBM)] * 7,
         out_specs=(vmem, vmem),
         out_shape=(
-            jax.ShapeDtypeStruct((half, LANES), jnp.bfloat16),
+            jax.ShapeDtypeStruct((n // 8, half, LANES), jnp.bfloat16),
             jax.ShapeDtypeStruct((n, 8, LANES), jnp.bfloat16),
         ),
         scratch_shapes=[pltpu.VMEM(a.shape, a.dtype) for a in sources] + [pltpu.SemaphoreType.DMA((7,))],
@@ -210,11 +210,13 @@
 
     right = lax.all_to_all(right, "row", split_axis=0, concat_axis=0, tiled=True)
 
-    alone = [_xor(left, m, n) for m in range(8, n, 8)]
-    firsts = [_xor(left, m, n) for m in (2, 4, 6)]
-    partner = _xor(left, 1, n)
-    rest = jnp.stack(alone)
-    plane = [_xor(rest, m, n) for m in (2, 4, 6)]
+    places = n // 8
+    along = [[i * 8 + g for i in range(places)] for g in range(8)]
+    across = [[i * 8 + g * 2 + c for g in range(4)] for i in range(places) for c in range(2)]
+    line = lax.all_to_all(left, "row", 0, 0, axis_index_groups=along, tiled=True)
+    plane = jnp.broadcast_to(line[None], (4,) + line.shape)
+    plane = lax.all_to_all(plane, "row", 0, 0, axis_index_groups=across, tiled=True)
+
     part = 32
     parts = n // part
     fold_cost = pl.CostEstimate(
@@ -272,18 +274,11 @@
             ),
         )(*operands)
 
-    more = len(alone)
-    whole = lambda first, i: [first] + [(i, k) for k in range(more)]
-    alone, firsts, folded = lax.optimization_barrier((alone, firsts, folded))
-    across = _xor(jnp.stack(alone + firsts), 1, n)
-    total = add([left, rest], {0: whole((0, None), 1)}, None, False)
+    total = add([line, _xor(line, 1, n)], [(0, 0, False), (1, 1, False)], None, False)
     plane, total = lax.optimization_barrier((plane, total))
-    others = [_xor(o, 1, n) for o in plane]
-    lines = {2 * g + 2: whole((g, None), 3 + g) for g in range(3)}
-    lines[1] = whole((6, None), 7)
-    total = add(firsts + plane + [partner, across], lines, total, False)
-    lines = {2 * g + 3: whole((0, more + g), 1 + g) for g in range(3)}
-    return add([across] + others, lines, total, True)
+    other = _xor(plane, 1, n)
+    total = add([plane], [(m, 0, True) for m in (2, 4, 6)], total, False)
+    return add([other], [(m, 0, True) for m in (3, 5, 7)], total, True)
 
 
 def solution(mesh):

time: 42.8 us -> 59.8 us (1.40)
  blocking collectives: 0 us -> 27.5 us
  starting transfers between devices: 19.4 us -> 3.59 us
  local copies, waits for them, and re-layouts: 1.05 us -> 11.9 us
  waiting for transfers between devices: 8.66 us -> 2.93 us
    all_to_all x0 -> x2, blocking collectives: none -> 27.5 us  [the longest x1 14.7 us: shards(): lax.all_to_all(right, 'row', split_axis=0, concat_axis=0, tiled=True)]
    ppermute x14 -> x2, starting transfers between devices: 12.1 us -> 0.07 us  [_xor(): return lax.ppermute(x, 'row', [(i, i ^ mask) for i in range(n)])]
    unnamed x13 -> x14, local copies, waits for them, and re-layouts: 1.03 us -> 10.7 us
    ppermute x14 -> x2, waiting for transfers between devices: 8.65 us -> 0.01 us  [_xor(): return lax.ppermute(x, 'row', [(i, i ^ mask) for i in range(n)])]
    all_to_all x1, starting transfers between devices: 7.3 us -> 3.52 us  [shards(): lax.all_to_all(plane, 'row', 0, 0, axis_index_groups=across, tiled=True)]
    all_to_all x1, waiting for transfers between devices: 0.01 us -> 2.92 us  [shards(): lax.all_to_all(plane, 'row', 0, 0, axis_index_groups=across, tiled=True)]
    broadcast_in_dim x0 -> x1, local copies, waits for them, and re-layouts: none -> 1.17 us  [shards(): plane = jnp.broadcast_to(line[None], (4,) + line.shape)]
  transfers between devices with their start and end apart: 15 -> 3, of which waited for: 4 -> 1; matrix products, arithmetic and copies ran while one was open for 0% -> 0% of each run, Pallas kernels for 17% -> 12%
where the time goes in v5:
time: 59.8 us; the launch traced here: 59.4 us
  blocking collectives  27.5 us (46%)
  Pallas kernels  13.3 us (22%)
  local copies, waits for them, and re-layouts  11.9 us (20%)
  starting transfers between devices  3.59 us (6%)
  waiting for transfers between devices  2.93 us (5%)
    all_to_all x1, blocking collectives, shards(): lax.all_to_all(right, 'row', split_axis=0, concat_axis=0, tiled=True)  14.7 us
    all_to_all x1, blocking collectives, shards(): lax.all_to_all(left, 'row', 0, 0, axis_index_groups=along, tiled=True)  12.8 us
    unnamed x14, local copies, waits for them, and re-layouts  10.7 us
    pallas_call x3, Pallas kernels, add(): pl.pallas_call(functools.partial(_band_kernel, lines, len(blocks), total...  7.47 us
    all_to_all x1, starting transfers between devices, shards(): lax.all_to_all(plane, 'row', 0, 0, axis_index_groups=across, tiled=True)  3.52 us
    pallas_call x1, Pallas kernels, shards(): pl.pallas_call(_fold_kernel, out_shape=fold_out, compiler_params=params,...  3.23 us
    all_to_all x1, waiting for transfers between devices, shards(): lax.all_to_all(plane, 'row', 0, 0, axis_index_groups=across, tiled=True)  2.92 us
    pallas_call x1, Pallas kernels, shards(): pl.pallas_call(_project_kernel, in_specs=[pl.BlockSpec(memory_space=pltpu...  2.6 us
  transfers between devices with their start and end apart: 3, of which 1 were waited for; matrix products, arithmetic and copies ran while one was open for 0% of the time, Pallas kernels for 12%

profile of v5, /device:TPU:0, one launch (start us, length us, event | category | flops | bytes accessed | tf_op | source)
XLA Modules:
  0.0 59.4 jit_solution(4982030701554333264)
XLA Ops:
  0.0 0.0 copy-start.6
  0.0 2.6 %shard_map.100 = (bf16[4,256,128]{2,1,0:T(8,128)(2,1)}, bf16[32,8,128]{2,1,0:T(8,128)(2,1)}) custom-call(bf16[2,512,256]{2,1,0:T(8,128)(2,1)} %refs_0_.1, f32[1,256]{1,0:T(1,128)} %bitcast.10, f32[1,256]{1,0:T(1,128)} %bitcast.11, bf16[32,256]{1,0:T(8,128)(2,1)} %bitcast.8, f32[1,32]{1,0:T(1,128)} %bitcast.12, bf16[32,256]{1,0:T(8,128)(2,1)} %bitcast.9, ...), custom_call_target="tpu_custom_call" | custom-call | flops 33554432 | bytes 524288 | tf_op jit(solution)/shard_map/pallas_call | solution.py:196
  2.6 14.7 %all_to_all.15.right_ref = bf16[32,8,128]{2,1,0:T(8,128)(2,1)S(1)} all-to-all(bf16[32,8,128]{2,1,0:T(8,128)(2,1)} %get-tuple-element.12), channel_id=1, replica_groups=mesh['group'=1,'row'=32] {'row'}, dimensions={0} | all-to-all | bytes 131072 | tf_op jit(solution)/shard_map/all_to_all | solution.py:211
  17.3 12.8 %all_to_all.16.refs_0_ = bf16[4,256,128]{2,1,0:T(8,128)(2,1)S(1)} all-to-all(bf16[4,256,128]{2,1,0:T(8,128)(2,1)} %get-tuple-element.11), channel_id=1, replica_groups={{0,8,16,24},{1,9,17,25},{2,10,18,26},{3,11,19,27},{4,12,20,28},{5,13,21..., dimensions={0} | all-to-all | bytes 524288 | tf_op jit(solution)/shard_map/all_to_all | solution.py:216
  30.1 1.2 %broadcast_in_dim.2 = bf16[4,4,256,128]{3,2,1,0:T(8,128)(2,1)} broadcast(bf16[4,256,128]{2,1,0:T(8,128)(2,1)S(1)} %all_to_all.16.refs_0_), dimensions={1,2,3} | broadcast | bytes 1310720 | tf_op jit(solution)/shard_map/broadcast_in_dim | solution.py:217
  31.3 3.5 %all-to-all-start.1 = ((bf16[4,4,256,128]{3,2,1,0:T(8,128)(2,1)}), bf16[4,4,256,128]{3,2,1,0:T(8,128)(2,1)S(1)}, u32[]{:S(2)}, u32[]{:S(2)}) async-start(bf16[4,4,256,128]{3,2,1,0:T(8,128)(2,1)} %broadcast_in_dim.2), calls=%async_computation.1 | async-start | bytes 2097152 | tf_op jit(solution)/shard_map/all_to_all | solution.py:218
  34.8 0.1 collective-permute-start
  34.9 0.0 copy-done.6
  34.9 3.2 %shard_map.101 = (bf16[8,1,256,2048]{3,2,1,0:T(8,128)(2,1)S(1)}, bf16[2,512,256]{2,1,0:T(8,128)(2,1)S(1)}) custom-call(bf16[32,8,128]{2,1,0:T(8,128)(2,1)S(1)} %all_to_all.15.right_ref, bf16[1024,128]{1,0:T(8,128)(2,1)S(1)} %copy-done.6), custom_call_target="tpu_custom_call" | custom-call | flops 2147483648 | bytes 8388608 | tf_op jit(solution)/shard_map/pallas_call | solution.py:243
  38.2 0.0 collective-permute-done.refs_1_
  38.2 0.0 copy-start.5
  38.2 1.5 %shard_map.102.refs_3_ = f32[512,2048]{1,0:T(8,128)S(1)} custom-call(bf16[4,256,128]{2,1,0:T(8,128)(2,1)S(1)} %all_to_all.16.refs_0_, bf16[4,256,128]{2,1,0:T(8,128)(2,1)S(1)} %collective-permute-done.refs_1_, bf16[8,1,256,2048]{3,2,1,0:T(8,128)(2,1)S(1)} %get-tuple-element.13.refs_2_.refs_1_, bf16[2,512,256]{2,1,0:T(8,128)(2,1)S(1)} %get-tuple-element.14.refs_3_.refs_2_), custom_call_target="tpu_custom_call" | custom-call | flops 1073741824 | bytes 2097152 | tf_op jit(solution)/shard_map/pallas_call | solution.py:263
  39.7 0.0 copy-start
  39.7 3.2 %copy-done = bf16[8,1,256,2048]{3,2,1,0:T(8,128)(2,1)} copy-done((bf16[8,1,256,2048]{3,2,1,0:T(8,128)(2,1)}, bf16[8,1,256,2048]{3,2,1,0:T(8,128)(2,1)S(1)}, u32[]{:S(2)}) %copy-start) | copy-done | bytes 8388632
  42.9 0.0 copy-start.2
  42.9 2.0 %copy-done.2 = f32[512,2048]{1,0:T(8,128)} copy-done((f32[512,2048]{1,0:T(8,128)}, f32[512,2048]{1,0:T(8,128)S(1)}, u32[]{:S(2)}) %copy-start.2) | copy-done | bytes 4194328
  44.9 2.9 %all-to-all-done.1.refs_0_ = bf16[4,4,256,128]{3,2,1,0:T(8,128)(2,1)S(1)} async-done(((bf16[4,4,256,128]{3,2,1,0:T(8,128)(2,1)}), bf16[4,4,256,128]{3,2,1,0:T(8,128)(2,1)S(1)}, u32[]{:S(2)}, u32[]{:S(2)}) %all-to-all-start.1) | async-done | bytes 1048608 | tf_op jit(solution)/shard_map/all_to_all | solution.py:218
  47.8 0.0 collective-permute-start.1
  47.8 0.0 copy-start.1
  47.8 3.4 %copy-done.1 = bf16[8,1,256,2048]{3,2,1,0:T(8,128)(2,1)S(1)} copy-done((bf16[8,1,256,2048]{3,2,1,0:T(8,128)(2,1)S(1)}, bf16[8,1,256,2048]{3,2,1,0:T(8,128)(2,1)}, u32[]{:S(2)}) %copy-start.1) | copy-done | bytes 8388632
  51.2 0.0 copy-start.3
  51.2 2.2 %copy-done.3 = f32[512,2048]{1,0:T(8,128)S(1)} copy-done((f32[512,2048]{1,0:T(8,128)S(1)}, f32[512,2048]{1,0:T(8,128)}, u32[]{:S(2)}) %copy-start.3) | copy-done | bytes 4194328
  53.4 0.0 copy-start.4
  53.4 2.2 %shard_map.103.refs_3_ = f32[512,2048]{1,0:T(8,128)S(1)} custom-call(bf16[4,4,256,128]{3,2,1,0:T(8,128)(2,1)S(1)} %all-to-all-done.1.refs_0_, bf16[8,1,256,2048]{3,2,1,0:T(8,128)(2,1)S(1)} %copy-done.1, bf16[2,512,256]{2,1,0:T(8,128)(2,1)S(1)} %get-tuple-element.14.refs_3_.refs_2_, f32[512,2048]{1,0:T(8,128)S(1)} %copy-done.3), custom_call_target="tpu_custom_call" | custom-call | flops 1610612736 | bytes 3145728 | tf_op jit(solution)/shard_map/pallas_call | solution.py:263
  55.6 0.0 collective-permute-done.1.refs_0_
  55.6 0.0 copy-done.5
  55.6 0.0 copy-done.4
  55.6 3.7 %shard_map.104 = bf16[512,16,128]{2,1,0:T(8,128)(2,1)} custom-call(bf16[4,4,256,128]{3,2,1,0:T(8,128)(2,1)S(1)} %collective-permute-done.1.refs_0_, bf16[8,1,256,2048]{3,2,1,0:T(8,128)(2,1)S(1)} %copy-done.1, bf16[2,512,256]{2,1,0:T(8,128)(2,1)S(1)} %get-tuple-element.14.refs_3_.refs_2_, f32[512,2048]{1,0:T(8,128)S(1)} %shard_map.103.refs_3_, ...), custom_call_target="tpu_custom_call" | custom-call | flops 1610612736 | bytes 3145728 | tf_op jit(solution)/shard_map/pallas_call | solution.py:263
Async XLA Ops:
  0.0 34.9 %copy-start.6 = (bf16[1024,128]{1,0:T(8,128)(2,1)S(1)}, bf16[1024,128]{1,0:T(8,128)(2,1)}, u32[]{:S(2)}) copy-start(bf16[1024,128]{1,0:T(8,128)(2,1)} %final_ref.1) | copy-start | bytes 786436
  31.3 16.5 %all-to-all-start.1 = ((bf16[4,4,256,128]{3,2,1,0:T(8,128)(2,1)}), bf16[4,4,256,128]{3,2,1,0:T(8,128)(2,1)S(1)}, u32[]{:S(2)}, u32[]{:S(2)}) async-start(bf16[4,4,256,128]{3,2,1,0:T(8,128)(2,1)} %broadcast_in_dim.2), calls=%async_computation.1 | async-start | bytes 2097152 | tf_op jit(solution)/shard_map/all_to_all | solution.py:218
  34.8 3.3 %collective-permute-start = (bf16[4,256,128]{2,1,0:T(8,128)(2,1)S(1)}, bf16[4,256,128]{2,1,0:T(8,128)(2,1)S(1)}, u32[]{:S(2)}, u32[]{:S(2)}) collective-permute-start(bf16[4,256,128]{2,1,0:T(8,128)(2,1)S(1)} %all_to_all.16.refs_0_), channel_id=1, source_target_pairs={{0,1},{1,0},{2,3},{3,2},{4,5},{5,4},{6,7},{7,6},{8,9},{9,8},{10,11... | collective-permute-start | bytes 786440 | tf_op jit(solution)/shard_map/ppermute | solution.py:180
  38.2 17.4 %copy-start.5 = (f32[128]{0:T(128)S(1)}, f32[128]{0:T(128)}, u32[]{:S(2)}) copy-start(f32[128]{0:T(128)} %param.19) | copy-start | bytes 1540
  39.7 3.2 %copy-start = (bf16[8,1,256,2048]{3,2,1,0:T(8,128)(2,1)}, bf16[8,1,256,2048]{3,2,1,0:T(8,128)(2,1)S(1)}, u32[]{:S(2)}) copy-start(bf16[8,1,256,2048]{3,2,1,0:T(8,128)(2,1)S(1)} %get-tuple-element.13.refs_2_.refs_1_) | copy-start | bytes 25165828
  42.9 2.0 %copy-start.2 = (f32[512,2048]{1,0:T(8,128)}, f32[512,2048]{1,0:T(8,128)S(1)}, u32[]{:S(2)}) copy-start(f32[512,2048]{1,0:T(8,128)S(1)} %shard_map.102.refs_3_) | copy-start | bytes 12582916
  47.8 7.8 %collective-permute-start.1 = (bf16[4,4,256,128]{3,2,1,0:T(8,128)(2,1)S(1)}, bf16[4,4,256,128]{3,2,1,0:T(8,128)(2,1)S(1)}, u32[]{:S(2)}, u32[]{:S(2)}) collective-permute-start(bf16[4,4,256,128]{3,2,1,0:T(8,128)(2,1)S(1)} %all-to-all-done.1.refs_0_), channel_id=1, source_target_pairs={{0,1},{1,0},{2,3},{3,2},{4,5},{5,4},{6,7},{7,6},{8,9},{9,8},{10,11... | collective-permute-start | bytes 3145736 | tf_op jit(solution)/shard_map/ppermute | solution.py:180
  47.8 3.4 %copy-start.1 = (bf16[8,1,256,2048]{3,2,1,0:T(8,128)(2,1)S(1)}, bf16[8,1,256,2048]{3,2,1,0:T(8,128)(2,1)}, u32[]{:S(2)}) copy-start(bf16[8,1,256,2048]{3,2,1,0:T(8,128)(2,1)} %copy-done) | copy-start | bytes 25165828
  51.2 2.2 %copy-start.3 = (f32[512,2048]{1,0:T(8,128)S(1)}, f32[512,2048]{1,0:T(8,128)}, u32[]{:S(2)}) copy-start(f32[512,2048]{1,0:T(8,128)} %copy-done.2) | copy-start | bytes 12582916
  53.4 2.2 %copy-start.4 = (bf16[512,16,128]{2,1,0:T(8,128)(2,1)S(1)}, bf16[512,16,128]{2,1,0:T(8,128)(2,1)}, u32[]{:S(2)}) copy-start(bf16[512,16,128]{2,1,0:T(8,128)(2,1)} %refs_4_.1) | copy-start | bytes 6291460

commit v6 on v3

--- a/solution.py
+++ b/solution.py
@@ -67,7 +67,9 @@
     return jnp.where(hit, 1.0, 0.0).astype(jnp.bfloat16)
 
 
-def _fold_kernel(right_ref, final_ref, out_ref, order_ref):
+def _fold_kernel(right_ref, source_ref, out_ref, order_ref, final_ref, sem):
+    fetch = pltpu.make_async_copy(source_ref, final_ref, sem)
+    fetch.start()
     me = lax.axis_index("row")
     for h in range(2):
         order_ref[h] = _order(me, h)
@@ -88,6 +90,7 @@
         lhs.append(moved.astype(jnp.bfloat16))
     lhs = jnp.concatenate(lhs, axis=0)
 
+    fetch.wait()
     for pair in range(CHANS // 2):
         rhs = []
         for k in range(2):
@@ -192,6 +195,7 @@
     sources = [
         alignment, gain.reshape(1, -1), bias.reshape(1, -1), w1.T, b1.reshape(1, -1), w2.T, b2.reshape(1, -1)
     ]
+    sources = [pltpu.with_memory_space_constraint(a, pltpu.HBM) for a in sources]
     left, right = pl.pallas_call(
         _project_kernel,
         in_specs=[pl.BlockSpec(memory_space=pltpu.HBM)] * 7,
@@ -201,7 +205,7 @@
             jax.ShapeDtypeStruct((n, 8, LANES), jnp.bfloat16),
         ),
         scratch_shapes=[pltpu.VMEM(a.shape, a.dtype) for a in sources] + [pltpu.SemaphoreType.DMA((7,))],
-        compiler_params=pltpu.CompilerParams(vmem_limit_bytes=60 * 1024 * 1024),
+        compiler_params=params,
         cost_estimate=pl.CostEstimate(
             flops=4 * seqs * residues * feats * CHANS, bytes_accessed=2 * seqs * residues * feats, transcendentals=0
         ),
@@ -223,13 +227,13 @@
         jax.ShapeDtypeStruct((2, 4 * LANES, 8 * CHANS), jnp.bfloat16),
     )
     if small:
-        specs = dict(in_specs=[vmem, vmem], out_specs=(vmem, vmem))
+        specs = dict(in_specs=[vmem, anywhere], out_specs=(vmem, vmem))
     else:
         specs = dict(
             grid=(parts,),
             in_specs=[
                 pl.BlockSpec((part, 8, LANES), lambda i: (i, 0, 0)),
-                pl.BlockSpec(final.shape, lambda i: (0, 0)),
+                anywhere,
             ],
             out_specs=(
                 pl.BlockSpec((8, 1, 8 * CHANS, cols * zdim), lambda i: (0, i, 0, 0)),
@@ -237,8 +241,13 @@
             ),
         )
     folded, order = pl.pallas_call(
-        _fold_kernel, out_shape=fold_out, compiler_params=params, cost_estimate=fold_cost, **specs
-    )(right, final)
+        _fold_kernel,
+        out_shape=fold_out,
+        scratch_shapes=[pltpu.VMEM(final.shape, final.dtype), pltpu.SemaphoreType.DMA(())],
+        compiler_params=params,
+        cost_estimate=fold_cost,
+        **specs,
+    )(right, pltpu.with_memory_space_constraint(final, pltpu.HBM))
 
     def add(lines, masks, total, last):
         depth = len(masks) * parts * 8 * CHANS
@@ -270,11 +279,15 @@
             ),
         )(*operands)
 
-    total = add([line, _xor(line, 1, n)], (0, 1), None, False)
-    plane, total = lax.optimization_barrier((plane, total))
-    other = [_xor(o, 1, n) for o in plane]
-    total = add(plane, (2, 4, 6), total, False)
-    return add(other, (3, 5, 7), total, True)
+    sent, _ = lax.optimization_barrier((line, right))
+    total = add([line, _xor(sent, 1, n)], (0, 1), None, False)
+    diagonal, total = lax.optimization_barrier((plane[2], total))
+    crossed = _xor(diagonal, 1, n)
+    total = add([diagonal], (6,), total, False)
+    x, y, total = lax.optimization_barrier((plane[0], plane[1], total))
+    others = [_xor(x, 1, n), _xor(y, 1, n)]
+    total = add([x, y, crossed], (2, 4, 7), total, False)
+    return add(others, (3, 5), total, True)
 
 
 def solution(mesh):

time: 37.8 us -> 42.9 us (1.13)
  waiting for transfers between devices: 6.28 us -> 12.6 us
  local copies, waits for them, and re-layouts: 0.96 us -> 0.01 us
  other arithmetic: 0.88 us -> 0.04 us
  Pallas kernels: 13.2 us -> 14 us
    all_to_all x1, waiting for transfers between devices: 2.74 us -> 7.33 us  [shards(): lax.all_to_all(right, 'row', split_axis=0, concat_axis=0, tiled=True)]
    ppermute x10, waiting for transfers between devices: 3.54 us -> 5.27 us  [_xor(): return lax.ppermute(x, 'row', [(i, i ^ mask) for i in range(n)])]
    unnamed x6 -> x4, local copies, waits for them, and re-layouts: 0.96 us -> 0.01 us
    another operation x1, other arithmetic: 0.88 us -> 0.04 us  [shards(): line = jnp.stack(line)]
    pallas_call x1, Pallas kernels: 3.24 us -> 3.84 us  [shards(): pl.pallas_call(_fold_kernel, out_shape=fold_out, scratch_shapes=[pltpu.VM...]
    pallas_call x3 -> x4, Pallas kernels: 7.44 us -> 7.69 us  [add(): pl.pallas_call(functools.partial(_band_kernel, masks, total is None, coun...]
  transfers between devices with their start and end apart: 11 -> 11, of which waited for: 3 -> 4; matrix products, arithmetic and copies ran while one was open for 2% -> 0% of each run, Pallas kernels for 19% -> 20%
where the time goes in v6:
time: 42.9 us; the launch traced here: 42.7 us
  starting transfers between devices  15.9 us (37%)
  Pallas kernels  14 us (33%)
  waiting for transfers between devices  12.6 us (29%)
    ppermute x10, starting transfers between devices, _xor(): return lax.ppermute(x, 'row', [(i, i ^ mask) for i in range(n)])  9.83 us
    pallas_call x4, Pallas kernels, add(): pl.pallas_call(functools.partial(_band_kernel, masks, total is None, coun...  7.69 us
    all_to_all x1, waiting for transfers between devices, shards(): lax.all_to_all(right, 'row', split_axis=0, concat_axis=0, tiled=True)  7.33 us
    all_to_all x1, starting transfers between devices, shards(): lax.all_to_all(right, 'row', split_axis=0, concat_axis=0, tiled=True)  6.07 us
    ppermute x10, waiting for transfers between devices, _xor(): return lax.ppermute(x, 'row', [(i, i ^ mask) for i in range(n)])  5.27 us
    pallas_call x1, Pallas kernels, shards(): pl.pallas_call(_fold_kernel, out_shape=fold_out, scratch_shapes=[pltpu.VM...  3.84 us
    pallas_call x1, Pallas kernels, shards(): pl.pallas_call(_project_kernel, in_specs=[pl.BlockSpec(memory_space=pltpu...  2.45 us
  transfers between devices with their start and end apart: 11, of which 4 were waited for; matrix products, arithmetic and copies ran while one was open for 0% of the time, Pallas kernels for 20%

profile of v6, /device:TPU:0, one launch (start us, length us, event | category | flops | bytes accessed | tf_op | source)
XLA Modules:
  0.0 42.7 jit_solution(16017090771981896932)
XLA Ops:
  0.0 2.5 %shard_map.100 = (bf16[256,128]{1,0:T(8,128)(2,1)S(1)}, bf16[32,8,128]{2,1,0:T(8,128)(2,1)}) custom-call(bf16[2,512,256]{2,1,0:T(8,128)(2,1)} %refs_0_.1, f32[1,256]{1,0:T(1,128)} %bitcast.18, f32[1,256]{1,0:T(1,128)} %bitcast.19, bf16[32,256]{1,0:T(8,128)(2,1)} %bitcast.16, f32[1,32]{1,0:T(1,128)} %bitcast.20, bf16[32,256]{1,0:T(8,128)(2,1)} %bitcast.17, ...), custom_call_target="tpu_custom_call" | custom-call | flops 33554432 | bytes 524288 | tf_op jit(solution)/shard_map/pallas_call | solution.py:199
  2.5 3.1 %collective-permute-start = (bf16[256,128]{1,0:T(8,128)(2,1)S(1)}, bf16[256,128]{1,0:T(8,128)(2,1)S(1)}, u32[]{:S(2)}, u32[]{:S(2)}) collective-permute-start(bf16[256,128]{1,0:T(8,128)(2,1)S(1)} %get-tuple-element.15), channel_id=1, source_target_pairs={{0,8},{1,9},{2,10},{3,11},{4,12},{5,13},{6,14},{7,15},{8,0},{9,1},... | collective-permute-start | bytes 196616 | tf_op jit(solution)/shard_map/ppermute | solution.py:182
  5.6 2.6 %collective-permute-start.1 = (bf16[256,128]{1,0:T(8,128)(2,1)S(1)}, bf16[256,128]{1,0:T(8,128)(2,1)S(1)}, u32[]{:S(2)}, u32[]{:S(2)}) collective-permute-start(bf16[256,128]{1,0:T(8,128)(2,1)S(1)} %get-tuple-element.15), channel_id=1, source_target_pairs={{0,16},{1,17},{2,18},{3,19},{4,20},{5,21},{6,22},{7,23},{8,24},{9,... | collective-permute-start | bytes 196616 | tf_op jit(solution)/shard_map/ppermute | solution.py:182
  8.1 0.0 collective-permute-start.2
  8.1 6.1 %all-to-all-start = ((bf16[32,8,128]{2,1,0:T(8,128)(2,1)}), bf16[32,8,128]{2,1,0:T(8,128)(2,1)S(1)}, u32[]{:S(2)}, u32[]{:S(2)}) async-start(bf16[32,8,128]{2,1,0:T(8,128)(2,1)} %get-tuple-element.16), calls=%async_computation | async-start | bytes 131072 | tf_op jit(solution)/shard_map/all_to_all | solution.py:214
  14.2 0.0 collective-permute-done
  14.2 0.0 collective-permute-done.1
  14.2 0.0 collective-permute-done.2
  14.3 7.3 %all-to-all-done.right_ref = bf16[32,8,128]{2,1,0:T(8,128)(2,1)S(1)} async-done(((bf16[32,8,128]{2,1,0:T(8,128)(2,1)}), bf16[32,8,128]{2,1,0:T(8,128)(2,1)S(1)}, u32[]{:S(2)}, u32[]{:S(2)}) %all-to-all-start) | async-done | bytes 65568 | tf_op jit(solution)/shard_map/all_to_all | solution.py:214
  21.6 0.1 collective-permute-start.6
  21.7 0.6 %collective-permute-start.5 = (bf16[4,256,128]{2,1,0:T(8,128)(2,1)S(1)}, bf16[4,256,128]{2,1,0:T(8,128)(2,1)S(1)}, u32[]{:S(2)}, u32[]{:S(2)}) collective-permute-start(bf16[4,256,128]{2,1,0:T(8,128)(2,1)S(1)} %pad_maximum_fusion.refs_0_), channel_id=1, source_target_pairs={{0,6},{1,7},{2,4},{3,5},{4,2},{5,3},{6,0},{7,1},{8,14},{9,15},{10,... | collective-permute-start | bytes 786440 | tf_op jit(solution)/shard_map/ppermute | solution.py:182
  22.4 1.4 %collective-permute-start.3 = (bf16[4,256,128]{2,1,0:T(8,128)(2,1)S(1)}, bf16[4,256,128]{2,1,0:T(8,128)(2,1)S(1)}, u32[]{:S(2)}, u32[]{:S(2)}) collective-permute-start(bf16[4,256,128]{2,1,0:T(8,128)(2,1)S(1)} %pad_maximum_fusion.refs_0_), channel_id=1, source_target_pairs={{0,2},{1,3},{2,0},{3,1},{4,6},{5,7},{6,4},{7,5},{8,10},{9,11},{10,... | collective-permute-start | bytes 786440 | tf_op jit(solution)/shard_map/ppermute | solution.py:182
  23.7 1.5 %collective-permute-start.4 = (bf16[4,256,128]{2,1,0:T(8,128)(2,1)S(1)}, bf16[4,256,128]{2,1,0:T(8,128)(2,1)S(1)}, u32[]{:S(2)}, u32[]{:S(2)}) collective-permute-start(bf16[4,256,128]{2,1,0:T(8,128)(2,1)S(1)} %pad_maximum_fusion.refs_0_), channel_id=1, source_target_pairs={{0,4},{1,5},{2,6},{3,7},{4,0},{5,1},{6,2},{7,3},{8,12},{9,13},{10,... | collective-permute-start | bytes 786440 | tf_op jit(solution)/shard_map/ppermute | solution.py:182
  25.3 3.8 %shard_map.101 = (bf16[8,1,256,2048]{3,2,1,0:T(8,128)(2,1)S(1)}, bf16[2,512,256]{2,1,0:T(8,128)(2,1)S(1)}) custom-call(bf16[32,8,128]{2,1,0:T(8,128)(2,1)S(1)} %all-to-all-done.right_ref, bf16[1024,128]{1,0:T(8,128)(2,1)} %source_ref.1), custom_call_target="tpu_custom_call" | custom-call | flops 2147483648 | bytes 8388608 | tf_op jit(solution)/shard_map/pallas_call | solution.py:243
  29.1 0.0 collective-permute-done.6.refs_1_
  29.1 1.5 %shard_map.102.refs_3_ = f32[512,2048]{1,0:T(8,128)S(1)} custom-call(bf16[4,256,128]{2,1,0:T(8,128)(2,1)S(1)} %pad_maximum_fusion.refs_0_, bf16[4,256,128]{2,1,0:T(8,128)(2,1)S(1)} %collective-permute-done.6.refs_1_, bf16[8,1,256,2048]{3,2,1,0:T(8,128)(2,1)S(1)} %get-tuple-element.18.refs_2_.refs_1_.refs_3_, ...), custom_call_target="tpu_custom_call" | custom-call | flops 1073741824 | bytes 2097152 | tf_op jit(solution)/shard_map/pallas_call | solution.py:268
  30.7 1.2 %collective-permute-done.5.refs_0_ = bf16[4,256,128]{2,1,0:T(8,128)(2,1)S(1)} collective-permute-done((bf16[4,256,128]{2,1,0:T(8,128)(2,1)S(1)}, bf16[4,256,128]{2,1,0:T(8,128)(2,1)S(1)}, u32[]{:S(2)}, u32[]{:S(2)}) %collective-permute-start.5) | collective-permute-done | bytes 262176 | tf_op jit(solution)/shard_map/ppermute | solution.py:182
  31.8 0.0 collective-permute-start.9
  31.8 0.9 %shard_map.103.refs_5_ = f32[512,2048]{1,0:T(8,128)S(1)} custom-call(bf16[4,256,128]{2,1,0:T(8,128)(2,1)S(1)} %collective-permute-done.5.refs_0_, bf16[8,1,256,2048]{3,2,1,0:T(8,128)(2,1)S(1)} %get-tuple-element.18.refs_2_.refs_1_.refs_3_, bf16[2,512,256]{2,1,0:T(8,128)(2,1)S(1)} %get-tuple-element.19.refs_3_.refs_2_.refs_4_, f32[512,2048]{1,0:T(8,128)S(1)} %shard_map.102.refs_3_), custom_call_target="tpu_custom_call" | custom-call | flops 536870912 | bytes 1048576 | tf_op jit(solution)/shard_map/pallas_call | solution.py:268
  32.8 0.0 copy-start
  32.8 0.0 copy-start.1
  32.8 3.2 %collective-permute-done.3.refs_0_ = bf16[4,256,128]{2,1,0:T(8,128)(2,1)S(1)} collective-permute-done((bf16[4,256,128]{2,1,0:T(8,128)(2,1)S(1)}, bf16[4,256,128]{2,1,0:T(8,128)(2,1)S(1)}, u32[]{:S(2)}, u32[]{:S(2)}) %collective-permute-start.3) | collective-permute-done | bytes 262176 | tf_op jit(solution)/shard_map/ppermute | solution.py:182
  36.0 0.8 %collective-permute-done.4.refs_1_ = bf16[4,256,128]{2,1,0:T(8,128)(2,1)S(1)} collective-permute-done((bf16[4,256,128]{2,1,0:T(8,128)(2,1)S(1)}, bf16[4,256,128]{2,1,0:T(8,128)(2,1)S(1)}, u32[]{:S(2)}, u32[]{:S(2)}) %collective-permute-start.4) | collective-permute-done | bytes 262176 | tf_op jit(solution)/shard_map/ppermute | solution.py:182
  36.9 0.0 collective-permute-start.7
  36.9 0.5 %collective-permute-start.8 = (bf16[4,256,128]{2,1,0:T(8,128)(2,1)S(1)}, bf16[4,256,128]{2,1,0:T(8,128)(2,1)S(1)}, u32[]{:S(2)}, u32[]{:S(2)}) collective-permute-start(bf16[4,256,128]{2,1,0:T(8,128)(2,1)S(1)} %collective-permute-done.4.refs_1_), channel_id=1, source_target_pairs={{0,1},{1,0},{2,3},{3,2},{4,5},{5,4},{6,7},{7,6},{8,9},{9,8},{10,11... | collective-permute-start | bytes 786440 | tf_op jit(solution)/shard_map/ppermute | solution.py:182
  37.4 0.0 collective-permute-done.9.refs_2_
  37.4 2.2 %shard_map.104.refs_4_ = f32[512,2048]{1,0:T(8,128)S(1)} custom-call(bf16[4,256,128]{2,1,0:T(8,128)(2,1)S(1)} %collective-permute-done.3.refs_0_, bf16[4,256,128]{2,1,0:T(8,128)(2,1)S(1)} %collective-permute-done.4.refs_1_, bf16[4,256,128]{2,1,0:T(8,128)(2,1)S(1)} %collective-permute-done.9.refs_2_, ...), custom_call_target="tpu_custom_call" | custom-call | flops 1610612736 | bytes 3145728 | tf_op jit(solution)/shard_map/pallas_call | solution.py:268
  39.6 0.0 collective-permute-done.7.refs_0_
  39.6 0.0 collective-permute-done.8.refs_1_
  39.6 0.0 copy-done
  39.6 0.0 copy-done.1
  39.6 3.0 %shard_map.105 = bf16[512,16,128]{2,1,0:T(8,128)(2,1)} custom-call(bf16[4,256,128]{2,1,0:T(8,128)(2,1)S(1)} %collective-permute-done.7.refs_0_, bf16[4,256,128]{2,1,0:T(8,128)(2,1)S(1)} %collective-permute-done.8.refs_1_, bf16[8,1,256,2048]{3,2,1,0:T(8,128)(2,1)S(1)} %get-tuple-element.18.refs_2_.refs_1_.refs_3_, ...), custom_call_target="tpu_custom_call" | custom-call | flops 1073741824 | bytes 2097152 | tf_op jit(solution)/shard_map/pallas_call | solution.py:268
  (1 shorter events, 0.0 us)
Async XLA Ops:
  2.5 11.8 %collective-permute-start = (bf16[256,128]{1,0:T(8,128)(2,1)S(1)}, bf16[256,128]{1,0:T(8,128)(2,1)S(1)}, u32[]{:S(2)}, u32[]{:S(2)}) collective-permute-start(bf16[256,128]{1,0:T(8,128)(2,1)S(1)} %get-tuple-element.15), channel_id=1, source_target_pairs={{0,8},{1,9},{2,10},{3,11},{4,12},{5,13},{6,14},{7,15},{8,0},{9,1},... | collective-permute-start | bytes 196616 | tf_op jit(solution)/shard_map/ppermute | solution.py:182
  5.6 8.7 %collective-permute-start.1 = (bf16[256,128]{1,0:T(8,128)(2,1)S(1)}, bf16[256,128]{1,0:T(8,128)(2,1)S(1)}, u32[]{:S(2)}, u32[]{:S(2)}) collective-permute-start(bf16[256,128]{1,0:T(8,128)(2,1)S(1)} %get-tuple-element.15), channel_id=1, source_target_pairs={{0,16},{1,17},{2,18},{3,19},{4,20},{5,21},{6,22},{7,23},{8,24},{9,... | collective-permute-start | bytes 196616 | tf_op jit(solution)/shard_map/ppermute | solution.py:182
  8.1 6.1 %collective-permute-start.2 = (bf16[256,128]{1,0:T(8,128)(2,1)S(1)}, bf16[256,128]{1,0:T(8,128)(2,1)S(1)}, u32[]{:S(2)}, u32[]{:S(2)}) collective-permute-start(bf16[256,128]{1,0:T(8,128)(2,1)S(1)} %get-tuple-element.15), channel_id=1, source_target_pairs={{0,24},{1,25},{2,26},{3,27},{4,28},{5,29},{6,30},{7,31},{8,16},{9,... | collective-permute-start | bytes 196616 | tf_op jit(solution)/shard_map/ppermute | solution.py:182
  8.1 13.5 %all-to-all-start = ((bf16[32,8,128]{2,1,0:T(8,128)(2,1)}), bf16[32,8,128]{2,1,0:T(8,128)(2,1)S(1)}, u32[]{:S(2)}, u32[]{:S(2)}) async-start(bf16[32,8,128]{2,1,0:T(8,128)(2,1)} %get-tuple-element.16), calls=%async_computation | async-start | bytes 131072 | tf_op jit(solution)/shard_map/all_to_all | solution.py:214
  21.6 7.5 %collective-permute-start.6 = (bf16[4,256,128]{2,1,0:T(8,128)(2,1)S(1)}, bf16[4,256,128]{2,1,0:T(8,128)(2,1)S(1)}, u32[]{:S(2)}, u32[]{:S(2)}) collective-permute-start(bf16[4,256,128]{2,1,0:T(8,128)(2,1)S(1)} %pad_maximum_fusion.refs_0_), channel_id=1, source_target_pairs={{0,1},{1,0},{2,3},{3,2},{4,5},{5,4},{6,7},{7,6},{8,9},{9,8},{10,11... | collective-permute-start | bytes 786440 | tf_op jit(solution)/shard_map/ppermute | solution.py:182
  21.7 10.1 %collective-permute-start.5 = (bf16[4,256,128]{2,1,0:T(8,128)(2,1)S(1)}, bf16[4,256,128]{2,1,0:T(8,128)(2,1)S(1)}, u32[]{:S(2)}, u32[]{:S(2)}) collective-permute-start(bf16[4,256,128]{2,1,0:T(8,128)(2,1)S(1)} %pad_maximum_fusion.refs_0_), channel_id=1, source_target_pairs={{0,6},{1,7},{2,4},{3,5},{4,2},{5,3},{6,0},{7,1},{8,14},{9,15},{10,... | collective-permute-start | bytes 786440 | tf_op jit(solution)/shard_map/ppermute | solution.py:182
  22.4 13.7 %collective-permute-start.3 = (bf16[4,256,128]{2,1,0:T(8,128)(2,1)S(1)}, bf16[4,256,128]{2,1,0:T(8,128)(2,1)S(1)}, u32[]{:S(2)}, u32[]{:S(2)}) collective-permute-start(bf16[4,256,128]{2,1,0:T(8,128)(2,1)S(1)} %pad_maximum_fusion.refs_0_), channel_id=1, source_target_pairs={{0,2},{1,3},{2,0},{3,1},{4,6},{5,7},{6,4},{7,5},{8,10},{9,11},{10,... | collective-permute-start | bytes 786440 | tf_op jit(solution)/shard_map/ppermute | solution.py:182
  23.7 13.1 %collective-permute-start.4 = (bf16[4,256,128]{2,1,0:T(8,128)(2,1)S(1)}, bf16[4,256,128]{2,1,0:T(8,128)(2,1)S(1)}, u32[]{:S(2)}, u32[]{:S(2)}) collective-permute-start(bf16[4,256,128]{2,1,0:T(8,128)(2,1)S(1)} %pad_maximum_fusion.refs_0_), channel_id=1, source_target_pairs={{0,4},{1,5},{2,6},{3,7},{4,0},{5,1},{6,2},{7,3},{8,12},{9,13},{10,... | collective-permute-start | bytes 786440 | tf_op jit(solution)/shard_map/ppermute | solution.py:182
  31.8 5.5 %collective-permute-start.9 = (bf16[4,256,128]{2,1,0:T(8,128)(2,1)S(1)}, bf16[4,256,128]{2,1,0:T(8,128)(2,1)S(1)}, u32[]{:S(2)}, u32[]{:S(2)}) collective-permute-start(bf16[4,256,128]{2,1,0:T(8,128)(2,1)S(1)} %collective-permute-done.5.refs_0_), channel_id=1, source_target_pairs={{0,1},{1,0},{2,3},{3,2},{4,5},{5,4},{6,7},{7,6},{8,9},{9,8},{10,11... | collective-permute-start | bytes 786440 | tf_op jit(solution)/shard_map/ppermute | solution.py:182
  32.8 6.8 %copy-start = (bf16[512,16,128]{2,1,0:T(8,128)(2,1)S(1)}, bf16[512,16,128]{2,1,0:T(8,128)(2,1)}, u32[]{:S(2)}) copy-start(bf16[512,16,128]{2,1,0:T(8,128)(2,1)} %refs_5_.1) | copy-start | bytes 6291460
  32.8 6.8 %copy-start.1 = (f32[128]{0:T(128)S(1)}, f32[128]{0:T(128)}, u32[]{:S(2)}) copy-start(f32[128]{0:T(128)} %param.19) | copy-start | bytes 1540
  36.9 2.7 %collective-permute-start.7 = (bf16[4,256,128]{2,1,0:T(8,128)(2,1)S(1)}, bf16[4,256,128]{2,1,0:T(8,128)(2,1)S(1)}, u32[]{:S(2)}, u32[]{:S(2)}) collective-permute-start(bf16[4,256,128]{2,1,0:T(8,128)(2,1)S(1)} %collective-permute-done.3.refs_0_), channel_id=1, source_target_pairs={{0,1},{1,0},{2,3},{3,2},{4,5},{5,4},{6,7},{7,6},{8,9},{9,8},{10,11... | collective-permute-start | bytes 786440 | tf_op jit(solution)/shard_map/ppermute | solution.py:182
  36.9 2.7 %collective-permute-start.8 = (bf16[4,256,128]{2,1,0:T(8,128)(2,1)S(1)}, bf16[4,256,128]{2,1,0:T(8,128)(2,1)S(1)}, u32[]{:S(2)}, u32[]{:S(2)}) collective-permute-start(bf16[4,256,128]{2,1,0:T(8,128)(2,1)S(1)} %collective-permute-done.4.refs_1_), channel_id=1, source_target_pairs={{0,1},{1,0},{2,3},{3,2},{4,5},{5,4},{6,7},{7,6},{8,9},{9,8},{10,11... | collective-permute-start | bytes 786440 | tf_op jit(solution)/shard_map/ppermute | solution.py:182

commit v7 on v6

--- a/solution.py
+++ b/solution.py
@@ -279,8 +279,7 @@
             ),
         )(*operands)
 
-    sent, _ = lax.optimization_barrier((line, right))
-    total = add([line, _xor(sent, 1, n)], (0, 1), None, False)
+    total = add([line, _xor(line, 1, n)], (0, 1), None, False)
     diagonal, total = lax.optimization_barrier((plane[2], total))
     crossed = _xor(diagonal, 1, n)
     total = add([diagonal], (6,), total, False)

time: 42.9 us -> 36.3 us (0.85)
  waiting for transfers between devices: 12.6 us -> 5.72 us
    all_to_all x1, waiting for transfers between devices: 7.33 us -> 3.58 us  [shards(): lax.all_to_all(right, 'row', split_axis=0, concat_axis=0, tiled=True)]
    ppermute x10, waiting for transfers between devices: 5.27 us -> 2.14 us  [_xor(): return lax.ppermute(x, 'row', [(i, i ^ mask) for i in range(n)])]
  transfers between devices with their start and end apart: 11 -> 11, of which waited for: 4 -> 2; matrix products, arithmetic and copies ran while one was open for 0% -> 0% of each run, Pallas kernels for 20% -> 24%
where the time goes in v7:
time: 36.3 us; the launch traced here: 36.1 us
  starting transfers between devices  16.2 us (45%)
  Pallas kernels  14 us (39%)
  waiting for transfers between devices  5.72 us (16%)
    ppermute x10, starting transfers between devices, _xor(): return lax.ppermute(x, 'row', [(i, i ^ mask) for i in range(n)])  10.1 us
    pallas_call x4, Pallas kernels, add(): pl.pallas_call(functools.partial(_band_kernel, masks, total is None, coun...  7.7 us
    all_to_all x1, starting transfers between devices, shards(): lax.all_to_all(right, 'row', split_axis=0, concat_axis=0, tiled=True)  6.07 us
    pallas_call x1, Pallas kernels, shards(): pl.pallas_call(_fold_kernel, out_shape=fold_out, scratch_shapes=[pltpu.VM...  3.84 us
    all_to_all x1, waiting for transfers between devices, shards(): lax.all_to_all(right, 'row', split_axis=0, concat_axis=0, tiled=True)  3.58 us
    pallas_call x1, Pallas kernels, shards(): pl.pallas_call(_project_kernel, in_specs=[pl.BlockSpec(memory_space=pltpu...  2.45 us
    ppermute x10, waiting for transfers between devices, _xor(): return lax.ppermute(x, 'row', [(i, i ^ mask) for i in range(n)])  2.14 us
  transfers between devices with their start and end apart: 11, of which 2 were waited for; matrix products, arithmetic and copies ran while one was open for 0% of the time, Pallas kernels for 24%

profile of v7, /device:TPU:0, one launch (start us, length us, event | category | flops | bytes accessed | tf_op | source)
XLA Modules:
  0.0 36.1 jit_solution(8006544973868624642)
XLA Ops:
  0.0 2.5 %shard_map.100 = (bf16[256,128]{1,0:T(8,128)(2,1)S(1)}, bf16[32,8,128]{2,1,0:T(8,128)(2,1)}) custom-call(bf16[2,512,256]{2,1,0:T(8,128)(2,1)} %refs_0_.1, f32[1,256]{1,0:T(1,128)} %bitcast.18, f32[1,256]{1,0:T(1,128)} %bitcast.19, bf16[32,256]{1,0:T(8,128)(2,1)} %bitcast.16, f32[1,32]{1,0:T(1,128)} %bitcast.20, bf16[32,256]{1,0:T(8,128)(2,1)} %bitcast.17, ...), custom_call_target="tpu_custom_call" | custom-call | flops 33554432 | bytes 524288 | tf_op jit(solution)/shard_map/pallas_call | solution.py:199
  2.5 3.1 %collective-permute-start = (bf16[256,128]{1,0:T(8,128)(2,1)S(1)}, bf16[256,128]{1,0:T(8,128)(2,1)S(1)}, u32[]{:S(2)}, u32[]{:S(2)}) collective-permute-start(bf16[256,128]{1,0:T(8,128)(2,1)S(1)} %get-tuple-element.14), channel_id=1, source_target_pairs={{0,8},{1,9},{2,10},{3,11},{4,12},{5,13},{6,14},{7,15},{8,0},{9,1},... | collective-permute-start | bytes 196616 | tf_op jit(solution)/shard_map/ppermute | solution.py:182
  5.6 2.6 %collective-permute-start.1 = (bf16[256,128]{1,0:T(8,128)(2,1)S(1)}, bf16[256,128]{1,0:T(8,128)(2,1)S(1)}, u32[]{:S(2)}, u32[]{:S(2)}) collective-permute-start(bf16[256,128]{1,0:T(8,128)(2,1)S(1)} %get-tuple-element.14), channel_id=1, source_target_pairs={{0,16},{1,17},{2,18},{3,19},{4,20},{5,21},{6,22},{7,23},{8,24},{9,... | collective-permute-start | bytes 196616 | tf_op jit(solution)/shard_map/ppermute | solution.py:182
  8.1 0.0 collective-permute-start.2
  8.1 6.1 %all-to-all-start = ((bf16[32,8,128]{2,1,0:T(8,128)(2,1)}), bf16[32,8,128]{2,1,0:T(8,128)(2,1)S(1)}, u32[]{:S(2)}, u32[]{:S(2)}) async-start(bf16[32,8,128]{2,1,0:T(8,128)(2,1)} %get-tuple-element.15), calls=%async_computation | async-start | bytes 131072 | tf_op jit(solution)/shard_map/all_to_all | solution.py:214
  14.2 0.0 collective-permute-done
  14.2 0.0 collective-permute-done.1
  14.2 0.0 collective-permute-done.2
  14.3 0.3 collective-permute-start.6
  14.6 2.6 %collective-permute-start.5 = (bf16[4,256,128]{2,1,0:T(8,128)(2,1)S(1)}, bf16[4,256,128]{2,1,0:T(8,128)(2,1)S(1)}, u32[]{:S(2)}, u32[]{:S(2)}) collective-permute-start(bf16[4,256,128]{2,1,0:T(8,128)(2,1)S(1)} %pad_maximum_fusion.refs_0_), channel_id=1, source_target_pairs={{0,6},{1,7},{2,4},{3,5},{4,2},{5,3},{6,0},{7,1},{8,14},{9,15},{10,... | collective-permute-start | bytes 786440 | tf_op jit(solution)/shard_map/ppermute | solution.py:182
  17.2 0.6 %collective-permute-start.3 = (bf16[4,256,128]{2,1,0:T(8,128)(2,1)S(1)}, bf16[4,256,128]{2,1,0:T(8,128)(2,1)S(1)}, u32[]{:S(2)}, u32[]{:S(2)}) collective-permute-start(bf16[4,256,128]{2,1,0:T(8,128)(2,1)S(1)} %pad_maximum_fusion.refs_0_), channel_id=1, source_target_pairs={{0,2},{1,3},{2,0},{3,1},{4,6},{5,7},{6,4},{7,5},{8,10},{9,11},{10,... | collective-permute-start | bytes 786440 | tf_op jit(solution)/shard_map/ppermute | solution.py:182
  17.8 0.3 collective-permute-start.4
  18.1 3.6 %all-to-all-done.right_ref = bf16[32,8,128]{2,1,0:T(8,128)(2,1)S(1)} async-done(((bf16[32,8,128]{2,1,0:T(8,128)(2,1)}), bf16[32,8,128]{2,1,0:T(8,128)(2,1)S(1)}, u32[]{:S(2)}, u32[]{:S(2)}) %all-to-all-start) | async-done | bytes 65568 | tf_op jit(solution)/shard_map/all_to_all | solution.py:214
  21.7 3.8 %shard_map.101 = (bf16[8,1,256,2048]{3,2,1,0:T(8,128)(2,1)S(1)}, bf16[2,512,256]{2,1,0:T(8,128)(2,1)S(1)}) custom-call(bf16[32,8,128]{2,1,0:T(8,128)(2,1)S(1)} %all-to-all-done.right_ref, bf16[1024,128]{1,0:T(8,128)(2,1)} %source_ref.1), custom_call_target="tpu_custom_call" | custom-call | flops 2147483648 | bytes 8388608 | tf_op jit(solution)/shard_map/pallas_call | solution.py:243
  25.5 0.0 collective-permute-done.6.refs_1_
  25.5 1.5 %shard_map.102.refs_3_ = f32[512,2048]{1,0:T(8,128)S(1)} custom-call(bf16[4,256,128]{2,1,0:T(8,128)(2,1)S(1)} %pad_maximum_fusion.refs_0_, bf16[4,256,128]{2,1,0:T(8,128)(2,1)S(1)} %collective-permute-done.6.refs_1_, bf16[8,1,256,2048]{3,2,1,0:T(8,128)(2,1)S(1)} %get-tuple-element.16.refs_2_.refs_1_.refs_3_, ...), custom_call_target="tpu_custom_call" | custom-call | flops 1073741824 | bytes 2097152 | tf_op jit(solution)/shard_map/pallas_call | solution.py:268
  27.1 0.0 collective-permute-done.5.refs_0_
  27.1 0.1 collective-permute-start.9
  27.2 0.9 %shard_map.103.refs_5_ = f32[512,2048]{1,0:T(8,128)S(1)} custom-call(bf16[4,256,128]{2,1,0:T(8,128)(2,1)S(1)} %collective-permute-done.5.refs_0_, bf16[8,1,256,2048]{3,2,1,0:T(8,128)(2,1)S(1)} %get-tuple-element.16.refs_2_.refs_1_.refs_3_, bf16[2,512,256]{2,1,0:T(8,128)(2,1)S(1)} %get-tuple-element.17.refs_3_.refs_2_.refs_4_, f32[512,2048]{1,0:T(8,128)S(1)} %shard_map.102.refs_3_), custom_call_target="tpu_custom_call" | custom-call | flops 536870912 | bytes 1048576 | tf_op jit(solution)/shard_map/pallas_call | solution.py:268
  28.1 0.0 copy-start
  28.2 0.0 copy-start.1
  28.2 2.1 %collective-permute-done.3.refs_0_ = bf16[4,256,128]{2,1,0:T(8,128)(2,1)S(1)} collective-permute-done((bf16[4,256,128]{2,1,0:T(8,128)(2,1)S(1)}, bf16[4,256,128]{2,1,0:T(8,128)(2,1)S(1)}, u32[]{:S(2)}, u32[]{:S(2)}) %collective-permute-start.3) | collective-permute-done | bytes 262176 | tf_op jit(solution)/shard_map/ppermute | solution.py:182
  30.3 0.0 collective-permute-done.4.refs_1_
  30.3 0.0 collective-permute-start.7
  30.3 0.5 %collective-permute-start.8 = (bf16[4,256,128]{2,1,0:T(8,128)(2,1)S(1)}, bf16[4,256,128]{2,1,0:T(8,128)(2,1)S(1)}, u32[]{:S(2)}, u32[]{:S(2)}) collective-permute-start(bf16[4,256,128]{2,1,0:T(8,128)(2,1)S(1)} %collective-permute-done.4.refs_1_), channel_id=1, source_target_pairs={{0,1},{1,0},{2,3},{3,2},{4,5},{5,4},{6,7},{7,6},{8,9},{9,8},{10,11... | collective-permute-start | bytes 786440 | tf_op jit(solution)/shard_map/ppermute | solution.py:182
  30.8 0.0 collective-permute-done.9.refs_2_
  30.8 2.2 %shard_map.104.refs_4_ = f32[512,2048]{1,0:T(8,128)S(1)} custom-call(bf16[4,256,128]{2,1,0:T(8,128)(2,1)S(1)} %collective-permute-done.3.refs_0_, bf16[4,256,128]{2,1,0:T(8,128)(2,1)S(1)} %collective-permute-done.4.refs_1_, bf16[4,256,128]{2,1,0:T(8,128)(2,1)S(1)} %collective-permute-done.9.refs_2_, ...), custom_call_target="tpu_custom_call" | custom-call | flops 1610612736 | bytes 3145728 | tf_op jit(solution)/shard_map/pallas_call | solution.py:268
  33.0 0.0 collective-permute-done.7.refs_0_
  33.0 0.0 collective-permute-done.8.refs_1_
  33.0 0.0 copy-done
  33.1 0.0 copy-done.1
  33.1 3.0 %shard_map.105 = bf16[512,16,128]{2,1,0:T(8,128)(2,1)} custom-call(bf16[4,256,128]{2,1,0:T(8,128)(2,1)S(1)} %collective-permute-done.7.refs_0_, bf16[4,256,128]{2,1,0:T(8,128)(2,1)S(1)} %collective-permute-done.8.refs_1_, bf16[8,1,256,2048]{3,2,1,0:T(8,128)(2,1)S(1)} %get-tuple-element.16.refs_2_.refs_1_.refs_3_, ...), custom_call_target="tpu_custom_call" | custom-call | flops 1073741824 | bytes 2097152 | tf_op jit(solution)/shard_map/pallas_call | solution.py:268
  (1 shorter events, 0.0 us)
Async XLA Ops:
  2.5 11.8 %collective-permute-start = (bf16[256,128]{1,0:T(8,128)(2,1)S(1)}, bf16[256,128]{1,0:T(8,128)(2,1)S(1)}, u32[]{:S(2)}, u32[]{:S(2)}) collective-permute-start(bf16[256,128]{1,0:T(8,128)(2,1)S(1)} %get-tuple-element.14), channel_id=1, source_target_pairs={{0,8},{1,9},{2,10},{3,11},{4,12},{5,13},{6,14},{7,15},{8,0},{9,1},... | collective-permute-start | bytes 196616 | tf_op jit(solution)/shard_map/ppermute | solution.py:182
  5.6 8.7 %collective-permute-start.1 = (bf16[256,128]{1,0:T(8,128)(2,1)S(1)}, bf16[256,128]{1,0:T(8,128)(2,1)S(1)}, u32[]{:S(2)}, u32[]{:S(2)}) collective-permute-start(bf16[256,128]{1,0:T(8,128)(2,1)S(1)} %get-tuple-element.14), channel_id=1, source_target_pairs={{0,16},{1,17},{2,18},{3,19},{4,20},{5,21},{6,22},{7,23},{8,24},{9,... | collective-permute-start | bytes 196616 | tf_op jit(solution)/shard_map/ppermute | solution.py:182
  8.1 6.1 %collective-permute-start.2 = (bf16[256,128]{1,0:T(8,128)(2,1)S(1)}, bf16[256,128]{1,0:T(8,128)(2,1)S(1)}, u32[]{:S(2)}, u32[]{:S(2)}) collective-permute-start(bf16[256,128]{1,0:T(8,128)(2,1)S(1)} %get-tuple-element.14), channel_id=1, source_target_pairs={{0,24},{1,25},{2,26},{3,27},{4,28},{5,29},{6,30},{7,31},{8,16},{9,... | collective-permute-start | bytes 196616 | tf_op jit(solution)/shard_map/ppermute | solution.py:182
  8.1 13.5 %all-to-all-start = ((bf16[32,8,128]{2,1,0:T(8,128)(2,1)}), bf16[32,8,128]{2,1,0:T(8,128)(2,1)S(1)}, u32[]{:S(2)}, u32[]{:S(2)}) async-start(bf16[32,8,128]{2,1,0:T(8,128)(2,1)} %get-tuple-element.15), calls=%async_computation | async-start | bytes 131072 | tf_op jit(solution)/shard_map/all_to_all | solution.py:214
  14.3 11.2 %collective-permute-start.6 = (bf16[4,256,128]{2,1,0:T(8,128)(2,1)S(1)}, bf16[4,256,128]{2,1,0:T(8,128)(2,1)S(1)}, u32[]{:S(2)}, u32[]{:S(2)}) collective-permute-start(bf16[4,256,128]{2,1,0:T(8,128)(2,1)S(1)} %pad_maximum_fusion.refs_0_), channel_id=1, source_target_pairs={{0,1},{1,0},{2,3},{3,2},{4,5},{5,4},{6,7},{7,6},{8,9},{9,8},{10,11... | collective-permute-start | bytes 786440 | tf_op jit(solution)/shard_map/ppermute | solution.py:182
  14.6 12.5 %collective-permute-start.5 = (bf16[4,256,128]{2,1,0:T(8,128)(2,1)S(1)}, bf16[4,256,128]{2,1,0:T(8,128)(2,1)S(1)}, u32[]{:S(2)}, u32[]{:S(2)}) collective-permute-start(bf16[4,256,128]{2,1,0:T(8,128)(2,1)S(1)} %pad_maximum_fusion.refs_0_), channel_id=1, source_target_pairs={{0,6},{1,7},{2,4},{3,5},{4,2},{5,3},{6,0},{7,1},{8,14},{9,15},{10,... | collective-permute-start | bytes 786440 | tf_op jit(solution)/shard_map/ppermute | solution.py:182
  17.2 13.1 %collective-permute-start.3 = (bf16[4,256,128]{2,1,0:T(8,128)(2,1)S(1)}, bf16[4,256,128]{2,1,0:T(8,128)(2,1)S(1)}, u32[]{:S(2)}, u32[]{:S(2)}) collective-permute-start(bf16[4,256,128]{2,1,0:T(8,128)(2,1)S(1)} %pad_maximum_fusion.refs_0_), channel_id=1, source_target_pairs={{0,2},{1,3},{2,0},{3,1},{4,6},{5,7},{6,4},{7,5},{8,10},{9,11},{10,... | collective-permute-start | bytes 786440 | tf_op jit(solution)/shard_map/ppermute | solution.py:182
  17.8 12.5 %collective-permute-start.4 = (bf16[4,256,128]{2,1,0:T(8,128)(2,1)S(1)}, bf16[4,256,128]{2,1,0:T(8,128)(2,1)S(1)}, u32[]{:S(2)}, u32[]{:S(2)}) collective-permute-start(bf16[4,256,128]{2,1,0:T(8,128)(2,1)S(1)} %pad_maximum_fusion.refs_0_), channel_id=1, source_target_pairs={{0,4},{1,5},{2,6},{3,7},{4,0},{5,1},{6,2},{7,3},{8,12},{9,13},{10,... | collective-permute-start | bytes 786440 | tf_op jit(solution)/shard_map/ppermute | solution.py:182
  27.1 3.7 %collective-permute-start.9 = (bf16[4,256,128]{2,1,0:T(8,128)(2,1)S(1)}, bf16[4,256,128]{2,1,0:T(8,128)(2,1)S(1)}, u32[]{:S(2)}, u32[]{:S(2)}) collective-permute-start(bf16[4,256,128]{2,1,0:T(8,128)(2,1)S(1)} %collective-permute-done.5.refs_0_), channel_id=1, source_target_pairs={{0,1},{1,0},{2,3},{3,2},{4,5},{5,4},{6,7},{7,6},{8,9},{9,8},{10,11... | collective-permute-start | bytes 786440 | tf_op jit(solution)/shard_map/ppermute | solution.py:182
  28.1 4.9 %copy-start = (bf16[512,16,128]{2,1,0:T(8,128)(2,1)S(1)}, bf16[512,16,128]{2,1,0:T(8,128)(2,1)}, u32[]{:S(2)}) copy-start(bf16[512,16,128]{2,1,0:T(8,128)(2,1)} %refs_5_.1) | copy-start | bytes 6291460
  28.2 4.9 %copy-start.1 = (f32[128]{0:T(128)S(1)}, f32[128]{0:T(128)}, u32[]{:S(2)}) copy-start(f32[128]{0:T(128)} %param.19) | copy-start | bytes 1540
  30.3 2.7 %collective-permute-start.7 = (bf16[4,256,128]{2,1,0:T(8,128)(2,1)S(1)}, bf16[4,256,128]{2,1,0:T(8,128)(2,1)S(1)}, u32[]{:S(2)}, u32[]{:S(2)}) collective-permute-start(bf16[4,256,128]{2,1,0:T(8,128)(2,1)S(1)} %collective-permute-done.3.refs_0_), channel_id=1, source_target_pairs={{0,1},{1,0},{2,3},{3,2},{4,5},{5,4},{6,7},{7,6},{8,9},{9,8},{10,11... | collective-permute-start | bytes 786440 | tf_op jit(solution)/shard_map/ppermute | solution.py:182
  30.3 2.7 %collective-permute-start.8 = (bf16[4,256,128]{2,1,0:T(8,128)(2,1)S(1)}, bf16[4,256,128]{2,1,0:T(8,128)(2,1)S(1)}, u32[]{:S(2)}, u32[]{:S(2)}) collective-permute-start(bf16[4,256,128]{2,1,0:T(8,128)(2,1)S(1)} %collective-permute-done.4.refs_1_), channel_id=1, source_target_pairs={{0,1},{1,0},{2,3},{3,2},{4,5},{5,4},{6,7},{7,6},{8,9},{9,8},{10,11... | collective-permute-start | bytes 786440 | tf_op jit(solution)/shard_map/ppermute | solution.py:182

commit v8 on v3

--- a/solution.py
+++ b/solution.py
@@ -22,12 +22,26 @@
     return jnp.concatenate(rows, axis=0)
 
 
+def _order(me, half):
+    row = lax.broadcasted_iota(jnp.int32, (4 * LANES, 8 * CHANS), 0)
+    col = lax.broadcasted_iota(jnp.int32, (4 * LANES, 8 * CHANS), 1)
+    device = (row // LANES) ^ (me // 8 % 4)
+    wanted = (row % CHANS) * 8 + ((row // CHANS) % 2) * 4 + device
+    hit = (wanted == col) & ((row // (2 * CHANS)) % 2 == half)
+    return jnp.where(hit, 1.0, 0.0).astype(jnp.bfloat16)
+
+
 def _project_kernel(*refs):
-    sources, (left_ref, right_ref), held = refs[:7], refs[7:9], refs[9:16]
-    sems = refs[16]
+    sources, final_source, outs, held = refs[:7], refs[7], refs[8:12], refs[12:19]
+    left_ref, right_ref, final_ref, order_ref = outs
+    sems = refs[19]
     copies = [pltpu.make_async_copy(a, b, sems.at[i]) for i, (a, b) in enumerate(zip(sources, held))]
+    copies.append(pltpu.make_async_copy(final_source, final_ref, sems.at[7]))
     for copy in copies:
         copy.start()
+    me = lax.axis_index("row")
+    for h in range(2):
+        order_ref[h] = _order(me, h)
     for copy in copies:
         copy.wait()
     x_ref, gain_ref, bias_ref, w1_ref, b1_ref, w2_ref, b2_ref = held
@@ -58,34 +72,30 @@
     right_ref[...] = (right + shift2).reshape(n, 8, LANES).astype(jnp.bfloat16)
 
 
-def _order(me, half):
-    row = lax.broadcasted_iota(jnp.int32, (4 * LANES, 8 * CHANS), 0)
-    col = lax.broadcasted_iota(jnp.int32, (4 * LANES, 8 * CHANS), 1)
-    device = (row // LANES) ^ (me // 8 % 4)
-    wanted = (row % CHANS) * 8 + ((row // CHANS) % 2) * 4 + device
-    hit = (wanted == col) & ((row // (2 * CHANS)) % 2 == half)
-    return jnp.where(hit, 1.0, 0.0).astype(jnp.bfloat16)
-
-
-def _fold_kernel(right_ref, final_ref, out_ref, order_ref):
-    me = lax.axis_index("row")
-    for h in range(2):
-        order_ref[h] = _order(me, h)
+def _line_kernel(*refs):
+    pieces, order_ref, out_ref = refs[:-2], refs[-2], refs[-1]
+    half = pieces[0].shape[0]
+    wide = order_ref.shape[2]
+    for q in range(len(pieces) // 4):
+        lhs = jnp.concatenate([piece[...] for piece in pieces[q * 4 : q * 4 + 4]], axis=1)
+        for h in range(2):
+            moved = jnp.dot(lhs, order_ref[h], preferred_element_type=jnp.float32)
+            out_ref[pl.ds(h * half, half), pl.ds(q * wide, wide)] = moved.astype(jnp.bfloat16)
+
+
+def _fold_kernel(right_ref, final_ref, out_ref, block_ref, pairs_ref):
     devices = right_ref.shape[0]
     groups = devices // 4
-    rows = devices * 8
-    block = right_ref[...].astype(jnp.float32).reshape(rows, LANES)
-    row = lax.broadcasted_iota(jnp.int32, (2 * rows, 2 * rows), 0)
-    col = lax.broadcasted_iota(jnp.int32, (2 * rows, 2 * rows), 1)
-    device = (row // 8) % groups + row % 4 * groups
-    wanted = ((row // 4) % 2) * rows + device * 8 + row // (8 * groups)
-    spread = jnp.where(wanted == col, 1.0, 0.0).astype(jnp.bfloat16)
+    block_ref[...] = right_ref[...].astype(jnp.float32).reshape(devices * 8, LANES)
+    for jr in range(8):
+        for g in range(groups):
+            four = block_ref[pl.ds(g * 8 + jr, 4, stride=groups * 8), :]
+            for s in range(2):
+                pairs_ref[pl.ds((jr * groups + g) * 8 + s * 4, 4), :] = four
+    block = pairs_ref[...]
     lane = lax.broadcasted_iota(jnp.int32, block.shape, 1) // CHANS
-    lhs = []
-    for jh in range(2):
-        both = jnp.concatenate([jnp.where(lane == jh * 2 + s, block, 0.0) for s in range(2)], axis=0)
-        moved = jnp.dot(spread, both.astype(jnp.bfloat16), preferred_element_type=jnp.float32)
-        lhs.append(moved.astype(jnp.bfloat16))
+    s = lax.broadcasted_iota(jnp.int32, block.shape, 0) // 4 % 2
+    lhs = [jnp.where(lane == jh * 2 + s, block, 0.0).astype(jnp.bfloat16) for jh in range(2)]
     lhs = jnp.concatenate(lhs, axis=0)
 
     for pair in range(CHANS // 2):
@@ -104,27 +114,20 @@
 def _band_kernel(masks, begins, count, held, *refs):
     refs = list(refs)
     take = lambda k: [refs.pop(0) for _ in range(k)]
-    lines = take(len(masks))
-    t_ref, order_ref = take(2)
+    lines = []
+    for mask in masks:
+        parts = take(2 if mask == 6 else 1)
+        lines.append(parts)
+    (t_ref,) = take(1)
     (sum_ref,) = (None,) if begins else take(1)
     pair_ref, shift_ref = (None, None) if count is None else take(2)
     (out_ref,) = take(1)
-    (l_ref,) = take(1)
     me = lax.axis_index("row")
-    wide = 8 * CHANS
-    places, half, _ = lines[0].shape
-    chunks = []
-    for line, mask in zip(lines, masks):
-        for q in range(places // 4):
-            lhs = jnp.concatenate([line[q * 4 + u] for u in range(4)], axis=1)
-            at = pl.ds(len(chunks) * wide, wide)
-            for h in range(2):
-                moved = jnp.dot(lhs, order_ref[h], preferred_element_type=jnp.float32)
-                l_ref[pl.ds(h * half, half), at] = moved.astype(jnp.bfloat16)
-            chunks.append(((me % 8) ^ mask, q ^ (me // 32)))
+    wide = t_ref.shape[2]
+    chunks = [((me % 8) ^ mask, q ^ (me // 32)) for mask in masks for q in range(t_ref.shape[1])]
 
     tile = 256
-    band = 2 * half
+    band = sum(part.shape[0] for part in lines[0])
     if count is not None:
         acc_ref, done_ref, sems = take(3)
         cols = pair_ref.shape[1]
@@ -132,13 +135,14 @@
 
     def column(step):
         at = pl.ds(step * tile, tile)
+        lhs = jnp.concatenate([jnp.concatenate([part[...] for part in line], axis=0) for line in lines], axis=1)
         if held:
             rhs = jnp.concatenate([t_ref[g, q, :, at] for g, q in chunks], axis=0)
         else:
             for i, (g, q) in enumerate(chunks):
                 pltpu.sync_copy(t_ref.at[g, q, :, at], refs[0].at[pl.ds(i * wide, wide)])
             rhs = refs[0][...]
-        res = jnp.dot(l_ref[...], rhs, preferred_element_type=jnp.float32)
+        res = jnp.dot(lhs, rhs, preferred_element_type=jnp.float32)
         if sum_ref is not None:
             res = res + sum_ref[:, at]
         if count is None:
@@ -192,38 +196,45 @@
     sources = [
         alignment, gain.reshape(1, -1), bias.reshape(1, -1), w1.T, b1.reshape(1, -1), w2.T, b2.reshape(1, -1)
     ]
-    left, right = pl.pallas_call(
+    sources = [pltpu.with_memory_space_constraint(a, pltpu.HBM) for a in sources]
+    left, right, final, order = pl.pallas_call(
         _project_kernel,
-        in_specs=[pl.BlockSpec(memory_space=pltpu.HBM)] * 7,
-        out_specs=(vmem, vmem),
+        in_specs=[anywhere] * 8,
+        out_specs=(vmem,) * 4,
         out_shape=(
             jax.ShapeDtypeStruct((half, LANES), jnp.bfloat16),
             jax.ShapeDtypeStruct((n, 8, LANES), jnp.bfloat16),
+            jax.ShapeDtypeStruct(final.shape, final.dtype),
+            jax.ShapeDtypeStruct((2, 4 * LANES, 8 * CHANS), jnp.bfloat16),
         ),
-        scratch_shapes=[pltpu.VMEM(a.shape, a.dtype) for a in sources] + [pltpu.SemaphoreType.DMA((7,))],
-        compiler_params=pltpu.CompilerParams(vmem_limit_bytes=60 * 1024 * 1024),
+        scratch_shapes=[pltpu.VMEM(a.shape, a.dtype) for a in sources] + [pltpu.SemaphoreType.DMA((8,))],
+        compiler_params=params,
         cost_estimate=pl.CostEstimate(
             flops=4 * seqs * residues * feats * CHANS, bytes_accessed=2 * seqs * residues * feats, transcendentals=0
         ),
-    )(*sources)
+    )(*sources, pltpu.with_memory_space_constraint(final, pltpu.HBM))
 
     right = lax.all_to_all(right, "row", split_axis=0, concat_axis=0, tiled=True)
-
-    line = [left] + [_xor(left, m, n) for m in range(8, n, 8)]
-    line = jnp.stack(line)
-    plane = [_xor(line, m, n) for m in (2, 4, 6)]
 
     part = 32
     parts = n // part
+    pieces = [left] + [_xor(left, m, n) for m in range(8, n, 8)]
+    line = pl.pallas_call(
+        _line_kernel,
+        in_specs=[vmem] * (len(pieces) + 1),
+        out_specs=vmem,
+        out_shape=jax.ShapeDtypeStruct((band, parts * 8 * CHANS), jnp.bfloat16),
+        compiler_params=params,
+        cost_estimate=pl.CostEstimate(flops=2**27, bytes_accessed=2**20, transcendentals=0),
+    )(*pieces, order)
+    x, y = _xor(line, 2, n), _xor(line, 4, n)
+
     fold_cost = pl.CostEstimate(
         flops=2 * n * 32 * 256 * CHANS * zdim, bytes_accessed=4 * n * CHANS * cols * zdim, transcendentals=0
     )
-    fold_out = (
-        jax.ShapeDtypeStruct((8, parts, 8 * CHANS, cols * zdim), jnp.bfloat16),
-        jax.ShapeDtypeStruct((2, 4 * LANES, 8 * CHANS), jnp.bfloat16),
-    )
+    fold_out = jax.ShapeDtypeStruct((8, parts, 8 * CHANS, cols * zdim), jnp.bfloat16)
     if small:
-        specs = dict(in_specs=[vmem, vmem], out_specs=(vmem, vmem))
+        specs = dict(in_specs=[vmem, vmem], out_specs=vmem)
     else:
         specs = dict(
             grid=(parts,),
@@ -231,19 +242,21 @@
                 pl.BlockSpec((part, 8, LANES), lambda i: (i, 0, 0)),
                 pl.BlockSpec(final.shape, lambda i: (0, 0)),
             ],
-            out_specs=(
-                pl.BlockSpec((8, 1, 8 * CHANS, cols * zdim), lambda i: (0, i, 0, 0)),
-                pl.BlockSpec((2, 4 * LANES, 8 * CHANS), lambda i: (0, 0, 0)),
-            ),
+            out_specs=pl.BlockSpec((8, 1, 8 * CHANS, cols * zdim), lambda i: (0, i, 0, 0)),
         )
-    folded, order = pl.pallas_call(
-        _fold_kernel, out_shape=fold_out, compiler_params=params, cost_estimate=fold_cost, **specs
+    folded = pl.pallas_call(
+        _fold_kernel,
+        out_shape=fold_out,
+        scratch_shapes=[pltpu.VMEM((part * 8, LANES), jnp.float32), pltpu.VMEM((part * 16, LANES), jnp.float32)],
+        compiler_params=params,
+        cost_estimate=fold_cost,
+        **specs,
     )(right, final)
 
     def add(lines, masks, total, last):
         depth = len(masks) * parts * 8 * CHANS
-        scratch = [pltpu.VMEM((band, depth), jnp.bfloat16)]
-        operands = [*lines, folded, order] + ([] if total is None else [total])
+        scratch = []
+        operands = [*lines, folded] + ([] if total is None else [total])
         if last:
             operands += [pair, shift.reshape(1, -1)]
             scratch += [
@@ -271,10 +284,16 @@
         )(*operands)
 
     total = add([line, _xor(line, 1, n)], (0, 1), None, False)
-    plane, total = lax.optimization_barrier((plane, total))
-    other = [_xor(o, 1, n) for o in plane]
-    total = add(plane, (2, 4, 6), total, False)
-    return add(other, (3, 5, 7), total, True)
+    x, y, total = lax.optimization_barrier((x, y, total))
+    upper, lower = _xor(x[:half], 4, n), _xor(y[half:], 2, n)
+    total = add([x, y], (2, 4), total, False)
+    x, y, total = lax.optimization_barrier((x, y, total))
+    across = [_xor(x, 1, n), _xor(y, 1, n)]
+    total = add(across, (3, 5), total, False)
+    upper, lower, total = lax.optimization_barrier((upper, lower, total))
+    last = _xor(jnp.concatenate([upper, lower], axis=0), 1, n)
+    total = add([upper, lower], (6,), total, False)
+    return add([last], (7,), total, True)
 
 
 def solution(mesh):

time: 37.8 us -> 37.8 us (level)
  waiting for transfers between devices: 6.28 us -> 7.76 us
  starting transfers between devices: 16.1 us -> 17.2 us
  local copies, waits for them, and re-layouts: 0.96 us -> 0.03 us
  other arithmetic: 0.88 us -> 0.02 us
  Pallas kernels: 13.2 us -> 12.4 us
    ppermute x10 -> x11, starting transfers between devices: 10.1 us -> 11.2 us  [_xor(): return lax.ppermute(x, 'row', [(i, i ^ mask) for i in range(n)])]
    all_to_all x1, waiting for transfers between devices: 2.74 us -> 3.71 us  [shards(): lax.all_to_all(right, 'row', split_axis=0, concat_axis=0, tiled=True)]
    unnamed x6 -> x4, local copies, waits for them, and re-layouts: 0.96 us -> 0.01 us
    another operation x1 -> x0, other arithmetic: 0.88 us -> none  [shards(): line = jnp.stack(line)]
    pallas_call x3 -> x5, Pallas kernels: 7.44 us -> 6.74 us  [add(): pl.pallas_call(functools.partial(_band_kernel, masks, total is None, coun...]
    ppermute x10 -> x11, waiting for transfers between devices: 3.54 us -> 4.04 us  [_xor(): return lax.ppermute(x, 'row', [(i, i ^ mask) for i in range(n)])]
    pallas_call x2 -> x3, Pallas kernels: 5.72 us -> 5.68 us  [the longest x1 2.76 us: shards(): pl.pallas_call(_fold_kernel, out_shape=fold_out, scratch_shapes=[pltpu.VM...]
  transfers between devices with their start and end apart: 11 -> 12, of which waited for: 3 -> 4; matrix products, arithmetic and copies ran while one was open for 2% -> 0% of each run, Pallas kernels for 19% -> 17%
where the time goes in v8:
time: 37.8 us; the launch traced here: 37.6 us
  starting transfers between devices  17.2 us (46%)
  Pallas kernels  12.4 us (33%)
  waiting for transfers between devices  7.76 us (21%)
    ppermute x11, starting transfers between devices, _xor(): return lax.ppermute(x, 'row', [(i, i ^ mask) for i in range(n)])  11.2 us
    pallas_call x5, Pallas kernels, add(): pl.pallas_call(functools.partial(_band_kernel, masks, total is None, coun...  6.74 us
    all_to_all x1, starting transfers between devices, shards(): lax.all_to_all(right, 'row', split_axis=0, concat_axis=0, tiled=True)  5.99 us
    ppermute x11, waiting for transfers between devices, _xor(): return lax.ppermute(x, 'row', [(i, i ^ mask) for i in range(n)])  4.04 us
    all_to_all x1, waiting for transfers between devices, shards(): lax.all_to_all(right, 'row', split_axis=0, concat_axis=0, tiled=True)  3.71 us
    pallas_call x1, Pallas kernels, shards(): pl.pallas_call(_fold_kernel, out_shape=fold_out, scratch_shapes=[pltpu.VM...  2.76 us
    pallas_call x1, Pallas kernels, shards(): pl.pallas_call(_project_kernel, in_specs=[anywhere] * 8, out_specs=(vmem,...  2.61 us
  transfers between devices with their start and end apart: 12, of which 4 were waited for; matrix products, arithmetic and copies ran while one was open for 0% of the time, Pallas kernels for 17%

profile of v8, /device:TPU:0, one launch (start us, length us, event | category | flops | bytes accessed | tf_op | source)
XLA Modules:
  0.0 37.6 jit_solution(1108633037610484159)
XLA Ops:
  0.0 2.6 %shard_map.100 = (bf16[256,128]{1,0:T(8,128)(2,1)S(1)}, bf16[32,8,128]{2,1,0:T(8,128)(2,1)}, bf16[1024,128]{1,0:T(8,128)(2,1)S(1)}, bf16[2,512,256]{2,1,0:T(8,128)(2,1)S(1)}) custom-call(bf16[2,512,256]{2,1,0:T(8,128)(2,1)} %refs_0_.1, f32[1,256]{1,0:T(1,128)} %bitcast.10, f32[1,256]{1,0:T(1,128)} %bitcast.11, bf16[32,256]{1,0:T(8,128)(2,1)} %bitcast.8, ...), custom_call_target="tpu_custom_call" | custom-call | flops 33554432 | bytes 524288 | tf_op jit(solution)/shard_map/pallas_call | solution.py:200
  2.6 5.1 %collective-permute-start.2 = (bf16[256,128]{1,0:T(8,128)(2,1)S(1)}, bf16[256,128]{1,0:T(8,128)(2,1)S(1)}, u32[]{:S(2)}, u32[]{:S(2)}) collective-permute-start(bf16[256,128]{1,0:T(8,128)(2,1)S(1)} %get-tuple-element.18.refs_0_), channel_id=1, source_target_pairs={{0,24},{1,25},{2,26},{3,27},{4,28},{5,29},{6,30},{7,31},{8,16},{9,... | collective-permute-start | bytes 196616 | tf_op jit(solution)/shard_map/ppermute | solution.py:183
  7.7 0.0 collective-permute-start.1
  7.7 0.6 %collective-permute-start = (bf16[256,128]{1,0:T(8,128)(2,1)S(1)}, bf16[256,128]{1,0:T(8,128)(2,1)S(1)}, u32[]{:S(2)}, u32[]{:S(2)}) collective-permute-start(bf16[256,128]{1,0:T(8,128)(2,1)S(1)} %get-tuple-element.18.refs_0_), channel_id=1, source_target_pairs={{0,8},{1,9},{2,10},{3,11},{4,12},{5,13},{6,14},{7,15},{8,0},{9,1},... | collective-permute-start | bytes 196616 | tf_op jit(solution)/shard_map/ppermute | solution.py:183
  8.4 6.0 %all-to-all-start = ((bf16[32,8,128]{2,1,0:T(8,128)(2,1)}), bf16[32,8,128]{2,1,0:T(8,128)(2,1)S(1)}, u32[]{:S(2)}, u32[]{:S(2)}) async-start(bf16[32,8,128]{2,1,0:T(8,128)(2,1)} %get-tuple-element.20), calls=%async_computation | async-start | bytes 131072 | tf_op jit(solution)/shard_map/all_to_all | solution.py:217
  14.4 0.0 collective-permute-done.2.refs_3_
  14.4 0.0 collective-permute-done.refs_1_
  14.4 0.3 shard_map.101.refs_0_
  14.7 0.3 collective-permute-start.5
  15.0 1.7 %collective-permute-start.4 = (bf16[512,256]{1,0:T(8,128)(2,1)S(1)}, bf16[512,256]{1,0:T(8,128)(2,1)S(1)}, u32[]{:S(2)}, u32[]{:S(2)}) collective-permute-start(bf16[512,256]{1,0:T(8,128)(2,1)S(1)} %shard_map.101.refs_0_), channel_id=1, source_target_pairs={{0,4},{1,5},{2,6},{3,7},{4,0},{5,1},{6,2},{7,3},{8,12},{9,13},{10,... | collective-permute-start | bytes 786440 | tf_op jit(solution)/shard_map/ppermute | solution.py:183
  16.7 1.5 %collective-permute-start.3 = (bf16[512,256]{1,0:T(8,128)(2,1)S(1)}, bf16[512,256]{1,0:T(8,128)(2,1)S(1)}, u32[]{:S(2)}, u32[]{:S(2)}) collective-permute-start(bf16[512,256]{1,0:T(8,128)(2,1)S(1)} %shard_map.101.refs_0_), channel_id=1, source_target_pairs={{0,2},{1,3},{2,0},{3,1},{4,6},{5,7},{6,4},{7,5},{8,10},{9,11},{10,... | collective-permute-start | bytes 786440 | tf_op jit(solution)/shard_map/ppermute | solution.py:183
  18.2 3.7 %all-to-all-done.right_ref = bf16[32,8,128]{2,1,0:T(8,128)(2,1)S(1)} async-done(((bf16[32,8,128]{2,1,0:T(8,128)(2,1)}), bf16[32,8,128]{2,1,0:T(8,128)(2,1)S(1)}, u32[]{:S(2)}, u32[]{:S(2)}) %all-to-all-start) | async-done | bytes 65568 | tf_op jit(solution)/shard_map/all_to_all | solution.py:217
  21.9 2.8 %shard_map.102.refs_2_.refs_1_ = bf16[8,1,256,2048]{3,2,1,0:T(8,128)(2,1)S(1)} custom-call(bf16[32,8,128]{2,1,0:T(8,128)(2,1)S(1)} %all-to-all-done.right_ref, bf16[1024,128]{1,0:T(8,128)(2,1)S(1)} %get-tuple-element.21.final_ref), custom_call_target="tpu_custom_call" | custom-call | flops 2147483648 | bytes 8388608 | tf_op jit(solution)/shard_map/pallas_call | solution.py:247
  24.7 0.0 collective-permute-done.5.refs_1_
  24.7 1.3 %shard_map.103.refs_3_ = f32[512,2048]{1,0:T(8,128)S(1)} custom-call(bf16[512,256]{1,0:T(8,128)(2,1)S(1)} %shard_map.101.refs_0_, bf16[512,256]{1,0:T(8,128)(2,1)S(1)} %collective-permute-done.5.refs_1_, bf16[8,1,256,2048]{3,2,1,0:T(8,128)(2,1)S(1)} %shard_map.102.refs_2_.refs_1_), custom_call_target="tpu_custom_call" | custom-call | flops 1073741824 | bytes 2097152 | tf_op jit(solution)/shard_map/pallas_call | solution.py:272
  26.0 0.0 collective-permute-done.4.refs_1_
  26.0 0.0 collective-permute-done.3.refs_0_
  26.0 1.3 %shard_map.104.refs_3_ = f32[512,2048]{1,0:T(8,128)S(1)} custom-call(bf16[512,256]{1,0:T(8,128)(2,1)S(1)} %collective-permute-done.3.refs_0_, bf16[512,256]{1,0:T(8,128)(2,1)S(1)} %collective-permute-done.4.refs_1_, bf16[8,1,256,2048]{3,2,1,0:T(8,128)(2,1)S(1)} %shard_map.102.refs_2_.refs_1_, f32[512,2048]{1,0:T(8,128)S(1)} %shard_map.103.refs_3_), custom_call_target="tpu_custom_call" | custom-call | flops 1073741824 | bytes 2097152 | tf_op jit(solution)/shard_map/pallas_call | solution.py:272
  27.3 0.1 collective-permute-start.8
  27.3 0.5 %collective-permute-start.9 = (bf16[512,256]{1,0:T(8,128)(2,1)S(1)}, bf16[512,256]{1,0:T(8,128)(2,1)S(1)}, u32[]{:S(2)}, u32[]{:S(2)}) collective-permute-start(bf16[512,256]{1,0:T(8,128)(2,1)S(1)} %collective-permute-done.4.refs_1_), channel_id=1, source_target_pairs={{0,1},{1,0},{2,3},{3,2},{4,5},{5,4},{6,7},{7,6},{8,9},{9,8},{10,11... | collective-permute-start | bytes 786440 | tf_op jit(solution)/shard_map/ppermute | solution.py:183
  27.9 0.7 %collective-permute-start.7 = (bf16[256,256]{1,0:T(8,128)(2,1)S(1)}, bf16[256,256]{1,0:T(8,128)(2,1)S(1)}, u32[]{:S(2)}, u32[]{:S(2)}) collective-permute-start(bf16[256,256]{1,0:T(8,128)(2,1)S(1)} %slice.7), channel_id=1, source_target_pairs={{0,2},{1,3},{2,0},{3,1},{4,6},{5,7},{6,4},{7,5},{8,10},{9,11},{10,... | collective-permute-start | bytes 393224 | tf_op jit(solution)/shard_map/ppermute | solution.py:183
  28.5 0.7 %collective-permute-start.6 = (bf16[256,256]{1,0:T(8,128)(2,1)S(1)}, bf16[256,256]{1,0:T(8,128)(2,1)S(1)}, u32[]{:S(2)}, u32[]{:S(2)}) collective-permute-start(bf16[256,256]{1,0:T(8,128)(2,1)S(1)} %slice.6), channel_id=1, source_target_pairs={{0,4},{1,5},{2,6},{3,7},{4,0},{5,1},{6,2},{7,3},{8,12},{9,13},{10,... | collective-permute-start | bytes 393224 | tf_op jit(solution)/shard_map/ppermute | solution.py:183
  29.2 0.0 collective-permute-done.8.refs_0_
  29.2 1.3 %shard_map.105.refs_3_ = f32[512,2048]{1,0:T(8,128)S(1)} custom-call(bf16[512,256]{1,0:T(8,128)(2,1)S(1)} %collective-permute-done.8.refs_0_, bf16[512,256]{1,0:T(8,128)(2,1)S(1)} %collective-permute-done.9.refs_1_, bf16[8,1,256,2048]{3,2,1,0:T(8,128)(2,1)S(1)} %shard_map.102.refs_2_.refs_1_, f32[512,2048]{1,0:T(8,128)S(1)} %shard_map.104.refs_3_), custom_call_target="tpu_custom_call" | custom-call | flops 1073741824 | bytes 2097152 | tf_op jit(solution)/shard_map/pallas_call | solution.py:272
  30.5 2.9 %collective-permute-done.7.refs_1_ = bf16[256,256]{1,0:T(8,128)(2,1)S(1)} collective-permute-done((bf16[256,256]{1,0:T(8,128)(2,1)S(1)}, bf16[256,256]{1,0:T(8,128)(2,1)S(1)}, u32[]{:S(2)}, u32[]{:S(2)}) %collective-permute-start.7) | collective-permute-done | bytes 131104 | tf_op jit(solution)/shard_map/ppermute | solution.py:183
  33.4 0.3 collective-permute-done.6.refs_0_
  33.8 0.0 copy-start
  33.8 0.0 copy-start.1
  33.8 0.1 collective-permute-start.10
  33.9 0.7 %shard_map.106.refs_2_ = f32[512,2048]{1,0:T(8,128)S(1)} custom-call(bf16[256,256]{1,0:T(8,128)(2,1)S(1)} %collective-permute-done.6.refs_0_, bf16[256,256]{1,0:T(8,128)(2,1)S(1)} %collective-permute-done.7.refs_1_, bf16[8,1,256,2048]{3,2,1,0:T(8,128)(2,1)S(1)} %shard_map.102.refs_2_.refs_1_, f32[512,2048]{1,0:T(8,128)S(1)} %shard_map.105.refs_3_), custom_call_target="tpu_custom_call" | custom-call | flops 536870912 | bytes 1048576 | tf_op jit(solution)/shard_map/pallas_call | solution.py:272
  34.6 0.8 %collective-permute-done.10.refs_0_ = bf16[512,256]{1,0:T(8,128)(2,1)S(1)} collective-permute-done((bf16[512,256]{1,0:T(8,128)(2,1)S(1)}, bf16[512,256]{1,0:T(8,128)(2,1)S(1)}, u32[]{:S(2)}, u32[]{:S(2)}) %collective-permute-start.10) | collective-permute-done | bytes 262176 | tf_op jit(solution)/shard_map/ppermute | solution.py:183
  35.4 2.2 %shard_map.107 = bf16[512,16,128]{2,1,0:T(8,128)(2,1)} custom-call(bf16[512,256]{1,0:T(8,128)(2,1)S(1)} %collective-permute-done.10.refs_0_, bf16[8,1,256,2048]{3,2,1,0:T(8,128)(2,1)S(1)} %shard_map.102.refs_2_.refs_1_, f32[512,2048]{1,0:T(8,128)S(1)} %shard_map.106.refs_2_, bf16[512,16,128]{2,1,0:T(8,128)(2,1)S(1)} %copy-done, f32[1,128]{1,0:T(1,128)S(1)} %bitcast.7), custom_call_target="tpu_custom_call" | custom-call | flops 536870912 | bytes 1048576 | tf_op jit(solution)/shard_map/pallas_call | solution.py:272
  (7 shorter events, 0.0 us)
Async XLA Ops:
  2.6 11.8 %collective-permute-start.2 = (bf16[256,128]{1,0:T(8,128)(2,1)S(1)}, bf16[256,128]{1,0:T(8,128)(2,1)S(1)}, u32[]{:S(2)}, u32[]{:S(2)}) collective-permute-start(bf16[256,128]{1,0:T(8,128)(2,1)S(1)} %get-tuple-element.18.refs_0_), channel_id=1, source_target_pairs={{0,24},{1,25},{2,26},{3,27},{4,28},{5,29},{6,30},{7,31},{8,16},{9,... | collective-permute-start | bytes 196616 | tf_op jit(solution)/shard_map/ppermute | solution.py:183
  7.7 6.7 %collective-permute-start.1 = (bf16[256,128]{1,0:T(8,128)(2,1)S(1)}, bf16[256,128]{1,0:T(8,128)(2,1)S(1)}, u32[]{:S(2)}, u32[]{:S(2)}) collective-permute-start(bf16[256,128]{1,0:T(8,128)(2,1)S(1)} %get-tuple-element.18.refs_0_), channel_id=1, source_target_pairs={{0,16},{1,17},{2,18},{3,19},{4,20},{5,21},{6,22},{7,23},{8,24},{9,... | collective-permute-start | bytes 196616 | tf_op jit(solution)/shard_map/ppermute | solution.py:183
  7.7 6.7 %collective-permute-start = (bf16[256,128]{1,0:T(8,128)(2,1)S(1)}, bf16[256,128]{1,0:T(8,128)(2,1)S(1)}, u32[]{:S(2)}, u32[]{:S(2)}) collective-permute-start(bf16[256,128]{1,0:T(8,128)(2,1)S(1)} %get-tuple-element.18.refs_0_), channel_id=1, source_target_pairs={{0,8},{1,9},{2,10},{3,11},{4,12},{5,13},{6,14},{7,15},{8,0},{9,1},... | collective-permute-start | bytes 196616 | tf_op jit(solution)/shard_map/ppermute | solution.py:183
  8.4 13.5 %all-to-all-start = ((bf16[32,8,128]{2,1,0:T(8,128)(2,1)}), bf16[32,8,128]{2,1,0:T(8,128)(2,1)S(1)}, u32[]{:S(2)}, u32[]{:S(2)}) async-start(bf16[32,8,128]{2,1,0:T(8,128)(2,1)} %get-tuple-element.20), calls=%async_computation | async-start | bytes 131072 | tf_op jit(solution)/shard_map/all_to_all | solution.py:217
  14.7 9.9 %collective-permute-start.5 = (bf16[512,256]{1,0:T(8,128)(2,1)S(1)}, bf16[512,256]{1,0:T(8,128)(2,1)S(1)}, u32[]{:S(2)}, u32[]{:S(2)}) collective-permute-start(bf16[512,256]{1,0:T(8,128)(2,1)S(1)} %shard_map.101.refs_0_), channel_id=1, source_target_pairs={{0,1},{1,0},{2,3},{3,2},{4,5},{5,4},{6,7},{7,6},{8,9},{9,8},{10,11... | collective-permute-start | bytes 786440 | tf_op jit(solution)/shard_map/ppermute | solution.py:183
  15.0 10.9 %collective-permute-start.4 = (bf16[512,256]{1,0:T(8,128)(2,1)S(1)}, bf16[512,256]{1,0:T(8,128)(2,1)S(1)}, u32[]{:S(2)}, u32[]{:S(2)}) collective-permute-start(bf16[512,256]{1,0:T(8,128)(2,1)S(1)} %shard_map.101.refs_0_), channel_id=1, source_target_pairs={{0,4},{1,5},{2,6},{3,7},{4,0},{5,1},{6,2},{7,3},{8,12},{9,13},{10,... | collective-permute-start | bytes 786440 | tf_op jit(solution)/shard_map/ppermute | solution.py:183
  16.7 9.2 %collective-permute-start.3 = (bf16[512,256]{1,0:T(8,128)(2,1)S(1)}, bf16[512,256]{1,0:T(8,128)(2,1)S(1)}, u32[]{:S(2)}, u32[]{:S(2)}) collective-permute-start(bf16[512,256]{1,0:T(8,128)(2,1)S(1)} %shard_map.101.refs_0_), channel_id=1, source_target_pairs={{0,2},{1,3},{2,0},{3,1},{4,6},{5,7},{6,4},{7,5},{8,10},{9,11},{10,... | collective-permute-start | bytes 786440 | tf_op jit(solution)/shard_map/ppermute | solution.py:183
  27.3 2.0 %collective-permute-start.8 = (bf16[512,256]{1,0:T(8,128)(2,1)S(1)}, bf16[512,256]{1,0:T(8,128)(2,1)S(1)}, u32[]{:S(2)}, u32[]{:S(2)}) collective-permute-start(bf16[512,256]{1,0:T(8,128)(2,1)S(1)} %collective-permute-done.3.refs_0_), channel_id=1, source_target_pairs={{0,1},{1,0},{2,3},{3,2},{4,5},{5,4},{6,7},{7,6},{8,9},{9,8},{10,11... | collective-permute-start | bytes 786440 | tf_op jit(solution)/shard_map/ppermute | solution.py:183
  27.3 1.9 %collective-permute-start.9 = (bf16[512,256]{1,0:T(8,128)(2,1)S(1)}, bf16[512,256]{1,0:T(8,128)(2,1)S(1)}, u32[]{:S(2)}, u32[]{:S(2)}) collective-permute-start(bf16[512,256]{1,0:T(8,128)(2,1)S(1)} %collective-permute-done.4.refs_1_), channel_id=1, source_target_pairs={{0,1},{1,0},{2,3},{3,2},{4,5},{5,4},{6,7},{7,6},{8,9},{9,8},{10,11... | collective-permute-start | bytes 786440 | tf_op jit(solution)/shard_map/ppermute | solution.py:183
  27.9 5.5 %collective-permute-start.7 = (bf16[256,256]{1,0:T(8,128)(2,1)S(1)}, bf16[256,256]{1,0:T(8,128)(2,1)S(1)}, u32[]{:S(2)}, u32[]{:S(2)}) collective-permute-start(bf16[256,256]{1,0:T(8,128)(2,1)S(1)} %slice.7), channel_id=1, source_target_pairs={{0,2},{1,3},{2,0},{3,1},{4,6},{5,7},{6,4},{7,5},{8,10},{9,11},{10,... | collective-permute-start | bytes 393224 | tf_op jit(solution)/shard_map/ppermute | solution.py:183
  28.5 5.2 %collective-permute-start.6 = (bf16[256,256]{1,0:T(8,128)(2,1)S(1)}, bf16[256,256]{1,0:T(8,128)(2,1)S(1)}, u32[]{:S(2)}, u32[]{:S(2)}) collective-permute-start(bf16[256,256]{1,0:T(8,128)(2,1)S(1)} %slice.6), channel_id=1, source_target_pairs={{0,4},{1,5},{2,6},{3,7},{4,0},{5,1},{6,2},{7,3},{8,12},{9,13},{10,... | collective-permute-start | bytes 393224 | tf_op jit(solution)/shard_map/ppermute | solution.py:183
  33.8 1.6 %copy-start = (bf16[512,16,128]{2,1,0:T(8,128)(2,1)S(1)}, bf16[512,16,128]{2,1,0:T(8,128)(2,1)}, u32[]{:S(2)}) copy-start(bf16[512,16,128]{2,1,0:T(8,128)(2,1)} %refs_3_.1) | copy-start | bytes 6291460
  33.8 1.6 %copy-start.1 = (f32[128]{0:T(128)S(1)}, f32[128]{0:T(128)}, u32[]{:S(2)}) copy-start(f32[128]{0:T(128)} %param.19) | copy-start | bytes 1540
  33.8 1.6 %collective-permute-start.10 = (bf16[512,256]{1,0:T(8,128)(2,1)S(1)}, bf16[512,256]{1,0:T(8,128)(2,1)S(1)}, u32[]{:S(2)}, u32[]{:S(2)}) collective-permute-start(bf16[512,256]{1,0:T(8,128)(2,1)S(1)} %pad_maximum_fusion), channel_id=1, source_target_pairs={{0,1},{1,0},{2,3},{3,2},{4,5},{5,4},{6,7},{7,6},{8,9},{9,8},{10,11... | collective-permute-start | bytes 786440 | tf_op jit(solution)/shard_map/ppermute | solution.py:183

commit v9 on v8

--- a/solution.py
+++ b/solution.py
@@ -114,10 +114,11 @@
 def _band_kernel(masks, begins, count, held, *refs):
     refs = list(refs)
     take = lambda k: [refs.pop(0) for _ in range(k)]
-    lines = []
-    for mask in masks:
-        parts = take(2 if mask == 6 else 1)
-        lines.append(parts)
+    if masks == (1, 3, 5):
+        (block,) = take(1)
+        lines = [[block.at[k]] for k in range(3)]
+    else:
+        lines = [take(2 if mask == 6 else 1) for mask in masks]
     (t_ref,) = take(1)
     (sum_ref,) = (None,) if begins else take(1)
     pair_ref, shift_ref = (None, None) if count is None else take(2)
@@ -279,17 +280,15 @@
             scratch_shapes=scratch,
             compiler_params=params,
             cost_estimate=pl.CostEstimate(
-                flops=2 * band * depth * cols * zdim, bytes_accessed=2 * depth * cols * zdim, transcendentals=0
+                flops=band * cols * zdim, bytes_accessed=band * cols, transcendentals=0
             ),
         )(*operands)
 
-    total = add([line, _xor(line, 1, n)], (0, 1), None, False)
-    x, y, total = lax.optimization_barrier((x, y, total))
+    x, y, folded = lax.optimization_barrier((x, y, folded))
     upper, lower = _xor(x[:half], 4, n), _xor(y[half:], 2, n)
-    total = add([x, y], (2, 4), total, False)
-    x, y, total = lax.optimization_barrier((x, y, total))
-    across = [_xor(x, 1, n), _xor(y, 1, n)]
-    total = add(across, (3, 5), total, False)
+    across = _xor(jnp.stack([line, x, y]), 1, n)
+    total = add([line, x, y], (0, 2, 4), None, False)
+    total = add([across], (1, 3, 5), total, False)
     upper, lower, total = lax.optimization_barrier((upper, lower, total))
     last = _xor(jnp.concatenate([upper, lower], axis=0), 1, n)
     total = add([upper, lower], (6,), total, False)

time: 37.8 us -> 36.2 us (0.958)
  waiting for transfers between devices: 7.76 us -> 6.24 us
    ppermute x11 -> x9, waiting for transfers between devices: 4.04 us -> 2.36 us  [_xor(): return lax.ppermute(x, 'row', [(i, i ^ mask) for i in range(n)])]
    pallas_call x5 -> x4, Pallas kernels: 6.74 us -> 6.55 us  [add(): pl.pallas_call(functools.partial(_band_kernel, masks, total is None, coun...]
    ppermute x11 -> x9, starting transfers between devices: 11.2 us -> 11.3 us  [_xor(): return lax.ppermute(x, 'row', [(i, i ^ mask) for i in range(n)])]
  transfers between devices with their start and end apart: 12 -> 10, of which waited for: 4 -> 5; matrix products, arithmetic and copies ran while one was open for 0% -> 0% of each run, Pallas kernels for 17% -> 21%
where the time goes in v9:
time: 36.2 us; the launch traced here: 36 us
  starting transfers between devices  17.3 us (48%)
  Pallas kernels  12.2 us (34%)
  waiting for transfers between devices  6.24 us (17%)
    ppermute x9, starting transfers between devices, _xor(): return lax.ppermute(x, 'row', [(i, i ^ mask) for i in range(n)])  11.3 us
    pallas_call x4, Pallas kernels, add(): pl.pallas_call(functools.partial(_band_kernel, masks, total is None, coun...  6.55 us
    all_to_all x1, starting transfers between devices, shards(): lax.all_to_all(right, 'row', split_axis=0, concat_axis=0, tiled=True)  5.99 us
    all_to_all x1, waiting for transfers between devices, shards(): lax.all_to_all(right, 'row', split_axis=0, concat_axis=0, tiled=True)  3.87 us
    pallas_call x1, Pallas kernels, shards(): pl.pallas_call(_fold_kernel, out_shape=fold_out, scratch_shapes=[pltpu.VM...  2.76 us
    pallas_call x1, Pallas kernels, shards(): pl.pallas_call(_project_kernel, in_specs=[anywhere] * 8, out_specs=(vmem,...  2.61 us
    ppermute x9, waiting for transfers between devices, _xor(): return lax.ppermute(x, 'row', [(i, i ^ mask) for i in range(n)])  2.36 us
  transfers between devices with their start and end apart: 10, of which 5 were waited for; matrix products, arithmetic and copies ran while one was open for 0% of the time, Pallas kernels for 21%

profile of v9, /device:TPU:0, one launch (start us, length us, event | category | flops | bytes accessed | tf_op | source)
XLA Modules:
  0.0 36.0 jit_solution(1963237163469839818)
XLA Ops:
  0.0 2.6 %shard_map.100 = (bf16[256,128]{1,0:T(8,128)(2,1)S(1)}, bf16[32,8,128]{2,1,0:T(8,128)(2,1)}, bf16[1024,128]{1,0:T(8,128)(2,1)S(1)}, bf16[2,512,256]{2,1,0:T(8,128)(2,1)S(1)}) custom-call(bf16[2,512,256]{2,1,0:T(8,128)(2,1)} %refs_0_.1, f32[1,256]{1,0:T(1,128)} %bitcast.16, f32[1,256]{1,0:T(1,128)} %bitcast.17, bf16[32,256]{1,0:T(8,128)(2,1)} %bitcast.14, ...), custom_call_target="tpu_custom_call" | custom-call | flops 33554432 | bytes 524288 | tf_op jit(solution)/shard_map/pallas_call | solution.py:201
  2.6 5.1 %collective-permute-start.2 = (bf16[256,128]{1,0:T(8,128)(2,1)S(1)}, bf16[256,128]{1,0:T(8,128)(2,1)S(1)}, u32[]{:S(2)}, u32[]{:S(2)}) collective-permute-start(bf16[256,128]{1,0:T(8,128)(2,1)S(1)} %get-tuple-element.15.refs_0_), channel_id=1, source_target_pairs={{0,24},{1,25},{2,26},{3,27},{4,28},{5,29},{6,30},{7,31},{8,16},{9,... | collective-permute-start | bytes 196616 | tf_op jit(solution)/shard_map/ppermute | solution.py:184
  7.7 0.0 collective-permute-start.1
  7.7 0.6 %collective-permute-start = (bf16[256,128]{1,0:T(8,128)(2,1)S(1)}, bf16[256,128]{1,0:T(8,128)(2,1)S(1)}, u32[]{:S(2)}, u32[]{:S(2)}) collective-permute-start(bf16[256,128]{1,0:T(8,128)(2,1)S(1)} %get-tuple-element.15.refs_0_), channel_id=1, source_target_pairs={{0,8},{1,9},{2,10},{3,11},{4,12},{5,13},{6,14},{7,15},{8,0},{9,1},... | collective-permute-start | bytes 196616 | tf_op jit(solution)/shard_map/ppermute | solution.py:184
  8.4 6.0 %all-to-all-start = ((bf16[32,8,128]{2,1,0:T(8,128)(2,1)}), bf16[32,8,128]{2,1,0:T(8,128)(2,1)S(1)}, u32[]{:S(2)}, u32[]{:S(2)}) async-start(bf16[32,8,128]{2,1,0:T(8,128)(2,1)} %get-tuple-element.17), calls=%async_computation | async-start | bytes 131072 | tf_op jit(solution)/shard_map/all_to_all | solution.py:218
  14.4 0.0 collective-permute-done.2.refs_3_
  14.4 0.0 collective-permute-done.1.refs_2_
  14.4 0.0 collective-permute-done.refs_1_
  14.4 0.3 shard_map.101.refs_0_
  14.7 1.8 %collective-permute-start.4 = (bf16[512,256]{1,0:T(8,128)(2,1)S(1)}, bf16[512,256]{1,0:T(8,128)(2,1)S(1)}, u32[]{:S(2)}, u32[]{:S(2)}) collective-permute-start(bf16[512,256]{1,0:T(8,128)(2,1)S(1)} %shard_map.101.refs_0_), channel_id=1, source_target_pairs={{0,4},{1,5},{2,6},{3,7},{4,0},{5,1},{6,2},{7,3},{8,12},{9,13},{10,... | collective-permute-start | bytes 786440 | tf_op jit(solution)/shard_map/ppermute | solution.py:184
  16.6 1.5 %collective-permute-start.3 = (bf16[512,256]{1,0:T(8,128)(2,1)S(1)}, bf16[512,256]{1,0:T(8,128)(2,1)S(1)}, u32[]{:S(2)}, u32[]{:S(2)}) collective-permute-start(bf16[512,256]{1,0:T(8,128)(2,1)S(1)} %shard_map.101.refs_0_), channel_id=1, source_target_pairs={{0,2},{1,3},{2,0},{3,1},{4,6},{5,7},{6,4},{7,5},{8,10},{9,11},{10,... | collective-permute-start | bytes 786440 | tf_op jit(solution)/shard_map/ppermute | solution.py:184
  18.0 3.9 %all-to-all-done.right_ref = bf16[32,8,128]{2,1,0:T(8,128)(2,1)S(1)} async-done(((bf16[32,8,128]{2,1,0:T(8,128)(2,1)}), bf16[32,8,128]{2,1,0:T(8,128)(2,1)S(1)}, u32[]{:S(2)}, u32[]{:S(2)}) %all-to-all-start) | async-done | bytes 65568 | tf_op jit(solution)/shard_map/all_to_all | solution.py:218
  21.9 2.8 %shard_map.102.refs_3_.refs_1_.refs_2_ = bf16[8,1,256,2048]{3,2,1,0:T(8,128)(2,1)S(1)} custom-call(bf16[32,8,128]{2,1,0:T(8,128)(2,1)S(1)} %all-to-all-done.right_ref, bf16[1024,128]{1,0:T(8,128)(2,1)S(1)} %get-tuple-element.18.final_ref), custom_call_target="tpu_custom_call" | custom-call | flops 2147483648 | bytes 8388608 | tf_op jit(solution)/shard_map/pallas_call | solution.py:248
  24.7 0.0 collective-permute-done.4.refs_2_
  24.7 0.3 collective-permute-done.3.refs_1_
  25.0 0.1 pad_maximum_fusion
  25.1 0.1 collective-permute-start.7
  25.2 1.4 %collective-permute-start.6 = (bf16[256,256]{1,0:T(8,128)(2,1)S(1)}, bf16[256,256]{1,0:T(8,128)(2,1)S(1)}, u32[]{:S(2)}, u32[]{:S(2)}) collective-permute-start(bf16[256,256]{1,0:T(8,128)(2,1)S(1)} %slice.7), channel_id=1, source_target_pairs={{0,2},{1,3},{2,0},{3,1},{4,6},{5,7},{6,4},{7,5},{8,10},{9,11},{10,... | collective-permute-start | bytes 393224 | tf_op jit(solution)/shard_map/ppermute | solution.py:184
  26.6 0.7 %collective-permute-start.5 = (bf16[256,256]{1,0:T(8,128)(2,1)S(1)}, bf16[256,256]{1,0:T(8,128)(2,1)S(1)}, u32[]{:S(2)}, u32[]{:S(2)}) collective-permute-start(bf16[256,256]{1,0:T(8,128)(2,1)S(1)} %slice.6), channel_id=1, source_target_pairs={{0,4},{1,5},{2,6},{3,7},{4,0},{5,1},{6,2},{7,3},{8,12},{9,13},{10,... | collective-permute-start | bytes 393224 | tf_op jit(solution)/shard_map/ppermute | solution.py:184
  27.3 1.8 %shard_map.103.refs_2_ = f32[512,2048]{1,0:T(8,128)S(1)} custom-call(bf16[512,256]{1,0:T(8,128)(2,1)S(1)} %shard_map.101.refs_0_, bf16[512,256]{1,0:T(8,128)(2,1)S(1)} %collective-permute-done.3.refs_1_, bf16[512,256]{1,0:T(8,128)(2,1)S(1)} %collective-permute-done.4.refs_2_, bf16[8,1,256,2048]{3,2,1,0:T(8,128)(2,1)S(1)} %shard_map.102.refs_3_.refs_1_.refs_2_), custom_call_target="tpu_custom_call" | custom-call | flops 1048576 | bytes 8192 | tf_op jit(solution)/shard_map/pallas_call | solution.py:273
  29.1 0.0 collective-permute-done.7.refs_0_
  29.1 1.8 %shard_map.104.refs_3_ = f32[512,2048]{1,0:T(8,128)S(1)} custom-call(bf16[3,512,256]{2,1,0:T(8,128)(2,1)S(1)} %collective-permute-done.7.refs_0_, bf16[8,1,256,2048]{3,2,1,0:T(8,128)(2,1)S(1)} %shard_map.102.refs_3_.refs_1_.refs_2_, f32[512,2048]{1,0:T(8,128)S(1)} %shard_map.103.refs_2_), custom_call_target="tpu_custom_call" | custom-call | flops 1048576 | bytes 8192 | tf_op jit(solution)/shard_map/pallas_call | solution.py:273
  30.9 0.2 collective-permute-done.6.refs_1_
  31.2 1.0 %collective-permute-done.5.refs_0_ = bf16[256,256]{1,0:T(8,128)(2,1)S(1)} collective-permute-done((bf16[256,256]{1,0:T(8,128)(2,1)S(1)}, bf16[256,256]{1,0:T(8,128)(2,1)S(1)}, u32[]{:S(2)}, u32[]{:S(2)}) %collective-permute-start.5) | collective-permute-done | bytes 131104 | tf_op jit(solution)/shard_map/ppermute | solution.py:184
  32.2 0.0 copy-start
  32.2 0.0 copy-start.1
  32.2 0.1 collective-permute-start.8
  32.3 0.7 %shard_map.105.refs_2_ = f32[512,2048]{1,0:T(8,128)S(1)} custom-call(bf16[256,256]{1,0:T(8,128)(2,1)S(1)} %collective-permute-done.5.refs_0_, bf16[256,256]{1,0:T(8,128)(2,1)S(1)} %collective-permute-done.6.refs_1_, bf16[8,1,256,2048]{3,2,1,0:T(8,128)(2,1)S(1)} %shard_map.102.refs_3_.refs_1_.refs_2_, f32[512,2048]{1,0:T(8,128)S(1)} %shard_map.104.refs_3_), custom_call_target="tpu_custom_call" | custom-call | flops 1048576 | bytes 8192 | tf_op jit(solution)/shard_map/pallas_call | solution.py:273
  33.0 0.8 %collective-permute-done.8.refs_0_ = bf16[512,256]{1,0:T(8,128)(2,1)S(1)} collective-permute-done((bf16[512,256]{1,0:T(8,128)(2,1)S(1)}, bf16[512,256]{1,0:T(8,128)(2,1)S(1)}, u32[]{:S(2)}, u32[]{:S(2)}) %collective-permute-start.8) | collective-permute-done | bytes 262176 | tf_op jit(solution)/shard_map/ppermute | solution.py:184
  33.8 0.0 copy-done
  33.8 0.0 copy-done.1
  33.8 2.2 %shard_map.106 = bf16[512,16,128]{2,1,0:T(8,128)(2,1)} custom-call(bf16[512,256]{1,0:T(8,128)(2,1)S(1)} %collective-permute-done.8.refs_0_, bf16[8,1,256,2048]{3,2,1,0:T(8,128)(2,1)S(1)} %shard_map.102.refs_3_.refs_1_.refs_2_, f32[512,2048]{1,0:T(8,128)S(1)} %shard_map.105.refs_2_, bf16[512,16,128]{2,1,0:T(8,128)(2,1)S(1)} %copy-done, f32[1,128]{1,0:T(1,128)S(1)} %bitcast.13), custom_call_target="tpu_custom_call" | custom-call | flops 1048576 | bytes 8192 | tf_op jit(solution)/shard_map/pallas_call | solution.py:273
  (3 shorter events, 0.0 us)
Async XLA Ops:
  2.6 11.8 %collective-permute-start.2 = (bf16[256,128]{1,0:T(8,128)(2,1)S(1)}, bf16[256,128]{1,0:T(8,128)(2,1)S(1)}, u32[]{:S(2)}, u32[]{:S(2)}) collective-permute-start(bf16[256,128]{1,0:T(8,128)(2,1)S(1)} %get-tuple-element.15.refs_0_), channel_id=1, source_target_pairs={{0,24},{1,25},{2,26},{3,27},{4,28},{5,29},{6,30},{7,31},{8,16},{9,... | collective-permute-start | bytes 196616 | tf_op jit(solution)/shard_map/ppermute | solution.py:184
  7.7 6.7 %collective-permute-start.1 = (bf16[256,128]{1,0:T(8,128)(2,1)S(1)}, bf16[256,128]{1,0:T(8,128)(2,1)S(1)}, u32[]{:S(2)}, u32[]{:S(2)}) collective-permute-start(bf16[256,128]{1,0:T(8,128)(2,1)S(1)} %get-tuple-element.15.refs_0_), channel_id=1, source_target_pairs={{0,16},{1,17},{2,18},{3,19},{4,20},{5,21},{6,22},{7,23},{8,24},{9,... | collective-permute-start | bytes 196616 | tf_op jit(solution)/shard_map/ppermute | solution.py:184
  7.7 6.7 %collective-permute-start = (bf16[256,128]{1,0:T(8,128)(2,1)S(1)}, bf16[256,128]{1,0:T(8,128)(2,1)S(1)}, u32[]{:S(2)}, u32[]{:S(2)}) collective-permute-start(bf16[256,128]{1,0:T(8,128)(2,1)S(1)} %get-tuple-element.15.refs_0_), channel_id=1, source_target_pairs={{0,8},{1,9},{2,10},{3,11},{4,12},{5,13},{6,14},{7,15},{8,0},{9,1},... | collective-permute-start | bytes 196616 | tf_op jit(solution)/shard_map/ppermute | solution.py:184
  8.4 13.5 %all-to-all-start = ((bf16[32,8,128]{2,1,0:T(8,128)(2,1)}), bf16[32,8,128]{2,1,0:T(8,128)(2,1)S(1)}, u32[]{:S(2)}, u32[]{:S(2)}) async-start(bf16[32,8,128]{2,1,0:T(8,128)(2,1)} %get-tuple-element.17), calls=%async_computation | async-start | bytes 131072 | tf_op jit(solution)/shard_map/all_to_all | solution.py:218
  14.7 9.9 %collective-permute-start.4 = (bf16[512,256]{1,0:T(8,128)(2,1)S(1)}, bf16[512,256]{1,0:T(8,128)(2,1)S(1)}, u32[]{:S(2)}, u32[]{:S(2)}) collective-permute-start(bf16[512,256]{1,0:T(8,128)(2,1)S(1)} %shard_map.101.refs_0_), channel_id=1, source_target_pairs={{0,4},{1,5},{2,6},{3,7},{4,0},{5,1},{6,2},{7,3},{8,12},{9,13},{10,... | collective-permute-start | bytes 786440 | tf_op jit(solution)/shard_map/ppermute | solution.py:184
  16.6 8.4 %collective-permute-start.3 = (bf16[512,256]{1,0:T(8,128)(2,1)S(1)}, bf16[512,256]{1,0:T(8,128)(2,1)S(1)}, u32[]{:S(2)}, u32[]{:S(2)}) collective-permute-start(bf16[512,256]{1,0:T(8,128)(2,1)S(1)} %shard_map.101.refs_0_), channel_id=1, source_target_pairs={{0,2},{1,3},{2,0},{3,1},{4,6},{5,7},{6,4},{7,5},{8,10},{9,11},{10,... | collective-permute-start | bytes 786440 | tf_op jit(solution)/shard_map/ppermute | solution.py:184
  25.1 4.0 %collective-permute-start.7 = (bf16[3,512,256]{2,1,0:T(8,128)(2,1)S(1)}, bf16[3,512,256]{2,1,0:T(8,128)(2,1)S(1)}, u32[]{:S(2)}, u32[]{:S(2)}) collective-permute-start(bf16[3,512,256]{2,1,0:T(8,128)(2,1)S(1)} %pad_maximum_fusion), channel_id=1, source_target_pairs={{0,1},{1,0},{2,3},{3,2},{4,5},{5,4},{6,7},{7,6},{8,9},{9,8},{10,11... | collective-permute-start | bytes 2359304 | tf_op jit(solution)/shard_map/ppermute | solution.py:184
  25.2 6.0 %collective-permute-start.6 = (bf16[256,256]{1,0:T(8,128)(2,1)S(1)}, bf16[256,256]{1,0:T(8,128)(2,1)S(1)}, u32[]{:S(2)}, u32[]{:S(2)}) collective-permute-start(bf16[256,256]{1,0:T(8,128)(2,1)S(1)} %slice.7), channel_id=1, source_target_pairs={{0,2},{1,3},{2,0},{3,1},{4,6},{5,7},{6,4},{7,5},{8,10},{9,11},{10,... | collective-permute-start | bytes 393224 | tf_op jit(solution)/shard_map/ppermute | solution.py:184
  26.6 5.6 %collective-permute-start.5 = (bf16[256,256]{1,0:T(8,128)(2,1)S(1)}, bf16[256,256]{1,0:T(8,128)(2,1)S(1)}, u32[]{:S(2)}, u32[]{:S(2)}) collective-permute-start(bf16[256,256]{1,0:T(8,128)(2,1)S(1)} %slice.6), channel_id=1, source_target_pairs={{0,4},{1,5},{2,6},{3,7},{4,0},{5,1},{6,2},{7,3},{8,12},{9,13},{10,... | collective-permute-start | bytes 393224 | tf_op jit(solution)/shard_map/ppermute | solution.py:184
  32.2 1.6 %copy-start = (bf16[512,16,128]{2,1,0:T(8,128)(2,1)S(1)}, bf16[512,16,128]{2,1,0:T(8,128)(2,1)}, u32[]{:S(2)}) copy-start(bf16[512,16,128]{2,1,0:T(8,128)(2,1)} %refs_3_.1) | copy-start | bytes 6291460
  32.2 1.6 %copy-start.1 = (f32[128]{0:T(128)S(1)}, f32[128]{0:T(128)}, u32[]{:S(2)}) copy-start(f32[128]{0:T(128)} %param.19) | copy-start | bytes 1540
  32.2 1.6 %collective-permute-start.8 = (bf16[512,256]{1,0:T(8,128)(2,1)S(1)}, bf16[512,256]{1,0:T(8,128)(2,1)S(1)}, u32[]{:S(2)}, u32[]{:S(2)}) collective-permute-start(bf16[512,256]{1,0:T(8,128)(2,1)S(1)} %pad_maximum_fusion.1), channel_id=1, source_target_pairs={{0,1},{1,0},{2,3},{3,2},{4,5},{5,4},{6,7},{7,6},{8,9},{9,8},{10,11... | collective-permute-start | bytes 786440 | tf_op jit(solution)/shard_map/ppermute | solution.py:184

commit v10 on v9

--- a/solution.py
+++ b/solution.py
@@ -46,7 +46,7 @@
         copy.wait()
     x_ref, gain_ref, bias_ref, w1_ref, b1_ref, w2_ref, b2_ref = held
     band_half = left_ref.shape[0]
-    n = right_ref.shape[0]
+    n = right_ref.shape[0] * 2
     feats = x_ref.shape[2]
     normed = []
     for s in range(2):
@@ -69,7 +69,7 @@
     right = lax.dot_general(
         jnp.concatenate(parts, axis=1), _stacked(w2_ref[...], 4), NT, preferred_element_type=jnp.float32
     )
-    right_ref[...] = (right + shift2).reshape(n, 8, LANES).astype(jnp.bfloat16)
+    right_ref[...] = (right + shift2).reshape(n // 2, 16, LANES).astype(jnp.bfloat16)
 
 
 def _line_kernel(*refs):
@@ -83,10 +83,17 @@
             out_ref[pl.ds(h * half, half), pl.ds(q * wide, wide)] = moved.astype(jnp.bfloat16)
 
 
-def _fold_kernel(right_ref, final_ref, out_ref, block_ref, pairs_ref):
-    devices = right_ref.shape[0]
+def _fold_kernel(own_ref, other_ref, final_ref, out_ref, block_ref, pairs_ref):
+    chips = own_ref.shape[0]
+    devices = chips * 2
     groups = devices // 4
-    block_ref[...] = right_ref[...].astype(jnp.float32).reshape(devices * 8, LANES)
+    core = lax.axis_index("row") % 2
+    own, other = (ref[...].astype(jnp.float32).reshape(chips, 2, 8, LANES) for ref in (own_ref, other_ref))
+    own, other = (jnp.where(core == 0, block[:, 0], block[:, 1]) for block in (own, other))
+    by_core = jnp.where(core == 0, own, other), jnp.where(core == 0, other, own)
+    for p in range(chips):
+        for c in range(2):
+            block_ref[pl.ds((p * 2 + c) * 8, 8), :] = by_core[c][p]
     for jr in range(8):
         for g in range(groups):
             four = block_ref[pl.ds(g * 8 + jr, 4, stride=groups * 8), :]
@@ -204,7 +211,7 @@
         out_specs=(vmem,) * 4,
         out_shape=(
             jax.ShapeDtypeStruct((half, LANES), jnp.bfloat16),
-            jax.ShapeDtypeStruct((n, 8, LANES), jnp.bfloat16),
+            jax.ShapeDtypeStruct((n // 2, 16, LANES), jnp.bfloat16),
             jax.ShapeDtypeStruct(final.shape, final.dtype),
             jax.ShapeDtypeStruct((2, 4 * LANES, 8 * CHANS), jnp.bfloat16),
         ),
@@ -215,7 +222,9 @@
         ),
     )(*sources, pltpu.with_memory_space_constraint(final, pltpu.HBM))
 
-    right = lax.all_to_all(right, "row", split_axis=0, concat_axis=0, tiled=True)
+    cores = [[chip * 2 + core for chip in range(n // 2)] for core in range(2)]
+    right = lax.all_to_all(right, "row", split_axis=0, concat_axis=0, axis_index_groups=cores, tiled=True)
+    right_other = _xor(right, 1, n)
 
     part = 32
     parts = n // part
@@ -235,12 +244,13 @@
     )
     fold_out = jax.ShapeDtypeStruct((8, parts, 8 * CHANS, cols * zdim), jnp.bfloat16)
     if small:
-        specs = dict(in_specs=[vmem, vmem], out_specs=vmem)
+        specs = dict(in_specs=[vmem] * 3, out_specs=vmem)
     else:
         specs = dict(
             grid=(parts,),
             in_specs=[
-                pl.BlockSpec((part, 8, LANES), lambda i: (i, 0, 0)),
+                pl.BlockSpec((part // 2, 16, LANES), lambda i: (i, 0, 0)),
+                pl.BlockSpec((part // 2, 16, LANES), lambda i: (i, 0, 0)),
                 pl.BlockSpec(final.shape, lambda i: (0, 0)),
             ],
             out_specs=pl.BlockSpec((8, 1, 8 * CHANS, cols * zdim), lambda i: (0, i, 0, 0)),
@@ -252,7 +262,7 @@
         compiler_params=params,
         cost_estimate=fold_cost,
         **specs,
-    )(right, final)
+    )(right, right_other, final)
 
     def add(lines, masks, total, last):
         depth = len(masks) * parts * 8 * CHANS

time: 36.2 us -> 41.2 us (1.14)
  waiting for transfers between devices: 6.24 us -> 10.6 us
  starting transfers between devices: 17.3 us -> 18 us
    ppermute x9 -> x10, waiting for transfers between devices: 2.36 us -> 5.67 us  [_xor(): return lax.ppermute(x, 'row', [(i, i ^ mask) for i in range(n)])]
    all_to_all x1, starting transfers between devices: 5.99 us -> 8.33 us  [shards(): lax.all_to_all(right, 'row', split_axis=0, concat_axis=0, axis_index_grou...]
    ppermute x9 -> x10, starting transfers between devices: 11.3 us -> 9.65 us  [_xor(): return lax.ppermute(x, 'row', [(i, i ^ mask) for i in range(n)])]
    all_to_all x1, waiting for transfers between devices: 3.87 us -> 4.88 us  [shards(): lax.all_to_all(right, 'row', split_axis=0, concat_axis=0, axis_index_grou...]
  transfers between devices with their start and end apart: 10 -> 11, of which waited for: 5 -> 7; matrix products, arithmetic and copies ran while one was open for 0% -> 0% of each run, Pallas kernels for 21% -> 18%
where the time goes in v10:
time: 41.2 us; the launch traced here: 41 us
  starting transfers between devices  18 us (44%)
  Pallas kernels  12.2 us (30%)
  waiting for transfers between devices  10.6 us (26%)
    ppermute x10, starting transfers between devices, _xor(): return lax.ppermute(x, 'row', [(i, i ^ mask) for i in range(n)])  9.65 us
    all_to_all x1, starting transfers between devices, shards(): lax.all_to_all(right, 'row', split_axis=0, concat_axis=0, axis_index_grou...  8.33 us
    pallas_call x4, Pallas kernels, add(): pl.pallas_call(functools.partial(_band_kernel, masks, total is None, coun...  6.55 us
    ppermute x10, waiting for transfers between devices, _xor(): return lax.ppermute(x, 'row', [(i, i ^ mask) for i in range(n)])  5.67 us
    all_to_all x1, waiting for transfers between devices, shards(): lax.all_to_all(right, 'row', split_axis=0, concat_axis=0, axis_index_grou...  4.88 us
    pallas_call x1, Pallas kernels, shards(): pl.pallas_call(_fold_kernel, out_shape=fold_out, scratch_shapes=[pltpu.VM...  2.78 us
    pallas_call x1, Pallas kernels, shards(): pl.pallas_call(_project_kernel, in_specs=[anywhere] * 8, out_specs=(vmem,...  2.61 us
  transfers between devices with their start and end apart: 11, of which 7 were waited for; matrix products, arithmetic and copies ran while one was open for 0% of the time, Pallas kernels for 18%

profile of v10, /device:TPU:0, one launch (start us, length us, event | category | flops | bytes accessed | tf_op | source)
XLA Modules:
  0.0 41.0 jit_solution(7276371620618263747)
XLA Ops:
  0.0 2.6 %shard_map.100 = (bf16[256,128]{1,0:T(8,128)(2,1)S(1)}, bf16[16,16,128]{2,1,0:T(8,128)(2,1)}, bf16[1024,128]{1,0:T(8,128)(2,1)S(1)}, bf16[2,512,256]{2,1,0:T(8,128)(2,1)S(1)}) custom-call(bf16[2,512,256]{2,1,0:T(8,128)(2,1)} %refs_0_.1, f32[1,256]{1,0:T(1,128)} %bitcast.16, f32[1,256]{1,0:T(1,128)} %bitcast.17, bf16[32,256]{1,0:T(8,128)(2,1)} %bitcast.14, ...), custom_call_target="tpu_custom_call" | custom-call | flops 33554432 | bytes 524288 | tf_op jit(solution)/shard_map/pallas_call | solution.py:208
  2.6 8.3 %all-to-all-start = ((bf16[16,16,128]{2,1,0:T(8,128)(2,1)}), bf16[16,16,128]{2,1,0:T(8,128)(2,1)S(1)}, u32[]{:S(2)}, u32[]{:S(2)}) async-start(bf16[16,16,128]{2,1,0:T(8,128)(2,1)} %get-tuple-element.17), calls=%async_computation | async-start | bytes 131072 | tf_op jit(solution)/shard_map/all_to_all | solution.py:226
  11.0 3.7 %collective-permute-start.2 = (bf16[256,128]{1,0:T(8,128)(2,1)S(1)}, bf16[256,128]{1,0:T(8,128)(2,1)S(1)}, u32[]{:S(2)}, u32[]{:S(2)}) collective-permute-start(bf16[256,128]{1,0:T(8,128)(2,1)S(1)} %get-tuple-element.15.refs_0_), channel_id=1, source_target_pairs={{0,24},{1,25},{2,26},{3,27},{4,28},{5,29},{6,30},{7,31},{8,16},{9,... | collective-permute-start | bytes 196616 | tf_op jit(solution)/shard_map/ppermute | solution.py:191
  14.7 0.0 collective-permute-start.1
  14.7 0.7 %collective-permute-start = (bf16[256,128]{1,0:T(8,128)(2,1)S(1)}, bf16[256,128]{1,0:T(8,128)(2,1)S(1)}, u32[]{:S(2)}, u32[]{:S(2)}) collective-permute-start(bf16[256,128]{1,0:T(8,128)(2,1)S(1)} %get-tuple-element.15.refs_0_), channel_id=1, source_target_pairs={{0,8},{1,9},{2,10},{3,11},{4,12},{5,13},{6,14},{7,15},{8,0},{9,1},... | collective-permute-start | bytes 196616 | tf_op jit(solution)/shard_map/ppermute | solution.py:191
  15.4 4.9 %all-to-all-done.own_ref = bf16[16,16,128]{2,1,0:T(8,128)(2,1)S(1)} async-done(((bf16[16,16,128]{2,1,0:T(8,128)(2,1)}), bf16[16,16,128]{2,1,0:T(8,128)(2,1)S(1)}, u32[]{:S(2)}, u32[]{:S(2)}) %all-to-all-start) | async-done | bytes 65568 | tf_op jit(solution)/shard_map/all_to_all | solution.py:226
  20.3 0.0 collective-permute-start.5
  20.3 0.0 collective-permute-done.2.refs_3_
  20.3 0.8 %collective-permute-done.1.refs_2_ = bf16[256,128]{1,0:T(8,128)(2,1)S(1)} collective-permute-done((bf16[256,128]{1,0:T(8,128)(2,1)S(1)}, bf16[256,128]{1,0:T(8,128)(2,1)S(1)}, u32[]{:S(2)}, u32[]{:S(2)}) %collective-permute-start.1) | collective-permute-done | bytes 65568 | tf_op jit(solution)/shard_map/ppermute | solution.py:191
  21.1 0.0 collective-permute-done.refs_1_
  21.1 0.3 shard_map.101.refs_0_
  21.5 1.5 %collective-permute-start.4 = (bf16[512,256]{1,0:T(8,128)(2,1)S(1)}, bf16[512,256]{1,0:T(8,128)(2,1)S(1)}, u32[]{:S(2)}, u32[]{:S(2)}) collective-permute-start(bf16[512,256]{1,0:T(8,128)(2,1)S(1)} %shard_map.101.refs_0_), channel_id=1, source_target_pairs={{0,4},{1,5},{2,6},{3,7},{4,0},{5,1},{6,2},{7,3},{8,12},{9,13},{10,... | collective-permute-start | bytes 786440 | tf_op jit(solution)/shard_map/ppermute | solution.py:191
  23.0 1.5 %collective-permute-start.3 = (bf16[512,256]{1,0:T(8,128)(2,1)S(1)}, bf16[512,256]{1,0:T(8,128)(2,1)S(1)}, u32[]{:S(2)}, u32[]{:S(2)}) collective-permute-start(bf16[512,256]{1,0:T(8,128)(2,1)S(1)} %shard_map.101.refs_0_), channel_id=1, source_target_pairs={{0,2},{1,3},{2,0},{3,1},{4,6},{5,7},{6,4},{7,5},{8,10},{9,11},{10,... | collective-permute-start | bytes 786440 | tf_op jit(solution)/shard_map/ppermute | solution.py:191
  24.5 0.0 collective-permute-done.5.other_ref
  24.5 2.8 %shard_map.102.refs_3_.refs_1_.refs_2_ = bf16[8,1,256,2048]{3,2,1,0:T(8,128)(2,1)S(1)} custom-call(bf16[16,16,128]{2,1,0:T(8,128)(2,1)S(1)} %all-to-all-done.own_ref, bf16[16,16,128]{2,1,0:T(8,128)(2,1)S(1)} %collective-permute-done.5.other_ref, bf16[1024,128]{1,0:T(8,128)(2,1)S(1)} %get-tuple-element.18.final_ref), custom_call_target="tpu_custom_call" | custom-call | flops 2147483648 | bytes 8388608 | tf_op jit(solution)/shard_map/pallas_call | solution.py:258
  27.2 2.1 %collective-permute-done.4.refs_2_ = bf16[512,256]{1,0:T(8,128)(2,1)S(1)} collective-permute-done((bf16[512,256]{1,0:T(8,128)(2,1)S(1)}, bf16[512,256]{1,0:T(8,128)(2,1)S(1)}, u32[]{:S(2)}, u32[]{:S(2)}) %collective-permute-start.4) | collective-permute-done | bytes 262176 | tf_op jit(solution)/shard_map/ppermute | solution.py:191
  29.4 0.5 %collective-permute-done.3.refs_1_ = bf16[512,256]{1,0:T(8,128)(2,1)S(1)} collective-permute-done((bf16[512,256]{1,0:T(8,128)(2,1)S(1)}, bf16[512,256]{1,0:T(8,128)(2,1)S(1)}, u32[]{:S(2)}, u32[]{:S(2)}) %collective-permute-start.3) | collective-permute-done | bytes 262176 | tf_op jit(solution)/shard_map/ppermute | solution.py:191
  29.9 0.1 pad_maximum_fusion
  29.9 0.1 collective-permute-start.8
  30.1 1.5 %collective-permute-start.7 = (bf16[256,256]{1,0:T(8,128)(2,1)S(1)}, bf16[256,256]{1,0:T(8,128)(2,1)S(1)}, u32[]{:S(2)}, u32[]{:S(2)}) collective-permute-start(bf16[256,256]{1,0:T(8,128)(2,1)S(1)} %slice.7), channel_id=1, source_target_pairs={{0,2},{1,3},{2,0},{3,1},{4,6},{5,7},{6,4},{7,5},{8,10},{9,11},{10,... | collective-permute-start | bytes 393224 | tf_op jit(solution)/shard_map/ppermute | solution.py:191
  31.5 0.6 %collective-permute-start.6 = (bf16[256,256]{1,0:T(8,128)(2,1)S(1)}, bf16[256,256]{1,0:T(8,128)(2,1)S(1)}, u32[]{:S(2)}, u32[]{:S(2)}) collective-permute-start(bf16[256,256]{1,0:T(8,128)(2,1)S(1)} %slice.6), channel_id=1, source_target_pairs={{0,4},{1,5},{2,6},{3,7},{4,0},{5,1},{6,2},{7,3},{8,12},{9,13},{10,... | collective-permute-start | bytes 393224 | tf_op jit(solution)/shard_map/ppermute | solution.py:191
  32.1 1.8 %shard_map.103.refs_2_ = f32[512,2048]{1,0:T(8,128)S(1)} custom-call(bf16[512,256]{1,0:T(8,128)(2,1)S(1)} %shard_map.101.refs_0_, bf16[512,256]{1,0:T(8,128)(2,1)S(1)} %collective-permute-done.3.refs_1_, bf16[512,256]{1,0:T(8,128)(2,1)S(1)} %collective-permute-done.4.refs_2_, bf16[8,1,256,2048]{3,2,1,0:T(8,128)(2,1)S(1)} %shard_map.102.refs_3_.refs_1_.refs_2_), custom_call_target="tpu_custom_call" | custom-call | flops 1048576 | bytes 8192 | tf_op jit(solution)/shard_map/pallas_call | solution.py:283
  33.9 0.0 collective-permute-done.8.refs_0_
  33.9 1.8 %shard_map.104.refs_3_ = f32[512,2048]{1,0:T(8,128)S(1)} custom-call(bf16[3,512,256]{2,1,0:T(8,128)(2,1)S(1)} %collective-permute-done.8.refs_0_, bf16[8,1,256,2048]{3,2,1,0:T(8,128)(2,1)S(1)} %shard_map.102.refs_3_.refs_1_.refs_2_, f32[512,2048]{1,0:T(8,128)S(1)} %shard_map.103.refs_2_), custom_call_target="tpu_custom_call" | custom-call | flops 1048576 | bytes 8192 | tf_op jit(solution)/shard_map/pallas_call | solution.py:283
  35.7 0.3 collective-permute-done.7.refs_1_
  36.0 1.1 %collective-permute-done.6.refs_0_ = bf16[256,256]{1,0:T(8,128)(2,1)S(1)} collective-permute-done((bf16[256,256]{1,0:T(8,128)(2,1)S(1)}, bf16[256,256]{1,0:T(8,128)(2,1)S(1)}, u32[]{:S(2)}, u32[]{:S(2)}) %collective-permute-start.6) | collective-permute-done | bytes 131104 | tf_op jit(solution)/shard_map/ppermute | solution.py:191
  37.2 0.0 copy-start
  37.2 0.0 copy-start.1
  37.2 0.1 collective-permute-start.9
  37.3 0.7 %shard_map.105.refs_2_ = f32[512,2048]{1,0:T(8,128)S(1)} custom-call(bf16[256,256]{1,0:T(8,128)(2,1)S(1)} %collective-permute-done.6.refs_0_, bf16[256,256]{1,0:T(8,128)(2,1)S(1)} %collective-permute-done.7.refs_1_, bf16[8,1,256,2048]{3,2,1,0:T(8,128)(2,1)S(1)} %shard_map.102.refs_3_.refs_1_.refs_2_, f32[512,2048]{1,0:T(8,128)S(1)} %shard_map.104.refs_3_), custom_call_target="tpu_custom_call" | custom-call | flops 1048576 | bytes 8192 | tf_op jit(solution)/shard_map/pallas_call | solution.py:283
  38.0 0.8 %collective-permute-done.9.refs_0_ = bf16[512,256]{1,0:T(8,128)(2,1)S(1)} collective-permute-done((bf16[512,256]{1,0:T(8,128)(2,1)S(1)}, bf16[512,256]{1,0:T(8,128)(2,1)S(1)}, u32[]{:S(2)}, u32[]{:S(2)}) %collective-permute-start.9) | collective-permute-done | bytes 262176 | tf_op jit(solution)/shard_map/ppermute | solution.py:191
  38.8 2.2 %shard_map.106 = bf16[512,16,128]{2,1,0:T(8,128)(2,1)} custom-call(bf16[512,256]{1,0:T(8,128)(2,1)S(1)} %collective-permute-done.9.refs_0_, bf16[8,1,256,2048]{3,2,1,0:T(8,128)(2,1)S(1)} %shard_map.102.refs_3_.refs_1_.refs_2_, f32[512,2048]{1,0:T(8,128)S(1)} %shard_map.105.refs_2_, bf16[512,16,128]{2,1,0:T(8,128)(2,1)S(1)} %copy-done, f32[1,128]{1,0:T(1,128)S(1)} %bitcast.13), custom_call_target="tpu_custom_call" | custom-call | flops 1048576 | bytes 8192 | tf_op jit(solution)/shard_map/pallas_call | solution.py:283
  (5 shorter events, 0.0 us)
Async XLA Ops:
  2.6 17.7 %all-to-all-start = ((bf16[16,16,128]{2,1,0:T(8,128)(2,1)}), bf16[16,16,128]{2,1,0:T(8,128)(2,1)S(1)}, u32[]{:S(2)}, u32[]{:S(2)}) async-start(bf16[16,16,128]{2,1,0:T(8,128)(2,1)} %get-tuple-element.17), calls=%async_computation | async-start | bytes 131072 | tf_op jit(solution)/shard_map/all_to_all | solution.py:226
  11.0 9.3 %collective-permute-start.2 = (bf16[256,128]{1,0:T(8,128)(2,1)S(1)}, bf16[256,128]{1,0:T(8,128)(2,1)S(1)}, u32[]{:S(2)}, u32[]{:S(2)}) collective-permute-start(bf16[256,128]{1,0:T(8,128)(2,1)S(1)} %get-tuple-element.15.refs_0_), channel_id=1, source_target_pairs={{0,24},{1,25},{2,26},{3,27},{4,28},{5,29},{6,30},{7,31},{8,16},{9,... | collective-permute-start | bytes 196616 | tf_op jit(solution)/shard_map/ppermute | solution.py:191
  14.7 6.5 %collective-permute-start.1 = (bf16[256,128]{1,0:T(8,128)(2,1)S(1)}, bf16[256,128]{1,0:T(8,128)(2,1)S(1)}, u32[]{:S(2)}, u32[]{:S(2)}) collective-permute-start(bf16[256,128]{1,0:T(8,128)(2,1)S(1)} %get-tuple-element.15.refs_0_), channel_id=1, source_target_pairs={{0,16},{1,17},{2,18},{3,19},{4,20},{5,21},{6,22},{7,23},{8,24},{9,... | collective-permute-start | bytes 196616 | tf_op jit(solution)/shard_map/ppermute | solution.py:191
  14.7 6.5 %collective-permute-start = (bf16[256,128]{1,0:T(8,128)(2,1)S(1)}, bf16[256,128]{1,0:T(8,128)(2,1)S(1)}, u32[]{:S(2)}, u32[]{:S(2)}) collective-permute-start(bf16[256,128]{1,0:T(8,128)(2,1)S(1)} %get-tuple-element.15.refs_0_), channel_id=1, source_target_pairs={{0,8},{1,9},{2,10},{3,11},{4,12},{5,13},{6,14},{7,15},{8,0},{9,1},... | collective-permute-start | bytes 196616 | tf_op jit(solution)/shard_map/ppermute | solution.py:191
  20.3 4.2 %collective-permute-start.5 = (bf16[16,16,128]{2,1,0:T(8,128)(2,1)S(1)}, bf16[16,16,128]{2,1,0:T(8,128)(2,1)S(1)}, u32[]{:S(2)}, u32[]{:S(2)}) collective-permute-start(bf16[16,16,128]{2,1,0:T(8,128)(2,1)S(1)} %all-to-all-done.own_ref), channel_id=1, source_target_pairs={{0,1},{1,0},{2,3},{3,2},{4,5},{5,4},{6,7},{7,6},{8,9},{9,8},{10,11... | collective-permute-start | bytes 196616 | tf_op jit(solution)/shard_map/ppermute | solution.py:191
  21.5 7.9 %collective-permute-start.4 = (bf16[512,256]{1,0:T(8,128)(2,1)S(1)}, bf16[512,256]{1,0:T(8,128)(2,1)S(1)}, u32[]{:S(2)}, u32[]{:S(2)}) collective-permute-start(bf16[512,256]{1,0:T(8,128)(2,1)S(1)} %shard_map.101.refs_0_), channel_id=1, source_target_pairs={{0,4},{1,5},{2,6},{3,7},{4,0},{5,1},{6,2},{7,3},{8,12},{9,13},{10,... | collective-permute-start | bytes 786440 | tf_op jit(solution)/shard_map/ppermute | solution.py:191
  23.0 6.9 %collective-permute-start.3 = (bf16[512,256]{1,0:T(8,128)(2,1)S(1)}, bf16[512,256]{1,0:T(8,128)(2,1)S(1)}, u32[]{:S(2)}, u32[]{:S(2)}) collective-permute-start(bf16[512,256]{1,0:T(8,128)(2,1)S(1)} %shard_map.101.refs_0_), channel_id=1, source_target_pairs={{0,2},{1,3},{2,0},{3,1},{4,6},{5,7},{6,4},{7,5},{8,10},{9,11},{10,... | collective-permute-start | bytes 786440 | tf_op jit(solution)/shard_map/ppermute | solution.py:191
  29.9 4.0 %collective-permute-start.8 = (bf16[3,512,256]{2,1,0:T(8,128)(2,1)S(1)}, bf16[3,512,256]{2,1,0:T(8,128)(2,1)S(1)}, u32[]{:S(2)}, u32[]{:S(2)}) collective-permute-start(bf16[3,512,256]{2,1,0:T(8,128)(2,1)S(1)} %pad_maximum_fusion), channel_id=1, source_target_pairs={{0,1},{1,0},{2,3},{3,2},{4,5},{5,4},{6,7},{7,6},{8,9},{9,8},{10,11... | collective-permute-start | bytes 2359304 | tf_op jit(solution)/shard_map/ppermute | solution.py:191
  30.1 6.0 %collective-permute-start.7 = (bf16[256,256]{1,0:T(8,128)(2,1)S(1)}, bf16[256,256]{1,0:T(8,128)(2,1)S(1)}, u32[]{:S(2)}, u32[]{:S(2)}) collective-permute-start(bf16[256,256]{1,0:T(8,128)(2,1)S(1)} %slice.7), channel_id=1, source_target_pairs={{0,2},{1,3},{2,0},{3,1},{4,6},{5,7},{6,4},{7,5},{8,10},{9,11},{10,... | collective-permute-start | bytes 393224 | tf_op jit(solution)/shard_map/ppermute | solution.py:191
  31.5 5.6 %collective-permute-start.6 = (bf16[256,256]{1,0:T(8,128)(2,1)S(1)}, bf16[256,256]{1,0:T(8,128)(2,1)S(1)}, u32[]{:S(2)}, u32[]{:S(2)}) collective-permute-start(bf16[256,256]{1,0:T(8,128)(2,1)S(1)} %slice.6), channel_id=1, source_target_pairs={{0,4},{1,5},{2,6},{3,7},{4,0},{5,1},{6,2},{7,3},{8,12},{9,13},{10,... | collective-permute-start | bytes 393224 | tf_op jit(solution)/shard_map/ppermute | solution.py:191
  37.2 1.6 %copy-start = (bf16[512,16,128]{2,1,0:T(8,128)(2,1)S(1)}, bf16[512,16,128]{2,1,0:T(8,128)(2,1)}, u32[]{:S(2)}) copy-start(bf16[512,16,128]{2,1,0:T(8,128)(2,1)} %refs_3_.1) | copy-start | bytes 6291460
  37.2 1.6 %copy-start.1 = (f32[128]{0:T(128)S(1)}, f32[128]{0:T(128)}, u32[]{:S(2)}) copy-start(f32[128]{0:T(128)} %param.19) | copy-start | bytes 1540
  37.2 1.6 %collective-permute-start.9 = (bf16[512,256]{1,0:T(8,128)(2,1)S(1)}, bf16[512,256]{1,0:T(8,128)(2,1)S(1)}, u32[]{:S(2)}, u32[]{:S(2)}) collective-permute-start(bf16[512,256]{1,0:T(8,128)(2,1)S(1)} %pad_maximum_fusion.1), channel_id=1, source_target_pairs={{0,1},{1,0},{2,3},{3,2},{4,5},{5,4},{6,7},{7,6},{8,9},{9,8},{10,11... | collective-permute-start | bytes 786440 | tf_op jit(solution)/shard_map/ppermute | solution.py:191

commit v11 on v9

--- a/solution.py
+++ b/solution.py
@@ -35,41 +35,37 @@
     sources, final_source, outs, held = refs[:7], refs[7], refs[8:12], refs[12:19]
     left_ref, right_ref, final_ref, order_ref = outs
     sems = refs[19]
-    copies = [pltpu.make_async_copy(a, b, sems.at[i]) for i, (a, b) in enumerate(zip(sources, held))]
-    copies.append(pltpu.make_async_copy(final_source, final_ref, sems.at[7]))
+    pairs = [(sources[0].at[s], held[0].at[s]) for s in range(2)]
+    pairs += list(zip(sources[1:], held[1:])) + [(final_source, final_ref)]
+    copies = [pltpu.make_async_copy(a, b, sems.at[i]) for i, (a, b) in enumerate(pairs)]
     for copy in copies:
         copy.start()
     me = lax.axis_index("row")
     for h in range(2):
         order_ref[h] = _order(me, h)
-    for copy in copies:
+    for copy in copies[:1] + copies[2:8]:
         copy.wait()
     x_ref, gain_ref, bias_ref, w1_ref, b1_ref, w2_ref, b2_ref = held
-    band_half = left_ref.shape[0]
+    half = left_ref.shape[0]
     n = right_ref.shape[0]
     feats = x_ref.shape[2]
-    normed = []
+    split = []
     for s in range(2):
+        if s:
+            copies[1].wait()
         x = x_ref[s].astype(jnp.float32)
         center = jnp.mean(x, axis=-1, keepdims=True)
         off = x - center
         spread = jnp.mean(off * off, axis=-1, keepdims=True)
-        normed.append(off * lax.rsqrt(spread + 1e-05) * gain_ref[...] + bias_ref[...])
-    low = [v[:band_half].astype(jnp.bfloat16) for v in normed]
-    high = [v[band_half : 2 * band_half].astype(jnp.bfloat16) for v in normed]
-    shift1 = jnp.concatenate([b1_ref[...]] * 4, axis=1)
-    left = lax.dot_general(
-        jnp.concatenate(low + high, axis=1), _stacked(w1_ref[...], 4), NT, preferred_element_type=jnp.float32
-    )
-    left_ref[...] = (left + shift1).astype(jnp.bfloat16)
-
-    split = [v.reshape(n, 2, 8, feats) for v in normed]
+        normed = off * lax.rsqrt(spread + 1e-05) * gain_ref[...] + bias_ref[...]
+        split.append(normed.reshape(n, 2, 8, feats))
     parts = [split[s][:, jh].reshape(n * 8, feats).astype(jnp.bfloat16) for jh in range(2) for s in range(2)]
-    shift2 = jnp.concatenate([b2_ref[...]] * 4, axis=1)
-    right = lax.dot_general(
-        jnp.concatenate(parts, axis=1), _stacked(w2_ref[...], 4), NT, preferred_element_type=jnp.float32
-    )
-    right_ref[...] = (right + shift2).reshape(n, 8, LANES).astype(jnp.bfloat16)
+    weights = jnp.concatenate([_stacked(w1_ref[...], 4), _stacked(w2_ref[...], 4)], axis=0)
+    shifts = jnp.concatenate([b1_ref[...]] * 4 + [b2_ref[...]] * 4, axis=1)
+    both = lax.dot_general(jnp.concatenate(parts, axis=1), weights, NT, preferred_element_type=jnp.float32) + shifts
+    left_ref[...] = both[:half, :LANES].astype(jnp.bfloat16)
+    right_ref[...] = both[:, LANES:].reshape(n, 8, LANES).astype(jnp.bfloat16)
+    copies[8].wait()
 
 
 def _line_kernel(*refs):
@@ -77,7 +73,7 @@
     half = pieces[0].shape[0]
     wide = order_ref.shape[2]
     for q in range(len(pieces) // 4):
-        lhs = jnp.concatenate([piece[...] for piece in pieces[q * 4 : q * 4 + 4]], axis=1)
+        lhs = jnp.concatenate([pieces[q * 4 + k][...] for k in (0, 1, 3, 2)], axis=1)
         for h in range(2):
             moved = jnp.dot(lhs, order_ref[h], preferred_element_type=jnp.float32)
             out_ref[pl.ds(h * half, half), pl.ds(q * wide, wide)] = moved.astype(jnp.bfloat16)
@@ -118,7 +114,7 @@
         (block,) = take(1)
         lines = [[block.at[k]] for k in range(3)]
     else:
-        lines = [take(2 if mask == 6 else 1) for mask in masks]
+        lines = [take(2 if mask in (6, 7) else 1) for mask in masks]
     (t_ref,) = take(1)
     (sum_ref,) = (None,) if begins else take(1)
     pair_ref, shift_ref = (None, None) if count is None else take(2)
@@ -129,55 +125,68 @@
 
     tile = 256
     band = sum(part.shape[0] for part in lines[0])
-    if count is not None:
-        acc_ref, done_ref, sems = take(3)
-        cols = pair_ref.shape[1]
-        pitch = cols + 1
-
-    def column(step):
+
+    def column(step, rows):
         at = pl.ds(step * tile, tile)
-        lhs = jnp.concatenate([jnp.concatenate([part[...] for part in line], axis=0) for line in lines], axis=1)
         if held:
             rhs = jnp.concatenate([t_ref[g, q, :, at] for g, q in chunks], axis=0)
         else:
             for i, (g, q) in enumerate(chunks):
                 pltpu.sync_copy(t_ref.at[g, q, :, at], refs[0].at[pl.ds(i * wide, wide)])
             rhs = refs[0][...]
-        res = jnp.dot(lhs, rhs, preferred_element_type=jnp.float32)
+        lhs = []
+        for line in lines:
+            ends = [sum(part.shape[0] for part in line[: k + 1]) for k in range(len(line))]
+            pieces = []
+            for first, size in rows:
+                k = next(k for k, end in enumerate(ends) if first < end)
+                begin = first - (ends[k] - line[k].shape[0])
+                pieces.append(line[k][pl.ds(begin, size), :])
+            lhs.append(jnp.concatenate(pieces, axis=0))
+        res = jnp.dot(jnp.concatenate(lhs, axis=1), rhs, preferred_element_type=jnp.float32)
         if sum_ref is not None:
-            res = res + sum_ref[:, at]
-        if count is None:
-            out_ref[:, at] = res
-        else:
+            res = res + jnp.concatenate([sum_ref[pl.ds(first, size), at] for first, size in rows], axis=0)
+        return res
+
+    halves = [(0, band // 2), (band // 2, band // 2)]
+    steps = t_ref.shape[3] // tile
+    if count is None:
+        for step in range(steps):
+            out_ref[:, pl.ds(step * tile, tile)] = column(step, halves)
+        return
+
+    acc_ref, done_ref, sems = take(3)
+    cols = pair_ref.shape[1]
+    pitch = cols + 1
+    shift = shift_ref[...]
+    chunk = band // 2 // steps
+
+    def finish(r):
+        for k in range(chunk):
+            i = r * chunk + k
+            row = (i // 8) % 2 * (band // 2) + i // 16 * 8 + i % 8
+            total = acc_ref[pl.ds(row * pitch, cols), :] * (1.0 / count) + shift
+            done_ref[i] = (pair_ref[i].astype(jnp.float32) + total).astype(jnp.bfloat16)
+        at = pl.ds(r * chunk, chunk)
+        pltpu.make_async_copy(done_ref.at[at], out_ref.at[at], sems.at[r]).start()
+
+    for part in range(2):
+        rows = [(first + part * size // 2, size // 2) for first, size in halves]
+        for step in range(steps):
+            res = column(step, rows)
             for k in range(tile // LANES):
                 j = step * (tile // LANES) + k
-                acc_ref[pl.ds(j, band, stride=pitch), :] = res[:, k * LANES : (k + 1) * LANES]
-
-    for step in range(t_ref.shape[3] // tile):
-        column(step)
-    if count is None:
-        return
-
-    rows = 32
-    shift = shift_ref[...]
-
-    def finish(r, _):
-        for k in range(rows):
-            i = r * rows + k
-            total = acc_ref[pl.ds(i * pitch, cols), :] * (1.0 / count) + shift
-            done_ref[i] = (pair_ref[i].astype(jnp.float32) + total).astype(jnp.bfloat16)
-        at = pl.ds(pl.multiple_of(r * rows, rows), rows)
-        pltpu.make_async_copy(done_ref.at[at], out_ref.at[at], sems.at[r]).start()
-        return 0
-
-    lax.fori_loop(0, band // rows, finish, 0)
-
-    def drain(r, _):
-        at = pl.ds(pl.multiple_of(r * rows, rows), rows)
+                for piece, (first, size) in enumerate(rows):
+                    acc_ref[pl.ds(first * pitch + j, size, stride=pitch), :] = res[
+                        piece * size : (piece + 1) * size, k * LANES : (k + 1) * LANES
+                    ]
+            if part:
+                finish(step)
+    for step in range(steps):
+        finish(steps + step)
+    for r in range(2 * steps):
+        at = pl.ds(r * chunk, chunk)
         pltpu.make_async_copy(done_ref.at[at], out_ref.at[at], sems.at[r]).wait()
-        return 0
-
-    lax.fori_loop(0, band // rows, drain, 0)
 
 
 def _xor(x, mask, n):
@@ -208,7 +217,7 @@
             jax.ShapeDtypeStruct(final.shape, final.dtype),
             jax.ShapeDtypeStruct((2, 4 * LANES, 8 * CHANS), jnp.bfloat16),
         ),
-        scratch_shapes=[pltpu.VMEM(a.shape, a.dtype) for a in sources] + [pltpu.SemaphoreType.DMA((8,))],
+        scratch_shapes=[pltpu.VMEM(a.shape, a.dtype) for a in sources] + [pltpu.SemaphoreType.DMA((9,))],
         compiler_params=params,
         cost_estimate=pl.CostEstimate(
             flops=4 * seqs * residues * feats * CHANS, bytes_accessed=2 * seqs * residues * feats, transcendentals=0
@@ -220,6 +229,7 @@
     part = 32
     parts = n // part
     pieces = [left] + [_xor(left, m, n) for m in range(8, n, 8)]
+    pieces = [pieces[k ^ (k // 2 % 2)] for k in range(len(pieces))]
     line = pl.pallas_call(
         _line_kernel,
         in_specs=[vmem] * (len(pieces) + 1),
@@ -263,7 +273,7 @@
             scratch += [
                 pltpu.VMEM((band * (cols + 1), zdim), jnp.float32),
                 pltpu.VMEM(pair.shape, jnp.bfloat16),
-                pltpu.SemaphoreType.DMA((band // 32,)),
+                pltpu.SemaphoreType.DMA((cols * zdim // 128,)),
             ]
         if not small:
             scratch.append(pltpu.VMEM((depth, 256), jnp.bfloat16))
@@ -289,10 +299,12 @@
     across = _xor(jnp.stack([line, x, y]), 1, n)
     total = add([line, x, y], (0, 2, 4), None, False)
     total = add([across], (1, 3, 5), total, False)
-    upper, lower, total = lax.optimization_barrier((upper, lower, total))
-    last = _xor(jnp.concatenate([upper, lower], axis=0), 1, n)
+    upper, total = lax.optimization_barrier((upper, total))
+    last = [_xor(upper, 1, n)]
+    lower, total = lax.optimization_barrier((lower, total))
+    last.append(_xor(lower, 1, n))
     total = add([upper, lower], (6,), total, False)
-    return add([last], (7,), total, True)
+    return add(last, (7,), total, True)
 
 
 def solution(mesh):

time: 36.2 us -> 34.6 us (0.956)
  waiting for transfers between devices: 6.24 us -> 4.98 us
  starting transfers between devices: 17.3 us -> 16.9 us
    ppermute x9 -> x10, waiting for transfers between devices: 2.36 us -> 1.1 us  [_xor(): return lax.ppermute(x, 'row', [(i, i ^ mask) for i in range(n)])]
    all_to_all x1, starting transfers between devices: 5.99 us -> 5.17 us  [shards(): lax.all_to_all(right, 'row', split_axis=0, concat_axis=0, tiled=True)]
    ppermute x9 -> x10, starting transfers between devices: 11.3 us -> 11.7 us  [_xor(): return lax.ppermute(x, 'row', [(i, i ^ mask) for i in range(n)])]
  transfers between devices with their start and end apart: 10 -> 11, of which waited for: 5 -> 6; matrix products, arithmetic and copies ran while one was open for 0% -> 0% of each run, Pallas kernels for 21% -> 21%
where the time goes in v11:
time: 34.6 us; the launch traced here: 34.4 us
  starting transfers between devices  16.9 us (49%)
  Pallas kernels  12.3 us (36%)
  waiting for transfers between devices  4.98 us (14%)
    ppermute x10, starting transfers between devices, _xor(): return lax.ppermute(x, 'row', [(i, i ^ mask) for i in range(n)])  11.7 us
    pallas_call x4, Pallas kernels, add(): pl.pallas_call(functools.partial(_band_kernel, masks, total is None, coun...  6.79 us
    all_to_all x1, starting transfers between devices, shards(): lax.all_to_all(right, 'row', split_axis=0, concat_axis=0, tiled=True)  5.17 us
    all_to_all x1, waiting for transfers between devices, shards(): lax.all_to_all(right, 'row', split_axis=0, concat_axis=0, tiled=True)  3.88 us
    pallas_call x1, Pallas kernels, shards(): pl.pallas_call(_fold_kernel, out_shape=fold_out, scratch_shapes=[pltpu.VM...  2.76 us
    pallas_call x1, Pallas kernels, shards(): pl.pallas_call(_project_kernel, in_specs=[anywhere] * 8, out_specs=(vmem,...  2.43 us
    ppermute x10, waiting for transfers between devices, _xor(): return lax.ppermute(x, 'row', [(i, i ^ mask) for i in range(n)])  1.1 us
  transfers between devices with their start and end apart: 11, of which 6 were waited for; matrix products, arithmetic and copies ran while one was open for 0% of the time, Pallas kernels for 21%

profile of v11, /device:TPU:0, one launch (start us, length us, event | category | flops | bytes accessed | tf_op | source)
XLA Modules:
  0.0 34.4 jit_solution(12195715946203517542)
XLA Ops:
  0.0 2.4 %shard_map.100 = (bf16[256,128]{1,0:T(8,128)(2,1)S(1)}, bf16[32,8,128]{2,1,0:T(8,128)(2,1)}, bf16[1024,128]{1,0:T(8,128)(2,1)S(1)}, bf16[2,512,256]{2,1,0:T(8,128)(2,1)S(1)}) custom-call(bf16[2,512,256]{2,1,0:T(8,128)(2,1)} %refs_0_.1, f32[1,256]{1,0:T(1,128)} %bitcast.16, f32[1,256]{1,0:T(1,128)} %bitcast.17, bf16[32,256]{1,0:T(8,128)(2,1)} %bitcast.14, ...), custom_call_target="tpu_custom_call" | custom-call | flops 33554432 | bytes 524288 | tf_op jit(solution)/shard_map/pallas_call | solution.py:210
  2.4 4.1 %collective-permute-start.2 = (bf16[256,128]{1,0:T(8,128)(2,1)S(1)}, bf16[256,128]{1,0:T(8,128)(2,1)S(1)}, u32[]{:S(2)}, u32[]{:S(2)}) collective-permute-start(bf16[256,128]{1,0:T(8,128)(2,1)S(1)} %get-tuple-element.16.refs_0_), channel_id=1, source_target_pairs={{0,16},{1,17},{2,18},{3,19},{4,20},{5,21},{6,22},{7,23},{8,24},{9,... | collective-permute-start | bytes 196616 | tf_op jit(solution)/shard_map/ppermute | solution.py:193
  6.5 1.3 %collective-permute-start.1 = (bf16[256,128]{1,0:T(8,128)(2,1)S(1)}, bf16[256,128]{1,0:T(8,128)(2,1)S(1)}, u32[]{:S(2)}, u32[]{:S(2)}) collective-permute-start(bf16[256,128]{1,0:T(8,128)(2,1)S(1)} %get-tuple-element.16.refs_0_), channel_id=1, source_target_pairs={{0,24},{1,25},{2,26},{3,27},{4,28},{5,29},{6,30},{7,31},{8,16},{9,... | collective-permute-start | bytes 196616 | tf_op jit(solution)/shard_map/ppermute | solution.py:193
  7.9 0.2 collective-permute-start
  8.1 5.2 %all-to-all-start = ((bf16[32,8,128]{2,1,0:T(8,128)(2,1)}), bf16[32,8,128]{2,1,0:T(8,128)(2,1)S(1)}, u32[]{:S(2)}, u32[]{:S(2)}) async-start(bf16[32,8,128]{2,1,0:T(8,128)(2,1)} %get-tuple-element.18), calls=%async_computation | async-start | bytes 131072 | tf_op jit(solution)/shard_map/all_to_all | solution.py:227
  13.3 0.0 collective-permute-done.2.refs_3_
  13.3 0.0 collective-permute-done.1.refs_2_
  13.3 0.0 collective-permute-done.refs_1_
  13.3 0.3 shard_map.101.refs_0_
  13.6 1.8 %collective-permute-start.4 = (bf16[512,256]{1,0:T(8,128)(2,1)S(1)}, bf16[512,256]{1,0:T(8,128)(2,1)S(1)}, u32[]{:S(2)}, u32[]{:S(2)}) collective-permute-start(bf16[512,256]{1,0:T(8,128)(2,1)S(1)} %shard_map.101.refs_0_), channel_id=1, source_target_pairs={{0,4},{1,5},{2,6},{3,7},{4,0},{5,1},{6,2},{7,3},{8,12},{9,13},{10,... | collective-permute-start | bytes 786440 | tf_op jit(solution)/shard_map/ppermute | solution.py:193
  15.5 1.5 %collective-permute-start.3 = (bf16[512,256]{1,0:T(8,128)(2,1)S(1)}, bf16[512,256]{1,0:T(8,128)(2,1)S(1)}, u32[]{:S(2)}, u32[]{:S(2)}) collective-permute-start(bf16[512,256]{1,0:T(8,128)(2,1)S(1)} %shard_map.101.refs_0_), channel_id=1, source_target_pairs={{0,2},{1,3},{2,0},{3,1},{4,6},{5,7},{6,4},{7,5},{8,10},{9,11},{10,... | collective-permute-start | bytes 786440 | tf_op jit(solution)/shard_map/ppermute | solution.py:193
  16.9 3.9 %all-to-all-done.right_ref = bf16[32,8,128]{2,1,0:T(8,128)(2,1)S(1)} async-done(((bf16[32,8,128]{2,1,0:T(8,128)(2,1)}), bf16[32,8,128]{2,1,0:T(8,128)(2,1)S(1)}, u32[]{:S(2)}, u32[]{:S(2)}) %all-to-all-start) | async-done | bytes 65568 | tf_op jit(solution)/shard_map/all_to_all | solution.py:227
  20.8 2.8 %shard_map.102.refs_3_.refs_1_.refs_2_ = bf16[8,1,256,2048]{3,2,1,0:T(8,128)(2,1)S(1)} custom-call(bf16[32,8,128]{2,1,0:T(8,128)(2,1)S(1)} %all-to-all-done.right_ref, bf16[1024,128]{1,0:T(8,128)(2,1)S(1)} %get-tuple-element.19.final_ref), custom_call_target="tpu_custom_call" | custom-call | flops 2147483648 | bytes 8388608 | tf_op jit(solution)/shard_map/pallas_call | solution.py:258
  23.6 0.0 collective-permute-done.4.refs_2_
  23.6 0.3 collective-permute-done.3.refs_1_
  23.9 0.1 pad_maximum_fusion
  24.0 0.1 collective-permute-start.6
  24.1 0.6 %collective-permute-start.5 = (bf16[256,256]{1,0:T(8,128)(2,1)S(1)}, bf16[256,256]{1,0:T(8,128)(2,1)S(1)}, u32[]{:S(2)}, u32[]{:S(2)}) collective-permute-start(bf16[256,256]{1,0:T(8,128)(2,1)S(1)} %slice.6), channel_id=1, source_target_pairs={{0,4},{1,5},{2,6},{3,7},{4,0},{5,1},{6,2},{7,3},{8,12},{9,13},{10,... | collective-permute-start | bytes 393224 | tf_op jit(solution)/shard_map/ppermute | solution.py:193
  24.7 1.6 %collective-permute-start.8 = (bf16[256,256]{1,0:T(8,128)(2,1)S(1)}, bf16[256,256]{1,0:T(8,128)(2,1)S(1)}, u32[]{:S(2)}, u32[]{:S(2)}) collective-permute-start(bf16[256,256]{1,0:T(8,128)(2,1)S(1)} %slice.7), channel_id=1, source_target_pairs={{0,2},{1,3},{2,0},{3,1},{4,6},{5,7},{6,4},{7,5},{8,10},{9,11},{10,... | collective-permute-start | bytes 393224 | tf_op jit(solution)/shard_map/ppermute | solution.py:193
  26.3 1.8 %shard_map.103.refs_2_ = f32[512,2048]{1,0:T(8,128)S(1)} custom-call(bf16[512,256]{1,0:T(8,128)(2,1)S(1)} %shard_map.101.refs_0_, bf16[512,256]{1,0:T(8,128)(2,1)S(1)} %collective-permute-done.3.refs_1_, bf16[512,256]{1,0:T(8,128)(2,1)S(1)} %collective-permute-done.4.refs_2_, bf16[8,1,256,2048]{3,2,1,0:T(8,128)(2,1)S(1)} %shard_map.102.refs_3_.refs_1_.refs_2_), custom_call_target="tpu_custom_call" | custom-call | flops 1048576 | bytes 8192 | tf_op jit(solution)/shard_map/pallas_call | solution.py:283
  28.1 0.0 collective-permute-done.6.refs_0_
  28.1 1.8 %shard_map.104.refs_3_ = f32[512,2048]{1,0:T(8,128)S(1)} custom-call(bf16[3,512,256]{2,1,0:T(8,128)(2,1)S(1)} %collective-permute-done.6.refs_0_, bf16[8,1,256,2048]{3,2,1,0:T(8,128)(2,1)S(1)} %shard_map.102.refs_3_.refs_1_.refs_2_, f32[512,2048]{1,0:T(8,128)S(1)} %shard_map.103.refs_2_), custom_call_target="tpu_custom_call" | custom-call | flops 1048576 | bytes 8192 | tf_op jit(solution)/shard_map/pallas_call | solution.py:283
  29.9 0.0 copy-start
  29.9 0.0 copy-start.1
  29.9 0.1 collective-permute-done.5.refs_0_
  30.0 0.3 collective-permute-done.8.refs_1_
  30.4 0.0 collective-permute-start.9
  30.4 0.5 %collective-permute-start.7 = (bf16[256,256]{1,0:T(8,128)(2,1)S(1)}, bf16[256,256]{1,0:T(8,128)(2,1)S(1)}, u32[]{:S(2)}, u32[]{:S(2)}) collective-permute-start(bf16[256,256]{1,0:T(8,128)(2,1)S(1)} %collective-permute-done.5.refs_0_), channel_id=1, source_target_pairs={{0,1},{1,0},{2,3},{3,2},{4,5},{5,4},{6,7},{7,6},{8,9},{9,8},{10,11... | collective-permute-start | bytes 393224 | tf_op jit(solution)/shard_map/ppermute | solution.py:193
  30.9 0.7 %shard_map.105.refs_3_ = f32[512,2048]{1,0:T(8,128)S(1)} custom-call(bf16[256,256]{1,0:T(8,128)(2,1)S(1)} %collective-permute-done.5.refs_0_, bf16[256,256]{1,0:T(8,128)(2,1)S(1)} %collective-permute-done.8.refs_1_, bf16[8,1,256,2048]{3,2,1,0:T(8,128)(2,1)S(1)} %shard_map.102.refs_3_.refs_1_.refs_2_, f32[512,2048]{1,0:T(8,128)S(1)} %shard_map.104.refs_3_), custom_call_target="tpu_custom_call" | custom-call | flops 1048576 | bytes 8192 | tf_op jit(solution)/shard_map/pallas_call | solution.py:283
  31.6 0.1 collective-permute-done.9.refs_1_
  31.7 0.2 collective-permute-done.7.refs_0_
  31.9 2.5 %shard_map.106 = bf16[512,16,128]{2,1,0:T(8,128)(2,1)} custom-call(bf16[256,256]{1,0:T(8,128)(2,1)S(1)} %collective-permute-done.7.refs_0_, bf16[256,256]{1,0:T(8,128)(2,1)S(1)} %collective-permute-done.9.refs_1_, bf16[8,1,256,2048]{3,2,1,0:T(8,128)(2,1)S(1)} %shard_map.102.refs_3_.refs_1_.refs_2_, f32[512,2048]{1,0:T(8,128)S(1)} %shard_map.105.refs_3_, ...), custom_call_target="tpu_custom_call" | custom-call | flops 1048576 | bytes 8192 | tf_op jit(solution)/shard_map/pallas_call | solution.py:283
  (4 shorter events, 0.0 us)
Async XLA Ops:
  2.4 10.9 %collective-permute-start.2 = (bf16[256,128]{1,0:T(8,128)(2,1)S(1)}, bf16[256,128]{1,0:T(8,128)(2,1)S(1)}, u32[]{:S(2)}, u32[]{:S(2)}) collective-permute-start(bf16[256,128]{1,0:T(8,128)(2,1)S(1)} %get-tuple-element.16.refs_0_), channel_id=1, source_target_pairs={{0,16},{1,17},{2,18},{3,19},{4,20},{5,21},{6,22},{7,23},{8,24},{9,... | collective-permute-start | bytes 196616 | tf_op jit(solution)/shard_map/ppermute | solution.py:193
  6.5 6.8 %collective-permute-start.1 = (bf16[256,128]{1,0:T(8,128)(2,1)S(1)}, bf16[256,128]{1,0:T(8,128)(2,1)S(1)}, u32[]{:S(2)}, u32[]{:S(2)}) collective-permute-start(bf16[256,128]{1,0:T(8,128)(2,1)S(1)} %get-tuple-element.16.refs_0_), channel_id=1, source_target_pairs={{0,24},{1,25},{2,26},{3,27},{4,28},{5,29},{6,30},{7,31},{8,16},{9,... | collective-permute-start | bytes 196616 | tf_op jit(solution)/shard_map/ppermute | solution.py:193
  7.9 5.4 %collective-permute-start = (bf16[256,128]{1,0:T(8,128)(2,1)S(1)}, bf16[256,128]{1,0:T(8,128)(2,1)S(1)}, u32[]{:S(2)}, u32[]{:S(2)}) collective-permute-start(bf16[256,128]{1,0:T(8,128)(2,1)S(1)} %get-tuple-element.16.refs_0_), channel_id=1, source_target_pairs={{0,8},{1,9},{2,10},{3,11},{4,12},{5,13},{6,14},{7,15},{8,0},{9,1},... | collective-permute-start | bytes 196616 | tf_op jit(solution)/shard_map/ppermute | solution.py:193
  8.1 12.7 %all-to-all-start = ((bf16[32,8,128]{2,1,0:T(8,128)(2,1)}), bf16[32,8,128]{2,1,0:T(8,128)(2,1)S(1)}, u32[]{:S(2)}, u32[]{:S(2)}) async-start(bf16[32,8,128]{2,1,0:T(8,128)(2,1)} %get-tuple-element.18), calls=%async_computation | async-start | bytes 131072 | tf_op jit(solution)/shard_map/all_to_all | solution.py:227
  13.6 9.9 %collective-permute-start.4 = (bf16[512,256]{1,0:T(8,128)(2,1)S(1)}, bf16[512,256]{1,0:T(8,128)(2,1)S(1)}, u32[]{:S(2)}, u32[]{:S(2)}) collective-permute-start(bf16[512,256]{1,0:T(8,128)(2,1)S(1)} %shard_map.101.refs_0_), channel_id=1, source_target_pairs={{0,4},{1,5},{2,6},{3,7},{4,0},{5,1},{6,2},{7,3},{8,12},{9,13},{10,... | collective-permute-start | bytes 786440 | tf_op jit(solution)/shard_map/ppermute | solution.py:193
  15.5 8.4 %collective-permute-start.3 = (bf16[512,256]{1,0:T(8,128)(2,1)S(1)}, bf16[512,256]{1,0:T(8,128)(2,1)S(1)}, u32[]{:S(2)}, u32[]{:S(2)}) collective-permute-start(bf16[512,256]{1,0:T(8,128)(2,1)S(1)} %shard_map.101.refs_0_), channel_id=1, source_target_pairs={{0,2},{1,3},{2,0},{3,1},{4,6},{5,7},{6,4},{7,5},{8,10},{9,11},{10,... | collective-permute-start | bytes 786440 | tf_op jit(solution)/shard_map/ppermute | solution.py:193
  24.0 4.1 %collective-permute-start.6 = (bf16[3,512,256]{2,1,0:T(8,128)(2,1)S(1)}, bf16[3,512,256]{2,1,0:T(8,128)(2,1)S(1)}, u32[]{:S(2)}, u32[]{:S(2)}) collective-permute-start(bf16[3,512,256]{2,1,0:T(8,128)(2,1)S(1)} %pad_maximum_fusion), channel_id=1, source_target_pairs={{0,1},{1,0},{2,3},{3,2},{4,5},{5,4},{6,7},{7,6},{8,9},{9,8},{10,11... | collective-permute-start | bytes 2359304 | tf_op jit(solution)/shard_map/ppermute | solution.py:193
  24.1 6.0 %collective-permute-start.5 = (bf16[256,256]{1,0:T(8,128)(2,1)S(1)}, bf16[256,256]{1,0:T(8,128)(2,1)S(1)}, u32[]{:S(2)}, u32[]{:S(2)}) collective-permute-start(bf16[256,256]{1,0:T(8,128)(2,1)S(1)} %slice.6), channel_id=1, source_target_pairs={{0,4},{1,5},{2,6},{3,7},{4,0},{5,1},{6,2},{7,3},{8,12},{9,13},{10,... | collective-permute-start | bytes 393224 | tf_op jit(solution)/shard_map/ppermute | solution.py:193
  24.7 5.7 %collective-permute-start.8 = (bf16[256,256]{1,0:T(8,128)(2,1)S(1)}, bf16[256,256]{1,0:T(8,128)(2,1)S(1)}, u32[]{:S(2)}, u32[]{:S(2)}) collective-permute-start(bf16[256,256]{1,0:T(8,128)(2,1)S(1)} %slice.7), channel_id=1, source_target_pairs={{0,2},{1,3},{2,0},{3,1},{4,6},{5,7},{6,4},{7,5},{8,10},{9,11},{10,... | collective-permute-start | bytes 393224 | tf_op jit(solution)/shard_map/ppermute | solution.py:193
  29.9 2.0 %copy-start = (bf16[512,16,128]{2,1,0:T(8,128)(2,1)S(1)}, bf16[512,16,128]{2,1,0:T(8,128)(2,1)}, u32[]{:S(2)}) copy-start(bf16[512,16,128]{2,1,0:T(8,128)(2,1)} %refs_4_.1) | copy-start | bytes 6291460
  29.9 2.0 %copy-start.1 = (f32[128]{0:T(128)S(1)}, f32[128]{0:T(128)}, u32[]{:S(2)}) copy-start(f32[128]{0:T(128)} %param.19) | copy-start | bytes 1540
  30.4 1.3 %collective-permute-start.9 = (bf16[256,256]{1,0:T(8,128)(2,1)S(1)}, bf16[256,256]{1,0:T(8,128)(2,1)S(1)}, u32[]{:S(2)}, u32[]{:S(2)}) collective-permute-start(bf16[256,256]{1,0:T(8,128)(2,1)S(1)} %collective-permute-done.8.refs_1_), channel_id=1, source_target_pairs={{0,1},{1,0},{2,3},{3,2},{4,5},{5,4},{6,7},{7,6},{8,9},{9,8},{10,11... | collective-permute-start | bytes 393224 | tf_op jit(solution)/shard_map/ppermute | solution.py:193
  30.4 1.5 %collective-permute-start.7 = (bf16[256,256]{1,0:T(8,128)(2,1)S(1)}, bf16[256,256]{1,0:T(8,128)(2,1)S(1)}, u32[]{:S(2)}, u32[]{:S(2)}) collective-permute-start(bf16[256,256]{1,0:T(8,128)(2,1)S(1)} %collective-permute-done.5.refs_0_), channel_id=1, source_target_pairs={{0,1},{1,0},{2,3},{3,2},{4,5},{5,4},{6,7},{7,6},{8,9},{9,8},{10,11... | collective-permute-start | bytes 393224 | tf_op jit(solution)/shard_map/ppermute | solution.py:193

commit v12 on v11

--- a/solution.py
+++ b/solution.py
@@ -110,11 +110,13 @@
 def _band_kernel(masks, begins, count, held, *refs):
     refs = list(refs)
     take = lambda k: [refs.pop(0) for _ in range(k)]
-    if masks == (1, 3, 5):
-        (block,) = take(1)
-        lines = [[block.at[k]] for k in range(3)]
-    else:
-        lines = [take(2 if mask in (6, 7) else 1) for mask in masks]
+    lines = []
+    for mask in masks:
+        if mask in (1, 3, 5):
+            block = take(1)[0] if mask == 1 else block
+            lines.append([block.at[mask // 2]])
+        else:
+            lines.append(take(2 if mask > 5 else 1))
     (t_ref,) = take(1)
     (sum_ref,) = (None,) if begins else take(1)
     pair_ref, shift_ref = (None, None) if count is None else take(2)
@@ -126,7 +128,7 @@
     tile = 256
     band = sum(part.shape[0] for part in lines[0])
 
-    def column(step, rows):
+    def column(step):
         at = pl.ds(step * tile, tile)
         if held:
             rhs = jnp.concatenate([t_ref[g, q, :, at] for g, q in chunks], axis=0)
@@ -134,25 +136,14 @@
             for i, (g, q) in enumerate(chunks):
                 pltpu.sync_copy(t_ref.at[g, q, :, at], refs[0].at[pl.ds(i * wide, wide)])
             rhs = refs[0][...]
-        lhs = []
-        for line in lines:
-            ends = [sum(part.shape[0] for part in line[: k + 1]) for k in range(len(line))]
-            pieces = []
-            for first, size in rows:
-                k = next(k for k, end in enumerate(ends) if first < end)
-                begin = first - (ends[k] - line[k].shape[0])
-                pieces.append(line[k][pl.ds(begin, size), :])
-            lhs.append(jnp.concatenate(pieces, axis=0))
-        res = jnp.dot(jnp.concatenate(lhs, axis=1), rhs, preferred_element_type=jnp.float32)
-        if sum_ref is not None:
-            res = res + jnp.concatenate([sum_ref[pl.ds(first, size), at] for first, size in rows], axis=0)
-        return res
-
-    halves = [(0, band // 2), (band // 2, band // 2)]
+        lhs = jnp.concatenate([jnp.concatenate([part[...] for part in line], axis=0) for line in lines], axis=1)
+        res = jnp.dot(lhs, rhs, preferred_element_type=jnp.float32)
+        return res if sum_ref is None else res + sum_ref[:, at]
+
     steps = t_ref.shape[3] // tile
     if count is None:
         for step in range(steps):
-            out_ref[:, pl.ds(step * tile, tile)] = column(step, halves)
+            out_ref[:, pl.ds(step * tile, tile)] = column(step)
         return
 
     acc_ref, done_ref, sems = take(3)
@@ -170,20 +161,13 @@
         at = pl.ds(r * chunk, chunk)
         pltpu.make_async_copy(done_ref.at[at], out_ref.at[at], sems.at[r]).start()
 
-    for part in range(2):
-        rows = [(first + part * size // 2, size // 2) for first, size in halves]
-        for step in range(steps):
-            res = column(step, rows)
-            for k in range(tile // LANES):
-                j = step * (tile // LANES) + k
-                for piece, (first, size) in enumerate(rows):
-                    acc_ref[pl.ds(first * pitch + j, size, stride=pitch), :] = res[
-                        piece * size : (piece + 1) * size, k * LANES : (k + 1) * LANES
-                    ]
-            if part:
-                finish(step)
     for step in range(steps):
-        finish(steps + step)
+        res = column(step)
+        for k in range(tile // LANES):
+            j = step * (tile // LANES) + k
+            acc_ref[pl.ds(j, band, stride=pitch), :] = res[:, k * LANES : (k + 1) * LANES]
+    for r in range(2 * steps):
+        finish(r)
     for r in range(2 * steps):
         at = pl.ds(r * chunk, chunk)
         pltpu.make_async_copy(done_ref.at[at], out_ref.at[at], sems.at[r]).wait()
@@ -224,11 +208,10 @@
         ),
     )(*sources, pltpu.with_memory_space_constraint(final, pltpu.HBM))
 
-    right = lax.all_to_all(right, "row", split_axis=0, concat_axis=0, tiled=True)
-
     part = 32
     parts = n // part
     pieces = [left] + [_xor(left, m, n) for m in range(8, n, 8)]
+    pieces, right = lax.optimization_barrier((pieces, right))
     pieces = [pieces[k ^ (k // 2 % 2)] for k in range(len(pieces))]
     line = pl.pallas_call(
         _line_kernel,
@@ -239,6 +222,7 @@
         cost_estimate=pl.CostEstimate(flops=2**27, bytes_accessed=2**20, transcendentals=0),
     )(*pieces, order)
     x, y = _xor(line, 2, n), _xor(line, 4, n)
+    right = lax.all_to_all(right, "row", split_axis=0, concat_axis=0, tiled=True)
 
     fold_cost = pl.CostEstimate(
         flops=2 * n * 32 * 256 * CHANS * zdim, bytes_accessed=4 * n * CHANS * cols * zdim, transcendentals=0
@@ -294,17 +278,11 @@
             ),
         )(*operands)
 
-    x, y, folded = lax.optimization_barrier((x, y, folded))
     upper, lower = _xor(x[:half], 4, n), _xor(y[half:], 2, n)
     across = _xor(jnp.stack([line, x, y]), 1, n)
-    total = add([line, x, y], (0, 2, 4), None, False)
-    total = add([across], (1, 3, 5), total, False)
-    upper, total = lax.optimization_barrier((upper, total))
-    last = [_xor(upper, 1, n)]
-    lower, total = lax.optimization_barrier((lower, total))
-    last.append(_xor(lower, 1, n))
-    total = add([upper, lower], (6,), total, False)
-    return add(last, (7,), total, True)
+    total = add([line, x, y, across], (0, 2, 4, 1, 3, 5), None, False)
+    last = [_xor(upper, 1, n), _xor(lower, 1, n)]
+    return add([upper, lower, *last], (6, 7), total, True)
 
 
 def solution(mesh):

time: 34.6 us -> 44.8 us (1.29)
  waiting for transfers between devices: 4.98 us -> 18.7 us
  starting transfers between devices: 16.9 us -> 13.8 us
    ppermute x10, waiting for transfers between devices: 1.1 us -> 13.6 us  [_xor(): return lax.ppermute(x, 'row', [(i, i ^ mask) for i in range(n)])]
    all_to_all x1, starting transfers between devices: 5.17 us -> 2.76 us  [shards(): lax.all_to_all(right, 'row', split_axis=0, concat_axis=0, tiled=True)]
    all_to_all x1, waiting for transfers between devices: 3.88 us -> 5.07 us  [shards(): lax.all_to_all(right, 'row', split_axis=0, concat_axis=0, tiled=True)]
    ppermute x10, starting transfers between devices: 11.7 us -> 11 us  [_xor(): return lax.ppermute(x, 'row', [(i, i ^ mask) for i in range(n)])]
    pallas_call x4 -> x2, Pallas kernels: 6.79 us -> 6.45 us  [add(): pl.pallas_call(functools.partial(_band_kernel, masks, total is None, coun...]
  transfers between devices with their start and end apart: 11 -> 11, of which waited for: 6 -> 7; matrix products, arithmetic and copies ran while one was open for 0% -> 0% of each run, Pallas kernels for 21% -> 14%
where the time goes in v12:
time: 44.8 us; the launch traced here: 44.6 us
  waiting for transfers between devices  18.7 us (42%)
  starting transfers between devices  13.8 us (31%)
  Pallas kernels  11.9 us (27%)
    ppermute x10, waiting for transfers between devices, _xor(): return lax.ppermute(x, 'row', [(i, i ^ mask) for i in range(n)])  13.6 us
    ppermute x10, starting transfers between devices, _xor(): return lax.ppermute(x, 'row', [(i, i ^ mask) for i in range(n)])  11 us
    pallas_call x2, Pallas kernels, add(): pl.pallas_call(functools.partial(_band_kernel, masks, total is None, coun...  6.45 us
    all_to_all x1, waiting for transfers between devices, shards(): lax.all_to_all(right, 'row', split_axis=0, concat_axis=0, tiled=True)  5.07 us
    pallas_call x1, Pallas kernels, shards(): pl.pallas_call(_fold_kernel, out_shape=fold_out, scratch_shapes=[pltpu.VM...  2.77 us
    all_to_all x1, starting transfers between devices, shards(): lax.all_to_all(right, 'row', split_axis=0, concat_axis=0, tiled=True)  2.76 us
    pallas_call x1, Pallas kernels, shards(): pl.pallas_call(_project_kernel, in_specs=[anywhere] * 8, out_specs=(vmem,...  2.43 us
  transfers between devices with their start and end apart: 11, of which 7 were waited for; matrix products, arithmetic and copies ran while one was open for 0% of the time, Pallas kernels for 14%

profile of v12, /device:TPU:0, one launch (start us, length us, event | category | flops | bytes accessed | tf_op | source)
XLA Modules:
  0.0 44.6 jit_solution(4375039565636312923)
XLA Ops:
  0.0 2.4 %shard_map.100 = (bf16[256,128]{1,0:T(8,128)(2,1)S(1)}, bf16[32,8,128]{2,1,0:T(8,128)(2,1)}, bf16[1024,128]{1,0:T(8,128)(2,1)S(1)}, bf16[2,512,256]{2,1,0:T(8,128)(2,1)S(1)}) custom-call(bf16[2,512,256]{2,1,0:T(8,128)(2,1)} %refs_0_.1, f32[1,256]{1,0:T(1,128)} %bitcast.16, f32[1,256]{1,0:T(1,128)} %bitcast.17, bf16[32,256]{1,0:T(8,128)(2,1)} %bitcast.14, ...), custom_call_target="tpu_custom_call" | custom-call | flops 33554432 | bytes 524288 | tf_op jit(solution)/shard_map/pallas_call | solution.py:194
  2.4 5.1 %collective-permute-start.2 = (bf16[256,128]{1,0:T(8,128)(2,1)S(1)}, bf16[256,128]{1,0:T(8,128)(2,1)S(1)}, u32[]{:S(2)}, u32[]{:S(2)}) collective-permute-start(bf16[256,128]{1,0:T(8,128)(2,1)S(1)} %get-tuple-element.16.refs_0_), channel_id=1, source_target_pairs={{0,24},{1,25},{2,26},{3,27},{4,28},{5,29},{6,30},{7,31},{8,16},{9,... | collective-permute-start | bytes 196616 | tf_op jit(solution)/shard_map/ppermute | solution.py:177
  7.5 0.0 collective-permute-start.1
  7.6 0.6 %collective-permute-start = (bf16[256,128]{1,0:T(8,128)(2,1)S(1)}, bf16[256,128]{1,0:T(8,128)(2,1)S(1)}, u32[]{:S(2)}, u32[]{:S(2)}) collective-permute-start(bf16[256,128]{1,0:T(8,128)(2,1)S(1)} %get-tuple-element.16.refs_0_), channel_id=1, source_target_pairs={{0,8},{1,9},{2,10},{3,11},{4,12},{5,13},{6,14},{7,15},{8,0},{9,1},... | collective-permute-start | bytes 196616 | tf_op jit(solution)/shard_map/ppermute | solution.py:177
  8.2 1.9 %collective-permute-done.2.refs_2_ = bf16[256,128]{1,0:T(8,128)(2,1)S(1)} collective-permute-done((bf16[256,128]{1,0:T(8,128)(2,1)S(1)}, bf16[256,128]{1,0:T(8,128)(2,1)S(1)}, u32[]{:S(2)}, u32[]{:S(2)}) %collective-permute-start.2) | collective-permute-done | bytes 65568 | tf_op jit(solution)/shard_map/ppermute | solution.py:177
  10.1 3.0 %collective-permute-done.1.refs_3_ = bf16[256,128]{1,0:T(8,128)(2,1)S(1)} collective-permute-done((bf16[256,128]{1,0:T(8,128)(2,1)S(1)}, bf16[256,128]{1,0:T(8,128)(2,1)S(1)}, u32[]{:S(2)}, u32[]{:S(2)}) %collective-permute-start.1) | collective-permute-done | bytes 65568 | tf_op jit(solution)/shard_map/ppermute | solution.py:177
  13.2 0.0 collective-permute-done.refs_1_
  13.2 0.3 shard_map.101.refs_0_
  13.5 1.6 %collective-permute-start.5 = (bf16[512,256]{1,0:T(8,128)(2,1)S(1)}, bf16[512,256]{1,0:T(8,128)(2,1)S(1)}, u32[]{:S(2)}, u32[]{:S(2)}) collective-permute-start(bf16[512,256]{1,0:T(8,128)(2,1)S(1)} %shard_map.101.refs_0_), channel_id=1, source_target_pairs={{0,4},{1,5},{2,6},{3,7},{4,0},{5,1},{6,2},{7,3},{8,12},{9,13},{10,... | collective-permute-start | bytes 786440 | tf_op jit(solution)/shard_map/ppermute | solution.py:177
  15.1 1.5 %collective-permute-start.3 = (bf16[512,256]{1,0:T(8,128)(2,1)S(1)}, bf16[512,256]{1,0:T(8,128)(2,1)S(1)}, u32[]{:S(2)}, u32[]{:S(2)}) collective-permute-start(bf16[512,256]{1,0:T(8,128)(2,1)S(1)} %shard_map.101.refs_0_), channel_id=1, source_target_pairs={{0,2},{1,3},{2,0},{3,1},{4,6},{5,7},{6,4},{7,5},{8,10},{9,11},{10,... | collective-permute-start | bytes 786440 | tf_op jit(solution)/shard_map/ppermute | solution.py:177
  16.5 4.9 %collective-permute-done.5.refs_2_ = bf16[512,256]{1,0:T(8,128)(2,1)S(1)} collective-permute-done((bf16[512,256]{1,0:T(8,128)(2,1)S(1)}, bf16[512,256]{1,0:T(8,128)(2,1)S(1)}, u32[]{:S(2)}, u32[]{:S(2)}) %collective-permute-start.5) | collective-permute-done | bytes 262176 | tf_op jit(solution)/shard_map/ppermute | solution.py:177
  21.4 1.4 %collective-permute-done.3.refs_1_ = bf16[512,256]{1,0:T(8,128)(2,1)S(1)} collective-permute-done((bf16[512,256]{1,0:T(8,128)(2,1)S(1)}, bf16[512,256]{1,0:T(8,128)(2,1)S(1)}, u32[]{:S(2)}, u32[]{:S(2)}) %collective-permute-start.3) | collective-permute-done | bytes 262176 | tf_op jit(solution)/shard_map/ppermute | solution.py:177
  22.8 0.1 pad_maximum_fusion
  22.9 0.1 collective-permute-start.9
  23.0 1.6 %collective-permute-start.6 = (bf16[256,256]{1,0:T(8,128)(2,1)S(1)}, bf16[256,256]{1,0:T(8,128)(2,1)S(1)}, u32[]{:S(2)}, u32[]{:S(2)}) collective-permute-start(bf16[256,256]{1,0:T(8,128)(2,1)S(1)} %slice.9), channel_id=1, source_target_pairs={{0,2},{1,3},{2,0},{3,1},{4,6},{5,7},{6,4},{7,5},{8,10},{9,11},{10,... | collective-permute-start | bytes 393224 | tf_op jit(solution)/shard_map/ppermute | solution.py:177
  24.6 0.6 %collective-permute-start.4 = (bf16[256,256]{1,0:T(8,128)(2,1)S(1)}, bf16[256,256]{1,0:T(8,128)(2,1)S(1)}, u32[]{:S(2)}, u32[]{:S(2)}) collective-permute-start(bf16[256,256]{1,0:T(8,128)(2,1)S(1)} %slice.8), channel_id=1, source_target_pairs={{0,4},{1,5},{2,6},{3,7},{4,0},{5,1},{6,2},{7,3},{8,12},{9,13},{10,... | collective-permute-start | bytes 393224 | tf_op jit(solution)/shard_map/ppermute | solution.py:177
  25.2 2.8 %all-to-all-start = ((bf16[32,8,128]{2,1,0:T(8,128)(2,1)}), bf16[32,8,128]{2,1,0:T(8,128)(2,1)S(1)}, u32[]{:S(2)}, u32[]{:S(2)}) async-start(bf16[32,8,128]{2,1,0:T(8,128)(2,1)} %get-tuple-element.21), calls=%async_computation | async-start | bytes 131072 | tf_op jit(solution)/shard_map/all_to_all | solution.py:225
  27.9 1.1 %collective-permute-done.6.refs_1_ = bf16[256,256]{1,0:T(8,128)(2,1)S(1)} collective-permute-done((bf16[256,256]{1,0:T(8,128)(2,1)S(1)}, bf16[256,256]{1,0:T(8,128)(2,1)S(1)}, u32[]{:S(2)}, u32[]{:S(2)}) %collective-permute-start.6) | collective-permute-done | bytes 131104 | tf_op jit(solution)/shard_map/ppermute | solution.py:177
  29.0 0.0 collective-permute-start.8
  29.0 1.3 %collective-permute-done.4.refs_0_ = bf16[256,256]{1,0:T(8,128)(2,1)S(1)} collective-permute-done((bf16[256,256]{1,0:T(8,128)(2,1)S(1)}, bf16[256,256]{1,0:T(8,128)(2,1)S(1)}, u32[]{:S(2)}, u32[]{:S(2)}) %collective-permute-start.4) | collective-permute-done | bytes 131104 | tf_op jit(solution)/shard_map/ppermute | solution.py:177
  30.3 0.0 collective-permute-start.7
  30.3 5.1 %all-to-all-done.right_ref = bf16[32,8,128]{2,1,0:T(8,128)(2,1)S(1)} async-done(((bf16[32,8,128]{2,1,0:T(8,128)(2,1)}), bf16[32,8,128]{2,1,0:T(8,128)(2,1)S(1)}, u32[]{:S(2)}, u32[]{:S(2)}) %all-to-all-start) | async-done | bytes 65568 | tf_op jit(solution)/shard_map/all_to_all | solution.py:225
  35.3 2.8 %shard_map.102.refs_4_ = bf16[8,1,256,2048]{3,2,1,0:T(8,128)(2,1)S(1)} custom-call(bf16[32,8,128]{2,1,0:T(8,128)(2,1)S(1)} %all-to-all-done.right_ref, bf16[1024,128]{1,0:T(8,128)(2,1)S(1)} %get-tuple-element.22.final_ref), custom_call_target="tpu_custom_call" | custom-call | flops 2147483648 | bytes 8388608 | tf_op jit(solution)/shard_map/pallas_call | solution.py:242
  38.1 0.0 copy-start
  38.1 0.0 copy-start.1
  38.1 0.0 collective-permute-done.9.refs_3_
  38.1 3.5 %shard_map.103.refs_5_ = f32[512,2048]{1,0:T(8,128)S(1)} custom-call(bf16[512,256]{1,0:T(8,128)(2,1)S(1)} %shard_map.101.refs_0_, bf16[512,256]{1,0:T(8,128)(2,1)S(1)} %collective-permute-done.3.refs_1_, bf16[512,256]{1,0:T(8,128)(2,1)S(1)} %collective-permute-done.5.refs_2_, bf16[3,512,256]{2,1,0:T(8,128)(2,1)S(1)} %collective-permute-done.9.refs_3_, ...), custom_call_target="tpu_custom_call" | custom-call | flops 1048576 | bytes 8192 | tf_op jit(solution)/shard_map/pallas_call | solution.py:267
  41.6 0.0 collective-permute-done.8.refs_3_
  41.6 0.0 collective-permute-done.7.refs_2_
  41.6 0.0 copy-done
  41.6 0.0 copy-done.1
  41.7 3.0 %shard_map.104 = bf16[512,16,128]{2,1,0:T(8,128)(2,1)} custom-call(bf16[256,256]{1,0:T(8,128)(2,1)S(1)} %collective-permute-done.4.refs_0_, bf16[256,256]{1,0:T(8,128)(2,1)S(1)} %collective-permute-done.6.refs_1_, bf16[256,256]{1,0:T(8,128)(2,1)S(1)} %collective-permute-done.7.refs_2_, bf16[256,256]{1,0:T(8,128)(2,1)S(1)} %collective-permute-done.8.refs_3_, ...), custom_call_target="tpu_custom_call" | custom-call | flops 1048576 | bytes 8192 | tf_op jit(solution)/shard_map/pallas_call | solution.py:267
  (2 shorter events, 0.0 us)
Async XLA Ops:
  2.4 7.7 %collective-permute-start.2 = (bf16[256,128]{1,0:T(8,128)(2,1)S(1)}, bf16[256,128]{1,0:T(8,128)(2,1)S(1)}, u32[]{:S(2)}, u32[]{:S(2)}) collective-permute-start(bf16[256,128]{1,0:T(8,128)(2,1)S(1)} %get-tuple-element.16.refs_0_), channel_id=1, source_target_pairs={{0,24},{1,25},{2,26},{3,27},{4,28},{5,29},{6,30},{7,31},{8,16},{9,... | collective-permute-start | bytes 196616 | tf_op jit(solution)/shard_map/ppermute | solution.py:177
  7.5 5.6 %collective-permute-start.1 = (bf16[256,128]{1,0:T(8,128)(2,1)S(1)}, bf16[256,128]{1,0:T(8,128)(2,1)S(1)}, u32[]{:S(2)}, u32[]{:S(2)}) collective-permute-start(bf16[256,128]{1,0:T(8,128)(2,1)S(1)} %get-tuple-element.16.refs_0_), channel_id=1, source_target_pairs={{0,16},{1,17},{2,18},{3,19},{4,20},{5,21},{6,22},{7,23},{8,24},{9,... | collective-permute-start | bytes 196616 | tf_op jit(solution)/shard_map/ppermute | solution.py:177
  7.6 5.6 %collective-permute-start = (bf16[256,128]{1,0:T(8,128)(2,1)S(1)}, bf16[256,128]{1,0:T(8,128)(2,1)S(1)}, u32[]{:S(2)}, u32[]{:S(2)}) collective-permute-start(bf16[256,128]{1,0:T(8,128)(2,1)S(1)} %get-tuple-element.16.refs_0_), channel_id=1, source_target_pairs={{0,8},{1,9},{2,10},{3,11},{4,12},{5,13},{6,14},{7,15},{8,0},{9,1},... | collective-permute-start | bytes 196616 | tf_op jit(solution)/shard_map/ppermute | solution.py:177
  13.5 7.9 %collective-permute-start.5 = (bf16[512,256]{1,0:T(8,128)(2,1)S(1)}, bf16[512,256]{1,0:T(8,128)(2,1)S(1)}, u32[]{:S(2)}, u32[]{:S(2)}) collective-permute-start(bf16[512,256]{1,0:T(8,128)(2,1)S(1)} %shard_map.101.refs_0_), channel_id=1, source_target_pairs={{0,4},{1,5},{2,6},{3,7},{4,0},{5,1},{6,2},{7,3},{8,12},{9,13},{10,... | collective-permute-start | bytes 786440 | tf_op jit(solution)/shard_map/ppermute | solution.py:177
  15.1 7.8 %collective-permute-start.3 = (bf16[512,256]{1,0:T(8,128)(2,1)S(1)}, bf16[512,256]{1,0:T(8,128)(2,1)S(1)}, u32[]{:S(2)}, u32[]{:S(2)}) collective-permute-start(bf16[512,256]{1,0:T(8,128)(2,1)S(1)} %shard_map.101.refs_0_), channel_id=1, source_target_pairs={{0,2},{1,3},{2,0},{3,1},{4,6},{5,7},{6,4},{7,5},{8,10},{9,11},{10,... | collective-permute-start | bytes 786440 | tf_op jit(solution)/shard_map/ppermute | solution.py:177
  22.9 15.2 %collective-permute-start.9 = (bf16[3,512,256]{2,1,0:T(8,128)(2,1)S(1)}, bf16[3,512,256]{2,1,0:T(8,128)(2,1)S(1)}, u32[]{:S(2)}, u32[]{:S(2)}) collective-permute-start(bf16[3,512,256]{2,1,0:T(8,128)(2,1)S(1)} %pad_maximum_fusion), channel_id=1, source_target_pairs={{0,1},{1,0},{2,3},{3,2},{4,5},{5,4},{6,7},{7,6},{8,9},{9,8},{10,11... | collective-permute-start | bytes 2359304 | tf_op jit(solution)/shard_map/ppermute | solution.py:177
  23.0 6.0 %collective-permute-start.6 = (bf16[256,256]{1,0:T(8,128)(2,1)S(1)}, bf16[256,256]{1,0:T(8,128)(2,1)S(1)}, u32[]{:S(2)}, u32[]{:S(2)}) collective-permute-start(bf16[256,256]{1,0:T(8,128)(2,1)S(1)} %slice.9), channel_id=1, source_target_pairs={{0,2},{1,3},{2,0},{3,1},{4,6},{5,7},{6,4},{7,5},{8,10},{9,11},{10,... | collective-permute-start | bytes 393224 | tf_op jit(solution)/shard_map/ppermute | solution.py:177
  24.6 5.7 %collective-permute-start.4 = (bf16[256,256]{1,0:T(8,128)(2,1)S(1)}, bf16[256,256]{1,0:T(8,128)(2,1)S(1)}, u32[]{:S(2)}, u32[]{:S(2)}) collective-permute-start(bf16[256,256]{1,0:T(8,128)(2,1)S(1)} %slice.8), channel_id=1, source_target_pairs={{0,4},{1,5},{2,6},{3,7},{4,0},{5,1},{6,2},{7,3},{8,12},{9,13},{10,... | collective-permute-start | bytes 393224 | tf_op jit(solution)/shard_map/ppermute | solution.py:177
  25.2 10.2 %all-to-all-start = ((bf16[32,8,128]{2,1,0:T(8,128)(2,1)}), bf16[32,8,128]{2,1,0:T(8,128)(2,1)S(1)}, u32[]{:S(2)}, u32[]{:S(2)}) async-start(bf16[32,8,128]{2,1,0:T(8,128)(2,1)} %get-tuple-element.21), calls=%async_computation | async-start | bytes 131072 | tf_op jit(solution)/shard_map/all_to_all | solution.py:225
  29.0 12.6 %collective-permute-start.8 = (bf16[256,256]{1,0:T(8,128)(2,1)S(1)}, bf16[256,256]{1,0:T(8,128)(2,1)S(1)}, u32[]{:S(2)}, u32[]{:S(2)}) collective-permute-start(bf16[256,256]{1,0:T(8,128)(2,1)S(1)} %collective-permute-done.6.refs_1_), channel_id=1, source_target_pairs={{0,1},{1,0},{2,3},{3,2},{4,5},{5,4},{6,7},{7,6},{8,9},{9,8},{10,11... | collective-permute-start | bytes 393224 | tf_op jit(solution)/shard_map/ppermute | solution.py:177
  30.3 11.4 %collective-permute-start.7 = (bf16[256,256]{1,0:T(8,128)(2,1)S(1)}, bf16[256,256]{1,0:T(8,128)(2,1)S(1)}, u32[]{:S(2)}, u32[]{:S(2)}) collective-permute-start(bf16[256,256]{1,0:T(8,128)(2,1)S(1)} %collective-permute-done.4.refs_0_), channel_id=1, source_target_pairs={{0,1},{1,0},{2,3},{3,2},{4,5},{5,4},{6,7},{7,6},{8,9},{9,8},{10,11... | collective-permute-start | bytes 393224 | tf_op jit(solution)/shard_map/ppermute | solution.py:177
  38.1 3.5 %copy-start = (bf16[512,16,128]{2,1,0:T(8,128)(2,1)S(1)}, bf16[512,16,128]{2,1,0:T(8,128)(2,1)}, u32[]{:S(2)}) copy-start(bf16[512,16,128]{2,1,0:T(8,128)(2,1)} %refs_6_.1) | copy-start | bytes 6291460
  38.1 3.5 %copy-start.1 = (f32[128]{0:T(128)S(1)}, f32[128]{0:T(128)}, u32[]{:S(2)}) copy-start(f32[128]{0:T(128)} %param.19) | copy-start | bytes 1540

commit v13 on v12

--- a/solution.py
+++ b/solution.py
@@ -110,13 +110,11 @@
 def _band_kernel(masks, begins, count, held, *refs):
     refs = list(refs)
     take = lambda k: [refs.pop(0) for _ in range(k)]
-    lines = []
-    for mask in masks:
-        if mask in (1, 3, 5):
-            block = take(1)[0] if mask == 1 else block
-            lines.append([block.at[mask // 2]])
-        else:
-            lines.append(take(2 if mask > 5 else 1))
+    if masks == (3, 5):
+        (block,) = take(1)
+        lines = [block.at[k] for k in range(2)]
+    else:
+        lines = take(len(masks))
     (t_ref,) = take(1)
     (sum_ref,) = (None,) if begins else take(1)
     pair_ref, shift_ref = (None, None) if count is None else take(2)
@@ -126,7 +124,7 @@
     chunks = [((me % 8) ^ mask, q ^ (me // 32)) for mask in masks for q in range(t_ref.shape[1])]
 
     tile = 256
-    band = sum(part.shape[0] for part in lines[0])
+    band = lines[0].shape[0]
 
     def column(step):
         at = pl.ds(step * tile, tile)
@@ -136,7 +134,7 @@
             for i, (g, q) in enumerate(chunks):
                 pltpu.sync_copy(t_ref.at[g, q, :, at], refs[0].at[pl.ds(i * wide, wide)])
             rhs = refs[0][...]
-        lhs = jnp.concatenate([jnp.concatenate([part[...] for part in line], axis=0) for line in lines], axis=1)
+        lhs = jnp.concatenate([line[...] for line in lines], axis=1)
         res = jnp.dot(lhs, rhs, preferred_element_type=jnp.float32)
         return res if sum_ref is None else res + sum_ref[:, at]
 
@@ -208,10 +206,11 @@
         ),
     )(*sources, pltpu.with_memory_space_constraint(final, pltpu.HBM))
 
+    right = lax.all_to_all(right, "row", split_axis=0, concat_axis=0, tiled=True)
+
     part = 32
     parts = n // part
     pieces = [left] + [_xor(left, m, n) for m in range(8, n, 8)]
-    pieces, right = lax.optimization_barrier((pieces, right))
     pieces = [pieces[k ^ (k // 2 % 2)] for k in range(len(pieces))]
     line = pl.pallas_call(
         _line_kernel,
@@ -221,8 +220,7 @@
         compiler_params=params,
         cost_estimate=pl.CostEstimate(flops=2**27, bytes_accessed=2**20, transcendentals=0),
     )(*pieces, order)
-    x, y = _xor(line, 2, n), _xor(line, 4, n)
-    right = lax.all_to_all(right, "row", split_axis=0, concat_axis=0, tiled=True)
+    x, y, diagonal = (_xor(line, m, n) for m in (2, 4, 6))
 
     fold_cost = pl.CostEstimate(
         flops=2 * n * 32 * 256 * CHANS * zdim, bytes_accessed=4 * n * CHANS * cols * zdim, transcendentals=0
@@ -278,11 +276,15 @@
             ),
         )(*operands)
 
-    upper, lower = _xor(x[:half], 4, n), _xor(y[half:], 2, n)
-    across = _xor(jnp.stack([line, x, y]), 1, n)
-    total = add([line, x, y, across], (0, 2, 4, 1, 3, 5), None, False)
-    last = [_xor(upper, 1, n), _xor(lower, 1, n)]
-    return add([upper, lower, *last], (6, 7), total, True)
+    total = add([line, _xor(line, 1, n)], (0, 1), None, False)
+    x, y, total = lax.optimization_barrier((x, y, total))
+    across = _xor(jnp.stack([x, y]), 1, n)
+    total = add([x, y], (2, 4), total, False)
+    total = add([across], (3, 5), total, False)
+    diagonal, total = lax.optimization_barrier((diagonal, total))
+    last = _xor(diagonal, 1, n)
+    total = add([diagonal], (6,), total, False)
+    return add([last], (7,), total, True)
 
 
 def solution(mesh):

time: 44.8 us -> 38.9 us (0.87)
  waiting for transfers between devices: 18.7 us -> 10.8 us
  starting transfers between devices: 13.8 us -> 15.2 us
  Pallas kernels: 11.9 us -> 12.6 us
    ppermute x10 -> x9, waiting for transfers between devices: 13.6 us -> 7.06 us  [_xor(): return lax.ppermute(x, 'row', [(i, i ^ mask) for i in range(n)])]
    all_to_all x1, starting transfers between devices: 2.76 us -> 5.17 us  [shards(): lax.all_to_all(right, 'row', split_axis=0, concat_axis=0, tiled=True)]
    all_to_all x1, waiting for transfers between devices: 5.07 us -> 3.71 us  [shards(): lax.all_to_all(right, 'row', split_axis=0, concat_axis=0, tiled=True)]
    ppermute x10 -> x9, starting transfers between devices: 11 us -> 10 us  [_xor(): return lax.ppermute(x, 'row', [(i, i ^ mask) for i in range(n)])]
    pallas_call x2 -> x5, Pallas kernels: 6.45 us -> 7.07 us  [add(): pl.pallas_call(functools.partial(_band_kernel, masks, total is None, coun...]
  transfers between devices with their start and end apart: 11 -> 10, of which waited for: 7 -> 3; matrix products, arithmetic and copies ran while one was open for 0% -> 0% of each run, Pallas kernels for 14% -> 20%
where the time goes in v13:
time: 38.9 us; the launch traced here: 38.7 us
  starting transfers between devices  15.2 us (39%)
  Pallas kernels  12.6 us (32%)
  waiting for transfers between devices  10.8 us (28%)
    ppermute x9, starting transfers between devices, _xor(): return lax.ppermute(x, 'row', [(i, i ^ mask) for i in range(n)])  10 us
    pallas_call x5, Pallas kernels, add(): pl.pallas_call(functools.partial(_band_kernel, masks, total is None, coun...  7.07 us
    ppermute x9, waiting for transfers between devices, _xor(): return lax.ppermute(x, 'row', [(i, i ^ mask) for i in range(n)])  7.06 us
    all_to_all x1, starting transfers between devices, shards(): lax.all_to_all(right, 'row', split_axis=0, concat_axis=0, tiled=True)  5.17 us
    all_to_all x1, waiting for transfers between devices, shards(): lax.all_to_all(right, 'row', split_axis=0, concat_axis=0, tiled=True)  3.71 us
    pallas_call x1, Pallas kernels, shards(): pl.pallas_call(_fold_kernel, out_shape=fold_out, scratch_shapes=[pltpu.VM...  2.76 us
    pallas_call x1, Pallas kernels, shards(): pl.pallas_call(_project_kernel, in_specs=[anywhere] * 8, out_specs=(vmem,...  2.43 us
  transfers between devices with their start and end apart: 10, of which 3 were waited for; matrix products, arithmetic and copies ran while one was open for 0% of the time, Pallas kernels for 20%

profile of v13, /device:TPU:0, one launch (start us, length us, event | category | flops | bytes accessed | tf_op | source)
XLA Modules:
  0.0 38.7 jit_solution(4926019655147918320)
XLA Ops:
  0.0 2.4 %shard_map.100 = (bf16[256,128]{1,0:T(8,128)(2,1)S(1)}, bf16[32,8,128]{2,1,0:T(8,128)(2,1)}, bf16[1024,128]{1,0:T(8,128)(2,1)S(1)}, bf16[2,512,256]{2,1,0:T(8,128)(2,1)S(1)}) custom-call(bf16[2,512,256]{2,1,0:T(8,128)(2,1)} %refs_0_.1, f32[1,256]{1,0:T(1,128)} %bitcast.14, f32[1,256]{1,0:T(1,128)} %bitcast.15, bf16[32,256]{1,0:T(8,128)(2,1)} %bitcast.12, ...), custom_call_target="tpu_custom_call" | custom-call | flops 33554432 | bytes 524288 | tf_op jit(solution)/shard_map/pallas_call | solution.py:192
  2.4 4.1 %collective-permute-start.2 = (bf16[256,128]{1,0:T(8,128)(2,1)S(1)}, bf16[256,128]{1,0:T(8,128)(2,1)S(1)}, u32[]{:S(2)}, u32[]{:S(2)}) collective-permute-start(bf16[256,128]{1,0:T(8,128)(2,1)S(1)} %get-tuple-element.14.refs_0_), channel_id=1, source_target_pairs={{0,16},{1,17},{2,18},{3,19},{4,20},{5,21},{6,22},{7,23},{8,24},{9,... | collective-permute-start | bytes 196616 | tf_op jit(solution)/shard_map/ppermute | solution.py:175
  6.5 1.3 %collective-permute-start.1 = (bf16[256,128]{1,0:T(8,128)(2,1)S(1)}, bf16[256,128]{1,0:T(8,128)(2,1)S(1)}, u32[]{:S(2)}, u32[]{:S(2)}) collective-permute-start(bf16[256,128]{1,0:T(8,128)(2,1)S(1)} %get-tuple-element.14.refs_0_), channel_id=1, source_target_pairs={{0,24},{1,25},{2,26},{3,27},{4,28},{5,29},{6,30},{7,31},{8,16},{9,... | collective-permute-start | bytes 196616 | tf_op jit(solution)/shard_map/ppermute | solution.py:175
  7.9 0.2 collective-permute-start
  8.1 5.2 %all-to-all-start = ((bf16[32,8,128]{2,1,0:T(8,128)(2,1)}), bf16[32,8,128]{2,1,0:T(8,128)(2,1)S(1)}, u32[]{:S(2)}, u32[]{:S(2)}) async-start(bf16[32,8,128]{2,1,0:T(8,128)(2,1)} %get-tuple-element.16), calls=%async_computation | async-start | bytes 131072 | tf_op jit(solution)/shard_map/all_to_all | solution.py:209
  13.3 0.0 collective-permute-done.2.refs_3_
  13.3 0.0 collective-permute-done.1.refs_2_
  13.3 0.0 collective-permute-done.refs_1_
  13.3 0.3 shard_map.101.refs_0_
  13.6 0.3 collective-permute-start.6
  14.0 1.7 %collective-permute-start.5 = (bf16[512,256]{1,0:T(8,128)(2,1)S(1)}, bf16[512,256]{1,0:T(8,128)(2,1)S(1)}, u32[]{:S(2)}, u32[]{:S(2)}) collective-permute-start(bf16[512,256]{1,0:T(8,128)(2,1)S(1)} %shard_map.101.refs_0_), channel_id=1, source_target_pairs={{0,4},{1,5},{2,6},{3,7},{4,0},{5,1},{6,2},{7,3},{8,12},{9,13},{10,... | collective-permute-start | bytes 786440 | tf_op jit(solution)/shard_map/ppermute | solution.py:175
  15.6 1.5 %collective-permute-start.4 = (bf16[512,256]{1,0:T(8,128)(2,1)S(1)}, bf16[512,256]{1,0:T(8,128)(2,1)S(1)}, u32[]{:S(2)}, u32[]{:S(2)}) collective-permute-start(bf16[512,256]{1,0:T(8,128)(2,1)S(1)} %shard_map.101.refs_0_), channel_id=1, source_target_pairs={{0,2},{1,3},{2,0},{3,1},{4,6},{5,7},{6,4},{7,5},{8,10},{9,11},{10,... | collective-permute-start | bytes 786440 | tf_op jit(solution)/shard_map/ppermute | solution.py:175
  17.1 3.7 %all-to-all-done.right_ref = bf16[32,8,128]{2,1,0:T(8,128)(2,1)S(1)} async-done(((bf16[32,8,128]{2,1,0:T(8,128)(2,1)}), bf16[32,8,128]{2,1,0:T(8,128)(2,1)S(1)}, u32[]{:S(2)}, u32[]{:S(2)}) %all-to-all-start) | async-done | bytes 65568 | tf_op jit(solution)/shard_map/all_to_all | solution.py:209
  20.8 2.8 %shard_map.102.refs_2_.refs_1_ = bf16[8,1,256,2048]{3,2,1,0:T(8,128)(2,1)S(1)} custom-call(bf16[32,8,128]{2,1,0:T(8,128)(2,1)S(1)} %all-to-all-done.right_ref, bf16[1024,128]{1,0:T(8,128)(2,1)S(1)} %get-tuple-element.17.final_ref), custom_call_target="tpu_custom_call" | custom-call | flops 2147483648 | bytes 8388608 | tf_op jit(solution)/shard_map/pallas_call | solution.py:240
  23.6 0.0 collective-permute-done.6.refs_1_
  23.6 1.3 %shard_map.103.refs_3_ = f32[512,2048]{1,0:T(8,128)S(1)} custom-call(bf16[512,256]{1,0:T(8,128)(2,1)S(1)} %shard_map.101.refs_0_, bf16[512,256]{1,0:T(8,128)(2,1)S(1)} %collective-permute-done.6.refs_1_, bf16[8,1,256,2048]{3,2,1,0:T(8,128)(2,1)S(1)} %shard_map.102.refs_2_.refs_1_), custom_call_target="tpu_custom_call" | custom-call | flops 1048576 | bytes 8192 | tf_op jit(solution)/shard_map/pallas_call | solution.py:265
  24.9 0.0 collective-permute-done.5.refs_1_
  24.9 0.0 collective-permute-done.4.refs_0_
  24.9 0.1 pad_maximum_fusion
  24.9 0.1 collective-permute-start.7
  25.0 0.8 %collective-permute-start.3 = (bf16[512,256]{1,0:T(8,128)(2,1)S(1)}, bf16[512,256]{1,0:T(8,128)(2,1)S(1)}, u32[]{:S(2)}, u32[]{:S(2)}) collective-permute-start(bf16[512,256]{1,0:T(8,128)(2,1)S(1)} %shard_map.101.refs_0_), channel_id=1, source_target_pairs={{0,6},{1,7},{2,4},{3,5},{4,2},{5,3},{6,0},{7,1},{8,14},{9,15},{10,... | collective-permute-start | bytes 786440 | tf_op jit(solution)/shard_map/ppermute | solution.py:175
  25.8 1.3 %shard_map.104.refs_2_ = f32[512,2048]{1,0:T(8,128)S(1)} custom-call(bf16[512,256]{1,0:T(8,128)(2,1)S(1)} %collective-permute-done.4.refs_0_, bf16[512,256]{1,0:T(8,128)(2,1)S(1)} %collective-permute-done.5.refs_1_, bf16[8,1,256,2048]{3,2,1,0:T(8,128)(2,1)S(1)} %shard_map.102.refs_2_.refs_1_, f32[512,2048]{1,0:T(8,128)S(1)} %shard_map.103.refs_3_), custom_call_target="tpu_custom_call" | custom-call | flops 1048576 | bytes 8192 | tf_op jit(solution)/shard_map/pallas_call | solution.py:265
  27.1 0.0 collective-permute-done.7.refs_0_
  27.1 1.3 %shard_map.105.refs_2_ = f32[512,2048]{1,0:T(8,128)S(1)} custom-call(bf16[2,512,256]{2,1,0:T(8,128)(2,1)S(1)} %collective-permute-done.7.refs_0_, bf16[8,1,256,2048]{3,2,1,0:T(8,128)(2,1)S(1)} %shard_map.102.refs_2_.refs_1_, f32[512,2048]{1,0:T(8,128)S(1)} %shard_map.104.refs_2_), custom_call_target="tpu_custom_call" | custom-call | flops 1048576 | bytes 8192 | tf_op jit(solution)/shard_map/pallas_call | solution.py:265
  28.4 0.0 copy-start
  28.4 0.0 copy-start.1
  28.4 6.2 %collective-permute-done.3.refs_0_ = bf16[512,256]{1,0:T(8,128)(2,1)S(1)} collective-permute-done((bf16[512,256]{1,0:T(8,128)(2,1)S(1)}, bf16[512,256]{1,0:T(8,128)(2,1)S(1)}, u32[]{:S(2)}, u32[]{:S(2)}) %collective-permute-start.3) | collective-permute-done | bytes 262176 | tf_op jit(solution)/shard_map/ppermute | solution.py:175
  34.6 0.0 collective-permute-start.8
  34.6 0.7 %shard_map.106.refs_2_ = f32[512,2048]{1,0:T(8,128)S(1)} custom-call(bf16[512,256]{1,0:T(8,128)(2,1)S(1)} %collective-permute-done.3.refs_0_, bf16[8,1,256,2048]{3,2,1,0:T(8,128)(2,1)S(1)} %shard_map.102.refs_2_.refs_1_, f32[512,2048]{1,0:T(8,128)S(1)} %shard_map.105.refs_2_), custom_call_target="tpu_custom_call" | custom-call | flops 1048576 | bytes 8192 | tf_op jit(solution)/shard_map/pallas_call | solution.py:265
  35.4 0.8 %collective-permute-done.8.refs_0_ = bf16[512,256]{1,0:T(8,128)(2,1)S(1)} collective-permute-done((bf16[512,256]{1,0:T(8,128)(2,1)S(1)}, bf16[512,256]{1,0:T(8,128)(2,1)S(1)}, u32[]{:S(2)}, u32[]{:S(2)}) %collective-permute-start.8) | collective-permute-done | bytes 262176 | tf_op jit(solution)/shard_map/ppermute | solution.py:175
  36.2 0.0 copy-done
  36.2 2.6 %shard_map.107 = bf16[512,16,128]{2,1,0:T(8,128)(2,1)} custom-call(bf16[512,256]{1,0:T(8,128)(2,1)S(1)} %collective-permute-done.8.refs_0_, bf16[8,1,256,2048]{3,2,1,0:T(8,128)(2,1)S(1)} %shard_map.102.refs_2_.refs_1_, f32[512,2048]{1,0:T(8,128)S(1)} %shard_map.106.refs_2_, bf16[512,16,128]{2,1,0:T(8,128)(2,1)S(1)} %copy-done, f32[1,128]{1,0:T(1,128)S(1)} %bitcast.11), custom_call_target="tpu_custom_call" | custom-call | flops 1048576 | bytes 8192 | tf_op jit(solution)/shard_map/pallas_call | solution.py:265
  (1 shorter events, 0.0 us)
Async XLA Ops:
  2.4 10.9 %collective-permute-start.2 = (bf16[256,128]{1,0:T(8,128)(2,1)S(1)}, bf16[256,128]{1,0:T(8,128)(2,1)S(1)}, u32[]{:S(2)}, u32[]{:S(2)}) collective-permute-start(bf16[256,128]{1,0:T(8,128)(2,1)S(1)} %get-tuple-element.14.refs_0_), channel_id=1, source_target_pairs={{0,16},{1,17},{2,18},{3,19},{4,20},{5,21},{6,22},{7,23},{8,24},{9,... | collective-permute-start | bytes 196616 | tf_op jit(solution)/shard_map/ppermute | solution.py:175
  6.5 6.8 %collective-permute-start.1 = (bf16[256,128]{1,0:T(8,128)(2,1)S(1)}, bf16[256,128]{1,0:T(8,128)(2,1)S(1)}, u32[]{:S(2)}, u32[]{:S(2)}) collective-permute-start(bf16[256,128]{1,0:T(8,128)(2,1)S(1)} %get-tuple-element.14.refs_0_), channel_id=1, source_target_pairs={{0,24},{1,25},{2,26},{3,27},{4,28},{5,29},{6,30},{7,31},{8,16},{9,... | collective-permute-start | bytes 196616 | tf_op jit(solution)/shard_map/ppermute | solution.py:175
  7.9 5.4 %collective-permute-start = (bf16[256,128]{1,0:T(8,128)(2,1)S(1)}, bf16[256,128]{1,0:T(8,128)(2,1)S(1)}, u32[]{:S(2)}, u32[]{:S(2)}) collective-permute-start(bf16[256,128]{1,0:T(8,128)(2,1)S(1)} %get-tuple-element.14.refs_0_), channel_id=1, source_target_pairs={{0,8},{1,9},{2,10},{3,11},{4,12},{5,13},{6,14},{7,15},{8,0},{9,1},... | collective-permute-start | bytes 196616 | tf_op jit(solution)/shard_map/ppermute | solution.py:175
  8.1 12.7 %all-to-all-start = ((bf16[32,8,128]{2,1,0:T(8,128)(2,1)}), bf16[32,8,128]{2,1,0:T(8,128)(2,1)S(1)}, u32[]{:S(2)}, u32[]{:S(2)}) async-start(bf16[32,8,128]{2,1,0:T(8,128)(2,1)} %get-tuple-element.16), calls=%async_computation | async-start | bytes 131072 | tf_op jit(solution)/shard_map/all_to_all | solution.py:209
  13.6 9.9 %collective-permute-start.6 = (bf16[512,256]{1,0:T(8,128)(2,1)S(1)}, bf16[512,256]{1,0:T(8,128)(2,1)S(1)}, u32[]{:S(2)}, u32[]{:S(2)}) collective-permute-start(bf16[512,256]{1,0:T(8,128)(2,1)S(1)} %shard_map.101.refs_0_), channel_id=1, source_target_pairs={{0,1},{1,0},{2,3},{3,2},{4,5},{5,4},{6,7},{7,6},{8,9},{9,8},{10,11... | collective-permute-start | bytes 786440 | tf_op jit(solution)/shard_map/ppermute | solution.py:175
  14.0 10.9 %collective-permute-start.5 = (bf16[512,256]{1,0:T(8,128)(2,1)S(1)}, bf16[512,256]{1,0:T(8,128)(2,1)S(1)}, u32[]{:S(2)}, u32[]{:S(2)}) collective-permute-start(bf16[512,256]{1,0:T(8,128)(2,1)S(1)} %shard_map.101.refs_0_), channel_id=1, source_target_pairs={{0,4},{1,5},{2,6},{3,7},{4,0},{5,1},{6,2},{7,3},{8,12},{9,13},{10,... | collective-permute-start | bytes 786440 | tf_op jit(solution)/shard_map/ppermute | solution.py:175
  15.6 9.2 %collective-permute-start.4 = (bf16[512,256]{1,0:T(8,128)(2,1)S(1)}, bf16[512,256]{1,0:T(8,128)(2,1)S(1)}, u32[]{:S(2)}, u32[]{:S(2)}) collective-permute-start(bf16[512,256]{1,0:T(8,128)(2,1)S(1)} %shard_map.101.refs_0_), channel_id=1, source_target_pairs={{0,2},{1,3},{2,0},{3,1},{4,6},{5,7},{6,4},{7,5},{8,10},{9,11},{10,... | collective-permute-start | bytes 786440 | tf_op jit(solution)/shard_map/ppermute | solution.py:175
  24.9 2.2 %collective-permute-start.7 = (bf16[2,512,256]{2,1,0:T(8,128)(2,1)S(1)}, bf16[2,512,256]{2,1,0:T(8,128)(2,1)S(1)}, u32[]{:S(2)}, u32[]{:S(2)}) collective-permute-start(bf16[2,512,256]{2,1,0:T(8,128)(2,1)S(1)} %pad_maximum_fusion), channel_id=1, source_target_pairs={{0,1},{1,0},{2,3},{3,2},{4,5},{5,4},{6,7},{7,6},{8,9},{9,8},{10,11... | collective-permute-start | bytes 1572872 | tf_op jit(solution)/shard_map/ppermute | solution.py:175
  25.0 9.6 %collective-permute-start.3 = (bf16[512,256]{1,0:T(8,128)(2,1)S(1)}, bf16[512,256]{1,0:T(8,128)(2,1)S(1)}, u32[]{:S(2)}, u32[]{:S(2)}) collective-permute-start(bf16[512,256]{1,0:T(8,128)(2,1)S(1)} %shard_map.101.refs_0_), channel_id=1, source_target_pairs={{0,6},{1,7},{2,4},{3,5},{4,2},{5,3},{6,0},{7,1},{8,14},{9,15},{10,... | collective-permute-start | bytes 786440 | tf_op jit(solution)/shard_map/ppermute | solution.py:175
  28.4 7.8 %copy-start = (bf16[512,16,128]{2,1,0:T(8,128)(2,1)S(1)}, bf16[512,16,128]{2,1,0:T(8,128)(2,1)}, u32[]{:S(2)}) copy-start(bf16[512,16,128]{2,1,0:T(8,128)(2,1)} %refs_3_.1) | copy-start | bytes 6291460
  28.4 7.8 %copy-start.1 = (f32[128]{0:T(128)S(1)}, f32[128]{0:T(128)}, u32[]{:S(2)}) copy-start(f32[128]{0:T(128)} %param.19) | copy-start | bytes 1540
  34.6 1.5 %collective-permute-start.8 = (bf16[512,256]{1,0:T(8,128)(2,1)S(1)}, bf16[512,256]{1,0:T(8,128)(2,1)S(1)}, u32[]{:S(2)}, u32[]{:S(2)}) collective-permute-start(bf16[512,256]{1,0:T(8,128)(2,1)S(1)} %collective-permute-done.3.refs_0_), channel_id=1, source_target_pairs={{0,1},{1,0},{2,3},{3,2},{4,5},{5,4},{6,7},{7,6},{8,9},{9,8},{10,11... | collective-permute-start | bytes 786440 | tf_op jit(solution)/shard_map/ppermute | solution.py:175

commit v14 on v12

--- a/solution.py
+++ b/solution.py
@@ -110,13 +110,11 @@
 def _band_kernel(masks, begins, count, held, *refs):
     refs = list(refs)
     take = lambda k: [refs.pop(0) for _ in range(k)]
-    lines = []
-    for mask in masks:
-        if mask in (1, 3, 5):
-            block = take(1)[0] if mask == 1 else block
-            lines.append([block.at[mask // 2]])
-        else:
-            lines.append(take(2 if mask > 5 else 1))
+    if masks == (1, 3, 5):
+        (block,) = take(1)
+        lines = [[block.at[k]] for k in range(3)]
+    else:
+        lines = [take(2 if mask in (6, 7) else 1) for mask in masks]
     (t_ref,) = take(1)
     (sum_ref,) = (None,) if begins else take(1)
     pair_ref, shift_ref = (None, None) if count is None else take(2)
@@ -150,27 +148,32 @@
     cols = pair_ref.shape[1]
     pitch = cols + 1
     shift = shift_ref[...]
-    chunk = band // 2 // steps
-
-    def finish(r):
-        for k in range(chunk):
-            i = r * chunk + k
-            row = (i // 8) % 2 * (band // 2) + i // 16 * 8 + i % 8
-            total = acc_ref[pl.ds(row * pitch, cols), :] * (1.0 / count) + shift
-            done_ref[i] = (pair_ref[i].astype(jnp.float32) + total).astype(jnp.bfloat16)
-        at = pl.ds(r * chunk, chunk)
-        pltpu.make_async_copy(done_ref.at[at], out_ref.at[at], sems.at[r]).start()
-
     for step in range(steps):
         res = column(step)
         for k in range(tile // LANES):
             j = step * (tile // LANES) + k
             acc_ref[pl.ds(j, band, stride=pitch), :] = res[:, k * LANES : (k + 1) * LANES]
-    for r in range(2 * steps):
-        finish(r)
-    for r in range(2 * steps):
-        at = pl.ds(r * chunk, chunk)
+
+    chunk = 32
+
+    def finish(r, _):
+        for k in range(chunk):
+            i = r * chunk + k
+            row = k // 8 % 2 * (band // 2) + (r * (chunk // 16) + k // 16) * 8 + k % 8
+            total = acc_ref[pl.ds(row * pitch, cols), :] * (1.0 / count) + shift
+            done_ref[i] = (pair_ref[i].astype(jnp.float32) + total).astype(jnp.bfloat16)
+        at = pl.ds(pl.multiple_of(r * chunk, chunk), chunk)
+        pltpu.make_async_copy(done_ref.at[at], out_ref.at[at], sems.at[r]).start()
+        return 0
+
+    lax.fori_loop(0, band // chunk, finish, 0)
+
+    def drain(r, _):
+        at = pl.ds(pl.multiple_of(r * chunk, chunk), chunk)
         pltpu.make_async_copy(done_ref.at[at], out_ref.at[at], sems.at[r]).wait()
+        return 0
+
+    lax.fori_loop(0, band // chunk, drain, 0)
 
 
 def _xor(x, mask, n):
@@ -208,10 +211,11 @@
         ),
     )(*sources, pltpu.with_memory_space_constraint(final, pltpu.HBM))
 
+    right = lax.all_to_all(right, "row", split_axis=0, concat_axis=0, tiled=True)
+
     part = 32
     parts = n // part
     pieces = [left] + [_xor(left, m, n) for m in range(8, n, 8)]
-    pieces, right = lax.optimization_barrier((pieces, right))
     pieces = [pieces[k ^ (k // 2 % 2)] for k in range(len(pieces))]
     line = pl.pallas_call(
         _line_kernel,
@@ -222,7 +226,6 @@
         cost_estimate=pl.CostEstimate(flops=2**27, bytes_accessed=2**20, transcendentals=0),
     )(*pieces, order)
     x, y = _xor(line, 2, n), _xor(line, 4, n)
-    right = lax.all_to_all(right, "row", split_axis=0, concat_axis=0, tiled=True)
 
     fold_cost = pl.CostEstimate(
         flops=2 * n * 32 * 256 * CHANS * zdim, bytes_accessed=4 * n * CHANS * cols * zdim, transcendentals=0
@@ -257,7 +260,7 @@
             scratch += [
                 pltpu.VMEM((band * (cols + 1), zdim), jnp.float32),
                 pltpu.VMEM(pair.shape, jnp.bfloat16),
-                pltpu.SemaphoreType.DMA((cols * zdim // 128,)),
+                pltpu.SemaphoreType.DMA((band // 32,)),
             ]
         if not small:
             scratch.append(pltpu.VMEM((depth, 256), jnp.bfloat16))
@@ -278,11 +281,18 @@
             ),
         )(*operands)
 
-    upper, lower = _xor(x[:half], 4, n), _xor(y[half:], 2, n)
+    x, y, folded = lax.optimization_barrier((x, y, folded))
+    cut = band * 9 // 16
+    upper, lower = _xor(x[:cut], 4, n), _xor(y[cut:], 2, n)
     across = _xor(jnp.stack([line, x, y]), 1, n)
-    total = add([line, x, y, across], (0, 2, 4, 1, 3, 5), None, False)
-    last = [_xor(upper, 1, n), _xor(lower, 1, n)]
-    return add([upper, lower, *last], (6, 7), total, True)
+    total = add([line, x, y], (0, 2, 4), None, False)
+    total = add([across], (1, 3, 5), total, False)
+    upper, total = lax.optimization_barrier((upper, total))
+    last = [_xor(upper, 1, n)]
+    lower, total = lax.optimization_barrier((lower, total))
+    last.append(_xor(lower, 1, n))
+    total = add([upper, lower], (6,), total, False)
+    return add(last, (7,), total, True)
 
 
 def solution(mesh):

time: 44.8 us -> 34.4 us (0.77)
  waiting for transfers between devices: 18.7 us -> 5 us
  starting transfers between devices: 13.8 us -> 16.9 us
    ppermute x10, waiting for transfers between devices: 13.6 us -> 1.13 us  [_xor(): return lax.ppermute(x, 'row', [(i, i ^ mask) for i in range(n)])]
    all_to_all x1, starting transfers between devices: 2.76 us -> 5.17 us  [shards(): lax.all_to_all(right, 'row', split_axis=0, concat_axis=0, tiled=True)]
    all_to_all x1, waiting for transfers between devices: 5.07 us -> 3.88 us  [shards(): lax.all_to_all(right, 'row', split_axis=0, concat_axis=0, tiled=True)]
    ppermute x10, starting transfers between devices: 11 us -> 11.7 us  [_xor(): return lax.ppermute(x, 'row', [(i, i ^ mask) for i in range(n)])]
    pallas_call x2 -> x4, Pallas kernels: 6.45 us -> 6.55 us  [add(): pl.pallas_call(functools.partial(_band_kernel, masks, total is None, coun...]
  transfers between devices with their start and end apart: 11 -> 11, of which waited for: 7 -> 4; matrix products, arithmetic and copies ran while one was open for 0% -> 0% of each run, Pallas kernels for 14% -> 22%
where the time goes in v14:
time: 34.4 us; the launch traced here: 34.2 us
  starting transfers between devices  16.9 us (49%)
  Pallas kernels  12 us (35%)
  waiting for transfers between devices  5 us (15%)
    ppermute x10, starting transfers between devices, _xor(): return lax.ppermute(x, 'row', [(i, i ^ mask) for i in range(n)])  11.7 us
    pallas_call x4, Pallas kernels, add(): pl.pallas_call(functools.partial(_band_kernel, masks, total is None, coun...  6.55 us
    all_to_all x1, starting transfers between devices, shards(): lax.all_to_all(right, 'row', split_axis=0, concat_axis=0, tiled=True)  5.17 us
    all_to_all x1, waiting for transfers between devices, shards(): lax.all_to_all(right, 'row', split_axis=0, concat_axis=0, tiled=True)  3.88 us
    pallas_call x1, Pallas kernels, shards(): pl.pallas_call(_fold_kernel, out_shape=fold_out, scratch_shapes=[pltpu.VM...  2.76 us
    pallas_call x1, Pallas kernels, shards(): pl.pallas_call(_project_kernel, in_specs=[anywhere] * 8, out_specs=(vmem,...  2.43 us
    ppermute x10, waiting for transfers between devices, _xor(): return lax.ppermute(x, 'row', [(i, i ^ mask) for i in range(n)])  1.13 us
  transfers between devices with their start and end apart: 11, of which 4 were waited for; matrix products, arithmetic and copies ran while one was open for 0% of the time, Pallas kernels for 22%

profile of v14, /device:TPU:0, one launch (start us, length us, event | category | flops | bytes accessed | tf_op | source)
XLA Modules:
  0.0 34.2 jit_solution(12118012312462684346)
XLA Ops:
  0.0 2.4 %shard_map.100 = (bf16[256,128]{1,0:T(8,128)(2,1)S(1)}, bf16[32,8,128]{2,1,0:T(8,128)(2,1)}, bf16[1024,128]{1,0:T(8,128)(2,1)S(1)}, bf16[2,512,256]{2,1,0:T(8,128)(2,1)S(1)}) custom-call(bf16[2,512,256]{2,1,0:T(8,128)(2,1)} %refs_0_.1, f32[1,256]{1,0:T(1,128)} %bitcast.16, f32[1,256]{1,0:T(1,128)} %bitcast.17, bf16[32,256]{1,0:T(8,128)(2,1)} %bitcast.14, ...), custom_call_target="tpu_custom_call" | custom-call | flops 33554432 | bytes 524288 | tf_op jit(solution)/shard_map/pallas_call | solution.py:197
  2.4 4.1 %collective-permute-start.2 = (bf16[256,128]{1,0:T(8,128)(2,1)S(1)}, bf16[256,128]{1,0:T(8,128)(2,1)S(1)}, u32[]{:S(2)}, u32[]{:S(2)}) collective-permute-start(bf16[256,128]{1,0:T(8,128)(2,1)S(1)} %get-tuple-element.16.refs_0_), channel_id=1, source_target_pairs={{0,16},{1,17},{2,18},{3,19},{4,20},{5,21},{6,22},{7,23},{8,24},{9,... | collective-permute-start | bytes 196616 | tf_op jit(solution)/shard_map/ppermute | solution.py:180
  6.5 1.3 %collective-permute-start.1 = (bf16[256,128]{1,0:T(8,128)(2,1)S(1)}, bf16[256,128]{1,0:T(8,128)(2,1)S(1)}, u32[]{:S(2)}, u32[]{:S(2)}) collective-permute-start(bf16[256,128]{1,0:T(8,128)(2,1)S(1)} %get-tuple-element.16.refs_0_), channel_id=1, source_target_pairs={{0,24},{1,25},{2,26},{3,27},{4,28},{5,29},{6,30},{7,31},{8,16},{9,... | collective-permute-start | bytes 196616 | tf_op jit(solution)/shard_map/ppermute | solution.py:180
  7.9 0.2 collective-permute-start
  8.1 5.2 %all-to-all-start = ((bf16[32,8,128]{2,1,0:T(8,128)(2,1)}), bf16[32,8,128]{2,1,0:T(8,128)(2,1)S(1)}, u32[]{:S(2)}, u32[]{:S(2)}) async-start(bf16[32,8,128]{2,1,0:T(8,128)(2,1)} %get-tuple-element.18), calls=%async_computation | async-start | bytes 131072 | tf_op jit(solution)/shard_map/all_to_all | solution.py:214
  13.3 0.0 collective-permute-done.2.refs_3_
  13.3 0.0 collective-permute-done.1.refs_2_
  13.3 0.0 collective-permute-done.refs_1_
  13.3 0.3 shard_map.101.refs_0_
  13.6 1.8 %collective-permute-start.4 = (bf16[512,256]{1,0:T(8,128)(2,1)S(1)}, bf16[512,256]{1,0:T(8,128)(2,1)S(1)}, u32[]{:S(2)}, u32[]{:S(2)}) collective-permute-start(bf16[512,256]{1,0:T(8,128)(2,1)S(1)} %shard_map.101.refs_0_), channel_id=1, source_target_pairs={{0,4},{1,5},{2,6},{3,7},{4,0},{5,1},{6,2},{7,3},{8,12},{9,13},{10,... | collective-permute-start | bytes 786440 | tf_op jit(solution)/shard_map/ppermute | solution.py:180
  15.5 1.5 %collective-permute-start.3 = (bf16[512,256]{1,0:T(8,128)(2,1)S(1)}, bf16[512,256]{1,0:T(8,128)(2,1)S(1)}, u32[]{:S(2)}, u32[]{:S(2)}) collective-permute-start(bf16[512,256]{1,0:T(8,128)(2,1)S(1)} %shard_map.101.refs_0_), channel_id=1, source_target_pairs={{0,2},{1,3},{2,0},{3,1},{4,6},{5,7},{6,4},{7,5},{8,10},{9,11},{10,... | collective-permute-start | bytes 786440 | tf_op jit(solution)/shard_map/ppermute | solution.py:180
  16.9 3.9 %all-to-all-done.right_ref = bf16[32,8,128]{2,1,0:T(8,128)(2,1)S(1)} async-done(((bf16[32,8,128]{2,1,0:T(8,128)(2,1)}), bf16[32,8,128]{2,1,0:T(8,128)(2,1)S(1)}, u32[]{:S(2)}, u32[]{:S(2)}) %all-to-all-start) | async-done | bytes 65568 | tf_op jit(solution)/shard_map/all_to_all | solution.py:214
  20.8 2.8 %shard_map.102.refs_3_.refs_1_.refs_2_ = bf16[8,1,256,2048]{3,2,1,0:T(8,128)(2,1)S(1)} custom-call(bf16[32,8,128]{2,1,0:T(8,128)(2,1)S(1)} %all-to-all-done.right_ref, bf16[1024,128]{1,0:T(8,128)(2,1)S(1)} %get-tuple-element.19.final_ref), custom_call_target="tpu_custom_call" | custom-call | flops 2147483648 | bytes 8388608 | tf_op jit(solution)/shard_map/pallas_call | solution.py:245
  23.6 0.0 collective-permute-done.4.refs_2_
  23.6 0.3 collective-permute-done.3.refs_1_
  23.9 0.1 pad_maximum_fusion
  24.0 0.1 collective-permute-start.6
  24.1 0.6 %collective-permute-start.5 = (bf16[288,256]{1,0:T(8,128)(2,1)S(1)}, bf16[288,256]{1,0:T(8,128)(2,1)S(1)}, u32[]{:S(2)}, u32[]{:S(2)}) collective-permute-start(bf16[288,256]{1,0:T(8,128)(2,1)S(1)} %slice.6), channel_id=1, source_target_pairs={{0,4},{1,5},{2,6},{3,7},{4,0},{5,1},{6,2},{7,3},{8,12},{9,13},{10,... | collective-permute-start | bytes 442376 | tf_op jit(solution)/shard_map/ppermute | solution.py:180
  24.7 1.6 %collective-permute-start.8 = (bf16[224,256]{1,0:T(8,128)(2,1)S(1)}, bf16[224,256]{1,0:T(8,128)(2,1)S(1)}, u32[]{:S(2)}, u32[]{:S(2)}) collective-permute-start(bf16[224,256]{1,0:T(8,128)(2,1)S(1)} %slice.7), channel_id=1, source_target_pairs={{0,2},{1,3},{2,0},{3,1},{4,6},{5,7},{6,4},{7,5},{8,10},{9,11},{10,... | collective-permute-start | bytes 344072 | tf_op jit(solution)/shard_map/ppermute | solution.py:180
  26.3 1.8 %shard_map.103.refs_2_ = f32[512,2048]{1,0:T(8,128)S(1)} custom-call(bf16[512,256]{1,0:T(8,128)(2,1)S(1)} %shard_map.101.refs_0_, bf16[512,256]{1,0:T(8,128)(2,1)S(1)} %collective-permute-done.3.refs_1_, bf16[512,256]{1,0:T(8,128)(2,1)S(1)} %collective-permute-done.4.refs_2_, bf16[8,1,256,2048]{3,2,1,0:T(8,128)(2,1)S(1)} %shard_map.102.refs_3_.refs_1_.refs_2_), custom_call_target="tpu_custom_call" | custom-call | flops 1048576 | bytes 8192 | tf_op jit(solution)/shard_map/pallas_call | solution.py:270
  28.1 0.0 collective-permute-done.6.refs_0_
  28.1 1.8 %shard_map.104.refs_3_ = f32[512,2048]{1,0:T(8,128)S(1)} custom-call(bf16[3,512,256]{2,1,0:T(8,128)(2,1)S(1)} %collective-permute-done.6.refs_0_, bf16[8,1,256,2048]{3,2,1,0:T(8,128)(2,1)S(1)} %shard_map.102.refs_3_.refs_1_.refs_2_, f32[512,2048]{1,0:T(8,128)S(1)} %shard_map.103.refs_2_), custom_call_target="tpu_custom_call" | custom-call | flops 1048576 | bytes 8192 | tf_op jit(solution)/shard_map/pallas_call | solution.py:270
  29.9 0.0 copy-start
  29.9 0.0 copy-start.1
  29.9 0.5 %collective-permute-done.5.refs_0_ = bf16[288,256]{1,0:T(8,128)(2,1)S(1)} collective-permute-done((bf16[288,256]{1,0:T(8,128)(2,1)S(1)}, bf16[288,256]{1,0:T(8,128)(2,1)S(1)}, u32[]{:S(2)}, u32[]{:S(2)}) %collective-permute-start.5) | collective-permute-done | bytes 147488 | tf_op jit(solution)/shard_map/ppermute | solution.py:180
  30.4 0.0 collective-permute-start.7
  30.4 0.0 collective-permute-done.8.refs_1_
  30.4 0.5 %collective-permute-start.9 = (bf16[224,256]{1,0:T(8,128)(2,1)S(1)}, bf16[224,256]{1,0:T(8,128)(2,1)S(1)}, u32[]{:S(2)}, u32[]{:S(2)}) collective-permute-start(bf16[224,256]{1,0:T(8,128)(2,1)S(1)} %collective-permute-done.8.refs_1_), channel_id=1, source_target_pairs={{0,1},{1,0},{2,3},{3,2},{4,5},{5,4},{6,7},{7,6},{8,9},{9,8},{10,11... | collective-permute-start | bytes 344072 | tf_op jit(solution)/shard_map/ppermute | solution.py:180
  30.9 0.7 %shard_map.105.refs_3_ = f32[512,2048]{1,0:T(8,128)S(1)} custom-call(bf16[288,256]{1,0:T(8,128)(2,1)S(1)} %collective-permute-done.5.refs_0_, bf16[224,256]{1,0:T(8,128)(2,1)S(1)} %collective-permute-done.8.refs_1_, bf16[8,1,256,2048]{3,2,1,0:T(8,128)(2,1)S(1)} %shard_map.102.refs_3_.refs_1_.refs_2_, f32[512,2048]{1,0:T(8,128)S(1)} %shard_map.104.refs_3_), custom_call_target="tpu_custom_call" | custom-call | flops 1048576 | bytes 8192 | tf_op jit(solution)/shard_map/pallas_call | solution.py:270
  31.6 0.3 collective-permute-done.9.refs_1_
  31.9 0.0 collective-permute-done.7.refs_0_
  31.9 2.2 %shard_map.106 = bf16[512,16,128]{2,1,0:T(8,128)(2,1)} custom-call(bf16[288,256]{1,0:T(8,128)(2,1)S(1)} %collective-permute-done.7.refs_0_, bf16[224,256]{1,0:T(8,128)(2,1)S(1)} %collective-permute-done.9.refs_1_, bf16[8,1,256,2048]{3,2,1,0:T(8,128)(2,1)S(1)} %shard_map.102.refs_3_.refs_1_.refs_2_, f32[512,2048]{1,0:T(8,128)S(1)} %shard_map.105.refs_3_, ...), custom_call_target="tpu_custom_call" | custom-call | flops 1048576 | bytes 8192 | tf_op jit(solution)/shard_map/pallas_call | solution.py:270
  (4 shorter events, 0.0 us)
Async XLA Ops:
  2.4 10.9 %collective-permute-start.2 = (bf16[256,128]{1,0:T(8,128)(2,1)S(1)}, bf16[256,128]{1,0:T(8,128)(2,1)S(1)}, u32[]{:S(2)}, u32[]{:S(2)}) collective-permute-start(bf16[256,128]{1,0:T(8,128)(2,1)S(1)} %get-tuple-element.16.refs_0_), channel_id=1, source_target_pairs={{0,16},{1,17},{2,18},{3,19},{4,20},{5,21},{6,22},{7,23},{8,24},{9,... | collective-permute-start | bytes 196616 | tf_op jit(solution)/shard_map/ppermute | solution.py:180
  6.5 6.8 %collective-permute-start.1 = (bf16[256,128]{1,0:T(8,128)(2,1)S(1)}, bf16[256,128]{1,0:T(8,128)(2,1)S(1)}, u32[]{:S(2)}, u32[]{:S(2)}) collective-permute-start(bf16[256,128]{1,0:T(8,128)(2,1)S(1)} %get-tuple-element.16.refs_0_), channel_id=1, source_target_pairs={{0,24},{1,25},{2,26},{3,27},{4,28},{5,29},{6,30},{7,31},{8,16},{9,... | collective-permute-start | bytes 196616 | tf_op jit(solution)/shard_map/ppermute | solution.py:180
  7.9 5.4 %collective-permute-start = (bf16[256,128]{1,0:T(8,128)(2,1)S(1)}, bf16[256,128]{1,0:T(8,128)(2,1)S(1)}, u32[]{:S(2)}, u32[]{:S(2)}) collective-permute-start(bf16[256,128]{1,0:T(8,128)(2,1)S(1)} %get-tuple-element.16.refs_0_), channel_id=1, source_target_pairs={{0,8},{1,9},{2,10},{3,11},{4,12},{5,13},{6,14},{7,15},{8,0},{9,1},... | collective-permute-start | bytes 196616 | tf_op jit(solution)/shard_map/ppermute | solution.py:180
  8.1 12.7 %all-to-all-start = ((bf16[32,8,128]{2,1,0:T(8,128)(2,1)}), bf16[32,8,128]{2,1,0:T(8,128)(2,1)S(1)}, u32[]{:S(2)}, u32[]{:S(2)}) async-start(bf16[32,8,128]{2,1,0:T(8,128)(2,1)} %get-tuple-element.18), calls=%async_computation | async-start | bytes 131072 | tf_op jit(solution)/shard_map/all_to_all | solution.py:214
  13.6 9.9 %collective-permute-start.4 = (bf16[512,256]{1,0:T(8,128)(2,1)S(1)}, bf16[512,256]{1,0:T(8,128)(2,1)S(1)}, u32[]{:S(2)}, u32[]{:S(2)}) collective-permute-start(bf16[512,256]{1,0:T(8,128)(2,1)S(1)} %shard_map.101.refs_0_), channel_id=1, source_target_pairs={{0,4},{1,5},{2,6},{3,7},{4,0},{5,1},{6,2},{7,3},{8,12},{9,13},{10,... | collective-permute-start | bytes 786440 | tf_op jit(solution)/shard_map/ppermute | solution.py:180
  15.5 8.4 %collective-permute-start.3 = (bf16[512,256]{1,0:T(8,128)(2,1)S(1)}, bf16[512,256]{1,0:T(8,128)(2,1)S(1)}, u32[]{:S(2)}, u32[]{:S(2)}) collective-permute-start(bf16[512,256]{1,0:T(8,128)(2,1)S(1)} %shard_map.101.refs_0_), channel_id=1, source_target_pairs={{0,2},{1,3},{2,0},{3,1},{4,6},{5,7},{6,4},{7,5},{8,10},{9,11},{10,... | collective-permute-start | bytes 786440 | tf_op jit(solution)/shard_map/ppermute | solution.py:180
  24.0 4.1 %collective-permute-start.6 = (bf16[3,512,256]{2,1,0:T(8,128)(2,1)S(1)}, bf16[3,512,256]{2,1,0:T(8,128)(2,1)S(1)}, u32[]{:S(2)}, u32[]{:S(2)}) collective-permute-start(bf16[3,512,256]{2,1,0:T(8,128)(2,1)S(1)} %pad_maximum_fusion), channel_id=1, source_target_pairs={{0,1},{1,0},{2,3},{3,2},{4,5},{5,4},{6,7},{7,6},{8,9},{9,8},{10,11... | collective-permute-start | bytes 2359304 | tf_op jit(solution)/shard_map/ppermute | solution.py:180
  24.1 6.3 %collective-permute-start.5 = (bf16[288,256]{1,0:T(8,128)(2,1)S(1)}, bf16[288,256]{1,0:T(8,128)(2,1)S(1)}, u32[]{:S(2)}, u32[]{:S(2)}) collective-permute-start(bf16[288,256]{1,0:T(8,128)(2,1)S(1)} %slice.6), channel_id=1, source_target_pairs={{0,4},{1,5},{2,6},{3,7},{4,0},{5,1},{6,2},{7,3},{8,12},{9,13},{10,... | collective-permute-start | bytes 442376 | tf_op jit(solution)/shard_map/ppermute | solution.py:180
  24.7 5.7 %collective-permute-start.8 = (bf16[224,256]{1,0:T(8,128)(2,1)S(1)}, bf16[224,256]{1,0:T(8,128)(2,1)S(1)}, u32[]{:S(2)}, u32[]{:S(2)}) collective-permute-start(bf16[224,256]{1,0:T(8,128)(2,1)S(1)} %slice.7), channel_id=1, source_target_pairs={{0,2},{1,3},{2,0},{3,1},{4,6},{5,7},{6,4},{7,5},{8,10},{9,11},{10,... | collective-permute-start | bytes 344072 | tf_op jit(solution)/shard_map/ppermute | solution.py:180
  29.9 2.1 %copy-start = (bf16[512,16,128]{2,1,0:T(8,128)(2,1)S(1)}, bf16[512,16,128]{2,1,0:T(8,128)(2,1)}, u32[]{:S(2)}) copy-start(bf16[512,16,128]{2,1,0:T(8,128)(2,1)} %refs_4_.1) | copy-start | bytes 6291460
  29.9 2.0 %copy-start.1 = (f32[128]{0:T(128)S(1)}, f32[128]{0:T(128)}, u32[]{:S(2)}) copy-start(f32[128]{0:T(128)} %param.19) | copy-start | bytes 1540
  30.4 1.5 %collective-permute-start.7 = (bf16[288,256]{1,0:T(8,128)(2,1)S(1)}, bf16[288,256]{1,0:T(8,128)(2,1)S(1)}, u32[]{:S(2)}, u32[]{:S(2)}) collective-permute-start(bf16[288,256]{1,0:T(8,128)(2,1)S(1)} %collective-permute-done.5.refs_0_), channel_id=1, source_target_pairs={{0,1},{1,0},{2,3},{3,2},{4,5},{5,4},{6,7},{7,6},{8,9},{9,8},{10,11... | collective-permute-start | bytes 442376 | tf_op jit(solution)/shard_map/ppermute | solution.py:180
  30.4 1.5 %collective-permute-start.9 = (bf16[224,256]{1,0:T(8,128)(2,1)S(1)}, bf16[224,256]{1,0:T(8,128)(2,1)S(1)}, u32[]{:S(2)}, u32[]{:S(2)}) collective-permute-start(bf16[224,256]{1,0:T(8,128)(2,1)S(1)} %collective-permute-done.8.refs_1_), channel_id=1, source_target_pairs={{0,1},{1,0},{2,3},{3,2},{4,5},{5,4},{6,7},{7,6},{8,9},{9,8},{10,11... | collective-permute-start | bytes 344072 | tf_op jit(solution)/shard_map/ppermute | solution.py:180

commit v15 on v14

--- a/solution.py
+++ b/solution.py
@@ -94,20 +94,29 @@
     lhs = [jnp.where(lane == jh * 2 + s, block, 0.0).astype(jnp.bfloat16) for jh in range(2)]
     lhs = jnp.concatenate(lhs, axis=0)
 
-    for pair in range(CHANS // 2):
+    def columns(r, _):
+        for u in range(4):
+            column(r * 4 + u)
+        return 0
+
+    def column(pair):
         rhs = []
         for k in range(2):
-            at = pair * 2 * CHANS + k * CHANS
+            at = pl.multiple_of(pair * 2 * CHANS + k * CHANS, CHANS)
             rhs.append(jnp.concatenate([final_ref[pl.ds(at, CHANS), :]] * 4, axis=0))
         res = jnp.dot(lhs, jnp.concatenate(rhs, axis=1), preferred_element_type=jnp.float32)
         for j in range(16):
             for g in range(groups):
                 r = (j * groups + g) * 8
                 tile = jnp.concatenate([res[r : r + 8, :LANES], res[r : r + 8, LANES:]], axis=0)
-                out_ref[g, 0, pl.ds(pair * 16, 16), pl.ds(j * LANES, LANES)] = tile.astype(jnp.bfloat16)
-
-
-def _band_kernel(masks, begins, count, held, *refs):
+                out_ref[g, 0, pl.ds(pl.multiple_of(pair * 16, 16), 16), pl.ds(j * LANES, LANES)] = tile.astype(
+                    jnp.bfloat16
+                )
+
+    lax.fori_loop(0, CHANS // 8, columns, 0)
+
+
+def _band_kernel(masks, begins, scale, last, held, *refs):
     refs = list(refs)
     take = lambda k: [refs.pop(0) for _ in range(k)]
     if masks == (1, 3, 5):
@@ -117,7 +126,8 @@
         lines = [take(2 if mask in (6, 7) else 1) for mask in masks]
     (t_ref,) = take(1)
     (sum_ref,) = (None,) if begins else take(1)
-    pair_ref, shift_ref = (None, None) if count is None else take(2)
+    shift_ref = None if scale is None or last else take(1)[0]
+    pair_ref = take(1)[0] if last else None
     (out_ref,) = take(1)
     me = lax.axis_index("row")
     wide = t_ref.shape[2]
@@ -126,8 +136,8 @@
     tile = 256
     band = sum(part.shape[0] for part in lines[0])
 
-    def column(step):
-        at = pl.ds(step * tile, tile)
+    def column(begin):
+        at = pl.ds(pl.multiple_of(begin, tile), tile)
         if held:
             rhs = jnp.concatenate([t_ref[g, q, :, at] for g, q in chunks], axis=0)
         else:
@@ -136,23 +146,35 @@
             rhs = refs[0][...]
         lhs = jnp.concatenate([jnp.concatenate([part[...] for part in line], axis=0) for line in lines], axis=1)
         res = jnp.dot(lhs, rhs, preferred_element_type=jnp.float32)
-        return res if sum_ref is None else res + sum_ref[:, at]
-
-    steps = t_ref.shape[3] // tile
-    if count is None:
-        for step in range(steps):
-            out_ref[:, pl.ds(step * tile, tile)] = column(step)
+        if last:
+            return res * scale + sum_ref[:, at]
+        if sum_ref is not None:
+            res = res + sum_ref[:, at]
+        if shift_ref is not None:
+            res = res * scale + jnp.concatenate([shift_ref[...]] * (tile // LANES), axis=1)
+        return res
+
+    if last:
+        acc_ref, done_ref, sems = take(3)
+        cols = pair_ref.shape[1]
+        pitch = cols + 1
+    unrolled = 4
+
+    def columns(r, _):
+        for u in range(unrolled):
+            step = r * unrolled + u
+            res = column(step * tile)
+            if not last:
+                out_ref[:, pl.ds(pl.multiple_of(step * tile, tile), tile)] = res
+                continue
+            for k in range(tile // LANES):
+                j = step * (tile // LANES) + k
+                acc_ref[pl.ds(j, band, stride=pitch), :] = res[:, k * LANES : (k + 1) * LANES]
+        return 0
+
+    lax.fori_loop(0, t_ref.shape[3] // tile // unrolled, columns, 0)
+    if not last:
         return
-
-    acc_ref, done_ref, sems = take(3)
-    cols = pair_ref.shape[1]
-    pitch = cols + 1
-    shift = shift_ref[...]
-    for step in range(steps):
-        res = column(step)
-        for k in range(tile // LANES):
-            j = step * (tile // LANES) + k
-            acc_ref[pl.ds(j, band, stride=pitch), :] = res[:, k * LANES : (k + 1) * LANES]
 
     chunk = 32
 
@@ -160,7 +182,7 @@
         for k in range(chunk):
             i = r * chunk + k
             row = k // 8 % 2 * (band // 2) + (r * (chunk // 16) + k // 16) * 8 + k % 8
-            total = acc_ref[pl.ds(row * pitch, cols), :] * (1.0 / count) + shift
+            total = acc_ref[pl.ds(row * pitch, cols), :]
             done_ref[i] = (pair_ref[i].astype(jnp.float32) + total).astype(jnp.bfloat16)
         at = pl.ds(pl.multiple_of(r * chunk, chunk), chunk)
         pltpu.make_async_copy(done_ref.at[at], out_ref.at[at], sems.at[r]).start()
@@ -251,12 +273,14 @@
         **specs,
     )(right, final)
 
-    def add(lines, masks, total, last):
+    def add(lines, masks, total, last, scaled=False):
         depth = len(masks) * parts * 8 * CHANS
         scratch = []
         operands = [*lines, folded] + ([] if total is None else [total])
+        if scaled and not last:
+            operands.append(shift.reshape(1, -1))
         if last:
-            operands += [pair, shift.reshape(1, -1)]
+            operands.append(pair)
             scratch += [
                 pltpu.VMEM((band * (cols + 1), zdim), jnp.float32),
                 pltpu.VMEM(pair.shape, jnp.bfloat16),
@@ -268,7 +292,7 @@
         if not small:
             in_specs[len(lines)] = anywhere
         return pl.pallas_call(
-            functools.partial(_band_kernel, masks, total is None, count if last else None, small),
+            functools.partial(_band_kernel, masks, total is None, 1.0 / count if scaled else None, last, small),
             in_specs=in_specs,
             out_specs=anywhere if last else vmem,
             out_shape=jax.ShapeDtypeStruct(pair.shape, jnp.bfloat16)
@@ -291,8 +315,8 @@
     last = [_xor(upper, 1, n)]
     lower, total = lax.optimization_barrier((lower, total))
     last.append(_xor(lower, 1, n))
-    total = add([upper, lower], (6,), total, False)
-    return add(last, (7,), total, True)
+    total = add([upper, lower], (6,), total, False, True)
+    return add(last, (7,), total, True, True)
 
 
 def solution(mesh):

time: 34.4 us -> 35.9 us (1.044)
  Pallas kernels: 12 us -> 14.5 us
  starting transfers between devices: 16.9 us -> 16.1 us
  waiting for transfers between devices: 5 us -> 4.28 us
  local copies, waits for them, and re-layouts: 0.03 us -> 0.51 us
    pallas_call x4, Pallas kernels: 6.55 us -> 7.94 us  [add(): pl.pallas_call(functools.partial(_band_kernel, masks, total is None, 1.0...]
    pallas_call x1, Pallas kernels: 2.76 us -> 3.83 us  [shards(): pl.pallas_call(_fold_kernel, out_shape=fold_out, scratch_shapes=[pltpu.VM...]
    ppermute x10, starting transfers between devices: 11.7 us -> 10.9 us  [_xor(): return lax.ppermute(x, 'row', [(i, i ^ mask) for i in range(n)])]
    ppermute x10, waiting for transfers between devices: 1.13 us -> 0.41 us  [_xor(): return lax.ppermute(x, 'row', [(i, i ^ mask) for i in range(n)])]
    unnamed x4, local copies, waits for them, and re-layouts: 0.01 us -> 0.49 us
  transfers between devices with their start and end apart: 11 -> 11, of which waited for: 4 -> 2; matrix products, arithmetic and copies ran while one was open for 0% -> 0% of each run, Pallas kernels for 22% -> 27%
where the time goes in v15:
time: 35.9 us; the launch traced here: 35.7 us
  starting transfers between devices  16.1 us (45%)
  Pallas kernels  14.5 us (40%)
  waiting for transfers between devices  4.28 us (12%)
  local copies, waits for them, and re-layouts  0.51 us (1%)
    ppermute x10, starting transfers between devices, _xor(): return lax.ppermute(x, 'row', [(i, i ^ mask) for i in range(n)])  10.9 us
    pallas_call x4, Pallas kernels, add(): pl.pallas_call(functools.partial(_band_kernel, masks, total is None, 1.0...  7.94 us
    all_to_all x1, starting transfers between devices, shards(): lax.all_to_all(right, 'row', split_axis=0, concat_axis=0, tiled=True)  5.17 us
    all_to_all x1, waiting for transfers between devices, shards(): lax.all_to_all(right, 'row', split_axis=0, concat_axis=0, tiled=True)  3.88 us
    pallas_call x1, Pallas kernels, shards(): pl.pallas_call(_fold_kernel, out_shape=fold_out, scratch_shapes=[pltpu.VM...  3.83 us
    pallas_call x1, Pallas kernels, shards(): pl.pallas_call(_project_kernel, in_specs=[anywhere] * 8, out_specs=(vmem,...  2.43 us
  transfers between devices with their start and end apart: 11, of which 2 were waited for; matrix products, arithmetic and copies ran while one was open for 0% of the time, Pallas kernels for 27%

profile of v15, /device:TPU:0, one launch (start us, length us, event | category | flops | bytes accessed | tf_op | source)
XLA Modules:
  0.0 35.7 jit_solution(3471861100723821559)
XLA Ops:
  0.0 2.4 %shard_map.100 = (bf16[256,128]{1,0:T(8,128)(2,1)S(1)}, bf16[32,8,128]{2,1,0:T(8,128)(2,1)}, bf16[1024,128]{1,0:T(8,128)(2,1)S(1)}, bf16[2,512,256]{2,1,0:T(8,128)(2,1)S(1)}) custom-call(bf16[2,512,256]{2,1,0:T(8,128)(2,1)} %refs_0_.1, f32[1,256]{1,0:T(1,128)} %bitcast.16, f32[1,256]{1,0:T(1,128)} %bitcast.17, bf16[32,256]{1,0:T(8,128)(2,1)} %bitcast.14, ...), custom_call_target="tpu_custom_call" | custom-call | flops 33554432 | bytes 524288 | tf_op jit(solution)/shard_map/pallas_call | solution.py:219
  2.4 4.1 %collective-permute-start.2 = (bf16[256,128]{1,0:T(8,128)(2,1)S(1)}, bf16[256,128]{1,0:T(8,128)(2,1)S(1)}, u32[]{:S(2)}, u32[]{:S(2)}) collective-permute-start(bf16[256,128]{1,0:T(8,128)(2,1)S(1)} %get-tuple-element.16.refs_0_), channel_id=1, source_target_pairs={{0,16},{1,17},{2,18},{3,19},{4,20},{5,21},{6,22},{7,23},{8,24},{9,... | collective-permute-start | bytes 196616 | tf_op jit(solution)/shard_map/ppermute | solution.py:202
  6.5 1.3 %collective-permute-start.1 = (bf16[256,128]{1,0:T(8,128)(2,1)S(1)}, bf16[256,128]{1,0:T(8,128)(2,1)S(1)}, u32[]{:S(2)}, u32[]{:S(2)}) collective-permute-start(bf16[256,128]{1,0:T(8,128)(2,1)S(1)} %get-tuple-element.16.refs_0_), channel_id=1, source_target_pairs={{0,24},{1,25},{2,26},{3,27},{4,28},{5,29},{6,30},{7,31},{8,16},{9,... | collective-permute-start | bytes 196616 | tf_op jit(solution)/shard_map/ppermute | solution.py:202
  7.9 0.2 collective-permute-start
  8.1 5.2 %all-to-all-start = ((bf16[32,8,128]{2,1,0:T(8,128)(2,1)}), bf16[32,8,128]{2,1,0:T(8,128)(2,1)S(1)}, u32[]{:S(2)}, u32[]{:S(2)}) async-start(bf16[32,8,128]{2,1,0:T(8,128)(2,1)} %get-tuple-element.18), calls=%async_computation | async-start | bytes 131072 | tf_op jit(solution)/shard_map/all_to_all | solution.py:236
  13.3 0.0 collective-permute-done.2.refs_3_
  13.3 0.0 collective-permute-done.1.refs_2_
  13.3 0.0 collective-permute-done.refs_1_
  13.3 0.3 shard_map.101.refs_0_
  13.6 1.8 %collective-permute-start.4 = (bf16[512,256]{1,0:T(8,128)(2,1)S(1)}, bf16[512,256]{1,0:T(8,128)(2,1)S(1)}, u32[]{:S(2)}, u32[]{:S(2)}) collective-permute-start(bf16[512,256]{1,0:T(8,128)(2,1)S(1)} %shard_map.101.refs_0_), channel_id=1, source_target_pairs={{0,4},{1,5},{2,6},{3,7},{4,0},{5,1},{6,2},{7,3},{8,12},{9,13},{10,... | collective-permute-start | bytes 786440 | tf_op jit(solution)/shard_map/ppermute | solution.py:202
  15.5 1.5 %collective-permute-start.3 = (bf16[512,256]{1,0:T(8,128)(2,1)S(1)}, bf16[512,256]{1,0:T(8,128)(2,1)S(1)}, u32[]{:S(2)}, u32[]{:S(2)}) collective-permute-start(bf16[512,256]{1,0:T(8,128)(2,1)S(1)} %shard_map.101.refs_0_), channel_id=1, source_target_pairs={{0,2},{1,3},{2,0},{3,1},{4,6},{5,7},{6,4},{7,5},{8,10},{9,11},{10,... | collective-permute-start | bytes 786440 | tf_op jit(solution)/shard_map/ppermute | solution.py:202
  16.9 3.9 %all-to-all-done.right_ref = bf16[32,8,128]{2,1,0:T(8,128)(2,1)S(1)} async-done(((bf16[32,8,128]{2,1,0:T(8,128)(2,1)}), bf16[32,8,128]{2,1,0:T(8,128)(2,1)S(1)}, u32[]{:S(2)}, u32[]{:S(2)}) %all-to-all-start) | async-done | bytes 65568 | tf_op jit(solution)/shard_map/all_to_all | solution.py:236
  20.8 3.8 %shard_map.102.refs_3_.refs_1_.refs_2_ = bf16[8,1,256,2048]{3,2,1,0:T(8,128)(2,1)S(1)} custom-call(bf16[32,8,128]{2,1,0:T(8,128)(2,1)S(1)} %all-to-all-done.right_ref, bf16[1024,128]{1,0:T(8,128)(2,1)S(1)} %get-tuple-element.19.final_ref), custom_call_target="tpu_custom_call" | custom-call | flops 2147483648 | bytes 8388608 | tf_op jit(solution)/shard_map/pallas_call | solution.py:267
  24.6 0.0 collective-permute-done.4.refs_2_
  24.7 0.0 collective-permute-done.3.refs_1_
  24.7 0.1 pad_maximum_fusion
  24.8 0.1 collective-permute-start.6
  24.9 0.6 %collective-permute-start.5 = (bf16[288,256]{1,0:T(8,128)(2,1)S(1)}, bf16[288,256]{1,0:T(8,128)(2,1)S(1)}, u32[]{:S(2)}, u32[]{:S(2)}) collective-permute-start(bf16[288,256]{1,0:T(8,128)(2,1)S(1)} %slice.6), channel_id=1, source_target_pairs={{0,4},{1,5},{2,6},{3,7},{4,0},{5,1},{6,2},{7,3},{8,12},{9,13},{10,... | collective-permute-start | bytes 442376 | tf_op jit(solution)/shard_map/ppermute | solution.py:202
  25.5 0.8 %collective-permute-start.8 = (bf16[224,256]{1,0:T(8,128)(2,1)S(1)}, bf16[224,256]{1,0:T(8,128)(2,1)S(1)}, u32[]{:S(2)}, u32[]{:S(2)}) collective-permute-start(bf16[224,256]{1,0:T(8,128)(2,1)S(1)} %slice.7), channel_id=1, source_target_pairs={{0,2},{1,3},{2,0},{3,1},{4,6},{5,7},{6,4},{7,5},{8,10},{9,11},{10,... | collective-permute-start | bytes 344072 | tf_op jit(solution)/shard_map/ppermute | solution.py:202
  26.3 2.2 %shard_map.103.refs_2_ = f32[512,2048]{1,0:T(8,128)S(1)} custom-call(bf16[512,256]{1,0:T(8,128)(2,1)S(1)} %shard_map.101.refs_0_, bf16[512,256]{1,0:T(8,128)(2,1)S(1)} %collective-permute-done.3.refs_1_, bf16[512,256]{1,0:T(8,128)(2,1)S(1)} %collective-permute-done.4.refs_2_, bf16[8,1,256,2048]{3,2,1,0:T(8,128)(2,1)S(1)} %shard_map.102.refs_3_.refs_1_.refs_2_), custom_call_target="tpu_custom_call" | custom-call | flops 1048576 | bytes 8192 | tf_op jit(solution)/shard_map/pallas_call | solution.py:294
  28.4 0.0 copy-start.1
  28.4 0.0 collective-permute-done.6.refs_0_
  28.4 2.3 %shard_map.104.refs_3_ = f32[512,2048]{1,0:T(8,128)S(1)} custom-call(bf16[3,512,256]{2,1,0:T(8,128)(2,1)S(1)} %collective-permute-done.6.refs_0_, bf16[8,1,256,2048]{3,2,1,0:T(8,128)(2,1)S(1)} %shard_map.102.refs_3_.refs_1_.refs_2_, f32[512,2048]{1,0:T(8,128)S(1)} %shard_map.103.refs_2_), custom_call_target="tpu_custom_call" | custom-call | flops 1048576 | bytes 8192 | tf_op jit(solution)/shard_map/pallas_call | solution.py:294
  30.8 0.4 %collective-permute-done.5.refs_0_ = bf16[288,256]{1,0:T(8,128)(2,1)S(1)} collective-permute-done((bf16[288,256]{1,0:T(8,128)(2,1)S(1)}, bf16[288,256]{1,0:T(8,128)(2,1)S(1)}, u32[]{:S(2)}, u32[]{:S(2)}) %collective-permute-start.5) | collective-permute-done | bytes 147488 | tf_op jit(solution)/shard_map/ppermute | solution.py:202
  31.2 0.0 collective-permute-start.7
  31.2 0.0 collective-permute-done.8.refs_1_
  31.2 0.5 %collective-permute-start.9 = (bf16[224,256]{1,0:T(8,128)(2,1)S(1)}, bf16[224,256]{1,0:T(8,128)(2,1)S(1)}, u32[]{:S(2)}, u32[]{:S(2)}) collective-permute-start(bf16[224,256]{1,0:T(8,128)(2,1)S(1)} %collective-permute-done.8.refs_1_), channel_id=1, source_target_pairs={{0,1},{1,0},{2,3},{3,2},{4,5},{5,4},{6,7},{7,6},{8,9},{9,8},{10,11... | collective-permute-start | bytes 344072 | tf_op jit(solution)/shard_map/ppermute | solution.py:202
  31.7 1.1 %shard_map.105.refs_3_ = f32[512,2048]{1,0:T(8,128)S(1)} custom-call(bf16[288,256]{1,0:T(8,128)(2,1)S(1)} %collective-permute-done.5.refs_0_, bf16[224,256]{1,0:T(8,128)(2,1)S(1)} %collective-permute-done.8.refs_1_, bf16[8,1,256,2048]{3,2,1,0:T(8,128)(2,1)S(1)} %shard_map.102.refs_3_.refs_1_.refs_2_, f32[512,2048]{1,0:T(8,128)S(1)} %shard_map.104.refs_3_, ...), custom_call_target="tpu_custom_call" | custom-call | flops 1048576 | bytes 8192 | tf_op jit(solution)/shard_map/pallas_call | solution.py:294
  32.8 0.0 collective-permute-done.9.refs_1_
  32.8 0.0 collective-permute-done.7.refs_0_
  32.8 0.5 %copy-done = bf16[512,16,128]{2,1,0:T(8,128)(2,1)S(1)} copy-done((bf16[512,16,128]{2,1,0:T(8,128)(2,1)S(1)}, bf16[512,16,128]{2,1,0:T(8,128)(2,1)}, u32[]{:S(2)}) %copy-start) | copy-done | bytes 2097176
  33.3 2.4 %shard_map.106 = bf16[512,16,128]{2,1,0:T(8,128)(2,1)} custom-call(bf16[288,256]{1,0:T(8,128)(2,1)S(1)} %collective-permute-done.7.refs_0_, bf16[224,256]{1,0:T(8,128)(2,1)S(1)} %collective-permute-done.9.refs_1_, bf16[8,1,256,2048]{3,2,1,0:T(8,128)(2,1)S(1)} %shard_map.102.refs_3_.refs_1_.refs_2_, f32[512,2048]{1,0:T(8,128)S(1)} %shard_map.105.refs_3_, ...), custom_call_target="tpu_custom_call" | custom-call | flops 1048576 | bytes 8192 | tf_op jit(solution)/shard_map/pallas_call | solution.py:294
  (4 shorter events, 0.0 us)
Async XLA Ops:
  2.4 10.9 %collective-permute-start.2 = (bf16[256,128]{1,0:T(8,128)(2,1)S(1)}, bf16[256,128]{1,0:T(8,128)(2,1)S(1)}, u32[]{:S(2)}, u32[]{:S(2)}) collective-permute-start(bf16[256,128]{1,0:T(8,128)(2,1)S(1)} %get-tuple-element.16.refs_0_), channel_id=1, source_target_pairs={{0,16},{1,17},{2,18},{3,19},{4,20},{5,21},{6,22},{7,23},{8,24},{9,... | collective-permute-start | bytes 196616 | tf_op jit(solution)/shard_map/ppermute | solution.py:202
  6.5 6.8 %collective-permute-start.1 = (bf16[256,128]{1,0:T(8,128)(2,1)S(1)}, bf16[256,128]{1,0:T(8,128)(2,1)S(1)}, u32[]{:S(2)}, u32[]{:S(2)}) collective-permute-start(bf16[256,128]{1,0:T(8,128)(2,1)S(1)} %get-tuple-element.16.refs_0_), channel_id=1, source_target_pairs={{0,24},{1,25},{2,26},{3,27},{4,28},{5,29},{6,30},{7,31},{8,16},{9,... | collective-permute-start | bytes 196616 | tf_op jit(solution)/shard_map/ppermute | solution.py:202
  7.9 5.4 %collective-permute-start = (bf16[256,128]{1,0:T(8,128)(2,1)S(1)}, bf16[256,128]{1,0:T(8,128)(2,1)S(1)}, u32[]{:S(2)}, u32[]{:S(2)}) collective-permute-start(bf16[256,128]{1,0:T(8,128)(2,1)S(1)} %get-tuple-element.16.refs_0_), channel_id=1, source_target_pairs={{0,8},{1,9},{2,10},{3,11},{4,12},{5,13},{6,14},{7,15},{8,0},{9,1},... | collective-permute-start | bytes 196616 | tf_op jit(solution)/shard_map/ppermute | solution.py:202
  8.1 12.7 %all-to-all-start = ((bf16[32,8,128]{2,1,0:T(8,128)(2,1)}), bf16[32,8,128]{2,1,0:T(8,128)(2,1)S(1)}, u32[]{:S(2)}, u32[]{:S(2)}) async-start(bf16[32,8,128]{2,1,0:T(8,128)(2,1)} %get-tuple-element.18), calls=%async_computation | async-start | bytes 131072 | tf_op jit(solution)/shard_map/all_to_all | solution.py:236
  13.6 11.0 %collective-permute-start.4 = (bf16[512,256]{1,0:T(8,128)(2,1)S(1)}, bf16[512,256]{1,0:T(8,128)(2,1)S(1)}, u32[]{:S(2)}, u32[]{:S(2)}) collective-permute-start(bf16[512,256]{1,0:T(8,128)(2,1)S(1)} %shard_map.101.refs_0_), channel_id=1, source_target_pairs={{0,4},{1,5},{2,6},{3,7},{4,0},{5,1},{6,2},{7,3},{8,12},{9,13},{10,... | collective-permute-start | bytes 786440 | tf_op jit(solution)/shard_map/ppermute | solution.py:202
  15.5 9.2 %collective-permute-start.3 = (bf16[512,256]{1,0:T(8,128)(2,1)S(1)}, bf16[512,256]{1,0:T(8,128)(2,1)S(1)}, u32[]{:S(2)}, u32[]{:S(2)}) collective-permute-start(bf16[512,256]{1,0:T(8,128)(2,1)S(1)} %shard_map.101.refs_0_), channel_id=1, source_target_pairs={{0,2},{1,3},{2,0},{3,1},{4,6},{5,7},{6,4},{7,5},{8,10},{9,11},{10,... | collective-permute-start | bytes 786440 | tf_op jit(solution)/shard_map/ppermute | solution.py:202
  24.8 3.7 %collective-permute-start.6 = (bf16[3,512,256]{2,1,0:T(8,128)(2,1)S(1)}, bf16[3,512,256]{2,1,0:T(8,128)(2,1)S(1)}, u32[]{:S(2)}, u32[]{:S(2)}) collective-permute-start(bf16[3,512,256]{2,1,0:T(8,128)(2,1)S(1)} %pad_maximum_fusion), channel_id=1, source_target_pairs={{0,1},{1,0},{2,3},{3,2},{4,5},{5,4},{6,7},{7,6},{8,9},{9,8},{10,11... | collective-permute-start | bytes 2359304 | tf_op jit(solution)/shard_map/ppermute | solution.py:202
  24.9 6.3 %collective-permute-start.5 = (bf16[288,256]{1,0:T(8,128)(2,1)S(1)}, bf16[288,256]{1,0:T(8,128)(2,1)S(1)}, u32[]{:S(2)}, u32[]{:S(2)}) collective-permute-start(bf16[288,256]{1,0:T(8,128)(2,1)S(1)} %slice.6), channel_id=1, source_target_pairs={{0,4},{1,5},{2,6},{3,7},{4,0},{5,1},{6,2},{7,3},{8,12},{9,13},{10,... | collective-permute-start | bytes 442376 | tf_op jit(solution)/shard_map/ppermute | solution.py:202
  25.5 5.7 %collective-permute-start.8 = (bf16[224,256]{1,0:T(8,128)(2,1)S(1)}, bf16[224,256]{1,0:T(8,128)(2,1)S(1)}, u32[]{:S(2)}, u32[]{:S(2)}) collective-permute-start(bf16[224,256]{1,0:T(8,128)(2,1)S(1)} %slice.7), channel_id=1, source_target_pairs={{0,2},{1,3},{2,0},{3,1},{4,6},{5,7},{6,4},{7,5},{8,10},{9,11},{10,... | collective-permute-start | bytes 344072 | tf_op jit(solution)/shard_map/ppermute | solution.py:202
  28.4 3.3 %copy-start.1 = (f32[128]{0:T(128)S(1)}, f32[128]{0:T(128)}, u32[]{:S(2)}) copy-start(f32[128]{0:T(128)} %param.19) | copy-start | bytes 1540
  31.2 1.6 %collective-permute-start.7 = (bf16[288,256]{1,0:T(8,128)(2,1)S(1)}, bf16[288,256]{1,0:T(8,128)(2,1)S(1)}, u32[]{:S(2)}, u32[]{:S(2)}) collective-permute-start(bf16[288,256]{1,0:T(8,128)(2,1)S(1)} %collective-permute-done.5.refs_0_), channel_id=1, source_target_pairs={{0,1},{1,0},{2,3},{3,2},{4,5},{5,4},{6,7},{7,6},{8,9},{9,8},{10,11... | collective-permute-start | bytes 442376 | tf_op jit(solution)/shard_map/ppermute | solution.py:202
  31.2 1.6 %collective-permute-start.9 = (bf16[224,256]{1,0:T(8,128)(2,1)S(1)}, bf16[224,256]{1,0:T(8,128)(2,1)S(1)}, u32[]{:S(2)}, u32[]{:S(2)}) collective-permute-start(bf16[224,256]{1,0:T(8,128)(2,1)S(1)} %collective-permute-done.8.refs_1_), channel_id=1, source_target_pairs={{0,1},{1,0},{2,3},{3,2},{4,5},{5,4},{6,7},{7,6},{8,9},{9,8},{10,11... | collective-permute-start | bytes 344072 | tf_op jit(solution)/shard_map/ppermute | solution.py:202
  31.7 1.6 %copy-start = (bf16[512,16,128]{2,1,0:T(8,128)(2,1)S(1)}, bf16[512,16,128]{2,1,0:T(8,128)(2,1)}, u32[]{:S(2)}) copy-start(bf16[512,16,128]{2,1,0:T(8,128)(2,1)} %refs_4_.1) | copy-start | bytes 6291460

commit v16 on v14

--- a/solution.py
+++ b/solution.py
@@ -107,7 +107,7 @@
                 out_ref[g, 0, pl.ds(pair * 16, 16), pl.ds(j * LANES, LANES)] = tile.astype(jnp.bfloat16)
 
 
-def _band_kernel(masks, begins, count, held, *refs):
+def _band_kernel(masks, begins, scale, last, held, *refs):
     refs = list(refs)
     take = lambda k: [refs.pop(0) for _ in range(k)]
     if masks == (1, 3, 5):
@@ -117,17 +117,18 @@
         lines = [take(2 if mask in (6, 7) else 1) for mask in masks]
     (t_ref,) = take(1)
     (sum_ref,) = (None,) if begins else take(1)
-    pair_ref, shift_ref = (None, None) if count is None else take(2)
+    shift_ref = None if scale is None or last else take(1)[0]
+    pair_ref = take(1)[0] if last else None
     (out_ref,) = take(1)
     me = lax.axis_index("row")
     wide = t_ref.shape[2]
     chunks = [((me % 8) ^ mask, q ^ (me // 32)) for mask in masks for q in range(t_ref.shape[1])]
 
-    tile = 256
+    tile = 256 if last or not held else 512
     band = sum(part.shape[0] for part in lines[0])
 
-    def column(step):
-        at = pl.ds(step * tile, tile)
+    def column(begin):
+        at = pl.ds(begin, tile)
         if held:
             rhs = jnp.concatenate([t_ref[g, q, :, at] for g, q in chunks], axis=0)
         else:
@@ -136,23 +137,30 @@
             rhs = refs[0][...]
         lhs = jnp.concatenate([jnp.concatenate([part[...] for part in line], axis=0) for line in lines], axis=1)
         res = jnp.dot(lhs, rhs, preferred_element_type=jnp.float32)
-        return res if sum_ref is None else res + sum_ref[:, at]
-
-    steps = t_ref.shape[3] // tile
-    if count is None:
-        for step in range(steps):
-            out_ref[:, pl.ds(step * tile, tile)] = column(step)
+        if last:
+            return res * scale + sum_ref[:, at]
+        if sum_ref is not None:
+            res = res + sum_ref[:, at]
+        if shift_ref is not None:
+            res = res * scale + jnp.concatenate([shift_ref[...]] * (tile // LANES), axis=1)
+        return res
+
+    if not last:
+        for begin in range(0, t_ref.shape[3], tile):
+            out_ref[:, pl.ds(begin, tile)] = column(begin)
         return
 
-    acc_ref, done_ref, sems = take(3)
+    acc_ref, done_ref, sems, fetched_sem = take(4)
     cols = pair_ref.shape[1]
     pitch = cols + 1
-    shift = shift_ref[...]
-    for step in range(steps):
-        res = column(step)
+    fetch = pltpu.make_async_copy(pair_ref, done_ref, fetched_sem)
+    fetch.start()
+    for begin in range(0, t_ref.shape[3], tile):
+        res = column(begin)
         for k in range(tile // LANES):
-            j = step * (tile // LANES) + k
+            j = begin // LANES + k
             acc_ref[pl.ds(j, band, stride=pitch), :] = res[:, k * LANES : (k + 1) * LANES]
+    fetch.wait()
 
     chunk = 32
 
@@ -160,8 +168,8 @@
         for k in range(chunk):
             i = r * chunk + k
             row = k // 8 % 2 * (band // 2) + (r * (chunk // 16) + k // 16) * 8 + k % 8
-            total = acc_ref[pl.ds(row * pitch, cols), :] * (1.0 / count) + shift
-            done_ref[i] = (pair_ref[i].astype(jnp.float32) + total).astype(jnp.bfloat16)
+            total = acc_ref[pl.ds(row * pitch, cols), :]
+            done_ref[i] = (done_ref[i].astype(jnp.float32) + total).astype(jnp.bfloat16)
         at = pl.ds(pl.multiple_of(r * chunk, chunk), chunk)
         pltpu.make_async_copy(done_ref.at[at], out_ref.at[at], sems.at[r]).start()
         return 0
@@ -251,24 +259,27 @@
         **specs,
     )(right, final)
 
-    def add(lines, masks, total, last):
+    def add(lines, masks, total, last, scaled=False):
         depth = len(masks) * parts * 8 * CHANS
         scratch = []
         operands = [*lines, folded] + ([] if total is None else [total])
+        if scaled and not last:
+            operands.append(shift.reshape(1, -1))
         if last:
-            operands += [pair, shift.reshape(1, -1)]
+            operands.append(pltpu.with_memory_space_constraint(pair, pltpu.HBM))
             scratch += [
                 pltpu.VMEM((band * (cols + 1), zdim), jnp.float32),
                 pltpu.VMEM(pair.shape, jnp.bfloat16),
                 pltpu.SemaphoreType.DMA((band // 32,)),
+                pltpu.SemaphoreType.DMA(()),
             ]
         if not small:
             scratch.append(pltpu.VMEM((depth, 256), jnp.bfloat16))
-        in_specs = [vmem] * len(operands)
+        in_specs = [vmem] * (len(operands) - last) + [anywhere] * last
         if not small:
             in_specs[len(lines)] = anywhere
         return pl.pallas_call(
-            functools.partial(_band_kernel, masks, total is None, count if last else None, small),
+            functools.partial(_band_kernel, masks, total is None, 1.0 / count if scaled else None, last, small),
             in_specs=in_specs,
             out_specs=anywhere if last else vmem,
             out_shape=jax.ShapeDtypeStruct(pair.shape, jnp.bfloat16)
@@ -291,8 +302,8 @@
     last = [_xor(upper, 1, n)]
     lower, total = lax.optimization_barrier((lower, total))
     last.append(_xor(lower, 1, n))
-    total = add([upper, lower], (6,), total, False)
-    return add(last, (7,), total, True)
+    total = add([upper, lower], (6,), total, False, True)
+    return add(last, (7,), total, True, True)
 
 
 def solution(mesh):

time: 34.4 us -> 35.2 us (1.023)
  Pallas kernels: 12 us -> 12.9 us
    pallas_call x4, Pallas kernels: 6.55 us -> 7.38 us  [add(): pl.pallas_call(functools.partial(_band_kernel, masks, total is None, 1.0...]
  transfers between devices with their start and end apart: 11 -> 11, of which waited for: 4 -> 4; matrix products, arithmetic and copies ran while one was open for 0% -> 0% of each run, Pallas kernels for 22% -> 21%
where the time goes in v16:
time: 35.2 us; the launch traced here: 35 us
  starting transfers between devices  16.9 us (48%)
  Pallas kernels  12.9 us (37%)
  waiting for transfers between devices  5 us (14%)
    ppermute x10, starting transfers between devices, _xor(): return lax.ppermute(x, 'row', [(i, i ^ mask) for i in range(n)])  11.7 us
    pallas_call x4, Pallas kernels, add(): pl.pallas_call(functools.partial(_band_kernel, masks, total is None, 1.0...  7.38 us
    all_to_all x1, starting transfers between devices, shards(): lax.all_to_all(right, 'row', split_axis=0, concat_axis=0, tiled=True)  5.17 us
    all_to_all x1, waiting for transfers between devices, shards(): lax.all_to_all(right, 'row', split_axis=0, concat_axis=0, tiled=True)  3.88 us
    pallas_call x1, Pallas kernels, shards(): pl.pallas_call(_fold_kernel, out_shape=fold_out, scratch_shapes=[pltpu.VM...  2.76 us
    pallas_call x1, Pallas kernels, shards(): pl.pallas_call(_project_kernel, in_specs=[anywhere] * 8, out_specs=(vmem,...  2.43 us
    ppermute x10, waiting for transfers between devices, _xor(): return lax.ppermute(x, 'row', [(i, i ^ mask) for i in range(n)])  1.13 us
  transfers between devices with their start and end apart: 11, of which 4 were waited for; matrix products, arithmetic and copies ran while one was open for 0% of the time, Pallas kernels for 21%

profile of v16, /device:TPU:0, one launch (start us, length us, event | category | flops | bytes accessed | tf_op | source)
XLA Modules:
  0.0 35.0 jit_solution(18120639788516224911)
XLA Ops:
  0.0 2.4 %shard_map.100 = (bf16[256,128]{1,0:T(8,128)(2,1)S(1)}, bf16[32,8,128]{2,1,0:T(8,128)(2,1)}, bf16[1024,128]{1,0:T(8,128)(2,1)S(1)}, bf16[2,512,256]{2,1,0:T(8,128)(2,1)S(1)}) custom-call(bf16[2,512,256]{2,1,0:T(8,128)(2,1)} %refs_0_.1, f32[1,256]{1,0:T(1,128)} %bitcast.16, f32[1,256]{1,0:T(1,128)} %bitcast.17, bf16[32,256]{1,0:T(8,128)(2,1)} %bitcast.14, ...), custom_call_target="tpu_custom_call" | custom-call | flops 33554432 | bytes 524288 | tf_op jit(solution)/shard_map/pallas_call | solution.py:205
  2.4 4.1 %collective-permute-start.2 = (bf16[256,128]{1,0:T(8,128)(2,1)S(1)}, bf16[256,128]{1,0:T(8,128)(2,1)S(1)}, u32[]{:S(2)}, u32[]{:S(2)}) collective-permute-start(bf16[256,128]{1,0:T(8,128)(2,1)S(1)} %get-tuple-element.16.refs_0_), channel_id=1, source_target_pairs={{0,16},{1,17},{2,18},{3,19},{4,20},{5,21},{6,22},{7,23},{8,24},{9,... | collective-permute-start | bytes 196616 | tf_op jit(solution)/shard_map/ppermute | solution.py:188
  6.5 1.3 %collective-permute-start.1 = (bf16[256,128]{1,0:T(8,128)(2,1)S(1)}, bf16[256,128]{1,0:T(8,128)(2,1)S(1)}, u32[]{:S(2)}, u32[]{:S(2)}) collective-permute-start(bf16[256,128]{1,0:T(8,128)(2,1)S(1)} %get-tuple-element.16.refs_0_), channel_id=1, source_target_pairs={{0,24},{1,25},{2,26},{3,27},{4,28},{5,29},{6,30},{7,31},{8,16},{9,... | collective-permute-start | bytes 196616 | tf_op jit(solution)/shard_map/ppermute | solution.py:188
  7.9 0.2 collective-permute-start
  8.1 5.2 %all-to-all-start = ((bf16[32,8,128]{2,1,0:T(8,128)(2,1)}), bf16[32,8,128]{2,1,0:T(8,128)(2,1)S(1)}, u32[]{:S(2)}, u32[]{:S(2)}) async-start(bf16[32,8,128]{2,1,0:T(8,128)(2,1)} %get-tuple-element.18), calls=%async_computation | async-start | bytes 131072 | tf_op jit(solution)/shard_map/all_to_all | solution.py:222
  13.3 0.0 collective-permute-done.2.refs_3_
  13.3 0.0 collective-permute-done.1.refs_2_
  13.3 0.0 collective-permute-done.refs_1_
  13.3 0.3 shard_map.101.refs_0_
  13.6 1.8 %collective-permute-start.4 = (bf16[512,256]{1,0:T(8,128)(2,1)S(1)}, bf16[512,256]{1,0:T(8,128)(2,1)S(1)}, u32[]{:S(2)}, u32[]{:S(2)}) collective-permute-start(bf16[512,256]{1,0:T(8,128)(2,1)S(1)} %shard_map.101.refs_0_), channel_id=1, source_target_pairs={{0,4},{1,5},{2,6},{3,7},{4,0},{5,1},{6,2},{7,3},{8,12},{9,13},{10,... | collective-permute-start | bytes 786440 | tf_op jit(solution)/shard_map/ppermute | solution.py:188
  15.5 1.5 %collective-permute-start.3 = (bf16[512,256]{1,0:T(8,128)(2,1)S(1)}, bf16[512,256]{1,0:T(8,128)(2,1)S(1)}, u32[]{:S(2)}, u32[]{:S(2)}) collective-permute-start(bf16[512,256]{1,0:T(8,128)(2,1)S(1)} %shard_map.101.refs_0_), channel_id=1, source_target_pairs={{0,2},{1,3},{2,0},{3,1},{4,6},{5,7},{6,4},{7,5},{8,10},{9,11},{10,... | collective-permute-start | bytes 786440 | tf_op jit(solution)/shard_map/ppermute | solution.py:188
  16.9 3.9 %all-to-all-done.right_ref = bf16[32,8,128]{2,1,0:T(8,128)(2,1)S(1)} async-done(((bf16[32,8,128]{2,1,0:T(8,128)(2,1)}), bf16[32,8,128]{2,1,0:T(8,128)(2,1)S(1)}, u32[]{:S(2)}, u32[]{:S(2)}) %all-to-all-start) | async-done | bytes 65568 | tf_op jit(solution)/shard_map/all_to_all | solution.py:222
  20.8 2.8 %shard_map.102.refs_3_.refs_1_.refs_2_ = bf16[8,1,256,2048]{3,2,1,0:T(8,128)(2,1)S(1)} custom-call(bf16[32,8,128]{2,1,0:T(8,128)(2,1)S(1)} %all-to-all-done.right_ref, bf16[1024,128]{1,0:T(8,128)(2,1)S(1)} %get-tuple-element.19.final_ref), custom_call_target="tpu_custom_call" | custom-call | flops 2147483648 | bytes 8388608 | tf_op jit(solution)/shard_map/pallas_call | solution.py:253
  23.6 0.0 collective-permute-done.4.refs_2_
  23.6 0.3 collective-permute-done.3.refs_1_
  23.9 0.1 pad_maximum_fusion
  24.0 0.1 collective-permute-start.6
  24.1 0.6 %collective-permute-start.5 = (bf16[288,256]{1,0:T(8,128)(2,1)S(1)}, bf16[288,256]{1,0:T(8,128)(2,1)S(1)}, u32[]{:S(2)}, u32[]{:S(2)}) collective-permute-start(bf16[288,256]{1,0:T(8,128)(2,1)S(1)} %slice.6), channel_id=1, source_target_pairs={{0,4},{1,5},{2,6},{3,7},{4,0},{5,1},{6,2},{7,3},{8,12},{9,13},{10,... | collective-permute-start | bytes 442376 | tf_op jit(solution)/shard_map/ppermute | solution.py:188
  24.7 1.6 %collective-permute-start.8 = (bf16[224,256]{1,0:T(8,128)(2,1)S(1)}, bf16[224,256]{1,0:T(8,128)(2,1)S(1)}, u32[]{:S(2)}, u32[]{:S(2)}) collective-permute-start(bf16[224,256]{1,0:T(8,128)(2,1)S(1)} %slice.7), channel_id=1, source_target_pairs={{0,2},{1,3},{2,0},{3,1},{4,6},{5,7},{6,4},{7,5},{8,10},{9,11},{10,... | collective-permute-start | bytes 344072 | tf_op jit(solution)/shard_map/ppermute | solution.py:188
  26.3 1.8 %shard_map.103.refs_2_ = f32[512,2048]{1,0:T(8,128)S(1)} custom-call(bf16[512,256]{1,0:T(8,128)(2,1)S(1)} %shard_map.101.refs_0_, bf16[512,256]{1,0:T(8,128)(2,1)S(1)} %collective-permute-done.3.refs_1_, bf16[512,256]{1,0:T(8,128)(2,1)S(1)} %collective-permute-done.4.refs_2_, bf16[8,1,256,2048]{3,2,1,0:T(8,128)(2,1)S(1)} %shard_map.102.refs_3_.refs_1_.refs_2_), custom_call_target="tpu_custom_call" | custom-call | flops 1048576 | bytes 8192 | tf_op jit(solution)/shard_map/pallas_call | solution.py:281
  28.1 0.0 copy-start
  28.1 0.0 collective-permute-done.6.refs_0_
  28.1 1.8 %shard_map.104.refs_3_ = f32[512,2048]{1,0:T(8,128)S(1)} custom-call(bf16[3,512,256]{2,1,0:T(8,128)(2,1)S(1)} %collective-permute-done.6.refs_0_, bf16[8,1,256,2048]{3,2,1,0:T(8,128)(2,1)S(1)} %shard_map.102.refs_3_.refs_1_.refs_2_, f32[512,2048]{1,0:T(8,128)S(1)} %shard_map.103.refs_2_), custom_call_target="tpu_custom_call" | custom-call | flops 1048576 | bytes 8192 | tf_op jit(solution)/shard_map/pallas_call | solution.py:281
  29.9 0.5 %collective-permute-done.5.refs_0_ = bf16[288,256]{1,0:T(8,128)(2,1)S(1)} collective-permute-done((bf16[288,256]{1,0:T(8,128)(2,1)S(1)}, bf16[288,256]{1,0:T(8,128)(2,1)S(1)}, u32[]{:S(2)}, u32[]{:S(2)}) %collective-permute-start.5) | collective-permute-done | bytes 147488 | tf_op jit(solution)/shard_map/ppermute | solution.py:188
  30.4 0.0 collective-permute-start.7
  30.4 0.0 collective-permute-done.8.refs_1_
  30.4 0.5 %collective-permute-start.9 = (bf16[224,256]{1,0:T(8,128)(2,1)S(1)}, bf16[224,256]{1,0:T(8,128)(2,1)S(1)}, u32[]{:S(2)}, u32[]{:S(2)}) collective-permute-start(bf16[224,256]{1,0:T(8,128)(2,1)S(1)} %collective-permute-done.8.refs_1_), channel_id=1, source_target_pairs={{0,1},{1,0},{2,3},{3,2},{4,5},{5,4},{6,7},{7,6},{8,9},{9,8},{10,11... | collective-permute-start | bytes 344072 | tf_op jit(solution)/shard_map/ppermute | solution.py:188
  30.9 0.0 copy-done
  30.9 0.7 %shard_map.105.refs_3_ = f32[512,2048]{1,0:T(8,128)S(1)} custom-call(bf16[288,256]{1,0:T(8,128)(2,1)S(1)} %collective-permute-done.5.refs_0_, bf16[224,256]{1,0:T(8,128)(2,1)S(1)} %collective-permute-done.8.refs_1_, bf16[8,1,256,2048]{3,2,1,0:T(8,128)(2,1)S(1)} %shard_map.102.refs_3_.refs_1_.refs_2_, f32[512,2048]{1,0:T(8,128)S(1)} %shard_map.104.refs_3_, ...), custom_call_target="tpu_custom_call" | custom-call | flops 1048576 | bytes 8192 | tf_op jit(solution)/shard_map/pallas_call | solution.py:281
  31.6 0.3 collective-permute-done.9.refs_1_
  31.9 0.0 collective-permute-done.7.refs_0_
  31.9 3.1 %shard_map.106 = bf16[512,16,128]{2,1,0:T(8,128)(2,1)} custom-call(bf16[288,256]{1,0:T(8,128)(2,1)S(1)} %collective-permute-done.7.refs_0_, bf16[224,256]{1,0:T(8,128)(2,1)S(1)} %collective-permute-done.9.refs_1_, bf16[8,1,256,2048]{3,2,1,0:T(8,128)(2,1)S(1)} %shard_map.102.refs_3_.refs_1_.refs_2_, f32[512,2048]{1,0:T(8,128)S(1)} %shard_map.105.refs_3_, ...), custom_call_target="tpu_custom_call" | custom-call | flops 1048576 | bytes 8192 | tf_op jit(solution)/shard_map/pallas_call | solution.py:281
  (2 shorter events, 0.0 us)
Async XLA Ops:
  2.4 10.9 %collective-permute-start.2 = (bf16[256,128]{1,0:T(8,128)(2,1)S(1)}, bf16[256,128]{1,0:T(8,128)(2,1)S(1)}, u32[]{:S(2)}, u32[]{:S(2)}) collective-permute-start(bf16[256,128]{1,0:T(8,128)(2,1)S(1)} %get-tuple-element.16.refs_0_), channel_id=1, source_target_pairs={{0,16},{1,17},{2,18},{3,19},{4,20},{5,21},{6,22},{7,23},{8,24},{9,... | collective-permute-start | bytes 196616 | tf_op jit(solution)/shard_map/ppermute | solution.py:188
  6.5 6.8 %collective-permute-start.1 = (bf16[256,128]{1,0:T(8,128)(2,1)S(1)}, bf16[256,128]{1,0:T(8,128)(2,1)S(1)}, u32[]{:S(2)}, u32[]{:S(2)}) collective-permute-start(bf16[256,128]{1,0:T(8,128)(2,1)S(1)} %get-tuple-element.16.refs_0_), channel_id=1, source_target_pairs={{0,24},{1,25},{2,26},{3,27},{4,28},{5,29},{6,30},{7,31},{8,16},{9,... | collective-permute-start | bytes 196616 | tf_op jit(solution)/shard_map/ppermute | solution.py:188
  7.9 5.4 %collective-permute-start = (bf16[256,128]{1,0:T(8,128)(2,1)S(1)}, bf16[256,128]{1,0:T(8,128)(2,1)S(1)}, u32[]{:S(2)}, u32[]{:S(2)}) collective-permute-start(bf16[256,128]{1,0:T(8,128)(2,1)S(1)} %get-tuple-element.16.refs_0_), channel_id=1, source_target_pairs={{0,8},{1,9},{2,10},{3,11},{4,12},{5,13},{6,14},{7,15},{8,0},{9,1},... | collective-permute-start | bytes 196616 | tf_op jit(solution)/shard_map/ppermute | solution.py:188
  8.1 12.7 %all-to-all-start = ((bf16[32,8,128]{2,1,0:T(8,128)(2,1)}), bf16[32,8,128]{2,1,0:T(8,128)(2,1)S(1)}, u32[]{:S(2)}, u32[]{:S(2)}) async-start(bf16[32,8,128]{2,1,0:T(8,128)(2,1)} %get-tuple-element.18), calls=%async_computation | async-start | bytes 131072 | tf_op jit(solution)/shard_map/all_to_all | solution.py:222
  13.6 9.9 %collective-permute-start.4 = (bf16[512,256]{1,0:T(8,128)(2,1)S(1)}, bf16[512,256]{1,0:T(8,128)(2,1)S(1)}, u32[]{:S(2)}, u32[]{:S(2)}) collective-permute-start(bf16[512,256]{1,0:T(8,128)(2,1)S(1)} %shard_map.101.refs_0_), channel_id=1, source_target_pairs={{0,4},{1,5},{2,6},{3,7},{4,0},{5,1},{6,2},{7,3},{8,12},{9,13},{10,... | collective-permute-start | bytes 786440 | tf_op jit(solution)/shard_map/ppermute | solution.py:188
  15.5 8.4 %collective-permute-start.3 = (bf16[512,256]{1,0:T(8,128)(2,1)S(1)}, bf16[512,256]{1,0:T(8,128)(2,1)S(1)}, u32[]{:S(2)}, u32[]{:S(2)}) collective-permute-start(bf16[512,256]{1,0:T(8,128)(2,1)S(1)} %shard_map.101.refs_0_), channel_id=1, source_target_pairs={{0,2},{1,3},{2,0},{3,1},{4,6},{5,7},{6,4},{7,5},{8,10},{9,11},{10,... | collective-permute-start | bytes 786440 | tf_op jit(solution)/shard_map/ppermute | solution.py:188
  24.0 4.1 %collective-permute-start.6 = (bf16[3,512,256]{2,1,0:T(8,128)(2,1)S(1)}, bf16[3,512,256]{2,1,0:T(8,128)(2,1)S(1)}, u32[]{:S(2)}, u32[]{:S(2)}) collective-permute-start(bf16[3,512,256]{2,1,0:T(8,128)(2,1)S(1)} %pad_maximum_fusion), channel_id=1, source_target_pairs={{0,1},{1,0},{2,3},{3,2},{4,5},{5,4},{6,7},{7,6},{8,9},{9,8},{10,11... | collective-permute-start | bytes 2359304 | tf_op jit(solution)/shard_map/ppermute | solution.py:188
  24.1 6.3 %collective-permute-start.5 = (bf16[288,256]{1,0:T(8,128)(2,1)S(1)}, bf16[288,256]{1,0:T(8,128)(2,1)S(1)}, u32[]{:S(2)}, u32[]{:S(2)}) collective-permute-start(bf16[288,256]{1,0:T(8,128)(2,1)S(1)} %slice.6), channel_id=1, source_target_pairs={{0,4},{1,5},{2,6},{3,7},{4,0},{5,1},{6,2},{7,3},{8,12},{9,13},{10,... | collective-permute-start | bytes 442376 | tf_op jit(solution)/shard_map/ppermute | solution.py:188
  24.7 5.7 %collective-permute-start.8 = (bf16[224,256]{1,0:T(8,128)(2,1)S(1)}, bf16[224,256]{1,0:T(8,128)(2,1)S(1)}, u32[]{:S(2)}, u32[]{:S(2)}) collective-permute-start(bf16[224,256]{1,0:T(8,128)(2,1)S(1)} %slice.7), channel_id=1, source_target_pairs={{0,2},{1,3},{2,0},{3,1},{4,6},{5,7},{6,4},{7,5},{8,10},{9,11},{10,... | collective-permute-start | bytes 344072 | tf_op jit(solution)/shard_map/ppermute | solution.py:188
  28.1 2.9 %copy-start = (f32[128]{0:T(128)S(1)}, f32[128]{0:T(128)}, u32[]{:S(2)}) copy-start(f32[128]{0:T(128)} %param.19) | copy-start | bytes 1540
  30.4 1.5 %collective-permute-start.7 = (bf16[288,256]{1,0:T(8,128)(2,1)S(1)}, bf16[288,256]{1,0:T(8,128)(2,1)S(1)}, u32[]{:S(2)}, u32[]{:S(2)}) collective-permute-start(bf16[288,256]{1,0:T(8,128)(2,1)S(1)} %collective-permute-done.5.refs_0_), channel_id=1, source_target_pairs={{0,1},{1,0},{2,3},{3,2},{4,5},{5,4},{6,7},{7,6},{8,9},{9,8},{10,11... | collective-permute-start | bytes 442376 | tf_op jit(solution)/shard_map/ppermute | solution.py:188
  30.4 1.5 %collective-permute-start.9 = (bf16[224,256]{1,0:T(8,128)(2,1)S(1)}, bf16[224,256]{1,0:T(8,128)(2,1)S(1)}, u32[]{:S(2)}, u32[]{:S(2)}) collective-permute-start(bf16[224,256]{1,0:T(8,128)(2,1)S(1)} %collective-permute-done.8.refs_1_), channel_id=1, source_target_pairs={{0,1},{1,0},{2,3},{3,2},{4,5},{5,4},{6,7},{7,6},{8,9},{9,8},{10,11... | collective-permute-start | bytes 344072 | tf_op jit(solution)/shard_map/ppermute | solution.py:188

commit v17 on v16

--- a/solution.py
+++ b/solution.py
@@ -118,8 +118,13 @@
     (t_ref,) = take(1)
     (sum_ref,) = (None,) if begins else take(1)
     shift_ref = None if scale is None or last else take(1)[0]
-    pair_ref = take(1)[0] if last else None
+    carries = masks == (1, 3, 5)
+    pair_ref = take(1)[0] if last or carries else None
     (out_ref,) = take(1)
+    if carries:
+        held_pair, pair_sem = take(2)
+        fetch = pltpu.make_async_copy(pair_ref, held_pair, pair_sem)
+        fetch.start()
     me = lax.axis_index("row")
     wide = t_ref.shape[2]
     chunks = [((me % 8) ^ mask, q ^ (me // 32)) for mask in masks for q in range(t_ref.shape[1])]
@@ -148,19 +153,18 @@
     if not last:
         for begin in range(0, t_ref.shape[3], tile):
             out_ref[:, pl.ds(begin, tile)] = column(begin)
+        if carries:
+            fetch.wait()
         return
 
-    acc_ref, done_ref, sems, fetched_sem = take(4)
+    acc_ref, done_ref, sems = take(3)
     cols = pair_ref.shape[1]
     pitch = cols + 1
-    fetch = pltpu.make_async_copy(pair_ref, done_ref, fetched_sem)
-    fetch.start()
     for begin in range(0, t_ref.shape[3], tile):
         res = column(begin)
         for k in range(tile // LANES):
             j = begin // LANES + k
             acc_ref[pl.ds(j, band, stride=pitch), :] = res[:, k * LANES : (k + 1) * LANES]
-    fetch.wait()
 
     chunk = 32
 
@@ -169,7 +173,7 @@
             i = r * chunk + k
             row = k // 8 % 2 * (band // 2) + (r * (chunk // 16) + k // 16) * 8 + k % 8
             total = acc_ref[pl.ds(row * pitch, cols), :]
-            done_ref[i] = (done_ref[i].astype(jnp.float32) + total).astype(jnp.bfloat16)
+            done_ref[i] = (pair_ref[i].astype(jnp.float32) + total).astype(jnp.bfloat16)
         at = pl.ds(pl.multiple_of(r * chunk, chunk), chunk)
         pltpu.make_async_copy(done_ref.at[at], out_ref.at[at], sems.at[r]).start()
         return 0
@@ -259,32 +263,40 @@
         **specs,
     )(right, final)
 
-    def add(lines, masks, total, last, scaled=False):
+    pinned = pltpu.with_memory_space_constraint(pair, pltpu.HBM)
+
+    def add(lines, masks, total, last=False, scaled=False, carried=None):
         depth = len(masks) * parts * 8 * CHANS
-        scratch = []
+        carries = masks == (1, 3, 5)
         operands = [*lines, folded] + ([] if total is None else [total])
+        in_specs = [vmem] * len(operands)
+        if not small:
+            in_specs[len(lines)] = anywhere
         if scaled and not last:
             operands.append(shift.reshape(1, -1))
+            in_specs.append(vmem)
+        out_shape, out_specs, scratch = jax.ShapeDtypeStruct((band, cols * zdim), jnp.float32), vmem, []
+        if carries:
+            operands.append(pinned)
+            in_specs.append(anywhere)
+            out_shape, out_specs = (out_shape, jax.ShapeDtypeStruct(pair.shape, pair.dtype)), (vmem, vmem)
+            scratch = [pltpu.SemaphoreType.DMA(())]
         if last:
-            operands.append(pltpu.with_memory_space_constraint(pair, pltpu.HBM))
-            scratch += [
+            operands.append(carried)
+            in_specs.append(vmem)
+            out_shape, out_specs = jax.ShapeDtypeStruct(pair.shape, jnp.bfloat16), anywhere
+            scratch = [
                 pltpu.VMEM((band * (cols + 1), zdim), jnp.float32),
                 pltpu.VMEM(pair.shape, jnp.bfloat16),
                 pltpu.SemaphoreType.DMA((band // 32,)),
-                pltpu.SemaphoreType.DMA(()),
             ]
         if not small:
             scratch.append(pltpu.VMEM((depth, 256), jnp.bfloat16))
-        in_specs = [vmem] * (len(operands) - last) + [anywhere] * last
-        if not small:
-            in_specs[len(lines)] = anywhere
         return pl.pallas_call(
             functools.partial(_band_kernel, masks, total is None, 1.0 / count if scaled else None, last, small),
             in_specs=in_specs,
-            out_specs=anywhere if last else vmem,
-            out_shape=jax.ShapeDtypeStruct(pair.shape, jnp.bfloat16)
-            if last
-            else jax.ShapeDtypeStruct((band, cols * zdim), jnp.float32),
+            out_specs=out_specs,
+            out_shape=out_shape,
             scratch_shapes=scratch,
             compiler_params=params,
             cost_estimate=pl.CostEstimate(
@@ -296,14 +308,14 @@
     cut = band * 9 // 16
     upper, lower = _xor(x[:cut], 4, n), _xor(y[cut:], 2, n)
     across = _xor(jnp.stack([line, x, y]), 1, n)
-    total = add([line, x, y], (0, 2, 4), None, False)
-    total = add([across], (1, 3, 5), total, False)
+    total = add([line, x, y], (0, 2, 4), None)
+    total, carried = add([across], (1, 3, 5), total)
     upper, total = lax.optimization_barrier((upper, total))
     last = [_xor(upper, 1, n)]
     lower, total = lax.optimization_barrier((lower, total))
     last.append(_xor(lower, 1, n))
-    total = add([upper, lower], (6,), total, False, True)
-    return add(last, (7,), total, True, True)
+    total = add([upper, lower], (6,), total, scaled=True)
+    return add(last, (7,), total, last=True, scaled=True, carried=carried)
 
 
 def solution(mesh):

time: 35.2 us -> 34.3 us (0.974)
  Pallas kernels: 12.9 us -> 12 us
    pallas_call x4, Pallas kernels: 7.38 us -> 6.51 us  [add(): pl.pallas_call(functools.partial(_band_kernel, masks, total is None, 1.0...]
  transfers between devices with their start and end apart: 11 -> 11, of which waited for: 4 -> 4; matrix products, arithmetic and copies ran while one was open for 0% -> 0% of each run, Pallas kernels for 21% -> 22%
where the time goes in v17:
time: 34.3 us; the launch traced here: 34.1 us
  starting transfers between devices  16.9 us (49%)
  Pallas kernels  12 us (35%)
  waiting for transfers between devices  4.99 us (15%)
    ppermute x10, starting transfers between devices, _xor(): return lax.ppermute(x, 'row', [(i, i ^ mask) for i in range(n)])  11.7 us
    pallas_call x4, Pallas kernels, add(): pl.pallas_call(functools.partial(_band_kernel, masks, total is None, 1.0...  6.51 us
    all_to_all x1, starting transfers between devices, shards(): lax.all_to_all(right, 'row', split_axis=0, concat_axis=0, tiled=True)  5.17 us
    all_to_all x1, waiting for transfers between devices, shards(): lax.all_to_all(right, 'row', split_axis=0, concat_axis=0, tiled=True)  3.88 us
    pallas_call x1, Pallas kernels, shards(): pl.pallas_call(_fold_kernel, out_shape=fold_out, scratch_shapes=[pltpu.VM...  2.76 us
    pallas_call x1, Pallas kernels, shards(): pl.pallas_call(_project_kernel, in_specs=[anywhere] * 8, out_specs=(vmem,...  2.43 us
    ppermute x10, waiting for transfers between devices, _xor(): return lax.ppermute(x, 'row', [(i, i ^ mask) for i in range(n)])  1.11 us
  transfers between devices with their start and end apart: 11, of which 4 were waited for; matrix products, arithmetic and copies ran while one was open for 0% of the time, Pallas kernels for 22%

profile of v17, /device:TPU:0, one launch (start us, length us, event | category | flops | bytes accessed | tf_op | source)
XLA Modules:
  0.0 34.1 jit_solution(14760268485874362104)
XLA Ops:
  0.0 2.4 %shard_map.100 = (bf16[256,128]{1,0:T(8,128)(2,1)S(1)}, bf16[32,8,128]{2,1,0:T(8,128)(2,1)}, bf16[1024,128]{1,0:T(8,128)(2,1)S(1)}, bf16[2,512,256]{2,1,0:T(8,128)(2,1)S(1)}) custom-call(bf16[2,512,256]{2,1,0:T(8,128)(2,1)} %refs_0_.1, f32[1,256]{1,0:T(1,128)} %bitcast.16, f32[1,256]{1,0:T(1,128)} %bitcast.17, bf16[32,256]{1,0:T(8,128)(2,1)} %bitcast.14, ...), custom_call_target="tpu_custom_call" | custom-call | flops 33554432 | bytes 524288 | tf_op jit(solution)/shard_map/pallas_call | solution.py:209
  2.4 4.1 %collective-permute-start.2 = (bf16[256,128]{1,0:T(8,128)(2,1)S(1)}, bf16[256,128]{1,0:T(8,128)(2,1)S(1)}, u32[]{:S(2)}, u32[]{:S(2)}) collective-permute-start(bf16[256,128]{1,0:T(8,128)(2,1)S(1)} %get-tuple-element.18.refs_0_), channel_id=1, source_target_pairs={{0,16},{1,17},{2,18},{3,19},{4,20},{5,21},{6,22},{7,23},{8,24},{9,... | collective-permute-start | bytes 196616 | tf_op jit(solution)/shard_map/ppermute | solution.py:192
  6.5 1.3 %collective-permute-start.1 = (bf16[256,128]{1,0:T(8,128)(2,1)S(1)}, bf16[256,128]{1,0:T(8,128)(2,1)S(1)}, u32[]{:S(2)}, u32[]{:S(2)}) collective-permute-start(bf16[256,128]{1,0:T(8,128)(2,1)S(1)} %get-tuple-element.18.refs_0_), channel_id=1, source_target_pairs={{0,24},{1,25},{2,26},{3,27},{4,28},{5,29},{6,30},{7,31},{8,16},{9,... | collective-permute-start | bytes 196616 | tf_op jit(solution)/shard_map/ppermute | solution.py:192
  7.9 0.2 collective-permute-start
  8.1 5.2 %all-to-all-start = ((bf16[32,8,128]{2,1,0:T(8,128)(2,1)}), bf16[32,8,128]{2,1,0:T(8,128)(2,1)S(1)}, u32[]{:S(2)}, u32[]{:S(2)}) async-start(bf16[32,8,128]{2,1,0:T(8,128)(2,1)} %get-tuple-element.20), calls=%async_computation | async-start | bytes 131072 | tf_op jit(solution)/shard_map/all_to_all | solution.py:226
  13.3 0.0 collective-permute-done.2.refs_3_
  13.3 0.0 collective-permute-done.1.refs_2_
  13.3 0.0 collective-permute-done.refs_1_
  13.3 0.3 shard_map.101.refs_0_
  13.6 1.8 %collective-permute-start.4 = (bf16[512,256]{1,0:T(8,128)(2,1)S(1)}, bf16[512,256]{1,0:T(8,128)(2,1)S(1)}, u32[]{:S(2)}, u32[]{:S(2)}) collective-permute-start(bf16[512,256]{1,0:T(8,128)(2,1)S(1)} %shard_map.101.refs_0_), channel_id=1, source_target_pairs={{0,4},{1,5},{2,6},{3,7},{4,0},{5,1},{6,2},{7,3},{8,12},{9,13},{10,... | collective-permute-start | bytes 786440 | tf_op jit(solution)/shard_map/ppermute | solution.py:192
  15.5 1.5 %collective-permute-start.3 = (bf16[512,256]{1,0:T(8,128)(2,1)S(1)}, bf16[512,256]{1,0:T(8,128)(2,1)S(1)}, u32[]{:S(2)}, u32[]{:S(2)}) collective-permute-start(bf16[512,256]{1,0:T(8,128)(2,1)S(1)} %shard_map.101.refs_0_), channel_id=1, source_target_pairs={{0,2},{1,3},{2,0},{3,1},{4,6},{5,7},{6,4},{7,5},{8,10},{9,11},{10,... | collective-permute-start | bytes 786440 | tf_op jit(solution)/shard_map/ppermute | solution.py:192
  16.9 3.9 %all-to-all-done.right_ref = bf16[32,8,128]{2,1,0:T(8,128)(2,1)S(1)} async-done(((bf16[32,8,128]{2,1,0:T(8,128)(2,1)}), bf16[32,8,128]{2,1,0:T(8,128)(2,1)S(1)}, u32[]{:S(2)}, u32[]{:S(2)}) %all-to-all-start) | async-done | bytes 65568 | tf_op jit(solution)/shard_map/all_to_all | solution.py:226
  20.8 2.8 %shard_map.102.refs_3_.refs_1_.refs_2_ = bf16[8,1,256,2048]{3,2,1,0:T(8,128)(2,1)S(1)} custom-call(bf16[32,8,128]{2,1,0:T(8,128)(2,1)S(1)} %all-to-all-done.right_ref, bf16[1024,128]{1,0:T(8,128)(2,1)S(1)} %get-tuple-element.21.final_ref), custom_call_target="tpu_custom_call" | custom-call | flops 2147483648 | bytes 8388608 | tf_op jit(solution)/shard_map/pallas_call | solution.py:257
  23.6 0.0 collective-permute-done.4.refs_2_
  23.6 0.3 collective-permute-done.3.refs_1_
  23.9 0.1 pad_maximum_fusion
  24.0 0.1 collective-permute-start.6
  24.1 0.6 %collective-permute-start.5 = (bf16[288,256]{1,0:T(8,128)(2,1)S(1)}, bf16[288,256]{1,0:T(8,128)(2,1)S(1)}, u32[]{:S(2)}, u32[]{:S(2)}) collective-permute-start(bf16[288,256]{1,0:T(8,128)(2,1)S(1)} %slice.6), channel_id=1, source_target_pairs={{0,4},{1,5},{2,6},{3,7},{4,0},{5,1},{6,2},{7,3},{8,12},{9,13},{10,... | collective-permute-start | bytes 442376 | tf_op jit(solution)/shard_map/ppermute | solution.py:192
  24.7 1.6 %collective-permute-start.8 = (bf16[224,256]{1,0:T(8,128)(2,1)S(1)}, bf16[224,256]{1,0:T(8,128)(2,1)S(1)}, u32[]{:S(2)}, u32[]{:S(2)}) collective-permute-start(bf16[224,256]{1,0:T(8,128)(2,1)S(1)} %slice.7), channel_id=1, source_target_pairs={{0,2},{1,3},{2,0},{3,1},{4,6},{5,7},{6,4},{7,5},{8,10},{9,11},{10,... | collective-permute-start | bytes 344072 | tf_op jit(solution)/shard_map/ppermute | solution.py:192
  26.3 1.8 %shard_map.103.refs_2_ = f32[512,2048]{1,0:T(8,128)S(1)} custom-call(bf16[512,256]{1,0:T(8,128)(2,1)S(1)} %shard_map.101.refs_0_, bf16[512,256]{1,0:T(8,128)(2,1)S(1)} %collective-permute-done.3.refs_1_, bf16[512,256]{1,0:T(8,128)(2,1)S(1)} %collective-permute-done.4.refs_2_, bf16[8,1,256,2048]{3,2,1,0:T(8,128)(2,1)S(1)} %shard_map.102.refs_3_.refs_1_.refs_2_), custom_call_target="tpu_custom_call" | custom-call | flops 1048576 | bytes 8192 | tf_op jit(solution)/shard_map/pallas_call | solution.py:295
  28.1 0.0 copy-start
  28.1 0.0 collective-permute-done.6.refs_0_
  28.1 1.8 %shard_map.104 = (f32[512,2048]{1,0:T(8,128)S(1)}, bf16[512,16,128]{2,1,0:T(8,128)(2,1)S(1)}) custom-call(bf16[3,512,256]{2,1,0:T(8,128)(2,1)S(1)} %collective-permute-done.6.refs_0_, bf16[8,1,256,2048]{3,2,1,0:T(8,128)(2,1)S(1)} %shard_map.102.refs_3_.refs_1_.refs_2_, f32[512,2048]{1,0:T(8,128)S(1)} %shard_map.103.refs_2_, bf16[512,16,128]{2,1,0:T(8,128)(2,1)} %refs_3_.1), custom_call_target="tpu_custom_call" | custom-call | flops 1048576 | bytes 8192 | tf_op jit(solution)/shard_map/pallas_call | solution.py:295
  29.9 0.5 %collective-permute-done.5.refs_0_ = bf16[288,256]{1,0:T(8,128)(2,1)S(1)} collective-permute-done((bf16[288,256]{1,0:T(8,128)(2,1)S(1)}, bf16[288,256]{1,0:T(8,128)(2,1)S(1)}, u32[]{:S(2)}, u32[]{:S(2)}) %collective-permute-start.5) | collective-permute-done | bytes 147488 | tf_op jit(solution)/shard_map/ppermute | solution.py:192
  30.4 0.0 collective-permute-start.7
  30.4 0.0 collective-permute-done.8.refs_1_
  30.4 0.5 %collective-permute-start.9 = (bf16[224,256]{1,0:T(8,128)(2,1)S(1)}, bf16[224,256]{1,0:T(8,128)(2,1)S(1)}, u32[]{:S(2)}, u32[]{:S(2)}) collective-permute-start(bf16[224,256]{1,0:T(8,128)(2,1)S(1)} %collective-permute-done.8.refs_1_), channel_id=1, source_target_pairs={{0,1},{1,0},{2,3},{3,2},{4,5},{5,4},{6,7},{7,6},{8,9},{9,8},{10,11... | collective-permute-start | bytes 344072 | tf_op jit(solution)/shard_map/ppermute | solution.py:192
  30.9 0.0 copy-done
  30.9 0.7 %shard_map.105.refs_3_ = f32[512,2048]{1,0:T(8,128)S(1)} custom-call(bf16[288,256]{1,0:T(8,128)(2,1)S(1)} %collective-permute-done.5.refs_0_, bf16[224,256]{1,0:T(8,128)(2,1)S(1)} %collective-permute-done.8.refs_1_, bf16[8,1,256,2048]{3,2,1,0:T(8,128)(2,1)S(1)} %shard_map.102.refs_3_.refs_1_.refs_2_, f32[512,2048]{1,0:T(8,128)S(1)} %get-tuple-element.29.refs_3_, ...), custom_call_target="tpu_custom_call" | custom-call | flops 1048576 | bytes 8192 | tf_op jit(solution)/shard_map/pallas_call | solution.py:295
  31.6 0.3 collective-permute-done.9.refs_1_
  31.9 0.0 collective-permute-done.7.refs_0_
  31.9 2.2 %shard_map.106 = bf16[512,16,128]{2,1,0:T(8,128)(2,1)} custom-call(bf16[288,256]{1,0:T(8,128)(2,1)S(1)} %collective-permute-done.7.refs_0_, bf16[224,256]{1,0:T(8,128)(2,1)S(1)} %collective-permute-done.9.refs_1_, bf16[8,1,256,2048]{3,2,1,0:T(8,128)(2,1)S(1)} %shard_map.102.refs_3_.refs_1_.refs_2_, f32[512,2048]{1,0:T(8,128)S(1)} %shard_map.105.refs_3_, ...), custom_call_target="tpu_custom_call" | custom-call | flops 1048576 | bytes 8192 | tf_op jit(solution)/shard_map/pallas_call | solution.py:295
  (2 shorter events, 0.0 us)
Async XLA Ops:
  2.4 10.9 %collective-permute-start.2 = (bf16[256,128]{1,0:T(8,128)(2,1)S(1)}, bf16[256,128]{1,0:T(8,128)(2,1)S(1)}, u32[]{:S(2)}, u32[]{:S(2)}) collective-permute-start(bf16[256,128]{1,0:T(8,128)(2,1)S(1)} %get-tuple-element.18.refs_0_), channel_id=1, source_target_pairs={{0,16},{1,17},{2,18},{3,19},{4,20},{5,21},{6,22},{7,23},{8,24},{9,... | collective-permute-start | bytes 196616 | tf_op jit(solution)/shard_map/ppermute | solution.py:192
  6.5 6.8 %collective-permute-start.1 = (bf16[256,128]{1,0:T(8,128)(2,1)S(1)}, bf16[256,128]{1,0:T(8,128)(2,1)S(1)}, u32[]{:S(2)}, u32[]{:S(2)}) collective-permute-start(bf16[256,128]{1,0:T(8,128)(2,1)S(1)} %get-tuple-element.18.refs_0_), channel_id=1, source_target_pairs={{0,24},{1,25},{2,26},{3,27},{4,28},{5,29},{6,30},{7,31},{8,16},{9,... | collective-permute-start | bytes 196616 | tf_op jit(solution)/shard_map/ppermute | solution.py:192
  7.9 5.4 %collective-permute-start = (bf16[256,128]{1,0:T(8,128)(2,1)S(1)}, bf16[256,128]{1,0:T(8,128)(2,1)S(1)}, u32[]{:S(2)}, u32[]{:S(2)}) collective-permute-start(bf16[256,128]{1,0:T(8,128)(2,1)S(1)} %get-tuple-element.18.refs_0_), channel_id=1, source_target_pairs={{0,8},{1,9},{2,10},{3,11},{4,12},{5,13},{6,14},{7,15},{8,0},{9,1},... | collective-permute-start | bytes 196616 | tf_op jit(solution)/shard_map/ppermute | solution.py:192
  8.1 12.7 %all-to-all-start = ((bf16[32,8,128]{2,1,0:T(8,128)(2,1)}), bf16[32,8,128]{2,1,0:T(8,128)(2,1)S(1)}, u32[]{:S(2)}, u32[]{:S(2)}) async-start(bf16[32,8,128]{2,1,0:T(8,128)(2,1)} %get-tuple-element.20), calls=%async_computation | async-start | bytes 131072 | tf_op jit(solution)/shard_map/all_to_all | solution.py:226
  13.6 9.9 %collective-permute-start.4 = (bf16[512,256]{1,0:T(8,128)(2,1)S(1)}, bf16[512,256]{1,0:T(8,128)(2,1)S(1)}, u32[]{:S(2)}, u32[]{:S(2)}) collective-permute-start(bf16[512,256]{1,0:T(8,128)(2,1)S(1)} %shard_map.101.refs_0_), channel_id=1, source_target_pairs={{0,4},{1,5},{2,6},{3,7},{4,0},{5,1},{6,2},{7,3},{8,12},{9,13},{10,... | collective-permute-start | bytes 786440 | tf_op jit(solution)/shard_map/ppermute | solution.py:192
  15.5 8.4 %collective-permute-start.3 = (bf16[512,256]{1,0:T(8,128)(2,1)S(1)}, bf16[512,256]{1,0:T(8,128)(2,1)S(1)}, u32[]{:S(2)}, u32[]{:S(2)}) collective-permute-start(bf16[512,256]{1,0:T(8,128)(2,1)S(1)} %shard_map.101.refs_0_), channel_id=1, source_target_pairs={{0,2},{1,3},{2,0},{3,1},{4,6},{5,7},{6,4},{7,5},{8,10},{9,11},{10,... | collective-permute-start | bytes 786440 | tf_op jit(solution)/shard_map/ppermute | solution.py:192
  24.0 4.1 %collective-permute-start.6 = (bf16[3,512,256]{2,1,0:T(8,128)(2,1)S(1)}, bf16[3,512,256]{2,1,0:T(8,128)(2,1)S(1)}, u32[]{:S(2)}, u32[]{:S(2)}) collective-permute-start(bf16[3,512,256]{2,1,0:T(8,128)(2,1)S(1)} %pad_maximum_fusion), channel_id=1, source_target_pairs={{0,1},{1,0},{2,3},{3,2},{4,5},{5,4},{6,7},{7,6},{8,9},{9,8},{10,11... | collective-permute-start | bytes 2359304 | tf_op jit(solution)/shard_map/ppermute | solution.py:192
  24.1 6.3 %collective-permute-start.5 = (bf16[288,256]{1,0:T(8,128)(2,1)S(1)}, bf16[288,256]{1,0:T(8,128)(2,1)S(1)}, u32[]{:S(2)}, u32[]{:S(2)}) collective-permute-start(bf16[288,256]{1,0:T(8,128)(2,1)S(1)} %slice.6), channel_id=1, source_target_pairs={{0,4},{1,5},{2,6},{3,7},{4,0},{5,1},{6,2},{7,3},{8,12},{9,13},{10,... | collective-permute-start | bytes 442376 | tf_op jit(solution)/shard_map/ppermute | solution.py:192
  24.7 5.7 %collective-permute-start.8 = (bf16[224,256]{1,0:T(8,128)(2,1)S(1)}, bf16[224,256]{1,0:T(8,128)(2,1)S(1)}, u32[]{:S(2)}, u32[]{:S(2)}) collective-permute-start(bf16[224,256]{1,0:T(8,128)(2,1)S(1)} %slice.7), channel_id=1, source_target_pairs={{0,2},{1,3},{2,0},{3,1},{4,6},{5,7},{6,4},{7,5},{8,10},{9,11},{10,... | collective-permute-start | bytes 344072 | tf_op jit(solution)/shard_map/ppermute | solution.py:192
  28.1 2.9 %copy-start = (f32[128]{0:T(128)S(1)}, f32[128]{0:T(128)}, u32[]{:S(2)}) copy-start(f32[128]{0:T(128)} %param.19) | copy-start | bytes 1540
  30.4 1.5 %collective-permute-start.7 = (bf16[288,256]{1,0:T(8,128)(2,1)S(1)}, bf16[288,256]{1,0:T(8,128)(2,1)S(1)}, u32[]{:S(2)}, u32[]{:S(2)}) collective-permute-start(bf16[288,256]{1,0:T(8,128)(2,1)S(1)} %collective-permute-done.5.refs_0_), channel_id=1, source_target_pairs={{0,1},{1,0},{2,3},{3,2},{4,5},{5,4},{6,7},{7,6},{8,9},{9,8},{10,11... | collective-permute-start | bytes 442376 | tf_op jit(solution)/shard_map/ppermute | solution.py:192
  30.4 1.5 %collective-permute-start.9 = (bf16[224,256]{1,0:T(8,128)(2,1)S(1)}, bf16[224,256]{1,0:T(8,128)(2,1)S(1)}, u32[]{:S(2)}, u32[]{:S(2)}) collective-permute-start(bf16[224,256]{1,0:T(8,128)(2,1)S(1)} %collective-permute-done.8.refs_1_), channel_id=1, source_target_pairs={{0,1},{1,0},{2,3},{3,2},{4,5},{5,4},{6,7},{7,6},{8,9},{9,8},{10,11... | collective-permute-start | bytes 344072 | tf_op jit(solution)/shard_map/ppermute | solution.py:192

commit v18 on v17

--- a/solution.py
+++ b/solution.py
@@ -49,15 +49,23 @@
     half = left_ref.shape[0]
     n = right_ref.shape[0]
     feats = x_ref.shape[2]
+    share = jnp.full((feats, LANES), 1.0 / feats, jnp.bfloat16)
+    widen = lambda mean: jnp.concatenate([mean] * (feats // LANES), axis=1)
     split = []
     for s in range(2):
         if s:
             copies[1].wait()
-        x = x_ref[s].astype(jnp.float32)
-        center = jnp.mean(x, axis=-1, keepdims=True)
-        off = x - center
-        spread = jnp.mean(off * off, axis=-1, keepdims=True)
-        normed = off * lax.rsqrt(spread + 1e-05) * gain_ref[...] + bias_ref[...]
+        x = x_ref[s]
+        off = x.astype(jnp.float32) - widen(jnp.dot(x, share, preferred_element_type=jnp.float32))
+        square = off * off
+        high = square.astype(jnp.bfloat16)
+        low = (square - high.astype(jnp.float32)).astype(jnp.bfloat16)
+        spread = jnp.dot(
+            jnp.concatenate([high, low], axis=1),
+            jnp.concatenate([share, share], axis=0),
+            preferred_element_type=jnp.float32,
+        )
+        normed = off * widen(lax.rsqrt(spread + 1e-05)) * gain_ref[...] + bias_ref[...]
         split.append(normed.reshape(n, 2, 8, feats))
     parts = [split[s][:, jh].reshape(n * 8, feats).astype(jnp.bfloat16) for jh in range(2) for s in range(2)]
     weights = jnp.concatenate([_stacked(w1_ref[...], 4), _stacked(w2_ref[...], 4)], axis=0)
@@ -159,12 +167,13 @@
 
     acc_ref, done_ref, sems = take(3)
     cols = pair_ref.shape[1]
-    pitch = cols + 1
+    gap = 3
+    pitch = gap * cols + 1
     for begin in range(0, t_ref.shape[3], tile):
         res = column(begin)
         for k in range(tile // LANES):
             j = begin // LANES + k
-            acc_ref[pl.ds(j, band, stride=pitch), :] = res[:, k * LANES : (k + 1) * LANES]
+            acc_ref[pl.ds(gap * j, band, stride=pitch), :] = res[:, k * LANES : (k + 1) * LANES]
 
     chunk = 32
 
@@ -172,7 +181,7 @@
         for k in range(chunk):
             i = r * chunk + k
             row = k // 8 % 2 * (band // 2) + (r * (chunk // 16) + k // 16) * 8 + k % 8
-            total = acc_ref[pl.ds(row * pitch, cols), :]
+            total = acc_ref[pl.ds(row * pitch, cols, stride=gap), :]
             done_ref[i] = (pair_ref[i].astype(jnp.float32) + total).astype(jnp.bfloat16)
         at = pl.ds(pl.multiple_of(r * chunk, chunk), chunk)
         pltpu.make_async_copy(done_ref.at[at], out_ref.at[at], sems.at[r]).start()
@@ -286,7 +295,7 @@
             in_specs.append(vmem)
             out_shape, out_specs = jax.ShapeDtypeStruct(pair.shape, jnp.bfloat16), anywhere
             scratch = [
-                pltpu.VMEM((band * (cols + 1), zdim), jnp.float32),
+                pltpu.VMEM((band * (3 * cols + 1), zdim), jnp.float32),
                 pltpu.VMEM(pair.shape, jnp.bfloat16),
                 pltpu.SemaphoreType.DMA((band // 32,)),
             ]

time: 34.3 us -> 34.9 us (1.017)
  Pallas kernels: 12 us -> 12.6 us
    pallas_call x1, Pallas kernels: 2.43 us -> 3.04 us  [shards(): pl.pallas_call(_project_kernel, in_specs=[anywhere] * 8, out_specs=(vmem,...]
  transfers between devices with their start and end apart: 11 -> 11, of which waited for: 4 -> 4; matrix products, arithmetic and copies ran while one was open for 0% -> 0% of each run, Pallas kernels for 22% -> 21%
where the time goes in v18:
time: 34.9 us; the launch traced here: 34.7 us
  starting transfers between devices  16.9 us (48%)
  Pallas kernels  12.6 us (36%)
  waiting for transfers between devices  4.99 us (14%)
    ppermute x10, starting transfers between devices, _xor(): return lax.ppermute(x, 'row', [(i, i ^ mask) for i in range(n)])  11.7 us
    pallas_call x4, Pallas kernels, add(): pl.pallas_call(functools.partial(_band_kernel, masks, total is None, 1.0...  6.51 us
    all_to_all x1, starting transfers between devices, shards(): lax.all_to_all(right, 'row', split_axis=0, concat_axis=0, tiled=True)  5.17 us
    all_to_all x1, waiting for transfers between devices, shards(): lax.all_to_all(right, 'row', split_axis=0, concat_axis=0, tiled=True)  3.87 us
    pallas_call x1, Pallas kernels, shards(): pl.pallas_call(_project_kernel, in_specs=[anywhere] * 8, out_specs=(vmem,...  3.04 us
    pallas_call x1, Pallas kernels, shards(): pl.pallas_call(_fold_kernel, out_shape=fold_out, scratch_shapes=[pltpu.VM...  2.76 us
    ppermute x10, waiting for transfers between devices, _xor(): return lax.ppermute(x, 'row', [(i, i ^ mask) for i in range(n)])  1.11 us
  transfers between devices with their start and end apart: 11, of which 4 were waited for; matrix products, arithmetic and copies ran while one was open for 0% of the time, Pallas kernels for 21%

profile of v18, /device:TPU:0, one launch (start us, length us, event | category | flops | bytes accessed | tf_op | source)
XLA Modules:
  0.0 34.7 jit_solution(9790418452101868412)
XLA Ops:
  0.0 3.0 %shard_map.100 = (bf16[256,128]{1,0:T(8,128)(2,1)S(1)}, bf16[32,8,128]{2,1,0:T(8,128)(2,1)}, bf16[1024,128]{1,0:T(8,128)(2,1)S(1)}, bf16[2,512,256]{2,1,0:T(8,128)(2,1)S(1)}) custom-call(bf16[2,512,256]{2,1,0:T(8,128)(2,1)} %refs_0_.1, f32[1,256]{1,0:T(1,128)} %bitcast.16, f32[1,256]{1,0:T(1,128)} %bitcast.17, bf16[32,256]{1,0:T(8,128)(2,1)} %bitcast.14, ...), custom_call_target="tpu_custom_call" | custom-call | flops 33554432 | bytes 524288 | tf_op jit(solution)/shard_map/pallas_call | solution.py:218
  3.0 4.1 %collective-permute-start.2 = (bf16[256,128]{1,0:T(8,128)(2,1)S(1)}, bf16[256,128]{1,0:T(8,128)(2,1)S(1)}, u32[]{:S(2)}, u32[]{:S(2)}) collective-permute-start(bf16[256,128]{1,0:T(8,128)(2,1)S(1)} %get-tuple-element.18.refs_0_), channel_id=1, source_target_pairs={{0,16},{1,17},{2,18},{3,19},{4,20},{5,21},{6,22},{7,23},{8,24},{9,... | collective-permute-start | bytes 196616 | tf_op jit(solution)/shard_map/ppermute | solution.py:201
  7.1 1.3 %collective-permute-start.1 = (bf16[256,128]{1,0:T(8,128)(2,1)S(1)}, bf16[256,128]{1,0:T(8,128)(2,1)S(1)}, u32[]{:S(2)}, u32[]{:S(2)}) collective-permute-start(bf16[256,128]{1,0:T(8,128)(2,1)S(1)} %get-tuple-element.18.refs_0_), channel_id=1, source_target_pairs={{0,24},{1,25},{2,26},{3,27},{4,28},{5,29},{6,30},{7,31},{8,16},{9,... | collective-permute-start | bytes 196616 | tf_op jit(solution)/shard_map/ppermute | solution.py:201
  8.5 0.2 collective-permute-start
  8.7 5.2 %all-to-all-start = ((bf16[32,8,128]{2,1,0:T(8,128)(2,1)}), bf16[32,8,128]{2,1,0:T(8,128)(2,1)S(1)}, u32[]{:S(2)}, u32[]{:S(2)}) async-start(bf16[32,8,128]{2,1,0:T(8,128)(2,1)} %get-tuple-element.20), calls=%async_computation | async-start | bytes 131072 | tf_op jit(solution)/shard_map/all_to_all | solution.py:235
  13.9 0.0 collective-permute-done.2.refs_3_
  13.9 0.0 collective-permute-done.1.refs_2_
  13.9 0.0 collective-permute-done.refs_1_
  13.9 0.3 shard_map.101.refs_0_
  14.3 1.8 %collective-permute-start.4 = (bf16[512,256]{1,0:T(8,128)(2,1)S(1)}, bf16[512,256]{1,0:T(8,128)(2,1)S(1)}, u32[]{:S(2)}, u32[]{:S(2)}) collective-permute-start(bf16[512,256]{1,0:T(8,128)(2,1)S(1)} %shard_map.101.refs_0_), channel_id=1, source_target_pairs={{0,4},{1,5},{2,6},{3,7},{4,0},{5,1},{6,2},{7,3},{8,12},{9,13},{10,... | collective-permute-start | bytes 786440 | tf_op jit(solution)/shard_map/ppermute | solution.py:201
  16.1 1.5 %collective-permute-start.3 = (bf16[512,256]{1,0:T(8,128)(2,1)S(1)}, bf16[512,256]{1,0:T(8,128)(2,1)S(1)}, u32[]{:S(2)}, u32[]{:S(2)}) collective-permute-start(bf16[512,256]{1,0:T(8,128)(2,1)S(1)} %shard_map.101.refs_0_), channel_id=1, source_target_pairs={{0,2},{1,3},{2,0},{3,1},{4,6},{5,7},{6,4},{7,5},{8,10},{9,11},{10,... | collective-permute-start | bytes 786440 | tf_op jit(solution)/shard_map/ppermute | solution.py:201
  17.5 3.9 %all-to-all-done.right_ref = bf16[32,8,128]{2,1,0:T(8,128)(2,1)S(1)} async-done(((bf16[32,8,128]{2,1,0:T(8,128)(2,1)}), bf16[32,8,128]{2,1,0:T(8,128)(2,1)S(1)}, u32[]{:S(2)}, u32[]{:S(2)}) %all-to-all-start) | async-done | bytes 65568 | tf_op jit(solution)/shard_map/all_to_all | solution.py:235
  21.4 2.8 %shard_map.102.refs_3_.refs_1_.refs_2_ = bf16[8,1,256,2048]{3,2,1,0:T(8,128)(2,1)S(1)} custom-call(bf16[32,8,128]{2,1,0:T(8,128)(2,1)S(1)} %all-to-all-done.right_ref, bf16[1024,128]{1,0:T(8,128)(2,1)S(1)} %get-tuple-element.21.final_ref), custom_call_target="tpu_custom_call" | custom-call | flops 2147483648 | bytes 8388608 | tf_op jit(solution)/shard_map/pallas_call | solution.py:266
  24.2 0.0 collective-permute-done.4.refs_2_
  24.2 0.3 collective-permute-done.3.refs_1_
  24.5 0.1 pad_maximum_fusion
  24.6 0.1 collective-permute-start.6
  24.7 0.6 %collective-permute-start.5 = (bf16[288,256]{1,0:T(8,128)(2,1)S(1)}, bf16[288,256]{1,0:T(8,128)(2,1)S(1)}, u32[]{:S(2)}, u32[]{:S(2)}) collective-permute-start(bf16[288,256]{1,0:T(8,128)(2,1)S(1)} %slice.6), channel_id=1, source_target_pairs={{0,4},{1,5},{2,6},{3,7},{4,0},{5,1},{6,2},{7,3},{8,12},{9,13},{10,... | collective-permute-start | bytes 442376 | tf_op jit(solution)/shard_map/ppermute | solution.py:201
  25.3 1.6 %collective-permute-start.8 = (bf16[224,256]{1,0:T(8,128)(2,1)S(1)}, bf16[224,256]{1,0:T(8,128)(2,1)S(1)}, u32[]{:S(2)}, u32[]{:S(2)}) collective-permute-start(bf16[224,256]{1,0:T(8,128)(2,1)S(1)} %slice.7), channel_id=1, source_target_pairs={{0,2},{1,3},{2,0},{3,1},{4,6},{5,7},{6,4},{7,5},{8,10},{9,11},{10,... | collective-permute-start | bytes 344072 | tf_op jit(solution)/shard_map/ppermute | solution.py:201
  26.9 1.8 %shard_map.103.refs_2_ = f32[512,2048]{1,0:T(8,128)S(1)} custom-call(bf16[512,256]{1,0:T(8,128)(2,1)S(1)} %shard_map.101.refs_0_, bf16[512,256]{1,0:T(8,128)(2,1)S(1)} %collective-permute-done.3.refs_1_, bf16[512,256]{1,0:T(8,128)(2,1)S(1)} %collective-permute-done.4.refs_2_, bf16[8,1,256,2048]{3,2,1,0:T(8,128)(2,1)S(1)} %shard_map.102.refs_3_.refs_1_.refs_2_), custom_call_target="tpu_custom_call" | custom-call | flops 1048576 | bytes 8192 | tf_op jit(solution)/shard_map/pallas_call | solution.py:304
  28.7 0.0 copy-start
  28.7 0.0 collective-permute-done.6.refs_0_
  28.7 1.8 %shard_map.104 = (f32[512,2048]{1,0:T(8,128)S(1)}, bf16[512,16,128]{2,1,0:T(8,128)(2,1)S(1)}) custom-call(bf16[3,512,256]{2,1,0:T(8,128)(2,1)S(1)} %collective-permute-done.6.refs_0_, bf16[8,1,256,2048]{3,2,1,0:T(8,128)(2,1)S(1)} %shard_map.102.refs_3_.refs_1_.refs_2_, f32[512,2048]{1,0:T(8,128)S(1)} %shard_map.103.refs_2_, bf16[512,16,128]{2,1,0:T(8,128)(2,1)} %refs_3_.1), custom_call_target="tpu_custom_call" | custom-call | flops 1048576 | bytes 8192 | tf_op jit(solution)/shard_map/pallas_call | solution.py:304
  30.5 0.5 %collective-permute-done.5.refs_0_ = bf16[288,256]{1,0:T(8,128)(2,1)S(1)} collective-permute-done((bf16[288,256]{1,0:T(8,128)(2,1)S(1)}, bf16[288,256]{1,0:T(8,128)(2,1)S(1)}, u32[]{:S(2)}, u32[]{:S(2)}) %collective-permute-start.5) | collective-permute-done | bytes 147488 | tf_op jit(solution)/shard_map/ppermute | solution.py:201
  31.0 0.0 collective-permute-start.7
  31.0 0.0 collective-permute-done.8.refs_1_
  31.0 0.5 %collective-permute-start.9 = (bf16[224,256]{1,0:T(8,128)(2,1)S(1)}, bf16[224,256]{1,0:T(8,128)(2,1)S(1)}, u32[]{:S(2)}, u32[]{:S(2)}) collective-permute-start(bf16[224,256]{1,0:T(8,128)(2,1)S(1)} %collective-permute-done.8.refs_1_), channel_id=1, source_target_pairs={{0,1},{1,0},{2,3},{3,2},{4,5},{5,4},{6,7},{7,6},{8,9},{9,8},{10,11... | collective-permute-start | bytes 344072 | tf_op jit(solution)/shard_map/ppermute | solution.py:201
  31.5 0.0 copy-done
  31.5 0.7 %shard_map.105.refs_3_ = f32[512,2048]{1,0:T(8,128)S(1)} custom-call(bf16[288,256]{1,0:T(8,128)(2,1)S(1)} %collective-permute-done.5.refs_0_, bf16[224,256]{1,0:T(8,128)(2,1)S(1)} %collective-permute-done.8.refs_1_, bf16[8,1,256,2048]{3,2,1,0:T(8,128)(2,1)S(1)} %shard_map.102.refs_3_.refs_1_.refs_2_, f32[512,2048]{1,0:T(8,128)S(1)} %get-tuple-element.29.refs_3_, ...), custom_call_target="tpu_custom_call" | custom-call | flops 1048576 | bytes 8192 | tf_op jit(solution)/shard_map/pallas_call | solution.py:304
  32.3 0.3 collective-permute-done.9.refs_1_
  32.6 0.0 collective-permute-done.7.refs_0_
  32.6 2.2 %shard_map.106 = bf16[512,16,128]{2,1,0:T(8,128)(2,1)} custom-call(bf16[288,256]{1,0:T(8,128)(2,1)S(1)} %collective-permute-done.7.refs_0_, bf16[224,256]{1,0:T(8,128)(2,1)S(1)} %collective-permute-done.9.refs_1_, bf16[8,1,256,2048]{3,2,1,0:T(8,128)(2,1)S(1)} %shard_map.102.refs_3_.refs_1_.refs_2_, f32[512,2048]{1,0:T(8,128)S(1)} %shard_map.105.refs_3_, ...), custom_call_target="tpu_custom_call" | custom-call | flops 1048576 | bytes 8192 | tf_op jit(solution)/shard_map/pallas_call | solution.py:304
  (2 shorter events, 0.0 us)
Async XLA Ops:
  3.0 10.9 %collective-permute-start.2 = (bf16[256,128]{1,0:T(8,128)(2,1)S(1)}, bf16[256,128]{1,0:T(8,128)(2,1)S(1)}, u32[]{:S(2)}, u32[]{:S(2)}) collective-permute-start(bf16[256,128]{1,0:T(8,128)(2,1)S(1)} %get-tuple-element.18.refs_0_), channel_id=1, source_target_pairs={{0,16},{1,17},{2,18},{3,19},{4,20},{5,21},{6,22},{7,23},{8,24},{9,... | collective-permute-start | bytes 196616 | tf_op jit(solution)/shard_map/ppermute | solution.py:201
  7.1 6.8 %collective-permute-start.1 = (bf16[256,128]{1,0:T(8,128)(2,1)S(1)}, bf16[256,128]{1,0:T(8,128)(2,1)S(1)}, u32[]{:S(2)}, u32[]{:S(2)}) collective-permute-start(bf16[256,128]{1,0:T(8,128)(2,1)S(1)} %get-tuple-element.18.refs_0_), channel_id=1, source_target_pairs={{0,24},{1,25},{2,26},{3,27},{4,28},{5,29},{6,30},{7,31},{8,16},{9,... | collective-permute-start | bytes 196616 | tf_op jit(solution)/shard_map/ppermute | solution.py:201
  8.5 5.4 %collective-permute-start = (bf16[256,128]{1,0:T(8,128)(2,1)S(1)}, bf16[256,128]{1,0:T(8,128)(2,1)S(1)}, u32[]{:S(2)}, u32[]{:S(2)}) collective-permute-start(bf16[256,128]{1,0:T(8,128)(2,1)S(1)} %get-tuple-element.18.refs_0_), channel_id=1, source_target_pairs={{0,8},{1,9},{2,10},{3,11},{4,12},{5,13},{6,14},{7,15},{8,0},{9,1},... | collective-permute-start | bytes 196616 | tf_op jit(solution)/shard_map/ppermute | solution.py:201
  8.7 12.7 %all-to-all-start = ((bf16[32,8,128]{2,1,0:T(8,128)(2,1)}), bf16[32,8,128]{2,1,0:T(8,128)(2,1)S(1)}, u32[]{:S(2)}, u32[]{:S(2)}) async-start(bf16[32,8,128]{2,1,0:T(8,128)(2,1)} %get-tuple-element.20), calls=%async_computation | async-start | bytes 131072 | tf_op jit(solution)/shard_map/all_to_all | solution.py:235
  14.3 9.9 %collective-permute-start.4 = (bf16[512,256]{1,0:T(8,128)(2,1)S(1)}, bf16[512,256]{1,0:T(8,128)(2,1)S(1)}, u32[]{:S(2)}, u32[]{:S(2)}) collective-permute-start(bf16[512,256]{1,0:T(8,128)(2,1)S(1)} %shard_map.101.refs_0_), channel_id=1, source_target_pairs={{0,4},{1,5},{2,6},{3,7},{4,0},{5,1},{6,2},{7,3},{8,12},{9,13},{10,... | collective-permute-start | bytes 786440 | tf_op jit(solution)/shard_map/ppermute | solution.py:201
  16.1 8.4 %collective-permute-start.3 = (bf16[512,256]{1,0:T(8,128)(2,1)S(1)}, bf16[512,256]{1,0:T(8,128)(2,1)S(1)}, u32[]{:S(2)}, u32[]{:S(2)}) collective-permute-start(bf16[512,256]{1,0:T(8,128)(2,1)S(1)} %shard_map.101.refs_0_), channel_id=1, source_target_pairs={{0,2},{1,3},{2,0},{3,1},{4,6},{5,7},{6,4},{7,5},{8,10},{9,11},{10,... | collective-permute-start | bytes 786440 | tf_op jit(solution)/shard_map/ppermute | solution.py:201
  24.6 4.1 %collective-permute-start.6 = (bf16[3,512,256]{2,1,0:T(8,128)(2,1)S(1)}, bf16[3,512,256]{2,1,0:T(8,128)(2,1)S(1)}, u32[]{:S(2)}, u32[]{:S(2)}) collective-permute-start(bf16[3,512,256]{2,1,0:T(8,128)(2,1)S(1)} %pad_maximum_fusion), channel_id=1, source_target_pairs={{0,1},{1,0},{2,3},{3,2},{4,5},{5,4},{6,7},{7,6},{8,9},{9,8},{10,11... | collective-permute-start | bytes 2359304 | tf_op jit(solution)/shard_map/ppermute | solution.py:201
  24.7 6.3 %collective-permute-start.5 = (bf16[288,256]{1,0:T(8,128)(2,1)S(1)}, bf16[288,256]{1,0:T(8,128)(2,1)S(1)}, u32[]{:S(2)}, u32[]{:S(2)}) collective-permute-start(bf16[288,256]{1,0:T(8,128)(2,1)S(1)} %slice.6), channel_id=1, source_target_pairs={{0,4},{1,5},{2,6},{3,7},{4,0},{5,1},{6,2},{7,3},{8,12},{9,13},{10,... | collective-permute-start | bytes 442376 | tf_op jit(solution)/shard_map/ppermute | solution.py:201
  25.3 5.7 %collective-permute-start.8 = (bf16[224,256]{1,0:T(8,128)(2,1)S(1)}, bf16[224,256]{1,0:T(8,128)(2,1)S(1)}, u32[]{:S(2)}, u32[]{:S(2)}) collective-permute-start(bf16[224,256]{1,0:T(8,128)(2,1)S(1)} %slice.7), channel_id=1, source_target_pairs={{0,2},{1,3},{2,0},{3,1},{4,6},{5,7},{6,4},{7,5},{8,10},{9,11},{10,... | collective-permute-start | bytes 344072 | tf_op jit(solution)/shard_map/ppermute | solution.py:201
  28.7 2.9 %copy-start = (f32[128]{0:T(128)S(1)}, f32[128]{0:T(128)}, u32[]{:S(2)}) copy-start(f32[128]{0:T(128)} %param.19) | copy-start | bytes 1540
  31.0 1.5 %collective-permute-start.7 = (bf16[288,256]{1,0:T(8,128)(2,1)S(1)}, bf16[288,256]{1,0:T(8,128)(2,1)S(1)}, u32[]{:S(2)}, u32[]{:S(2)}) collective-permute-start(bf16[288,256]{1,0:T(8,128)(2,1)S(1)} %collective-permute-done.5.refs_0_), channel_id=1, source_target_pairs={{0,1},{1,0},{2,3},{3,2},{4,5},{5,4},{6,7},{7,6},{8,9},{9,8},{10,11... | collective-permute-start | bytes 442376 | tf_op jit(solution)/shard_map/ppermute | solution.py:201
  31.0 1.5 %collective-permute-start.9 = (bf16[224,256]{1,0:T(8,128)(2,1)S(1)}, bf16[224,256]{1,0:T(8,128)(2,1)S(1)}, u32[]{:S(2)}, u32[]{:S(2)}) collective-permute-start(bf16[224,256]{1,0:T(8,128)(2,1)S(1)} %collective-permute-done.8.refs_1_), channel_id=1, source_target_pairs={{0,1},{1,0},{2,3},{3,2},{4,5},{5,4},{6,7},{7,6},{8,9},{9,8},{10,11... | collective-permute-start | bytes 344072 | tf_op jit(solution)/shard_map/ppermute | solution.py:201

commit v19 on v17

--- a/solution.py
+++ b/solution.py
@@ -35,7 +35,10 @@
     sources, final_source, outs, held = refs[:7], refs[7], refs[8:12], refs[12:19]
     left_ref, right_ref, final_ref, order_ref = outs
     sems = refs[19]
-    pairs = [(sources[0].at[s], held[0].at[s]) for s in range(2)]
+    pieces = 4
+    size = held[0].shape[1] // pieces
+    at = [(s, pl.ds(k * size, size)) for s in range(2) for k in range(pieces)]
+    pairs = [(sources[0].at[i], held[0].at[i]) for i in at]
     pairs += list(zip(sources[1:], held[1:])) + [(final_source, final_ref)]
     copies = [pltpu.make_async_copy(a, b, sems.at[i]) for i, (a, b) in enumerate(pairs)]
     for copy in copies:
@@ -43,7 +46,7 @@
     me = lax.axis_index("row")
     for h in range(2):
         order_ref[h] = _order(me, h)
-    for copy in copies[:1] + copies[2:8]:
+    for copy in copies[:pieces] + copies[2 * pieces : -1]:
         copy.wait()
     x_ref, gain_ref, bias_ref, w1_ref, b1_ref, w2_ref, b2_ref = held
     half = left_ref.shape[0]
@@ -52,7 +55,8 @@
     split = []
     for s in range(2):
         if s:
-            copies[1].wait()
+            for copy in copies[pieces : 2 * pieces]:
+                copy.wait()
         x = x_ref[s].astype(jnp.float32)
         center = jnp.mean(x, axis=-1, keepdims=True)
         off = x - center
@@ -65,7 +69,7 @@
     both = lax.dot_general(jnp.concatenate(parts, axis=1), weights, NT, preferred_element_type=jnp.float32) + shifts
     left_ref[...] = both[:half, :LANES].astype(jnp.bfloat16)
     right_ref[...] = both[:, LANES:].reshape(n, 8, LANES).astype(jnp.bfloat16)
-    copies[8].wait()
+    copies[-1].wait()
 
 
 def _line_kernel(*refs):
@@ -159,12 +163,13 @@
 
     acc_ref, done_ref, sems = take(3)
     cols = pair_ref.shape[1]
-    pitch = cols + 1
+    gap = 3
+    pitch = gap * cols + 1
     for begin in range(0, t_ref.shape[3], tile):
         res = column(begin)
         for k in range(tile // LANES):
             j = begin // LANES + k
-            acc_ref[pl.ds(j, band, stride=pitch), :] = res[:, k * LANES : (k + 1) * LANES]
+            acc_ref[pl.ds(gap * j, band, stride=pitch), :] = res[:, k * LANES : (k + 1) * LANES]
 
     chunk = 32
 
@@ -172,7 +177,7 @@
         for k in range(chunk):
             i = r * chunk + k
             row = k // 8 % 2 * (band // 2) + (r * (chunk // 16) + k // 16) * 8 + k % 8
-            total = acc_ref[pl.ds(row * pitch, cols), :]
+            total = acc_ref[pl.ds(row * pitch, cols, stride=gap), :]
             done_ref[i] = (pair_ref[i].astype(jnp.float32) + total).astype(jnp.bfloat16)
         at = pl.ds(pl.multiple_of(r * chunk, chunk), chunk)
         pltpu.make_async_copy(done_ref.at[at], out_ref.at[at], sems.at[r]).start()
@@ -216,7 +221,7 @@
             jax.ShapeDtypeStruct(final.shape, final.dtype),
             jax.ShapeDtypeStruct((2, 4 * LANES, 8 * CHANS), jnp.bfloat16),
         ),
-        scratch_shapes=[pltpu.VMEM(a.shape, a.dtype) for a in sources] + [pltpu.SemaphoreType.DMA((9,))],
+        scratch_shapes=[pltpu.VMEM(a.shape, a.dtype) for a in sources] + [pltpu.SemaphoreType.DMA((15,))],
         compiler_params=params,
         cost_estimate=pl.CostEstimate(
             flops=4 * seqs * residues * feats * CHANS, bytes_accessed=2 * seqs * residues * feats, transcendentals=0
@@ -286,7 +291,7 @@
             in_specs.append(vmem)
             out_shape, out_specs = jax.ShapeDtypeStruct(pair.shape, jnp.bfloat16), anywhere
             scratch = [
-                pltpu.VMEM((band * (cols + 1), zdim), jnp.float32),
+                pltpu.VMEM((band * (3 * cols + 1), zdim), jnp.float32),
                 pltpu.VMEM(pair.shape, jnp.bfloat16),
                 pltpu.SemaphoreType.DMA((band // 32,)),
             ]

time: 34.3 us -> 34.4 us (level)
  no operation moved by 1% of the time
where the time goes in v19:
time: 34.4 us; the launch traced here: 34.2 us
  starting transfers between devices  16.9 us (49%)
  Pallas kernels  12.1 us (35%)
  waiting for transfers between devices  4.99 us (15%)
    ppermute x10, starting transfers between devices, _xor(): return lax.ppermute(x, 'row', [(i, i ^ mask) for i in range(n)])  11.7 us
    pallas_call x4, Pallas kernels, add(): pl.pallas_call(functools.partial(_band_kernel, masks, total is None, 1.0...  6.51 us
    all_to_all x1, starting transfers between devices, shards(): lax.all_to_all(right, 'row', split_axis=0, concat_axis=0, tiled=True)  5.17 us
    all_to_all x1, waiting for transfers between devices, shards(): lax.all_to_all(right, 'row', split_axis=0, concat_axis=0, tiled=True)  3.87 us
    pallas_call x1, Pallas kernels, shards(): pl.pallas_call(_fold_kernel, out_shape=fold_out, scratch_shapes=[pltpu.VM...  2.76 us
    pallas_call x1, Pallas kernels, shards(): pl.pallas_call(_project_kernel, in_specs=[anywhere] * 8, out_specs=(vmem,...  2.51 us
    ppermute x10, waiting for transfers between devices, _xor(): return lax.ppermute(x, 'row', [(i, i ^ mask) for i in range(n)])  1.12 us
  transfers between devices with their start and end apart: 11, of which 4 were waited for; matrix products, arithmetic and copies ran while one was open for 0% of the time, Pallas kernels for 22%

profile of v19, /device:TPU:0, one launch (start us, length us, event | category | flops | bytes accessed | tf_op | source)
XLA Modules:
  0.0 34.2 jit_solution(11246705555320745055)
XLA Ops:
  0.0 2.5 %shard_map.100 = (bf16[256,128]{1,0:T(8,128)(2,1)S(1)}, bf16[32,8,128]{2,1,0:T(8,128)(2,1)}, bf16[1024,128]{1,0:T(8,128)(2,1)S(1)}, bf16[2,512,256]{2,1,0:T(8,128)(2,1)S(1)}) custom-call(bf16[2,512,256]{2,1,0:T(8,128)(2,1)} %refs_0_.1, f32[1,256]{1,0:T(1,128)} %bitcast.16, f32[1,256]{1,0:T(1,128)} %bitcast.17, bf16[32,256]{1,0:T(8,128)(2,1)} %bitcast.14, ...), custom_call_target="tpu_custom_call" | custom-call | flops 33554432 | bytes 524288 | tf_op jit(solution)/shard_map/pallas_call | solution.py:214
  2.5 4.1 %collective-permute-start.2 = (bf16[256,128]{1,0:T(8,128)(2,1)S(1)}, bf16[256,128]{1,0:T(8,128)(2,1)S(1)}, u32[]{:S(2)}, u32[]{:S(2)}) collective-permute-start(bf16[256,128]{1,0:T(8,128)(2,1)S(1)} %get-tuple-element.18.refs_0_), channel_id=1, source_target_pairs={{0,16},{1,17},{2,18},{3,19},{4,20},{5,21},{6,22},{7,23},{8,24},{9,... | collective-permute-start | bytes 196616 | tf_op jit(solution)/shard_map/ppermute | solution.py:197
  6.6 1.3 %collective-permute-start.1 = (bf16[256,128]{1,0:T(8,128)(2,1)S(1)}, bf16[256,128]{1,0:T(8,128)(2,1)S(1)}, u32[]{:S(2)}, u32[]{:S(2)}) collective-permute-start(bf16[256,128]{1,0:T(8,128)(2,1)S(1)} %get-tuple-element.18.refs_0_), channel_id=1, source_target_pairs={{0,24},{1,25},{2,26},{3,27},{4,28},{5,29},{6,30},{7,31},{8,16},{9,... | collective-permute-start | bytes 196616 | tf_op jit(solution)/shard_map/ppermute | solution.py:197
  8.0 0.2 collective-permute-start
  8.2 5.2 %all-to-all-start = ((bf16[32,8,128]{2,1,0:T(8,128)(2,1)}), bf16[32,8,128]{2,1,0:T(8,128)(2,1)S(1)}, u32[]{:S(2)}, u32[]{:S(2)}) async-start(bf16[32,8,128]{2,1,0:T(8,128)(2,1)} %get-tuple-element.20), calls=%async_computation | async-start | bytes 131072 | tf_op jit(solution)/shard_map/all_to_all | solution.py:231
  13.4 0.0 collective-permute-done.2.refs_3_
  13.4 0.0 collective-permute-done.1.refs_2_
  13.4 0.0 collective-permute-done.refs_1_
  13.4 0.3 shard_map.101.refs_0_
  13.7 1.8 %collective-permute-start.4 = (bf16[512,256]{1,0:T(8,128)(2,1)S(1)}, bf16[512,256]{1,0:T(8,128)(2,1)S(1)}, u32[]{:S(2)}, u32[]{:S(2)}) collective-permute-start(bf16[512,256]{1,0:T(8,128)(2,1)S(1)} %shard_map.101.refs_0_), channel_id=1, source_target_pairs={{0,4},{1,5},{2,6},{3,7},{4,0},{5,1},{6,2},{7,3},{8,12},{9,13},{10,... | collective-permute-start | bytes 786440 | tf_op jit(solution)/shard_map/ppermute | solution.py:197
  15.6 1.5 %collective-permute-start.3 = (bf16[512,256]{1,0:T(8,128)(2,1)S(1)}, bf16[512,256]{1,0:T(8,128)(2,1)S(1)}, u32[]{:S(2)}, u32[]{:S(2)}) collective-permute-start(bf16[512,256]{1,0:T(8,128)(2,1)S(1)} %shard_map.101.refs_0_), channel_id=1, source_target_pairs={{0,2},{1,3},{2,0},{3,1},{4,6},{5,7},{6,4},{7,5},{8,10},{9,11},{10,... | collective-permute-start | bytes 786440 | tf_op jit(solution)/shard_map/ppermute | solution.py:197
  17.0 3.9 %all-to-all-done.right_ref = bf16[32,8,128]{2,1,0:T(8,128)(2,1)S(1)} async-done(((bf16[32,8,128]{2,1,0:T(8,128)(2,1)}), bf16[32,8,128]{2,1,0:T(8,128)(2,1)S(1)}, u32[]{:S(2)}, u32[]{:S(2)}) %all-to-all-start) | async-done | bytes 65568 | tf_op jit(solution)/shard_map/all_to_all | solution.py:231
  20.9 2.8 %shard_map.102.refs_3_.refs_1_.refs_2_ = bf16[8,1,256,2048]{3,2,1,0:T(8,128)(2,1)S(1)} custom-call(bf16[32,8,128]{2,1,0:T(8,128)(2,1)S(1)} %all-to-all-done.right_ref, bf16[1024,128]{1,0:T(8,128)(2,1)S(1)} %get-tuple-element.21.final_ref), custom_call_target="tpu_custom_call" | custom-call | flops 2147483648 | bytes 8388608 | tf_op jit(solution)/shard_map/pallas_call | solution.py:262
  23.7 0.0 collective-permute-done.4.refs_2_
  23.7 0.3 collective-permute-done.3.refs_1_
  24.0 0.1 pad_maximum_fusion
  24.1 0.1 collective-permute-start.6
  24.2 0.6 %collective-permute-start.5 = (bf16[288,256]{1,0:T(8,128)(2,1)S(1)}, bf16[288,256]{1,0:T(8,128)(2,1)S(1)}, u32[]{:S(2)}, u32[]{:S(2)}) collective-permute-start(bf16[288,256]{1,0:T(8,128)(2,1)S(1)} %slice.6), channel_id=1, source_target_pairs={{0,4},{1,5},{2,6},{3,7},{4,0},{5,1},{6,2},{7,3},{8,12},{9,13},{10,... | collective-permute-start | bytes 442376 | tf_op jit(solution)/shard_map/ppermute | solution.py:197
  24.8 1.6 %collective-permute-start.8 = (bf16[224,256]{1,0:T(8,128)(2,1)S(1)}, bf16[224,256]{1,0:T(8,128)(2,1)S(1)}, u32[]{:S(2)}, u32[]{:S(2)}) collective-permute-start(bf16[224,256]{1,0:T(8,128)(2,1)S(1)} %slice.7), channel_id=1, source_target_pairs={{0,2},{1,3},{2,0},{3,1},{4,6},{5,7},{6,4},{7,5},{8,10},{9,11},{10,... | collective-permute-start | bytes 344072 | tf_op jit(solution)/shard_map/ppermute | solution.py:197
  26.3 1.8 %shard_map.103.refs_2_ = f32[512,2048]{1,0:T(8,128)S(1)} custom-call(bf16[512,256]{1,0:T(8,128)(2,1)S(1)} %shard_map.101.refs_0_, bf16[512,256]{1,0:T(8,128)(2,1)S(1)} %collective-permute-done.3.refs_1_, bf16[512,256]{1,0:T(8,128)(2,1)S(1)} %collective-permute-done.4.refs_2_, bf16[8,1,256,2048]{3,2,1,0:T(8,128)(2,1)S(1)} %shard_map.102.refs_3_.refs_1_.refs_2_), custom_call_target="tpu_custom_call" | custom-call | flops 1048576 | bytes 8192 | tf_op jit(solution)/shard_map/pallas_call | solution.py:300
  28.1 0.0 copy-start
  28.1 0.0 collective-permute-done.6.refs_0_
  28.2 1.8 %shard_map.104 = (f32[512,2048]{1,0:T(8,128)S(1)}, bf16[512,16,128]{2,1,0:T(8,128)(2,1)S(1)}) custom-call(bf16[3,512,256]{2,1,0:T(8,128)(2,1)S(1)} %collective-permute-done.6.refs_0_, bf16[8,1,256,2048]{3,2,1,0:T(8,128)(2,1)S(1)} %shard_map.102.refs_3_.refs_1_.refs_2_, f32[512,2048]{1,0:T(8,128)S(1)} %shard_map.103.refs_2_, bf16[512,16,128]{2,1,0:T(8,128)(2,1)} %refs_3_.1), custom_call_target="tpu_custom_call" | custom-call | flops 1048576 | bytes 8192 | tf_op jit(solution)/shard_map/pallas_call | solution.py:300
  30.0 0.5 %collective-permute-done.5.refs_0_ = bf16[288,256]{1,0:T(8,128)(2,1)S(1)} collective-permute-done((bf16[288,256]{1,0:T(8,128)(2,1)S(1)}, bf16[288,256]{1,0:T(8,128)(2,1)S(1)}, u32[]{:S(2)}, u32[]{:S(2)}) %collective-permute-start.5) | collective-permute-done | bytes 147488 | tf_op jit(solution)/shard_map/ppermute | solution.py:197
  30.5 0.0 collective-permute-start.7
  30.5 0.0 collective-permute-done.8.refs_1_
  30.5 0.5 %collective-permute-start.9 = (bf16[224,256]{1,0:T(8,128)(2,1)S(1)}, bf16[224,256]{1,0:T(8,128)(2,1)S(1)}, u32[]{:S(2)}, u32[]{:S(2)}) collective-permute-start(bf16[224,256]{1,0:T(8,128)(2,1)S(1)} %collective-permute-done.8.refs_1_), channel_id=1, source_target_pairs={{0,1},{1,0},{2,3},{3,2},{4,5},{5,4},{6,7},{7,6},{8,9},{9,8},{10,11... | collective-permute-start | bytes 344072 | tf_op jit(solution)/shard_map/ppermute | solution.py:197
  31.0 0.0 copy-done
  31.0 0.7 %shard_map.105.refs_3_ = f32[512,2048]{1,0:T(8,128)S(1)} custom-call(bf16[288,256]{1,0:T(8,128)(2,1)S(1)} %collective-permute-done.5.refs_0_, bf16[224,256]{1,0:T(8,128)(2,1)S(1)} %collective-permute-done.8.refs_1_, bf16[8,1,256,2048]{3,2,1,0:T(8,128)(2,1)S(1)} %shard_map.102.refs_3_.refs_1_.refs_2_, f32[512,2048]{1,0:T(8,128)S(1)} %get-tuple-element.29.refs_3_, ...), custom_call_target="tpu_custom_call" | custom-call | flops 1048576 | bytes 8192 | tf_op jit(solution)/shard_map/pallas_call | solution.py:300
  31.7 0.3 collective-permute-done.9.refs_1_
  32.0 0.0 collective-permute-done.7.refs_0_
  32.0 2.2 %shard_map.106 = bf16[512,16,128]{2,1,0:T(8,128)(2,1)} custom-call(bf16[288,256]{1,0:T(8,128)(2,1)S(1)} %collective-permute-done.7.refs_0_, bf16[224,256]{1,0:T(8,128)(2,1)S(1)} %collective-permute-done.9.refs_1_, bf16[8,1,256,2048]{3,2,1,0:T(8,128)(2,1)S(1)} %shard_map.102.refs_3_.refs_1_.refs_2_, f32[512,2048]{1,0:T(8,128)S(1)} %shard_map.105.refs_3_, ...), custom_call_target="tpu_custom_call" | custom-call | flops 1048576 | bytes 8192 | tf_op jit(solution)/shard_map/pallas_call | solution.py:300
  (2 shorter events, 0.0 us)
Async XLA Ops:
  2.5 10.9 %collective-permute-start.2 = (bf16[256,128]{1,0:T(8,128)(2,1)S(1)}, bf16[256,128]{1,0:T(8,128)(2,1)S(1)}, u32[]{:S(2)}, u32[]{:S(2)}) collective-permute-start(bf16[256,128]{1,0:T(8,128)(2,1)S(1)} %get-tuple-element.18.refs_0_), channel_id=1, source_target_pairs={{0,16},{1,17},{2,18},{3,19},{4,20},{5,21},{6,22},{7,23},{8,24},{9,... | collective-permute-start | bytes 196616 | tf_op jit(solution)/shard_map/ppermute | solution.py:197
  6.6 6.8 %collective-permute-start.1 = (bf16[256,128]{1,0:T(8,128)(2,1)S(1)}, bf16[256,128]{1,0:T(8,128)(2,1)S(1)}, u32[]{:S(2)}, u32[]{:S(2)}) collective-permute-start(bf16[256,128]{1,0:T(8,128)(2,1)S(1)} %get-tuple-element.18.refs_0_), channel_id=1, source_target_pairs={{0,24},{1,25},{2,26},{3,27},{4,28},{5,29},{6,30},{7,31},{8,16},{9,... | collective-permute-start | bytes 196616 | tf_op jit(solution)/shard_map/ppermute | solution.py:197
  8.0 5.4 %collective-permute-start = (bf16[256,128]{1,0:T(8,128)(2,1)S(1)}, bf16[256,128]{1,0:T(8,128)(2,1)S(1)}, u32[]{:S(2)}, u32[]{:S(2)}) collective-permute-start(bf16[256,128]{1,0:T(8,128)(2,1)S(1)} %get-tuple-element.18.refs_0_), channel_id=1, source_target_pairs={{0,8},{1,9},{2,10},{3,11},{4,12},{5,13},{6,14},{7,15},{8,0},{9,1},... | collective-permute-start | bytes 196616 | tf_op jit(solution)/shard_map/ppermute | solution.py:197
  8.2 12.7 %all-to-all-start = ((bf16[32,8,128]{2,1,0:T(8,128)(2,1)}), bf16[32,8,128]{2,1,0:T(8,128)(2,1)S(1)}, u32[]{:S(2)}, u32[]{:S(2)}) async-start(bf16[32,8,128]{2,1,0:T(8,128)(2,1)} %get-tuple-element.20), calls=%async_computation | async-start | bytes 131072 | tf_op jit(solution)/shard_map/all_to_all | solution.py:231
  13.7 9.9 %collective-permute-start.4 = (bf16[512,256]{1,0:T(8,128)(2,1)S(1)}, bf16[512,256]{1,0:T(8,128)(2,1)S(1)}, u32[]{:S(2)}, u32[]{:S(2)}) collective-permute-start(bf16[512,256]{1,0:T(8,128)(2,1)S(1)} %shard_map.101.refs_0_), channel_id=1, source_target_pairs={{0,4},{1,5},{2,6},{3,7},{4,0},{5,1},{6,2},{7,3},{8,12},{9,13},{10,... | collective-permute-start | bytes 786440 | tf_op jit(solution)/shard_map/ppermute | solution.py:197
  15.6 8.4 %collective-permute-start.3 = (bf16[512,256]{1,0:T(8,128)(2,1)S(1)}, bf16[512,256]{1,0:T(8,128)(2,1)S(1)}, u32[]{:S(2)}, u32[]{:S(2)}) collective-permute-start(bf16[512,256]{1,0:T(8,128)(2,1)S(1)} %shard_map.101.refs_0_), channel_id=1, source_target_pairs={{0,2},{1,3},{2,0},{3,1},{4,6},{5,7},{6,4},{7,5},{8,10},{9,11},{10,... | collective-permute-start | bytes 786440 | tf_op jit(solution)/shard_map/ppermute | solution.py:197
  24.1 4.1 %collective-permute-start.6 = (bf16[3,512,256]{2,1,0:T(8,128)(2,1)S(1)}, bf16[3,512,256]{2,1,0:T(8,128)(2,1)S(1)}, u32[]{:S(2)}, u32[]{:S(2)}) collective-permute-start(bf16[3,512,256]{2,1,0:T(8,128)(2,1)S(1)} %pad_maximum_fusion), channel_id=1, source_target_pairs={{0,1},{1,0},{2,3},{3,2},{4,5},{5,4},{6,7},{7,6},{8,9},{9,8},{10,11... | collective-permute-start | bytes 2359304 | tf_op jit(solution)/shard_map/ppermute | solution.py:197
  24.2 6.3 %collective-permute-start.5 = (bf16[288,256]{1,0:T(8,128)(2,1)S(1)}, bf16[288,256]{1,0:T(8,128)(2,1)S(1)}, u32[]{:S(2)}, u32[]{:S(2)}) collective-permute-start(bf16[288,256]{1,0:T(8,128)(2,1)S(1)} %slice.6), channel_id=1, source_target_pairs={{0,4},{1,5},{2,6},{3,7},{4,0},{5,1},{6,2},{7,3},{8,12},{9,13},{10,... | collective-permute-start | bytes 442376 | tf_op jit(solution)/shard_map/ppermute | solution.py:197
  24.8 5.7 %collective-permute-start.8 = (bf16[224,256]{1,0:T(8,128)(2,1)S(1)}, bf16[224,256]{1,0:T(8,128)(2,1)S(1)}, u32[]{:S(2)}, u32[]{:S(2)}) collective-permute-start(bf16[224,256]{1,0:T(8,128)(2,1)S(1)} %slice.7), channel_id=1, source_target_pairs={{0,2},{1,3},{2,0},{3,1},{4,6},{5,7},{6,4},{7,5},{8,10},{9,11},{10,... | collective-permute-start | bytes 344072 | tf_op jit(solution)/shard_map/ppermute | solution.py:197
  28.1 2.9 %copy-start = (f32[128]{0:T(128)S(1)}, f32[128]{0:T(128)}, u32[]{:S(2)}) copy-start(f32[128]{0:T(128)} %param.19) | copy-start | bytes 1540
  30.5 1.5 %collective-permute-start.7 = (bf16[288,256]{1,0:T(8,128)(2,1)S(1)}, bf16[288,256]{1,0:T(8,128)(2,1)S(1)}, u32[]{:S(2)}, u32[]{:S(2)}) collective-permute-start(bf16[288,256]{1,0:T(8,128)(2,1)S(1)} %collective-permute-done.5.refs_0_), channel_id=1, source_target_pairs={{0,1},{1,0},{2,3},{3,2},{4,5},{5,4},{6,7},{7,6},{8,9},{9,8},{10,11... | collective-permute-start | bytes 442376 | tf_op jit(solution)/shard_map/ppermute | solution.py:197
  30.5 1.5 %collective-permute-start.9 = (bf16[224,256]{1,0:T(8,128)(2,1)S(1)}, bf16[224,256]{1,0:T(8,128)(2,1)S(1)}, u32[]{:S(2)}, u32[]{:S(2)}) collective-permute-start(bf16[224,256]{1,0:T(8,128)(2,1)S(1)} %collective-permute-done.8.refs_1_), channel_id=1, source_target_pairs={{0,1},{1,0},{2,3},{3,2},{4,5},{5,4},{6,7},{7,6},{8,9},{9,8},{10,11... | collective-permute-start | bytes 344072 | tf_op jit(solution)/shard_map/ppermute | solution.py:197

commit v20 on v19

--- a/solution.py
+++ b/solution.py
@@ -35,7 +35,7 @@
     sources, final_source, outs, held = refs[:7], refs[7], refs[8:12], refs[12:19]
     left_ref, right_ref, final_ref, order_ref = outs
     sems = refs[19]
-    pieces = 4
+    pieces = 1
     size = held[0].shape[1] // pieces
     at = [(s, pl.ds(k * size, size)) for s in range(2) for k in range(pieces)]
     pairs = [(sources[0].at[i], held[0].at[i]) for i in at]
@@ -111,18 +111,13 @@
                 out_ref[g, 0, pl.ds(pair * 16, 16), pl.ds(j * LANES, LANES)] = tile.astype(jnp.bfloat16)
 
 
-def _band_kernel(masks, begins, scale, last, held, *refs):
+def _band_kernel(masks, begins, scale, last, carries, held, *refs):
     refs = list(refs)
     take = lambda k: [refs.pop(0) for _ in range(k)]
-    if masks == (1, 3, 5):
-        (block,) = take(1)
-        lines = [[block.at[k]] for k in range(3)]
-    else:
-        lines = [take(2 if mask in (6, 7) else 1) for mask in masks]
+    lines = take(len(masks))
     (t_ref,) = take(1)
     (sum_ref,) = (None,) if begins else take(1)
     shift_ref = None if scale is None or last else take(1)[0]
-    carries = masks == (1, 3, 5)
     pair_ref = take(1)[0] if last or carries else None
     (out_ref,) = take(1)
     if carries:
@@ -131,10 +126,12 @@
         fetch.start()
     me = lax.axis_index("row")
     wide = t_ref.shape[2]
-    chunks = [((me % 8) ^ mask, q ^ (me // 32)) for mask in masks for q in range(t_ref.shape[1])]
+    first = 2 + me % 2 * 2
+    offset = lambda mask: mask if mask < 8 else (first if mask < 10 else 6 - first) ^ (mask % 2)
+    chunks = [((me % 8) ^ offset(mask), q ^ (me // 32)) for mask in masks for q in range(t_ref.shape[1])]
 
     tile = 256 if last or not held else 512
-    band = sum(part.shape[0] for part in lines[0])
+    band = lines[0].shape[0]
 
     def column(begin):
         at = pl.ds(begin, tile)
@@ -144,7 +141,7 @@
             for i, (g, q) in enumerate(chunks):
                 pltpu.sync_copy(t_ref.at[g, q, :, at], refs[0].at[pl.ds(i * wide, wide)])
             rhs = refs[0][...]
-        lhs = jnp.concatenate([jnp.concatenate([part[...] for part in line], axis=0) for line in lines], axis=1)
+        lhs = jnp.concatenate([line[...] for line in lines], axis=1)
         res = jnp.dot(lhs, rhs, preferred_element_type=jnp.float32)
         if last:
             return res * scale + sum_ref[:, at]
@@ -221,7 +218,7 @@
             jax.ShapeDtypeStruct(final.shape, final.dtype),
             jax.ShapeDtypeStruct((2, 4 * LANES, 8 * CHANS), jnp.bfloat16),
         ),
-        scratch_shapes=[pltpu.VMEM(a.shape, a.dtype) for a in sources] + [pltpu.SemaphoreType.DMA((15,))],
+        scratch_shapes=[pltpu.VMEM(a.shape, a.dtype) for a in sources] + [pltpu.SemaphoreType.DMA((9,))],
         compiler_params=params,
         cost_estimate=pl.CostEstimate(
             flops=4 * seqs * residues * feats * CHANS, bytes_accessed=2 * seqs * residues * feats, transcendentals=0
@@ -242,7 +239,11 @@
         compiler_params=params,
         cost_estimate=pl.CostEstimate(flops=2**27, bytes_accessed=2**20, transcendentals=0),
     )(*pieces, order)
-    x, y = _xor(line, 2, n), _xor(line, 4, n)
+    turn = lambda a, masks: lax.ppermute(a, "row", [(i, i ^ masks[i % 2]) for i in range(n)])
+    partner = _xor(line, 1, n)
+    near = turn(line, (2, 4))
+    near_other = turn(partner, (2, 4))
+    diagonal = turn(near, (4, 2))
 
     fold_cost = pl.CostEstimate(
         flops=2 * n * 32 * 256 * CHANS * zdim, bytes_accessed=4 * n * CHANS * cols * zdim, transcendentals=0
@@ -270,9 +271,8 @@
 
     pinned = pltpu.with_memory_space_constraint(pair, pltpu.HBM)
 
-    def add(lines, masks, total, last=False, scaled=False, carried=None):
+    def add(lines, masks, total, last=False, scaled=False, carries=False, carried=None):
         depth = len(masks) * parts * 8 * CHANS
-        carries = masks == (1, 3, 5)
         operands = [*lines, folded] + ([] if total is None else [total])
         in_specs = [vmem] * len(operands)
         if not small:
@@ -298,7 +298,7 @@
         if not small:
             scratch.append(pltpu.VMEM((depth, 256), jnp.bfloat16))
         return pl.pallas_call(
-            functools.partial(_band_kernel, masks, total is None, 1.0 / count if scaled else None, last, small),
+            functools.partial(_band_kernel, masks, total is None, 1.0 / count if scaled else None, last, carries, small),
             in_specs=in_specs,
             out_specs=out_specs,
             out_shape=out_shape,
@@ -309,18 +309,15 @@
             ),
         )(*operands)
 
-    x, y, folded = lax.optimization_barrier((x, y, folded))
-    cut = band * 9 // 16
-    upper, lower = _xor(x[:cut], 4, n), _xor(y[cut:], 2, n)
-    across = _xor(jnp.stack([line, x, y]), 1, n)
-    total = add([line, x, y], (0, 2, 4), None)
-    total, carried = add([across], (1, 3, 5), total)
-    upper, total = lax.optimization_barrier((upper, total))
-    last = [_xor(upper, 1, n)]
-    lower, total = lax.optimization_barrier((lower, total))
-    last.append(_xor(lower, 1, n))
-    total = add([upper, lower], (6,), total, scaled=True)
-    return add(last, (7,), total, last=True, scaled=True, carried=carried)
+    far_other = _xor(near, 1, n)
+    near_other, folded = lax.optimization_barrier((near_other, folded))
+    far = _xor(near_other, 1, n)
+    total, carried = add([line, partner, near, near_other], (0, 1, 8, 9), None, carries=True)
+    diagonal, total = lax.optimization_barrier((diagonal, total))
+    last = _xor(diagonal, 1, n)
+    total = add([diagonal], (6,), total)
+    total = add([far, far_other], (10, 11), total, scaled=True)
+    return add([last], (7,), total, last=True, scaled=True, carried=carried)
 
 
 def solution(mesh):

time: 34.4 us -> 38.1 us (1.11)
  waiting for transfers between devices: 4.99 us -> 8.95 us
  starting transfers between devices: 16.9 us -> 15.6 us
  Pallas kernels: 12.1 us -> 13.1 us
    ppermute x10 -> x7, starting transfers between devices: 11.7 us -> 6.47 us  [_xor(): return lax.ppermute(x, 'row', [(i, i ^ mask) for i in range(n)])]
    ppermute x0 -> x3, starting transfers between devices: none -> 4.85 us  [shards(): lax.ppermute(a, 'row', [(i, i ^ masks[i % 2]) for i in range(n)])]
    ppermute x10 -> x7, waiting for transfers between devices: 1.12 us -> 4.75 us  [_xor(): return lax.ppermute(x, 'row', [(i, i ^ mask) for i in range(n)])]
    pallas_call x4, Pallas kernels: 6.51 us -> 7.64 us  [add(): pl.pallas_call(functools.partial(_band_kernel, masks, total is None, 1.0...]
    all_to_all x1, starting transfers between devices: 5.17 us -> 4.31 us  [shards(): lax.all_to_all(right, 'row', split_axis=0, concat_axis=0, tiled=True)]
where the time goes in v20:
time: 38.1 us; the launch traced here: 37.9 us
  starting transfers between devices  15.6 us (41%)
  Pallas kernels  13.1 us (34%)
  waiting for transfers between devices  8.95 us (23%)
    pallas_call x4, Pallas kernels, add(): pl.pallas_call(functools.partial(_band_kernel, masks, total is None, 1.0...  7.64 us
    ppermute x7, starting transfers between devices, _xor(): return lax.ppermute(x, 'row', [(i, i ^ mask) for i in range(n)])  6.47 us
    ppermute x3, starting transfers between devices, shards(): lax.ppermute(a, 'row', [(i, i ^ masks[i % 2]) for i in range(n)])  4.85 us
    ppermute x7, waiting for transfers between devices, _xor(): return lax.ppermute(x, 'row', [(i, i ^ mask) for i in range(n)])  4.75 us
    all_to_all x1, starting transfers between devices, shards(): lax.all_to_all(right, 'row', split_axis=0, concat_axis=0, tiled=True)  4.31 us
    all_to_all x1, waiting for transfers between devices, shards(): lax.all_to_all(right, 'row', split_axis=0, concat_axis=0, tiled=True)  4.2 us
    pallas_call x1, Pallas kernels, shards(): pl.pallas_call(_fold_kernel, out_shape=fold_out, scratch_shapes=[pltpu.VM...  2.76 us
    pallas_call x1, Pallas kernels, shards(): pl.pallas_call(_project_kernel, in_specs=[anywhere] * 8, out_specs=(vmem,...  2.43 us
  transfers between devices with their start and end apart: 11, of which 4 were waited for; matrix products, arithmetic and copies ran while one was open for 0% of the time, Pallas kernels for 22%

profile of v20, /device:TPU:0, one launch (start us, length us, event | category | flops | bytes accessed | tf_op | source)
XLA Modules:
  0.0 37.9 jit_solution(14854101262821026284)
XLA Ops:
  0.0 2.4 %shard_map.100 = (bf16[256,128]{1,0:T(8,128)(2,1)S(1)}, bf16[32,8,128]{2,1,0:T(8,128)(2,1)}, bf16[1024,128]{1,0:T(8,128)(2,1)S(1)}, bf16[2,512,256]{2,1,0:T(8,128)(2,1)S(1)}) custom-call(bf16[2,512,256]{2,1,0:T(8,128)(2,1)} %refs_0_.1, f32[1,256]{1,0:T(1,128)} %bitcast.10, f32[1,256]{1,0:T(1,128)} %bitcast.11, bf16[32,256]{1,0:T(8,128)(2,1)} %bitcast.8, ...), custom_call_target="tpu_custom_call" | custom-call | flops 33554432 | bytes 524288 | tf_op jit(solution)/shard_map/pallas_call | solution.py:211
  2.4 4.1 %collective-permute-start.2 = (bf16[256,128]{1,0:T(8,128)(2,1)S(1)}, bf16[256,128]{1,0:T(8,128)(2,1)S(1)}, u32[]{:S(2)}, u32[]{:S(2)}) collective-permute-start(bf16[256,128]{1,0:T(8,128)(2,1)S(1)} %get-tuple-element.15.refs_0_), channel_id=1, source_target_pairs={{0,16},{1,17},{2,18},{3,19},{4,20},{5,21},{6,22},{7,23},{8,24},{9,... | collective-permute-start | bytes 196616 | tf_op jit(solution)/shard_map/ppermute | solution.py:194
  6.5 1.3 %collective-permute-start.1 = (bf16[256,128]{1,0:T(8,128)(2,1)S(1)}, bf16[256,128]{1,0:T(8,128)(2,1)S(1)}, u32[]{:S(2)}, u32[]{:S(2)}) collective-permute-start(bf16[256,128]{1,0:T(8,128)(2,1)S(1)} %get-tuple-element.15.refs_0_), channel_id=1, source_target_pairs={{0,24},{1,25},{2,26},{3,27},{4,28},{5,29},{6,30},{7,31},{8,16},{9,... | collective-permute-start | bytes 196616 | tf_op jit(solution)/shard_map/ppermute | solution.py:194
  7.9 0.2 collective-permute-start
  8.1 2.2 %collective-permute-done.2.refs_3_ = bf16[256,128]{1,0:T(8,128)(2,1)S(1)} collective-permute-done((bf16[256,128]{1,0:T(8,128)(2,1)S(1)}, bf16[256,128]{1,0:T(8,128)(2,1)S(1)}, u32[]{:S(2)}, u32[]{:S(2)}) %collective-permute-start.2) | collective-permute-done | bytes 65568 | tf_op jit(solution)/shard_map/ppermute | solution.py:194
  10.3 2.5 %collective-permute-done.1.refs_2_ = bf16[256,128]{1,0:T(8,128)(2,1)S(1)} collective-permute-done((bf16[256,128]{1,0:T(8,128)(2,1)S(1)}, bf16[256,128]{1,0:T(8,128)(2,1)S(1)}, u32[]{:S(2)}, u32[]{:S(2)}) %collective-permute-start.1) | collective-permute-done | bytes 65568 | tf_op jit(solution)/shard_map/ppermute | solution.py:194
  12.8 0.1 collective-permute-done.refs_1_
  12.9 0.3 shard_map.101.refs_0_
  13.2 0.1 collective-permute-start.5
  13.2 1.6 %collective-permute-start.3 = (bf16[512,256]{1,0:T(8,128)(2,1)S(1)}, bf16[512,256]{1,0:T(8,128)(2,1)S(1)}, u32[]{:S(2)}, u32[]{:S(2)}) collective-permute-start(bf16[512,256]{1,0:T(8,128)(2,1)S(1)} %shard_map.101.refs_0_), channel_id=1, source_target_pairs={{0,2},{1,5},{2,0},{3,7},{4,6},{5,1},{6,4},{7,3},{8,10},{9,13},{10,... | collective-permute-start | bytes 786440 | tf_op jit(solution)/shard_map/ppermute | solution.py:242
  14.8 4.3 %all-to-all-start = ((bf16[32,8,128]{2,1,0:T(8,128)(2,1)}), bf16[32,8,128]{2,1,0:T(8,128)(2,1)S(1)}, u32[]{:S(2)}, u32[]{:S(2)}) async-start(bf16[32,8,128]{2,1,0:T(8,128)(2,1)} %get-tuple-element.17), calls=%async_computation | async-start | bytes 131072 | tf_op jit(solution)/shard_map/all_to_all | solution.py:228
  19.1 0.0 collective-permute-done.5.refs_1_
  19.1 1.8 %collective-permute-start.6 = (bf16[512,256]{1,0:T(8,128)(2,1)S(1)}, bf16[512,256]{1,0:T(8,128)(2,1)S(1)}, u32[]{:S(2)}, u32[]{:S(2)}) collective-permute-start(bf16[512,256]{1,0:T(8,128)(2,1)S(1)} %collective-permute-done.5.refs_1_), channel_id=1, source_target_pairs={{0,2},{1,5},{2,0},{3,7},{4,6},{5,1},{6,4},{7,3},{8,10},{9,13},{10,... | collective-permute-start | bytes 786440 | tf_op jit(solution)/shard_map/ppermute | solution.py:242
  21.0 0.0 collective-permute-done.3.refs_2_
  21.0 1.5 %collective-permute-start.4 = (bf16[512,256]{1,0:T(8,128)(2,1)S(1)}, bf16[512,256]{1,0:T(8,128)(2,1)S(1)}, u32[]{:S(2)}, u32[]{:S(2)}) collective-permute-start(bf16[512,256]{1,0:T(8,128)(2,1)S(1)} %collective-permute-done.3.refs_2_), channel_id=1, source_target_pairs={{0,4},{1,3},{2,6},{3,1},{4,0},{5,7},{6,2},{7,5},{8,12},{9,11},{10,... | collective-permute-start | bytes 786440 | tf_op jit(solution)/shard_map/ppermute | solution.py:242
  22.4 4.2 %all-to-all-done.right_ref = bf16[32,8,128]{2,1,0:T(8,128)(2,1)S(1)} async-done(((bf16[32,8,128]{2,1,0:T(8,128)(2,1)}), bf16[32,8,128]{2,1,0:T(8,128)(2,1)S(1)}, u32[]{:S(2)}, u32[]{:S(2)}) %all-to-all-start) | async-done | bytes 65568 | tf_op jit(solution)/shard_map/all_to_all | solution.py:228
  26.6 2.8 %shard_map.102.refs_4_.refs_1_.refs_2_ = bf16[8,1,256,2048]{3,2,1,0:T(8,128)(2,1)S(1)} custom-call(bf16[32,8,128]{2,1,0:T(8,128)(2,1)S(1)} %all-to-all-done.right_ref, bf16[1024,128]{1,0:T(8,128)(2,1)S(1)} %get-tuple-element.18.final_ref), custom_call_target="tpu_custom_call" | custom-call | flops 2147483648 | bytes 8388608 | tf_op jit(solution)/shard_map/pallas_call | solution.py:263
  29.4 0.1 collective-permute-start.9
  29.5 0.0 collective-permute-done.6.refs_3_
  29.5 0.5 %collective-permute-start.8 = (bf16[512,256]{1,0:T(8,128)(2,1)S(1)}, bf16[512,256]{1,0:T(8,128)(2,1)S(1)}, u32[]{:S(2)}, u32[]{:S(2)}) collective-permute-start(bf16[512,256]{1,0:T(8,128)(2,1)S(1)} %collective-permute-done.6.refs_3_), channel_id=1, source_target_pairs={{0,1},{1,0},{2,3},{3,2},{4,5},{5,4},{6,7},{7,6},{8,9},{9,8},{10,11... | collective-permute-start | bytes 786440 | tf_op jit(solution)/shard_map/ppermute | solution.py:194
  30.0 3.4 %shard_map.103 = (f32[512,2048]{1,0:T(8,128)S(1)}, bf16[512,16,128]{2,1,0:T(8,128)(2,1)S(1)}) custom-call(bf16[512,256]{1,0:T(8,128)(2,1)S(1)} %shard_map.101.refs_0_, bf16[512,256]{1,0:T(8,128)(2,1)S(1)} %collective-permute-done.5.refs_1_, bf16[512,256]{1,0:T(8,128)(2,1)S(1)} %collective-permute-done.3.refs_2_, ...), custom_call_target="tpu_custom_call" | custom-call | flops 1048576 | bytes 8192 | tf_op jit(solution)/shard_map/pallas_call | solution.py:300
  33.4 0.0 collective-permute-done.4.refs_0_
  33.4 0.0 copy-start
  33.4 0.2 collective-permute-start.7
  33.6 0.7 %shard_map.104.refs_3_ = f32[512,2048]{1,0:T(8,128)S(1)} custom-call(bf16[512,256]{1,0:T(8,128)(2,1)S(1)} %collective-permute-done.4.refs_0_, bf16[8,1,256,2048]{3,2,1,0:T(8,128)(2,1)S(1)} %shard_map.102.refs_4_.refs_1_.refs_2_, f32[512,2048]{1,0:T(8,128)S(1)} %get-tuple-element.23.refs_2_), custom_call_target="tpu_custom_call" | custom-call | flops 1048576 | bytes 8192 | tf_op jit(solution)/shard_map/pallas_call | solution.py:300
  34.3 0.0 collective-permute-done.9.refs_1_
  34.3 0.0 collective-permute-done.8.refs_0_
  34.3 0.0 copy-done
  34.3 1.3 %shard_map.105.refs_2_ = f32[512,2048]{1,0:T(8,128)S(1)} custom-call(bf16[512,256]{1,0:T(8,128)(2,1)S(1)} %collective-permute-done.8.refs_0_, bf16[512,256]{1,0:T(8,128)(2,1)S(1)} %collective-permute-done.9.refs_1_, bf16[8,1,256,2048]{3,2,1,0:T(8,128)(2,1)S(1)} %shard_map.102.refs_4_.refs_1_.refs_2_, f32[512,2048]{1,0:T(8,128)S(1)} %shard_map.104.refs_3_, ...), custom_call_target="tpu_custom_call" | custom-call | flops 1048576 | bytes 8192 | tf_op jit(solution)/shard_map/pallas_call | solution.py:300
  35.6 0.0 collective-permute-done.7.refs_0_
  35.6 2.2 %shard_map.106 = bf16[512,16,128]{2,1,0:T(8,128)(2,1)} custom-call(bf16[512,256]{1,0:T(8,128)(2,1)S(1)} %collective-permute-done.7.refs_0_, bf16[8,1,256,2048]{3,2,1,0:T(8,128)(2,1)S(1)} %shard_map.102.refs_4_.refs_1_.refs_2_, f32[512,2048]{1,0:T(8,128)S(1)} %shard_map.105.refs_2_, bf16[512,16,128]{2,1,0:T(8,128)(2,1)S(1)} %get-tuple-element.24.refs_3_), custom_call_target="tpu_custom_call" | custom-call | flops 1048576 | bytes 8192 | tf_op jit(solution)/shard_map/pallas_call | solution.py:300
Async XLA Ops:
  2.4 7.9 %collective-permute-start.2 = (bf16[256,128]{1,0:T(8,128)(2,1)S(1)}, bf16[256,128]{1,0:T(8,128)(2,1)S(1)}, u32[]{:S(2)}, u32[]{:S(2)}) collective-permute-start(bf16[256,128]{1,0:T(8,128)(2,1)S(1)} %get-tuple-element.15.refs_0_), channel_id=1, source_target_pairs={{0,16},{1,17},{2,18},{3,19},{4,20},{5,21},{6,22},{7,23},{8,24},{9,... | collective-permute-start | bytes 196616 | tf_op jit(solution)/shard_map/ppermute | solution.py:194
  6.5 6.2 %collective-permute-start.1 = (bf16[256,128]{1,0:T(8,128)(2,1)S(1)}, bf16[256,128]{1,0:T(8,128)(2,1)S(1)}, u32[]{:S(2)}, u32[]{:S(2)}) collective-permute-start(bf16[256,128]{1,0:T(8,128)(2,1)S(1)} %get-tuple-element.15.refs_0_), channel_id=1, source_target_pairs={{0,24},{1,25},{2,26},{3,27},{4,28},{5,29},{6,30},{7,31},{8,16},{9,... | collective-permute-start | bytes 196616 | tf_op jit(solution)/shard_map/ppermute | solution.py:194
  7.9 5.0 %collective-permute-start = (bf16[256,128]{1,0:T(8,128)(2,1)S(1)}, bf16[256,128]{1,0:T(8,128)(2,1)S(1)}, u32[]{:S(2)}, u32[]{:S(2)}) collective-permute-start(bf16[256,128]{1,0:T(8,128)(2,1)S(1)} %get-tuple-element.15.refs_0_), channel_id=1, source_target_pairs={{0,8},{1,9},{2,10},{3,11},{4,12},{5,13},{6,14},{7,15},{8,0},{9,1},... | collective-permute-start | bytes 196616 | tf_op jit(solution)/shard_map/ppermute | solution.py:194
  13.2 6.0 %collective-permute-start.5 = (bf16[512,256]{1,0:T(8,128)(2,1)S(1)}, bf16[512,256]{1,0:T(8,128)(2,1)S(1)}, u32[]{:S(2)}, u32[]{:S(2)}) collective-permute-start(bf16[512,256]{1,0:T(8,128)(2,1)S(1)} %shard_map.101.refs_0_), channel_id=1, source_target_pairs={{0,1},{1,0},{2,3},{3,2},{4,5},{5,4},{6,7},{7,6},{8,9},{9,8},{10,11... | collective-permute-start | bytes 786440 | tf_op jit(solution)/shard_map/ppermute | solution.py:194
  13.2 7.7 %collective-permute-start.3 = (bf16[512,256]{1,0:T(8,128)(2,1)S(1)}, bf16[512,256]{1,0:T(8,128)(2,1)S(1)}, u32[]{:S(2)}, u32[]{:S(2)}) collective-permute-start(bf16[512,256]{1,0:T(8,128)(2,1)S(1)} %shard_map.101.refs_0_), channel_id=1, source_target_pairs={{0,2},{1,5},{2,0},{3,7},{4,6},{5,1},{6,4},{7,3},{8,10},{9,13},{10,... | collective-permute-start | bytes 786440 | tf_op jit(solution)/shard_map/ppermute | solution.py:242
  14.8 11.8 %all-to-all-start = ((bf16[32,8,128]{2,1,0:T(8,128)(2,1)}), bf16[32,8,128]{2,1,0:T(8,128)(2,1)S(1)}, u32[]{:S(2)}, u32[]{:S(2)}) async-start(bf16[32,8,128]{2,1,0:T(8,128)(2,1)} %get-tuple-element.17), calls=%async_computation | async-start | bytes 131072 | tf_op jit(solution)/shard_map/all_to_all | solution.py:228
  19.1 10.4 %collective-permute-start.6 = (bf16[512,256]{1,0:T(8,128)(2,1)S(1)}, bf16[512,256]{1,0:T(8,128)(2,1)S(1)}, u32[]{:S(2)}, u32[]{:S(2)}) collective-permute-start(bf16[512,256]{1,0:T(8,128)(2,1)S(1)} %collective-permute-done.5.refs_1_), channel_id=1, source_target_pairs={{0,2},{1,5},{2,0},{3,7},{4,6},{5,1},{6,4},{7,3},{8,10},{9,13},{10,... | collective-permute-start | bytes 786440 | tf_op jit(solution)/shard_map/ppermute | solution.py:242
  21.0 12.4 %collective-permute-start.4 = (bf16[512,256]{1,0:T(8,128)(2,1)S(1)}, bf16[512,256]{1,0:T(8,128)(2,1)S(1)}, u32[]{:S(2)}, u32[]{:S(2)}) collective-permute-start(bf16[512,256]{1,0:T(8,128)(2,1)S(1)} %collective-permute-done.3.refs_2_), channel_id=1, source_target_pairs={{0,4},{1,3},{2,6},{3,1},{4,0},{5,7},{6,2},{7,5},{8,12},{9,11},{10,... | collective-permute-start | bytes 786440 | tf_op jit(solution)/shard_map/ppermute | solution.py:242
  29.4 4.9 %collective-permute-start.9 = (bf16[512,256]{1,0:T(8,128)(2,1)S(1)}, bf16[512,256]{1,0:T(8,128)(2,1)S(1)}, u32[]{:S(2)}, u32[]{:S(2)}) collective-permute-start(bf16[512,256]{1,0:T(8,128)(2,1)S(1)} %collective-permute-done.3.refs_2_), channel_id=1, source_target_pairs={{0,1},{1,0},{2,3},{3,2},{4,5},{5,4},{6,7},{7,6},{8,9},{9,8},{10,11... | collective-permute-start | bytes 786440 | tf_op jit(solution)/shard_map/ppermute | solution.py:194
  29.5 4.8 %collective-permute-start.8 = (bf16[512,256]{1,0:T(8,128)(2,1)S(1)}, bf16[512,256]{1,0:T(8,128)(2,1)S(1)}, u32[]{:S(2)}, u32[]{:S(2)}) collective-permute-start(bf16[512,256]{1,0:T(8,128)(2,1)S(1)} %collective-permute-done.6.refs_3_), channel_id=1, source_target_pairs={{0,1},{1,0},{2,3},{3,2},{4,5},{5,4},{6,7},{7,6},{8,9},{9,8},{10,11... | collective-permute-start | bytes 786440 | tf_op jit(solution)/shard_map/ppermute | solution.py:194
  33.4 0.9 %copy-start = (f32[128]{0:T(128)S(1)}, f32[128]{0:T(128)}, u32[]{:S(2)}) copy-start(f32[128]{0:T(128)} %param.19) | copy-start | bytes 1540
  33.4 2.2 %collective-permute-start.7 = (bf16[512,256]{1,0:T(8,128)(2,1)S(1)}, bf16[512,256]{1,0:T(8,128)(2,1)S(1)}, u32[]{:S(2)}, u32[]{:S(2)}) collective-permute-start(bf16[512,256]{1,0:T(8,128)(2,1)S(1)} %collective-permute-done.4.refs_0_), channel_id=1, source_target_pairs={{0,1},{1,0},{2,3},{3,2},{4,5},{5,4},{6,7},{7,6},{8,9},{9,8},{10,11... | collective-permute-start | bytes 786440 | tf_op jit(solution)/shard_map/ppermute | solution.py:194

commit v21 on v20

--- a/solution.py
+++ b/solution.py
@@ -243,7 +243,6 @@
     partner = _xor(line, 1, n)
     near = turn(line, (2, 4))
     near_other = turn(partner, (2, 4))
-    diagonal = turn(near, (4, 2))
 
     fold_cost = pl.CostEstimate(
         flops=2 * n * 32 * 256 * CHANS * zdim, bytes_accessed=4 * n * CHANS * cols * zdim, transcendentals=0
@@ -309,10 +308,11 @@
             ),
         )(*operands)
 
-    far_other = _xor(near, 1, n)
-    near_other, folded = lax.optimization_barrier((near_other, folded))
-    far = _xor(near_other, 1, n)
-    total, carried = add([line, partner, near, near_other], (0, 1, 8, 9), None, carries=True)
+    total = add([line, partner], (0, 1), None)
+    near, near_other, _ = lax.optimization_barrier((near, near_other, folded))
+    diagonal = turn(near, (4, 2))
+    far_other, far = _xor(near, 1, n), _xor(near_other, 1, n)
+    total, carried = add([near, near_other], (8, 9), total, carries=True)
     diagonal, total = lax.optimization_barrier((diagonal, total))
     last = _xor(diagonal, 1, n)
     total = add([diagonal], (6,), total)

time: 38.1 us -> 40.8 us (1.071)
  waiting for transfers between devices: 8.95 us -> 13.6 us
  starting transfers between devices: 15.6 us -> 14.3 us
  Pallas kernels: 13.1 us -> 12.5 us
    ppermute x3, waiting for transfers between devices: 0.01 us -> 1.84 us  [shards(): lax.ppermute(a, 'row', [(i, i ^ masks[i % 2]) for i in range(n)])]
    ppermute x3, starting transfers between devices: 4.85 us -> 3.25 us  [shards(): lax.ppermute(a, 'row', [(i, i ^ masks[i % 2]) for i in range(n)])]
    ppermute x7, waiting for transfers between devices: 4.75 us -> 6.34 us  [_xor(): return lax.ppermute(x, 'row', [(i, i ^ mask) for i in range(n)])]
    all_to_all x1, waiting for transfers between devices: 4.2 us -> 5.42 us  [shards(): lax.all_to_all(right, 'row', split_axis=0, concat_axis=0, tiled=True)]
    pallas_call x4 -> x5, Pallas kernels: 7.64 us -> 7.04 us  [add(): pl.pallas_call(functools.partial(_band_kernel, masks, total is None, 1.0...]
    all_to_all x1, starting transfers between devices: 4.31 us -> 4.76 us  [shards(): lax.all_to_all(right, 'row', split_axis=0, concat_axis=0, tiled=True)]
  transfers between devices with their start and end apart: 11 -> 11, of which waited for: 4 -> 4; matrix products, arithmetic and copies ran while one was open for 0% -> 0% of each run, Pallas kernels for 22% -> 19%
where the time goes in v21:
time: 40.8 us; the launch traced here: 40.6 us
  starting transfers between devices  14.3 us (35%)
  waiting for transfers between devices  13.6 us (33%)
  Pallas kernels  12.5 us (31%)
    pallas_call x5, Pallas kernels, add(): pl.pallas_call(functools.partial(_band_kernel, masks, total is None, 1.0...  7.04 us
    ppermute x7, waiting for transfers between devices, _xor(): return lax.ppermute(x, 'row', [(i, i ^ mask) for i in range(n)])  6.34 us
    ppermute x7, starting transfers between devices, _xor(): return lax.ppermute(x, 'row', [(i, i ^ mask) for i in range(n)])  6.32 us
    all_to_all x1, waiting for transfers between devices, shards(): lax.all_to_all(right, 'row', split_axis=0, concat_axis=0, tiled=True)  5.42 us
    all_to_all x1, starting transfers between devices, shards(): lax.all_to_all(right, 'row', split_axis=0, concat_axis=0, tiled=True)  4.76 us
    ppermute x3, starting transfers between devices, shards(): lax.ppermute(a, 'row', [(i, i ^ masks[i % 2]) for i in range(n)])  3.25 us
    pallas_call x1, Pallas kernels, shards(): pl.pallas_call(_fold_kernel, out_shape=fold_out, scratch_shapes=[pltpu.VM...  2.76 us
    pallas_call x1, Pallas kernels, shards(): pl.pallas_call(_project_kernel, in_specs=[anywhere] * 8, out_specs=(vmem,...  2.43 us
  transfers between devices with their start and end apart: 11, of which 4 were waited for; matrix products, arithmetic and copies ran while one was open for 0% of the time, Pallas kernels for 19%

profile of v21, /device:TPU:0, one launch (start us, length us, event | category | flops | bytes accessed | tf_op | source)
XLA Modules:
  0.0 40.6 jit_solution(13824905347484451208)
XLA Ops:
  0.0 2.4 %shard_map.100 = (bf16[256,128]{1,0:T(8,128)(2,1)S(1)}, bf16[32,8,128]{2,1,0:T(8,128)(2,1)}, bf16[1024,128]{1,0:T(8,128)(2,1)S(1)}, bf16[2,512,256]{2,1,0:T(8,128)(2,1)S(1)}) custom-call(bf16[2,512,256]{2,1,0:T(8,128)(2,1)} %refs_0_.1, f32[1,256]{1,0:T(1,128)} %bitcast.10, f32[1,256]{1,0:T(1,128)} %bitcast.11, bf16[32,256]{1,0:T(8,128)(2,1)} %bitcast.8, ...), custom_call_target="tpu_custom_call" | custom-call | flops 33554432 | bytes 524288 | tf_op jit(solution)/shard_map/pallas_call | solution.py:211
  2.4 3.1 %collective-permute-start = (bf16[256,128]{1,0:T(8,128)(2,1)S(1)}, bf16[256,128]{1,0:T(8,128)(2,1)S(1)}, u32[]{:S(2)}, u32[]{:S(2)}) collective-permute-start(bf16[256,128]{1,0:T(8,128)(2,1)S(1)} %get-tuple-element.15.refs_0_), channel_id=1, source_target_pairs={{0,8},{1,9},{2,10},{3,11},{4,12},{5,13},{6,14},{7,15},{8,0},{9,1},... | collective-permute-start | bytes 196616 | tf_op jit(solution)/shard_map/ppermute | solution.py:194
  5.5 2.5 %collective-permute-start.1 = (bf16[256,128]{1,0:T(8,128)(2,1)S(1)}, bf16[256,128]{1,0:T(8,128)(2,1)S(1)}, u32[]{:S(2)}, u32[]{:S(2)}) collective-permute-start(bf16[256,128]{1,0:T(8,128)(2,1)S(1)} %get-tuple-element.15.refs_0_), channel_id=1, source_target_pairs={{0,24},{1,25},{2,26},{3,27},{4,28},{5,29},{6,30},{7,31},{8,16},{9,... | collective-permute-start | bytes 196616 | tf_op jit(solution)/shard_map/ppermute | solution.py:194
  8.0 0.1 collective-permute-start.2
  8.1 0.0 collective-permute-done.refs_1_
  8.1 4.3 %collective-permute-done.1.refs_2_ = bf16[256,128]{1,0:T(8,128)(2,1)S(1)} collective-permute-done((bf16[256,128]{1,0:T(8,128)(2,1)S(1)}, bf16[256,128]{1,0:T(8,128)(2,1)S(1)}, u32[]{:S(2)}, u32[]{:S(2)}) %collective-permute-start.1) | collective-permute-done | bytes 65568 | tf_op jit(solution)/shard_map/ppermute | solution.py:194
  12.4 2.1 %collective-permute-done.2.refs_3_ = bf16[256,128]{1,0:T(8,128)(2,1)S(1)} collective-permute-done((bf16[256,128]{1,0:T(8,128)(2,1)S(1)}, bf16[256,128]{1,0:T(8,128)(2,1)S(1)}, u32[]{:S(2)}, u32[]{:S(2)}) %collective-permute-start.2) | collective-permute-done | bytes 65568 | tf_op jit(solution)/shard_map/ppermute | solution.py:194
  14.4 0.3 shard_map.101.refs_0_
  14.8 0.1 collective-permute-start.4
  14.8 4.8 %all-to-all-start = ((bf16[32,8,128]{2,1,0:T(8,128)(2,1)}), bf16[32,8,128]{2,1,0:T(8,128)(2,1)S(1)}, u32[]{:S(2)}, u32[]{:S(2)}) async-start(bf16[32,8,128]{2,1,0:T(8,128)(2,1)} %get-tuple-element.17), calls=%async_computation | async-start | bytes 131072 | tf_op jit(solution)/shard_map/all_to_all | solution.py:228
  19.6 1.8 %collective-permute-start.3 = (bf16[512,256]{1,0:T(8,128)(2,1)S(1)}, bf16[512,256]{1,0:T(8,128)(2,1)S(1)}, u32[]{:S(2)}, u32[]{:S(2)}) collective-permute-start(bf16[512,256]{1,0:T(8,128)(2,1)S(1)} %shard_map.101.refs_0_), channel_id=1, source_target_pairs={{0,2},{1,5},{2,0},{3,7},{4,6},{5,1},{6,4},{7,3},{8,10},{9,13},{10,... | collective-permute-start | bytes 786440 | tf_op jit(solution)/shard_map/ppermute | solution.py:242
  21.4 0.0 collective-permute-done.4.refs_1_
  21.4 0.3 collective-permute-start.5
  21.7 5.4 %all-to-all-done.right_ref = bf16[32,8,128]{2,1,0:T(8,128)(2,1)S(1)} async-done(((bf16[32,8,128]{2,1,0:T(8,128)(2,1)}), bf16[32,8,128]{2,1,0:T(8,128)(2,1)S(1)}, u32[]{:S(2)}, u32[]{:S(2)}) %all-to-all-start) | async-done | bytes 65568 | tf_op jit(solution)/shard_map/all_to_all | solution.py:228
  27.1 2.8 %shard_map.102.refs_2_.refs_1_ = bf16[8,1,256,2048]{3,2,1,0:T(8,128)(2,1)S(1)} custom-call(bf16[32,8,128]{2,1,0:T(8,128)(2,1)S(1)} %all-to-all-done.right_ref, bf16[1024,128]{1,0:T(8,128)(2,1)S(1)} %get-tuple-element.18.final_ref), custom_call_target="tpu_custom_call" | custom-call | flops 2147483648 | bytes 8388608 | tf_op jit(solution)/shard_map/pallas_call | solution.py:262
  29.9 0.0 collective-permute-done.3.refs_0_
  29.9 0.0 collective-permute-done.5.refs_1_
  29.9 1.2 %collective-permute-start.6 = (bf16[512,256]{1,0:T(8,128)(2,1)S(1)}, bf16[512,256]{1,0:T(8,128)(2,1)S(1)}, u32[]{:S(2)}, u32[]{:S(2)}) collective-permute-start(bf16[512,256]{1,0:T(8,128)(2,1)S(1)} %collective-permute-done.3.refs_0_), channel_id=1, source_target_pairs={{0,4},{1,3},{2,6},{3,1},{4,0},{5,7},{6,2},{7,5},{8,12},{9,11},{10,... | collective-permute-start | bytes 786440 | tf_op jit(solution)/shard_map/ppermute | solution.py:242
  31.1 1.3 %shard_map.103.refs_3_ = f32[512,2048]{1,0:T(8,128)S(1)} custom-call(bf16[512,256]{1,0:T(8,128)(2,1)S(1)} %shard_map.101.refs_0_, bf16[512,256]{1,0:T(8,128)(2,1)S(1)} %collective-permute-done.4.refs_1_, bf16[8,1,256,2048]{3,2,1,0:T(8,128)(2,1)S(1)} %shard_map.102.refs_2_.refs_1_), custom_call_target="tpu_custom_call" | custom-call | flops 1048576 | bytes 8192 | tf_op jit(solution)/shard_map/pallas_call | solution.py:299
  32.3 0.1 collective-permute-start.9
  32.4 0.5 %collective-permute-start.8 = (bf16[512,256]{1,0:T(8,128)(2,1)S(1)}, bf16[512,256]{1,0:T(8,128)(2,1)S(1)}, u32[]{:S(2)}, u32[]{:S(2)}) collective-permute-start(bf16[512,256]{1,0:T(8,128)(2,1)S(1)} %collective-permute-done.5.refs_1_), channel_id=1, source_target_pairs={{0,1},{1,0},{2,3},{3,2},{4,5},{5,4},{6,7},{7,6},{8,9},{9,8},{10,11... | collective-permute-start | bytes 786440 | tf_op jit(solution)/shard_map/ppermute | solution.py:194
  32.9 1.6 %shard_map.104 = (f32[512,2048]{1,0:T(8,128)S(1)}, bf16[512,16,128]{2,1,0:T(8,128)(2,1)S(1)}) custom-call(bf16[512,256]{1,0:T(8,128)(2,1)S(1)} %collective-permute-done.3.refs_0_, bf16[512,256]{1,0:T(8,128)(2,1)S(1)} %collective-permute-done.5.refs_1_, bf16[8,1,256,2048]{3,2,1,0:T(8,128)(2,1)S(1)} %shard_map.102.refs_2_.refs_1_, ...), custom_call_target="tpu_custom_call" | custom-call | flops 1048576 | bytes 8192 | tf_op jit(solution)/shard_map/pallas_call | solution.py:299
  34.5 1.8 %collective-permute-done.6.refs_0_ = bf16[512,256]{1,0:T(8,128)(2,1)S(1)} collective-permute-done((bf16[512,256]{1,0:T(8,128)(2,1)S(1)}, bf16[512,256]{1,0:T(8,128)(2,1)S(1)}, u32[]{:S(2)}, u32[]{:S(2)}) %collective-permute-start.6) | collective-permute-done | bytes 262176 | tf_op jit(solution)/shard_map/ppermute | solution.py:242
  36.3 0.0 copy-start
  36.3 0.0 collective-permute-start.7
  36.4 0.7 %shard_map.105.refs_3_ = f32[512,2048]{1,0:T(8,128)S(1)} custom-call(bf16[512,256]{1,0:T(8,128)(2,1)S(1)} %collective-permute-done.6.refs_0_, bf16[8,1,256,2048]{3,2,1,0:T(8,128)(2,1)S(1)} %shard_map.102.refs_2_.refs_1_, f32[512,2048]{1,0:T(8,128)S(1)} %get-tuple-element.23.refs_2_), custom_call_target="tpu_custom_call" | custom-call | flops 1048576 | bytes 8192 | tf_op jit(solution)/shard_map/pallas_call | solution.py:299
  37.1 0.0 collective-permute-done.8.refs_0_
  37.1 0.0 collective-permute-done.9.refs_1_
  37.1 0.0 copy-done
  37.1 1.3 %shard_map.106.refs_2_ = f32[512,2048]{1,0:T(8,128)S(1)} custom-call(bf16[512,256]{1,0:T(8,128)(2,1)S(1)} %collective-permute-done.8.refs_0_, bf16[512,256]{1,0:T(8,128)(2,1)S(1)} %collective-permute-done.9.refs_1_, bf16[8,1,256,2048]{3,2,1,0:T(8,128)(2,1)S(1)} %shard_map.102.refs_2_.refs_1_, f32[512,2048]{1,0:T(8,128)S(1)} %shard_map.105.refs_3_, ...), custom_call_target="tpu_custom_call" | custom-call | flops 1048576 | bytes 8192 | tf_op jit(solution)/shard_map/pallas_call | solution.py:299
  38.4 0.0 collective-permute-done.7.refs_0_
  38.4 2.2 %shard_map.107 = bf16[512,16,128]{2,1,0:T(8,128)(2,1)} custom-call(bf16[512,256]{1,0:T(8,128)(2,1)S(1)} %collective-permute-done.7.refs_0_, bf16[8,1,256,2048]{3,2,1,0:T(8,128)(2,1)S(1)} %shard_map.102.refs_2_.refs_1_, f32[512,2048]{1,0:T(8,128)S(1)} %shard_map.106.refs_2_, bf16[512,16,128]{2,1,0:T(8,128)(2,1)S(1)} %get-tuple-element.24.refs_3_), custom_call_target="tpu_custom_call" | custom-call | flops 1048576 | bytes 8192 | tf_op jit(solution)/shard_map/pallas_call | solution.py:299
Async XLA Ops:
  2.4 5.7 %collective-permute-start = (bf16[256,128]{1,0:T(8,128)(2,1)S(1)}, bf16[256,128]{1,0:T(8,128)(2,1)S(1)}, u32[]{:S(2)}, u32[]{:S(2)}) collective-permute-start(bf16[256,128]{1,0:T(8,128)(2,1)S(1)} %get-tuple-element.15.refs_0_), channel_id=1, source_target_pairs={{0,8},{1,9},{2,10},{3,11},{4,12},{5,13},{6,14},{7,15},{8,0},{9,1},... | collective-permute-start | bytes 196616 | tf_op jit(solution)/shard_map/ppermute | solution.py:194
  5.5 6.9 %collective-permute-start.1 = (bf16[256,128]{1,0:T(8,128)(2,1)S(1)}, bf16[256,128]{1,0:T(8,128)(2,1)S(1)}, u32[]{:S(2)}, u32[]{:S(2)}) collective-permute-start(bf16[256,128]{1,0:T(8,128)(2,1)S(1)} %get-tuple-element.15.refs_0_), channel_id=1, source_target_pairs={{0,24},{1,25},{2,26},{3,27},{4,28},{5,29},{6,30},{7,31},{8,16},{9,... | collective-permute-start | bytes 196616 | tf_op jit(solution)/shard_map/ppermute | solution.py:194
  8.0 6.4 %collective-permute-start.2 = (bf16[256,128]{1,0:T(8,128)(2,1)S(1)}, bf16[256,128]{1,0:T(8,128)(2,1)S(1)}, u32[]{:S(2)}, u32[]{:S(2)}) collective-permute-start(bf16[256,128]{1,0:T(8,128)(2,1)S(1)} %get-tuple-element.15.refs_0_), channel_id=1, source_target_pairs={{0,16},{1,17},{2,18},{3,19},{4,20},{5,21},{6,22},{7,23},{8,24},{9,... | collective-permute-start | bytes 196616 | tf_op jit(solution)/shard_map/ppermute | solution.py:194
  14.8 6.7 %collective-permute-start.4 = (bf16[512,256]{1,0:T(8,128)(2,1)S(1)}, bf16[512,256]{1,0:T(8,128)(2,1)S(1)}, u32[]{:S(2)}, u32[]{:S(2)}) collective-permute-start(bf16[512,256]{1,0:T(8,128)(2,1)S(1)} %shard_map.101.refs_0_), channel_id=1, source_target_pairs={{0,1},{1,0},{2,3},{3,2},{4,5},{5,4},{6,7},{7,6},{8,9},{9,8},{10,11... | collective-permute-start | bytes 786440 | tf_op jit(solution)/shard_map/ppermute | solution.py:194
  14.8 12.3 %all-to-all-start = ((bf16[32,8,128]{2,1,0:T(8,128)(2,1)}), bf16[32,8,128]{2,1,0:T(8,128)(2,1)S(1)}, u32[]{:S(2)}, u32[]{:S(2)}) async-start(bf16[32,8,128]{2,1,0:T(8,128)(2,1)} %get-tuple-element.17), calls=%async_computation | async-start | bytes 131072 | tf_op jit(solution)/shard_map/all_to_all | solution.py:228
  19.6 10.3 %collective-permute-start.3 = (bf16[512,256]{1,0:T(8,128)(2,1)S(1)}, bf16[512,256]{1,0:T(8,128)(2,1)S(1)}, u32[]{:S(2)}, u32[]{:S(2)}) collective-permute-start(bf16[512,256]{1,0:T(8,128)(2,1)S(1)} %shard_map.101.refs_0_), channel_id=1, source_target_pairs={{0,2},{1,5},{2,0},{3,7},{4,6},{5,1},{6,4},{7,3},{8,10},{9,13},{10,... | collective-permute-start | bytes 786440 | tf_op jit(solution)/shard_map/ppermute | solution.py:242
  21.4 8.5 %collective-permute-start.5 = (bf16[512,256]{1,0:T(8,128)(2,1)S(1)}, bf16[512,256]{1,0:T(8,128)(2,1)S(1)}, u32[]{:S(2)}, u32[]{:S(2)}) collective-permute-start(bf16[512,256]{1,0:T(8,128)(2,1)S(1)} %collective-permute-done.4.refs_1_), channel_id=1, source_target_pairs={{0,2},{1,5},{2,0},{3,7},{4,6},{5,1},{6,4},{7,3},{8,10},{9,13},{10,... | collective-permute-start | bytes 786440 | tf_op jit(solution)/shard_map/ppermute | solution.py:242
  29.9 6.4 %collective-permute-start.6 = (bf16[512,256]{1,0:T(8,128)(2,1)S(1)}, bf16[512,256]{1,0:T(8,128)(2,1)S(1)}, u32[]{:S(2)}, u32[]{:S(2)}) collective-permute-start(bf16[512,256]{1,0:T(8,128)(2,1)S(1)} %collective-permute-done.3.refs_0_), channel_id=1, source_target_pairs={{0,4},{1,3},{2,6},{3,1},{4,0},{5,7},{6,2},{7,5},{8,12},{9,11},{10,... | collective-permute-start | bytes 786440 | tf_op jit(solution)/shard_map/ppermute | solution.py:242
  32.3 4.8 %collective-permute-start.9 = (bf16[512,256]{1,0:T(8,128)(2,1)S(1)}, bf16[512,256]{1,0:T(8,128)(2,1)S(1)}, u32[]{:S(2)}, u32[]{:S(2)}) collective-permute-start(bf16[512,256]{1,0:T(8,128)(2,1)S(1)} %collective-permute-done.3.refs_0_), channel_id=1, source_target_pairs={{0,1},{1,0},{2,3},{3,2},{4,5},{5,4},{6,7},{7,6},{8,9},{9,8},{10,11... | collective-permute-start | bytes 786440 | tf_op jit(solution)/shard_map/ppermute | solution.py:194
  32.4 4.7 %collective-permute-start.8 = (bf16[512,256]{1,0:T(8,128)(2,1)S(1)}, bf16[512,256]{1,0:T(8,128)(2,1)S(1)}, u32[]{:S(2)}, u32[]{:S(2)}) collective-permute-start(bf16[512,256]{1,0:T(8,128)(2,1)S(1)} %collective-permute-done.5.refs_1_), channel_id=1, source_target_pairs={{0,1},{1,0},{2,3},{3,2},{4,5},{5,4},{6,7},{7,6},{8,9},{9,8},{10,11... | collective-permute-start | bytes 786440 | tf_op jit(solution)/shard_map/ppermute | solution.py:194
  36.3 0.7 %copy-start = (f32[128]{0:T(128)S(1)}, f32[128]{0:T(128)}, u32[]{:S(2)}) copy-start(f32[128]{0:T(128)} %param.19) | copy-start | bytes 1540
  36.3 2.0 %collective-permute-start.7 = (bf16[512,256]{1,0:T(8,128)(2,1)S(1)}, bf16[512,256]{1,0:T(8,128)(2,1)S(1)}, u32[]{:S(2)}, u32[]{:S(2)}) collective-permute-start(bf16[512,256]{1,0:T(8,128)(2,1)S(1)} %collective-permute-done.6.refs_0_), channel_id=1, source_target_pairs={{0,1},{1,0},{2,3},{3,2},{4,5},{5,4},{6,7},{7,6},{8,9},{9,8},{10,11... | collective-permute-start | bytes 786440 | tf_op jit(solution)/shard_map/ppermute | solution.py:194

commit v22 on v21

--- a/solution.py
+++ b/solution.py
@@ -242,7 +242,7 @@
     turn = lambda a, masks: lax.ppermute(a, "row", [(i, i ^ masks[i % 2]) for i in range(n)])
     partner = _xor(line, 1, n)
     near = turn(line, (2, 4))
-    near_other = turn(partner, (2, 4))
+    near_other = turn(line, (5, 3))
 
     fold_cost = pl.CostEstimate(
         flops=2 * n * 32 * 256 * CHANS * zdim, bytes_accessed=4 * n * CHANS * cols * zdim, transcendentals=0

time: 40.8 us -> 35.1 us (0.86)
  waiting for transfers between devices: 13.6 us -> 7.12 us
  starting transfers between devices: 14.3 us -> 15.1 us
    ppermute x7, waiting for transfers between devices: 6.34 us -> 1.15 us  [_xor(): return lax.ppermute(x, 'row', [(i, i ^ mask) for i in range(n)])]
    all_to_all x1, waiting for transfers between devices: 5.42 us -> 3.84 us  [shards(): lax.all_to_all(right, 'row', split_axis=0, concat_axis=0, tiled=True)]
    ppermute x7, starting transfers between devices: 6.32 us -> 6.84 us  [_xor(): return lax.ppermute(x, 'row', [(i, i ^ mask) for i in range(n)])]
  transfers between devices with their start and end apart: 11 -> 11, of which waited for: 4 -> 4; matrix products, arithmetic and copies ran while one was open for 0% -> 0% of each run, Pallas kernels for 19% -> 23%
where the time goes in v22:
time: 35.1 us; the launch traced here: 34.9 us
  starting transfers between devices  15.1 us (43%)
  Pallas kernels  12.6 us (36%)
  waiting for transfers between devices  7.12 us (20%)
    pallas_call x5, Pallas kernels, add(): pl.pallas_call(functools.partial(_band_kernel, masks, total is None, 1.0...  7.06 us
    ppermute x7, starting transfers between devices, _xor(): return lax.ppermute(x, 'row', [(i, i ^ mask) for i in range(n)])  6.84 us
    all_to_all x1, starting transfers between devices, shards(): lax.all_to_all(right, 'row', split_axis=0, concat_axis=0, tiled=True)  5.17 us
    all_to_all x1, waiting for transfers between devices, shards(): lax.all_to_all(right, 'row', split_axis=0, concat_axis=0, tiled=True)  3.84 us
    ppermute x3, starting transfers between devices, shards(): lax.ppermute(a, 'row', [(i, i ^ masks[i % 2]) for i in range(n)])  3.07 us
    pallas_call x1, Pallas kernels, shards(): pl.pallas_call(_fold_kernel, out_shape=fold_out, scratch_shapes=[pltpu.VM...  2.76 us
    pallas_call x1, Pallas kernels, shards(): pl.pallas_call(_project_kernel, in_specs=[anywhere] * 8, out_specs=(vmem,...  2.43 us
    ppermute x3, waiting for transfers between devices, shards(): lax.ppermute(a, 'row', [(i, i ^ masks[i % 2]) for i in range(n)])  2.13 us
  transfers between devices with their start and end apart: 11, of which 4 were waited for; matrix products, arithmetic and copies ran while one was open for 0% of the time, Pallas kernels for 23%

profile of v22, /device:TPU:0, one launch (start us, length us, event | category | flops | bytes accessed | tf_op | source)
XLA Modules:
  0.0 34.9 jit_solution(8429771805006005895)
XLA Ops:
  0.0 2.4 %shard_map.100 = (bf16[256,128]{1,0:T(8,128)(2,1)S(1)}, bf16[32,8,128]{2,1,0:T(8,128)(2,1)}, bf16[1024,128]{1,0:T(8,128)(2,1)S(1)}, bf16[2,512,256]{2,1,0:T(8,128)(2,1)S(1)}) custom-call(bf16[2,512,256]{2,1,0:T(8,128)(2,1)} %refs_0_.1, f32[1,256]{1,0:T(1,128)} %bitcast.10, f32[1,256]{1,0:T(1,128)} %bitcast.11, bf16[32,256]{1,0:T(8,128)(2,1)} %bitcast.8, ...), custom_call_target="tpu_custom_call" | custom-call | flops 33554432 | bytes 524288 | tf_op jit(solution)/shard_map/pallas_call | solution.py:211
  2.4 3.1 %collective-permute-start = (bf16[256,128]{1,0:T(8,128)(2,1)S(1)}, bf16[256,128]{1,0:T(8,128)(2,1)S(1)}, u32[]{:S(2)}, u32[]{:S(2)}) collective-permute-start(bf16[256,128]{1,0:T(8,128)(2,1)S(1)} %get-tuple-element.15.refs_0_), channel_id=1, source_target_pairs={{0,8},{1,9},{2,10},{3,11},{4,12},{5,13},{6,14},{7,15},{8,0},{9,1},... | collective-permute-start | bytes 196616 | tf_op jit(solution)/shard_map/ppermute | solution.py:194
  5.5 2.5 %collective-permute-start.1 = (bf16[256,128]{1,0:T(8,128)(2,1)S(1)}, bf16[256,128]{1,0:T(8,128)(2,1)S(1)}, u32[]{:S(2)}, u32[]{:S(2)}) collective-permute-start(bf16[256,128]{1,0:T(8,128)(2,1)S(1)} %get-tuple-element.15.refs_0_), channel_id=1, source_target_pairs={{0,24},{1,25},{2,26},{3,27},{4,28},{5,29},{6,30},{7,31},{8,16},{9,... | collective-permute-start | bytes 196616 | tf_op jit(solution)/shard_map/ppermute | solution.py:194
  8.0 0.1 collective-permute-start.2
  8.1 5.2 %all-to-all-start = ((bf16[32,8,128]{2,1,0:T(8,128)(2,1)}), bf16[32,8,128]{2,1,0:T(8,128)(2,1)S(1)}, u32[]{:S(2)}, u32[]{:S(2)}) async-start(bf16[32,8,128]{2,1,0:T(8,128)(2,1)} %get-tuple-element.17), calls=%async_computation | async-start | bytes 131072 | tf_op jit(solution)/shard_map/all_to_all | solution.py:228
  13.3 0.0 collective-permute-done.refs_1_
  13.3 0.0 collective-permute-done.1.refs_2_
  13.3 1.1 %collective-permute-done.2.refs_3_ = bf16[256,128]{1,0:T(8,128)(2,1)S(1)} collective-permute-done((bf16[256,128]{1,0:T(8,128)(2,1)S(1)}, bf16[256,128]{1,0:T(8,128)(2,1)S(1)}, u32[]{:S(2)}, u32[]{:S(2)}) %collective-permute-start.2) | collective-permute-done | bytes 65568 | tf_op jit(solution)/shard_map/ppermute | solution.py:194
  14.4 0.3 shard_map.101.refs_0_
  14.8 1.6 %collective-permute-start.3 = (bf16[512,256]{1,0:T(8,128)(2,1)S(1)}, bf16[512,256]{1,0:T(8,128)(2,1)S(1)}, u32[]{:S(2)}, u32[]{:S(2)}) collective-permute-start(bf16[512,256]{1,0:T(8,128)(2,1)S(1)} %shard_map.101.refs_0_), channel_id=1, source_target_pairs={{0,2},{1,5},{2,0},{3,7},{4,6},{5,1},{6,4},{7,3},{8,10},{9,13},{10,... | collective-permute-start | bytes 786440 | tf_op jit(solution)/shard_map/ppermute | solution.py:242
  16.3 0.0 collective-permute-start.4
  16.3 0.7 %collective-permute-start.6 = (bf16[512,256]{1,0:T(8,128)(2,1)S(1)}, bf16[512,256]{1,0:T(8,128)(2,1)S(1)}, u32[]{:S(2)}, u32[]{:S(2)}) collective-permute-start(bf16[512,256]{1,0:T(8,128)(2,1)S(1)} %shard_map.101.refs_0_), channel_id=1, source_target_pairs={{0,1},{1,0},{2,3},{3,2},{4,5},{5,4},{6,7},{7,6},{8,9},{9,8},{10,11... | collective-permute-start | bytes 786440 | tf_op jit(solution)/shard_map/ppermute | solution.py:194
  17.0 3.8 %all-to-all-done.right_ref = bf16[32,8,128]{2,1,0:T(8,128)(2,1)S(1)} async-done(((bf16[32,8,128]{2,1,0:T(8,128)(2,1)}), bf16[32,8,128]{2,1,0:T(8,128)(2,1)S(1)}, u32[]{:S(2)}, u32[]{:S(2)}) %all-to-all-start) | async-done | bytes 65568 | tf_op jit(solution)/shard_map/all_to_all | solution.py:228
  20.8 2.8 %shard_map.102.refs_2_.refs_1_ = bf16[8,1,256,2048]{3,2,1,0:T(8,128)(2,1)S(1)} custom-call(bf16[32,8,128]{2,1,0:T(8,128)(2,1)S(1)} %all-to-all-done.right_ref, bf16[1024,128]{1,0:T(8,128)(2,1)S(1)} %get-tuple-element.18.final_ref), custom_call_target="tpu_custom_call" | custom-call | flops 2147483648 | bytes 8388608 | tf_op jit(solution)/shard_map/pallas_call | solution.py:262
  23.6 0.0 collective-permute-done.3.refs_0_
  23.6 0.7 %collective-permute-done.4.refs_1_ = bf16[512,256]{1,0:T(8,128)(2,1)S(1)} collective-permute-done((bf16[512,256]{1,0:T(8,128)(2,1)S(1)}, bf16[512,256]{1,0:T(8,128)(2,1)S(1)}, u32[]{:S(2)}, u32[]{:S(2)}) %collective-permute-start.4) | collective-permute-done | bytes 262176 | tf_op jit(solution)/shard_map/ppermute | solution.py:242
  24.3 1.5 %collective-permute-start.5 = (bf16[512,256]{1,0:T(8,128)(2,1)S(1)}, bf16[512,256]{1,0:T(8,128)(2,1)S(1)}, u32[]{:S(2)}, u32[]{:S(2)}) collective-permute-start(bf16[512,256]{1,0:T(8,128)(2,1)S(1)} %collective-permute-done.3.refs_0_), channel_id=1, source_target_pairs={{0,4},{1,3},{2,6},{3,1},{4,0},{5,7},{6,2},{7,5},{8,12},{9,11},{10,... | collective-permute-start | bytes 786440 | tf_op jit(solution)/shard_map/ppermute | solution.py:242
  25.8 0.0 collective-permute-start.9
  25.8 0.5 %collective-permute-start.8 = (bf16[512,256]{1,0:T(8,128)(2,1)S(1)}, bf16[512,256]{1,0:T(8,128)(2,1)S(1)}, u32[]{:S(2)}, u32[]{:S(2)}) collective-permute-start(bf16[512,256]{1,0:T(8,128)(2,1)S(1)} %collective-permute-done.4.refs_1_), channel_id=1, source_target_pairs={{0,1},{1,0},{2,3},{3,2},{4,5},{5,4},{6,7},{7,6},{8,9},{9,8},{10,11... | collective-permute-start | bytes 786440 | tf_op jit(solution)/shard_map/ppermute | solution.py:194
  26.3 0.0 collective-permute-done.6.refs_1_
  26.3 1.3 %shard_map.103.refs_3_ = f32[512,2048]{1,0:T(8,128)S(1)} custom-call(bf16[512,256]{1,0:T(8,128)(2,1)S(1)} %shard_map.101.refs_0_, bf16[512,256]{1,0:T(8,128)(2,1)S(1)} %collective-permute-done.6.refs_1_, bf16[8,1,256,2048]{3,2,1,0:T(8,128)(2,1)S(1)} %shard_map.102.refs_2_.refs_1_), custom_call_target="tpu_custom_call" | custom-call | flops 1048576 | bytes 8192 | tf_op jit(solution)/shard_map/pallas_call | solution.py:299
  27.6 1.6 %shard_map.104 = (f32[512,2048]{1,0:T(8,128)S(1)}, bf16[512,16,128]{2,1,0:T(8,128)(2,1)S(1)}) custom-call(bf16[512,256]{1,0:T(8,128)(2,1)S(1)} %collective-permute-done.3.refs_0_, bf16[512,256]{1,0:T(8,128)(2,1)S(1)} %collective-permute-done.4.refs_1_, bf16[8,1,256,2048]{3,2,1,0:T(8,128)(2,1)S(1)} %shard_map.102.refs_2_.refs_1_, ...), custom_call_target="tpu_custom_call" | custom-call | flops 1048576 | bytes 8192 | tf_op jit(solution)/shard_map/pallas_call | solution.py:299
  29.2 1.5 %collective-permute-done.5.refs_0_ = bf16[512,256]{1,0:T(8,128)(2,1)S(1)} collective-permute-done((bf16[512,256]{1,0:T(8,128)(2,1)S(1)}, bf16[512,256]{1,0:T(8,128)(2,1)S(1)}, u32[]{:S(2)}, u32[]{:S(2)}) %collective-permute-start.5) | collective-permute-done | bytes 262176 | tf_op jit(solution)/shard_map/ppermute | solution.py:242
  30.6 0.0 copy-start
  30.6 0.0 collective-permute-start.7
  30.6 0.7 %shard_map.105.refs_3_ = f32[512,2048]{1,0:T(8,128)S(1)} custom-call(bf16[512,256]{1,0:T(8,128)(2,1)S(1)} %collective-permute-done.5.refs_0_, bf16[8,1,256,2048]{3,2,1,0:T(8,128)(2,1)S(1)} %shard_map.102.refs_2_.refs_1_, f32[512,2048]{1,0:T(8,128)S(1)} %get-tuple-element.23.refs_2_), custom_call_target="tpu_custom_call" | custom-call | flops 1048576 | bytes 8192 | tf_op jit(solution)/shard_map/pallas_call | solution.py:299
  31.4 0.0 collective-permute-done.8.refs_0_
  31.4 0.0 collective-permute-done.9.refs_1_
  31.4 0.0 copy-done
  31.4 1.3 %shard_map.106.refs_2_ = f32[512,2048]{1,0:T(8,128)S(1)} custom-call(bf16[512,256]{1,0:T(8,128)(2,1)S(1)} %collective-permute-done.8.refs_0_, bf16[512,256]{1,0:T(8,128)(2,1)S(1)} %collective-permute-done.9.refs_1_, bf16[8,1,256,2048]{3,2,1,0:T(8,128)(2,1)S(1)} %shard_map.102.refs_2_.refs_1_, f32[512,2048]{1,0:T(8,128)S(1)} %shard_map.105.refs_3_, ...), custom_call_target="tpu_custom_call" | custom-call | flops 1048576 | bytes 8192 | tf_op jit(solution)/shard_map/pallas_call | solution.py:299
  32.7 0.0 collective-permute-done.7.refs_0_
  32.7 2.2 %shard_map.107 = bf16[512,16,128]{2,1,0:T(8,128)(2,1)} custom-call(bf16[512,256]{1,0:T(8,128)(2,1)S(1)} %collective-permute-done.7.refs_0_, bf16[8,1,256,2048]{3,2,1,0:T(8,128)(2,1)S(1)} %shard_map.102.refs_2_.refs_1_, f32[512,2048]{1,0:T(8,128)S(1)} %shard_map.106.refs_2_, bf16[512,16,128]{2,1,0:T(8,128)(2,1)S(1)} %get-tuple-element.24.refs_3_), custom_call_target="tpu_custom_call" | custom-call | flops 1048576 | bytes 8192 | tf_op jit(solution)/shard_map/pallas_call | solution.py:299
Async XLA Ops:
  2.4 10.9 %collective-permute-start = (bf16[256,128]{1,0:T(8,128)(2,1)S(1)}, bf16[256,128]{1,0:T(8,128)(2,1)S(1)}, u32[]{:S(2)}, u32[]{:S(2)}) collective-permute-start(bf16[256,128]{1,0:T(8,128)(2,1)S(1)} %get-tuple-element.15.refs_0_), channel_id=1, source_target_pairs={{0,8},{1,9},{2,10},{3,11},{4,12},{5,13},{6,14},{7,15},{8,0},{9,1},... | collective-permute-start | bytes 196616 | tf_op jit(solution)/shard_map/ppermute | solution.py:194
  5.5 7.8 %collective-permute-start.1 = (bf16[256,128]{1,0:T(8,128)(2,1)S(1)}, bf16[256,128]{1,0:T(8,128)(2,1)S(1)}, u32[]{:S(2)}, u32[]{:S(2)}) collective-permute-start(bf16[256,128]{1,0:T(8,128)(2,1)S(1)} %get-tuple-element.15.refs_0_), channel_id=1, source_target_pairs={{0,24},{1,25},{2,26},{3,27},{4,28},{5,29},{6,30},{7,31},{8,16},{9,... | collective-permute-start | bytes 196616 | tf_op jit(solution)/shard_map/ppermute | solution.py:194
  8.0 6.4 %collective-permute-start.2 = (bf16[256,128]{1,0:T(8,128)(2,1)S(1)}, bf16[256,128]{1,0:T(8,128)(2,1)S(1)}, u32[]{:S(2)}, u32[]{:S(2)}) collective-permute-start(bf16[256,128]{1,0:T(8,128)(2,1)S(1)} %get-tuple-element.15.refs_0_), channel_id=1, source_target_pairs={{0,16},{1,17},{2,18},{3,19},{4,20},{5,21},{6,22},{7,23},{8,24},{9,... | collective-permute-start | bytes 196616 | tf_op jit(solution)/shard_map/ppermute | solution.py:194
  8.1 12.7 %all-to-all-start = ((bf16[32,8,128]{2,1,0:T(8,128)(2,1)}), bf16[32,8,128]{2,1,0:T(8,128)(2,1)S(1)}, u32[]{:S(2)}, u32[]{:S(2)}) async-start(bf16[32,8,128]{2,1,0:T(8,128)(2,1)} %get-tuple-element.17), calls=%async_computation | async-start | bytes 131072 | tf_op jit(solution)/shard_map/all_to_all | solution.py:228
  14.8 8.8 %collective-permute-start.3 = (bf16[512,256]{1,0:T(8,128)(2,1)S(1)}, bf16[512,256]{1,0:T(8,128)(2,1)S(1)}, u32[]{:S(2)}, u32[]{:S(2)}) collective-permute-start(bf16[512,256]{1,0:T(8,128)(2,1)S(1)} %shard_map.101.refs_0_), channel_id=1, source_target_pairs={{0,2},{1,5},{2,0},{3,7},{4,6},{5,1},{6,4},{7,3},{8,10},{9,13},{10,... | collective-permute-start | bytes 786440 | tf_op jit(solution)/shard_map/ppermute | solution.py:242
  16.3 8.0 %collective-permute-start.4 = (bf16[512,256]{1,0:T(8,128)(2,1)S(1)}, bf16[512,256]{1,0:T(8,128)(2,1)S(1)}, u32[]{:S(2)}, u32[]{:S(2)}) collective-permute-start(bf16[512,256]{1,0:T(8,128)(2,1)S(1)} %shard_map.101.refs_0_), channel_id=1, source_target_pairs={{0,5},{1,2},{2,7},{3,0},{4,1},{5,6},{6,3},{7,4},{8,13},{9,10},{10,... | collective-permute-start | bytes 786440 | tf_op jit(solution)/shard_map/ppermute | solution.py:242
  16.3 10.0 %collective-permute-start.6 = (bf16[512,256]{1,0:T(8,128)(2,1)S(1)}, bf16[512,256]{1,0:T(8,128)(2,1)S(1)}, u32[]{:S(2)}, u32[]{:S(2)}) collective-permute-start(bf16[512,256]{1,0:T(8,128)(2,1)S(1)} %shard_map.101.refs_0_), channel_id=1, source_target_pairs={{0,1},{1,0},{2,3},{3,2},{4,5},{5,4},{6,7},{7,6},{8,9},{9,8},{10,11... | collective-permute-start | bytes 786440 | tf_op jit(solution)/shard_map/ppermute | solution.py:194
  24.3 6.4 %collective-permute-start.5 = (bf16[512,256]{1,0:T(8,128)(2,1)S(1)}, bf16[512,256]{1,0:T(8,128)(2,1)S(1)}, u32[]{:S(2)}, u32[]{:S(2)}) collective-permute-start(bf16[512,256]{1,0:T(8,128)(2,1)S(1)} %collective-permute-done.3.refs_0_), channel_id=1, source_target_pairs={{0,4},{1,3},{2,6},{3,1},{4,0},{5,7},{6,2},{7,5},{8,12},{9,11},{10,... | collective-permute-start | bytes 786440 | tf_op jit(solution)/shard_map/ppermute | solution.py:242
  25.8 5.6 %collective-permute-start.9 = (bf16[512,256]{1,0:T(8,128)(2,1)S(1)}, bf16[512,256]{1,0:T(8,128)(2,1)S(1)}, u32[]{:S(2)}, u32[]{:S(2)}) collective-permute-start(bf16[512,256]{1,0:T(8,128)(2,1)S(1)} %collective-permute-done.3.refs_0_), channel_id=1, source_target_pairs={{0,1},{1,0},{2,3},{3,2},{4,5},{5,4},{6,7},{7,6},{8,9},{9,8},{10,11... | collective-permute-start | bytes 786440 | tf_op jit(solution)/shard_map/ppermute | solution.py:194
  25.8 5.6 %collective-permute-start.8 = (bf16[512,256]{1,0:T(8,128)(2,1)S(1)}, bf16[512,256]{1,0:T(8,128)(2,1)S(1)}, u32[]{:S(2)}, u32[]{:S(2)}) collective-permute-start(bf16[512,256]{1,0:T(8,128)(2,1)S(1)} %collective-permute-done.4.refs_1_), channel_id=1, source_target_pairs={{0,1},{1,0},{2,3},{3,2},{4,5},{5,4},{6,7},{7,6},{8,9},{9,8},{10,11... | collective-permute-start | bytes 786440 | tf_op jit(solution)/shard_map/ppermute | solution.py:194
  30.6 0.7 %copy-start = (f32[128]{0:T(128)S(1)}, f32[128]{0:T(128)}, u32[]{:S(2)}) copy-start(f32[128]{0:T(128)} %param.19) | copy-start | bytes 1540
  30.6 2.0 %collective-permute-start.7 = (bf16[512,256]{1,0:T(8,128)(2,1)S(1)}, bf16[512,256]{1,0:T(8,128)(2,1)S(1)}, u32[]{:S(2)}, u32[]{:S(2)}) collective-permute-start(bf16[512,256]{1,0:T(8,128)(2,1)S(1)} %collective-permute-done.5.refs_0_), channel_id=1, source_target_pairs={{0,1},{1,0},{2,3},{3,2},{4,5},{5,4},{6,7},{7,6},{8,9},{9,8},{10,11... | collective-permute-start | bytes 786440 | tf_op jit(solution)/shard_map/ppermute | solution.py:194

commit v23 on v20

--- a/solution.py
+++ b/solution.py
@@ -242,7 +242,8 @@
     turn = lambda a, masks: lax.ppermute(a, "row", [(i, i ^ masks[i % 2]) for i in range(n)])
     partner = _xor(line, 1, n)
     near = turn(line, (2, 4))
-    near_other = turn(partner, (2, 4))
+    near_other = turn(line, (5, 3))
+    near, right = lax.optimization_barrier((near, right))
     diagonal = turn(near, (4, 2))
 
     fold_cost = pl.CostEstimate(
@@ -312,7 +313,8 @@
     far_other = _xor(near, 1, n)
     near_other, folded = lax.optimization_barrier((near_other, folded))
     far = _xor(near_other, 1, n)
-    total, carried = add([line, partner, near, near_other], (0, 1, 8, 9), None, carries=True)
+    total = add([line, partner], (0, 1), None)
+    total, carried = add([near, near_other], (8, 9), total, carries=True)
     diagonal, total = lax.optimization_barrier((diagonal, total))
     last = _xor(diagonal, 1, n)
     total = add([diagonal], (6,), total)

time: 38.1 us -> 38.9 us (1.021)
  waiting for transfers between devices: 8.95 us -> 11.8 us
  starting transfers between devices: 15.6 us -> 14.2 us
  Pallas kernels: 13.1 us -> 12.5 us
    ppermute x7, waiting for transfers between devices: 4.75 us -> 6.34 us  [_xor(): return lax.ppermute(x, 'row', [(i, i ^ mask) for i in range(n)])]
    all_to_all x1, waiting for transfers between devices: 4.2 us -> 5.48 us  [shards(): lax.all_to_all(right, 'row', split_axis=0, concat_axis=0, tiled=True)]
    ppermute x3, starting transfers between devices: 4.85 us -> 3.72 us  [shards(): lax.ppermute(a, 'row', [(i, i ^ masks[i % 2]) for i in range(n)])]
    pallas_call x4 -> x5, Pallas kernels: 7.64 us -> 7.06 us  [add(): pl.pallas_call(functools.partial(_band_kernel, masks, total is None, 1.0...]
    all_to_all x1, starting transfers between devices: 4.31 us -> 3.74 us  [shards(): lax.all_to_all(right, 'row', split_axis=0, concat_axis=0, tiled=True)]
  transfers between devices with their start and end apart: 11 -> 11, of which waited for: 4 -> 3; matrix products, arithmetic and copies ran while one was open for 0% -> 0% of each run, Pallas kernels for 22% -> 20%
where the time goes in v23:
time: 38.9 us; the launch traced here: 38.7 us
  starting transfers between devices  14.2 us (37%)
  Pallas kernels  12.5 us (32%)
  waiting for transfers between devices  11.8 us (30%)
    pallas_call x5, Pallas kernels, add(): pl.pallas_call(functools.partial(_band_kernel, masks, total is None, 1.0...  7.06 us
    ppermute x7, starting transfers between devices, _xor(): return lax.ppermute(x, 'row', [(i, i ^ mask) for i in range(n)])  6.72 us
    ppermute x7, waiting for transfers between devices, _xor(): return lax.ppermute(x, 'row', [(i, i ^ mask) for i in range(n)])  6.34 us
    all_to_all x1, waiting for transfers between devices, shards(): lax.all_to_all(right, 'row', split_axis=0, concat_axis=0, tiled=True)  5.48 us
    all_to_all x1, starting transfers between devices, shards(): lax.all_to_all(right, 'row', split_axis=0, concat_axis=0, tiled=True)  3.74 us
    ppermute x3, starting transfers between devices, shards(): lax.ppermute(a, 'row', [(i, i ^ masks[i % 2]) for i in range(n)])  3.72 us
    pallas_call x1, Pallas kernels, shards(): pl.pallas_call(_fold_kernel, out_shape=fold_out, scratch_shapes=[pltpu.VM...  2.76 us
    pallas_call x1, Pallas kernels, shards(): pl.pallas_call(_project_kernel, in_specs=[anywhere] * 8, out_specs=(vmem,...  2.43 us
  transfers between devices with their start and end apart: 11, of which 3 were waited for; matrix products, arithmetic and copies ran while one was open for 0% of the time, Pallas kernels for 20%

profile of v23, /device:TPU:0, one launch (start us, length us, event | category | flops | bytes accessed | tf_op | source)
XLA Modules:
  0.0 38.7 jit_solution(10810440085801545737)
XLA Ops:
  0.0 2.4 %shard_map.100 = (bf16[256,128]{1,0:T(8,128)(2,1)S(1)}, bf16[32,8,128]{2,1,0:T(8,128)(2,1)}, bf16[1024,128]{1,0:T(8,128)(2,1)S(1)}, bf16[2,512,256]{2,1,0:T(8,128)(2,1)S(1)}) custom-call(bf16[2,512,256]{2,1,0:T(8,128)(2,1)} %refs_0_.1, f32[1,256]{1,0:T(1,128)} %bitcast.10, f32[1,256]{1,0:T(1,128)} %bitcast.11, bf16[32,256]{1,0:T(8,128)(2,1)} %bitcast.8, ...), custom_call_target="tpu_custom_call" | custom-call | flops 33554432 | bytes 524288 | tf_op jit(solution)/shard_map/pallas_call | solution.py:211
  2.4 3.1 %collective-permute-start = (bf16[256,128]{1,0:T(8,128)(2,1)S(1)}, bf16[256,128]{1,0:T(8,128)(2,1)S(1)}, u32[]{:S(2)}, u32[]{:S(2)}) collective-permute-start(bf16[256,128]{1,0:T(8,128)(2,1)S(1)} %get-tuple-element.17.refs_0_), channel_id=1, source_target_pairs={{0,8},{1,9},{2,10},{3,11},{4,12},{5,13},{6,14},{7,15},{8,0},{9,1},... | collective-permute-start | bytes 196616 | tf_op jit(solution)/shard_map/ppermute | solution.py:194
  5.5 2.5 %collective-permute-start.1 = (bf16[256,128]{1,0:T(8,128)(2,1)S(1)}, bf16[256,128]{1,0:T(8,128)(2,1)S(1)}, u32[]{:S(2)}, u32[]{:S(2)}) collective-permute-start(bf16[256,128]{1,0:T(8,128)(2,1)S(1)} %get-tuple-element.17.refs_0_), channel_id=1, source_target_pairs={{0,24},{1,25},{2,26},{3,27},{4,28},{5,29},{6,30},{7,31},{8,16},{9,... | collective-permute-start | bytes 196616 | tf_op jit(solution)/shard_map/ppermute | solution.py:194
  8.0 0.1 collective-permute-start.2
  8.1 0.0 collective-permute-done.refs_1_
  8.1 4.3 %collective-permute-done.1.refs_2_ = bf16[256,128]{1,0:T(8,128)(2,1)S(1)} collective-permute-done((bf16[256,128]{1,0:T(8,128)(2,1)S(1)}, bf16[256,128]{1,0:T(8,128)(2,1)S(1)}, u32[]{:S(2)}, u32[]{:S(2)}) %collective-permute-start.1) | collective-permute-done | bytes 65568 | tf_op jit(solution)/shard_map/ppermute | solution.py:194
  12.4 2.1 %collective-permute-done.2.refs_3_ = bf16[256,128]{1,0:T(8,128)(2,1)S(1)} collective-permute-done((bf16[256,128]{1,0:T(8,128)(2,1)S(1)}, bf16[256,128]{1,0:T(8,128)(2,1)S(1)}, u32[]{:S(2)}, u32[]{:S(2)}) %collective-permute-start.2) | collective-permute-done | bytes 65568 | tf_op jit(solution)/shard_map/ppermute | solution.py:194
  14.4 0.3 shard_map.101.refs_0_
  14.8 1.6 %collective-permute-start.3 = (bf16[512,256]{1,0:T(8,128)(2,1)S(1)}, bf16[512,256]{1,0:T(8,128)(2,1)S(1)}, u32[]{:S(2)}, u32[]{:S(2)}) collective-permute-start(bf16[512,256]{1,0:T(8,128)(2,1)S(1)} %shard_map.101.refs_0_), channel_id=1, source_target_pairs={{0,2},{1,5},{2,0},{3,7},{4,6},{5,1},{6,4},{7,3},{8,10},{9,13},{10,... | collective-permute-start | bytes 786440 | tf_op jit(solution)/shard_map/ppermute | solution.py:242
  16.3 3.7 %all-to-all-start = ((bf16[32,8,128]{2,1,0:T(8,128)(2,1)}), bf16[32,8,128]{2,1,0:T(8,128)(2,1)S(1)}, u32[]{:S(2)}, u32[]{:S(2)}) async-start(bf16[32,8,128]{2,1,0:T(8,128)(2,1)} %get-tuple-element.19), calls=%async_computation | async-start | bytes 131072 | tf_op jit(solution)/shard_map/all_to_all | solution.py:228
  20.1 1.6 %collective-permute-start.5 = (bf16[512,256]{1,0:T(8,128)(2,1)S(1)}, bf16[512,256]{1,0:T(8,128)(2,1)S(1)}, u32[]{:S(2)}, u32[]{:S(2)}) collective-permute-start(bf16[512,256]{1,0:T(8,128)(2,1)S(1)} %shard_map.101.refs_0_), channel_id=1, source_target_pairs={{0,5},{1,2},{2,7},{3,0},{4,1},{5,6},{6,3},{7,4},{8,13},{9,10},{10,... | collective-permute-start | bytes 786440 | tf_op jit(solution)/shard_map/ppermute | solution.py:242
  21.6 0.4 collective-permute-start.6
  22.0 5.5 %all-to-all-done.right_ref = bf16[32,8,128]{2,1,0:T(8,128)(2,1)S(1)} async-done(((bf16[32,8,128]{2,1,0:T(8,128)(2,1)}), bf16[32,8,128]{2,1,0:T(8,128)(2,1)S(1)}, u32[]{:S(2)}, u32[]{:S(2)}) %all-to-all-start) | async-done | bytes 65568 | tf_op jit(solution)/shard_map/all_to_all | solution.py:228
  27.5 0.0 collective-permute-done.3.refs_0_
  27.5 0.6 %collective-permute-start.4 = (bf16[512,256]{1,0:T(8,128)(2,1)S(1)}, bf16[512,256]{1,0:T(8,128)(2,1)S(1)}, u32[]{:S(2)}, u32[]{:S(2)}) collective-permute-start(bf16[512,256]{1,0:T(8,128)(2,1)S(1)} %collective-permute-done.3.refs_0_), channel_id=1, source_target_pairs={{0,4},{1,3},{2,6},{3,1},{4,0},{5,7},{6,2},{7,5},{8,12},{9,11},{10,... | collective-permute-start | bytes 786440 | tf_op jit(solution)/shard_map/ppermute | solution.py:242
  28.1 0.0 collective-permute-start.9
  28.1 2.8 %shard_map.102.refs_2_.refs_1_ = bf16[8,1,256,2048]{3,2,1,0:T(8,128)(2,1)S(1)} custom-call(bf16[32,8,128]{2,1,0:T(8,128)(2,1)S(1)} %all-to-all-done.right_ref, bf16[1024,128]{1,0:T(8,128)(2,1)S(1)} %get-tuple-element.22.final_ref), custom_call_target="tpu_custom_call" | custom-call | flops 2147483648 | bytes 8388608 | tf_op jit(solution)/shard_map/pallas_call | solution.py:264
  30.8 0.0 collective-permute-done.5.refs_1_
  30.8 0.6 %collective-permute-start.8 = (bf16[512,256]{1,0:T(8,128)(2,1)S(1)}, bf16[512,256]{1,0:T(8,128)(2,1)S(1)}, u32[]{:S(2)}, u32[]{:S(2)}) collective-permute-start(bf16[512,256]{1,0:T(8,128)(2,1)S(1)} %collective-permute-done.5.refs_1_), channel_id=1, source_target_pairs={{0,1},{1,0},{2,3},{3,2},{4,5},{5,4},{6,7},{7,6},{8,9},{9,8},{10,11... | collective-permute-start | bytes 786440 | tf_op jit(solution)/shard_map/ppermute | solution.py:194
  31.4 0.0 collective-permute-done.6.refs_1_
  31.4 1.3 %shard_map.103.refs_3_ = f32[512,2048]{1,0:T(8,128)S(1)} custom-call(bf16[512,256]{1,0:T(8,128)(2,1)S(1)} %shard_map.101.refs_0_, bf16[512,256]{1,0:T(8,128)(2,1)S(1)} %collective-permute-done.6.refs_1_, bf16[8,1,256,2048]{3,2,1,0:T(8,128)(2,1)S(1)} %shard_map.102.refs_2_.refs_1_), custom_call_target="tpu_custom_call" | custom-call | flops 1048576 | bytes 8192 | tf_op jit(solution)/shard_map/pallas_call | solution.py:301
  32.7 1.6 %shard_map.104 = (f32[512,2048]{1,0:T(8,128)S(1)}, bf16[512,16,128]{2,1,0:T(8,128)(2,1)S(1)}) custom-call(bf16[512,256]{1,0:T(8,128)(2,1)S(1)} %collective-permute-done.3.refs_0_, bf16[512,256]{1,0:T(8,128)(2,1)S(1)} %collective-permute-done.5.refs_1_, bf16[8,1,256,2048]{3,2,1,0:T(8,128)(2,1)S(1)} %shard_map.102.refs_2_.refs_1_, ...), custom_call_target="tpu_custom_call" | custom-call | flops 1048576 | bytes 8192 | tf_op jit(solution)/shard_map/pallas_call | solution.py:301
  34.3 0.0 collective-permute-done.4.refs_0_
  34.3 0.0 copy-start
  34.3 0.1 collective-permute-start.7
  34.4 0.7 %shard_map.105.refs_3_ = f32[512,2048]{1,0:T(8,128)S(1)} custom-call(bf16[512,256]{1,0:T(8,128)(2,1)S(1)} %collective-permute-done.4.refs_0_, bf16[8,1,256,2048]{3,2,1,0:T(8,128)(2,1)S(1)} %shard_map.102.refs_2_.refs_1_, f32[512,2048]{1,0:T(8,128)S(1)} %get-tuple-element.27.refs_2_), custom_call_target="tpu_custom_call" | custom-call | flops 1048576 | bytes 8192 | tf_op jit(solution)/shard_map/pallas_call | solution.py:301
  35.2 0.0 collective-permute-done.8.refs_0_
  35.2 0.0 collective-permute-done.9.refs_1_
  35.2 0.0 copy-done
  35.2 1.3 %shard_map.106.refs_2_ = f32[512,2048]{1,0:T(8,128)S(1)} custom-call(bf16[512,256]{1,0:T(8,128)(2,1)S(1)} %collective-permute-done.8.refs_0_, bf16[512,256]{1,0:T(8,128)(2,1)S(1)} %collective-permute-done.9.refs_1_, bf16[8,1,256,2048]{3,2,1,0:T(8,128)(2,1)S(1)} %shard_map.102.refs_2_.refs_1_, f32[512,2048]{1,0:T(8,128)S(1)} %shard_map.105.refs_3_, ...), custom_call_target="tpu_custom_call" | custom-call | flops 1048576 | bytes 8192 | tf_op jit(solution)/shard_map/pallas_call | solution.py:301
  36.5 0.0 collective-permute-done.7.refs_0_
  36.5 2.2 %shard_map.107 = bf16[512,16,128]{2,1,0:T(8,128)(2,1)} custom-call(bf16[512,256]{1,0:T(8,128)(2,1)S(1)} %collective-permute-done.7.refs_0_, bf16[8,1,256,2048]{3,2,1,0:T(8,128)(2,1)S(1)} %shard_map.102.refs_2_.refs_1_, f32[512,2048]{1,0:T(8,128)S(1)} %shard_map.106.refs_2_, bf16[512,16,128]{2,1,0:T(8,128)(2,1)S(1)} %get-tuple-element.28.refs_3_), custom_call_target="tpu_custom_call" | custom-call | flops 1048576 | bytes 8192 | tf_op jit(solution)/shard_map/pallas_call | solution.py:301
Async XLA Ops:
  2.4 5.7 %collective-permute-start = (bf16[256,128]{1,0:T(8,128)(2,1)S(1)}, bf16[256,128]{1,0:T(8,128)(2,1)S(1)}, u32[]{:S(2)}, u32[]{:S(2)}) collective-permute-start(bf16[256,128]{1,0:T(8,128)(2,1)S(1)} %get-tuple-element.17.refs_0_), channel_id=1, source_target_pairs={{0,8},{1,9},{2,10},{3,11},{4,12},{5,13},{6,14},{7,15},{8,0},{9,1},... | collective-permute-start | bytes 196616 | tf_op jit(solution)/shard_map/ppermute | solution.py:194
  5.5 6.9 %collective-permute-start.1 = (bf16[256,128]{1,0:T(8,128)(2,1)S(1)}, bf16[256,128]{1,0:T(8,128)(2,1)S(1)}, u32[]{:S(2)}, u32[]{:S(2)}) collective-permute-start(bf16[256,128]{1,0:T(8,128)(2,1)S(1)} %get-tuple-element.17.refs_0_), channel_id=1, source_target_pairs={{0,24},{1,25},{2,26},{3,27},{4,28},{5,29},{6,30},{7,31},{8,16},{9,... | collective-permute-start | bytes 196616 | tf_op jit(solution)/shard_map/ppermute | solution.py:194
  8.0 6.4 %collective-permute-start.2 = (bf16[256,128]{1,0:T(8,128)(2,1)S(1)}, bf16[256,128]{1,0:T(8,128)(2,1)S(1)}, u32[]{:S(2)}, u32[]{:S(2)}) collective-permute-start(bf16[256,128]{1,0:T(8,128)(2,1)S(1)} %get-tuple-element.17.refs_0_), channel_id=1, source_target_pairs={{0,16},{1,17},{2,18},{3,19},{4,20},{5,21},{6,22},{7,23},{8,24},{9,... | collective-permute-start | bytes 196616 | tf_op jit(solution)/shard_map/ppermute | solution.py:194
  14.8 12.7 %collective-permute-start.3 = (bf16[512,256]{1,0:T(8,128)(2,1)S(1)}, bf16[512,256]{1,0:T(8,128)(2,1)S(1)}, u32[]{:S(2)}, u32[]{:S(2)}) collective-permute-start(bf16[512,256]{1,0:T(8,128)(2,1)S(1)} %shard_map.101.refs_0_), channel_id=1, source_target_pairs={{0,2},{1,5},{2,0},{3,7},{4,6},{5,1},{6,4},{7,3},{8,10},{9,13},{10,... | collective-permute-start | bytes 786440 | tf_op jit(solution)/shard_map/ppermute | solution.py:242
  16.3 11.2 %all-to-all-start = ((bf16[32,8,128]{2,1,0:T(8,128)(2,1)}), bf16[32,8,128]{2,1,0:T(8,128)(2,1)S(1)}, u32[]{:S(2)}, u32[]{:S(2)}) async-start(bf16[32,8,128]{2,1,0:T(8,128)(2,1)} %get-tuple-element.19), calls=%async_computation | async-start | bytes 131072 | tf_op jit(solution)/shard_map/all_to_all | solution.py:228
  20.1 10.8 %collective-permute-start.5 = (bf16[512,256]{1,0:T(8,128)(2,1)S(1)}, bf16[512,256]{1,0:T(8,128)(2,1)S(1)}, u32[]{:S(2)}, u32[]{:S(2)}) collective-permute-start(bf16[512,256]{1,0:T(8,128)(2,1)S(1)} %shard_map.101.refs_0_), channel_id=1, source_target_pairs={{0,5},{1,2},{2,7},{3,0},{4,1},{5,6},{6,3},{7,4},{8,13},{9,10},{10,... | collective-permute-start | bytes 786440 | tf_op jit(solution)/shard_map/ppermute | solution.py:242
  21.6 9.8 %collective-permute-start.6 = (bf16[512,256]{1,0:T(8,128)(2,1)S(1)}, bf16[512,256]{1,0:T(8,128)(2,1)S(1)}, u32[]{:S(2)}, u32[]{:S(2)}) collective-permute-start(bf16[512,256]{1,0:T(8,128)(2,1)S(1)} %shard_map.101.refs_0_), channel_id=1, source_target_pairs={{0,1},{1,0},{2,3},{3,2},{4,5},{5,4},{6,7},{7,6},{8,9},{9,8},{10,11... | collective-permute-start | bytes 786440 | tf_op jit(solution)/shard_map/ppermute | solution.py:194
  27.5 6.8 %collective-permute-start.4 = (bf16[512,256]{1,0:T(8,128)(2,1)S(1)}, bf16[512,256]{1,0:T(8,128)(2,1)S(1)}, u32[]{:S(2)}, u32[]{:S(2)}) collective-permute-start(bf16[512,256]{1,0:T(8,128)(2,1)S(1)} %collective-permute-done.3.refs_0_), channel_id=1, source_target_pairs={{0,4},{1,3},{2,6},{3,1},{4,0},{5,7},{6,2},{7,5},{8,12},{9,11},{10,... | collective-permute-start | bytes 786440 | tf_op jit(solution)/shard_map/ppermute | solution.py:242
  28.1 7.1 %collective-permute-start.9 = (bf16[512,256]{1,0:T(8,128)(2,1)S(1)}, bf16[512,256]{1,0:T(8,128)(2,1)S(1)}, u32[]{:S(2)}, u32[]{:S(2)}) collective-permute-start(bf16[512,256]{1,0:T(8,128)(2,1)S(1)} %collective-permute-done.3.refs_0_), channel_id=1, source_target_pairs={{0,1},{1,0},{2,3},{3,2},{4,5},{5,4},{6,7},{7,6},{8,9},{9,8},{10,11... | collective-permute-start | bytes 786440 | tf_op jit(solution)/shard_map/ppermute | solution.py:194
  30.8 4.3 %collective-permute-start.8 = (bf16[512,256]{1,0:T(8,128)(2,1)S(1)}, bf16[512,256]{1,0:T(8,128)(2,1)S(1)}, u32[]{:S(2)}, u32[]{:S(2)}) collective-permute-start(bf16[512,256]{1,0:T(8,128)(2,1)S(1)} %collective-permute-done.5.refs_1_), channel_id=1, source_target_pairs={{0,1},{1,0},{2,3},{3,2},{4,5},{5,4},{6,7},{7,6},{8,9},{9,8},{10,11... | collective-permute-start | bytes 786440 | tf_op jit(solution)/shard_map/ppermute | solution.py:194
  34.3 0.9 %copy-start = (f32[128]{0:T(128)S(1)}, f32[128]{0:T(128)}, u32[]{:S(2)}) copy-start(f32[128]{0:T(128)} %param.19) | copy-start | bytes 1540
  34.3 2.1 %collective-permute-start.7 = (bf16[512,256]{1,0:T(8,128)(2,1)S(1)}, bf16[512,256]{1,0:T(8,128)(2,1)S(1)}, u32[]{:S(2)}, u32[]{:S(2)}) collective-permute-start(bf16[512,256]{1,0:T(8,128)(2,1)S(1)} %collective-permute-done.4.refs_0_), channel_id=1, source_target_pairs={{0,1},{1,0},{2,3},{3,2},{4,5},{5,4},{6,7},{7,6},{8,9},{9,8},{10,11... | collective-permute-start | bytes 786440 | tf_op jit(solution)/shard_map/ppermute | solution.py:194

commit v24 on v22

--- a/solution.py
+++ b/solution.py
@@ -313,10 +313,10 @@
     diagonal = turn(near, (4, 2))
     far_other, far = _xor(near, 1, n), _xor(near_other, 1, n)
     total, carried = add([near, near_other], (8, 9), total, carries=True)
+    total = add([far, far_other], (10, 11), total)
     diagonal, total = lax.optimization_barrier((diagonal, total))
     last = _xor(diagonal, 1, n)
-    total = add([diagonal], (6,), total)
-    total = add([far, far_other], (10, 11), total, scaled=True)
+    total = add([diagonal], (6,), total, scaled=True)
     return add([last], (7,), total, last=True, scaled=True, carried=carried)
 
 

time: 35.1 us -> 35.1 us (level)
    ppermute x3, waiting for transfers between devices: 2.13 us -> 1.33 us  [shards(): lax.ppermute(a, 'row', [(i, i ^ masks[i % 2]) for i in range(n)])]
    ppermute x7, waiting for transfers between devices: 1.15 us -> 1.95 us  [_xor(): return lax.ppermute(x, 'row', [(i, i ^ mask) for i in range(n)])]
  transfers between devices with their start and end apart: 11 -> 11, of which waited for: 4 -> 5; matrix products, arithmetic and copies ran while one was open for 0% -> 0% of each run, Pallas kernels for 23% -> 23%
where the time goes in v24:
time: 35.1 us; the launch traced here: 34.9 us
  starting transfers between devices  15.1 us (43%)
  Pallas kernels  12.5 us (36%)
  waiting for transfers between devices  7.12 us (20%)
    pallas_call x5, Pallas kernels, add(): pl.pallas_call(functools.partial(_band_kernel, masks, total is None, 1.0...  7.06 us
    ppermute x7, starting transfers between devices, _xor(): return lax.ppermute(x, 'row', [(i, i ^ mask) for i in range(n)])  6.84 us
    all_to_all x1, starting transfers between devices, shards(): lax.all_to_all(right, 'row', split_axis=0, concat_axis=0, tiled=True)  5.17 us
    all_to_all x1, waiting for transfers between devices, shards(): lax.all_to_all(right, 'row', split_axis=0, concat_axis=0, tiled=True)  3.84 us
    ppermute x3, starting transfers between devices, shards(): lax.ppermute(a, 'row', [(i, i ^ masks[i % 2]) for i in range(n)])  3.07 us
    pallas_call x1, Pallas kernels, shards(): pl.pallas_call(_fold_kernel, out_shape=fold_out, scratch_shapes=[pltpu.VM...  2.76 us
    pallas_call x1, Pallas kernels, shards(): pl.pallas_call(_project_kernel, in_specs=[anywhere] * 8, out_specs=(vmem,...  2.43 us
    ppermute x7, waiting for transfers between devices, _xor(): return lax.ppermute(x, 'row', [(i, i ^ mask) for i in range(n)])  1.95 us
  transfers between devices with their start and end apart: 11, of which 5 were waited for; matrix products, arithmetic and copies ran while one was open for 0% of the time, Pallas kernels for 23%

profile of v24, /device:TPU:0, one launch (start us, length us, event | category | flops | bytes accessed | tf_op | source)
XLA Modules:
  0.0 34.9 jit_solution(10172256066125160870)
XLA Ops:
  0.0 2.4 %shard_map.100 = (bf16[256,128]{1,0:T(8,128)(2,1)S(1)}, bf16[32,8,128]{2,1,0:T(8,128)(2,1)}, bf16[1024,128]{1,0:T(8,128)(2,1)S(1)}, bf16[2,512,256]{2,1,0:T(8,128)(2,1)S(1)}) custom-call(bf16[2,512,256]{2,1,0:T(8,128)(2,1)} %refs_0_.1, f32[1,256]{1,0:T(1,128)} %bitcast.10, f32[1,256]{1,0:T(1,128)} %bitcast.11, bf16[32,256]{1,0:T(8,128)(2,1)} %bitcast.8, ...), custom_call_target="tpu_custom_call" | custom-call | flops 33554432 | bytes 524288 | tf_op jit(solution)/shard_map/pallas_call | solution.py:211
  2.4 3.1 %collective-permute-start = (bf16[256,128]{1,0:T(8,128)(2,1)S(1)}, bf16[256,128]{1,0:T(8,128)(2,1)S(1)}, u32[]{:S(2)}, u32[]{:S(2)}) collective-permute-start(bf16[256,128]{1,0:T(8,128)(2,1)S(1)} %get-tuple-element.15.refs_0_), channel_id=1, source_target_pairs={{0,8},{1,9},{2,10},{3,11},{4,12},{5,13},{6,14},{7,15},{8,0},{9,1},... | collective-permute-start | bytes 196616 | tf_op jit(solution)/shard_map/ppermute | solution.py:194
  5.5 2.5 %collective-permute-start.1 = (bf16[256,128]{1,0:T(8,128)(2,1)S(1)}, bf16[256,128]{1,0:T(8,128)(2,1)S(1)}, u32[]{:S(2)}, u32[]{:S(2)}) collective-permute-start(bf16[256,128]{1,0:T(8,128)(2,1)S(1)} %get-tuple-element.15.refs_0_), channel_id=1, source_target_pairs={{0,24},{1,25},{2,26},{3,27},{4,28},{5,29},{6,30},{7,31},{8,16},{9,... | collective-permute-start | bytes 196616 | tf_op jit(solution)/shard_map/ppermute | solution.py:194
  8.0 0.1 collective-permute-start.2
  8.1 5.2 %all-to-all-start = ((bf16[32,8,128]{2,1,0:T(8,128)(2,1)}), bf16[32,8,128]{2,1,0:T(8,128)(2,1)S(1)}, u32[]{:S(2)}, u32[]{:S(2)}) async-start(bf16[32,8,128]{2,1,0:T(8,128)(2,1)} %get-tuple-element.17), calls=%async_computation | async-start | bytes 131072 | tf_op jit(solution)/shard_map/all_to_all | solution.py:228
  13.3 0.0 collective-permute-done.refs_1_
  13.3 0.0 collective-permute-done.1.refs_2_
  13.3 1.1 %collective-permute-done.2.refs_3_ = bf16[256,128]{1,0:T(8,128)(2,1)S(1)} collective-permute-done((bf16[256,128]{1,0:T(8,128)(2,1)S(1)}, bf16[256,128]{1,0:T(8,128)(2,1)S(1)}, u32[]{:S(2)}, u32[]{:S(2)}) %collective-permute-start.2) | collective-permute-done | bytes 65568 | tf_op jit(solution)/shard_map/ppermute | solution.py:194
  14.4 0.3 shard_map.101.refs_0_
  14.8 1.6 %collective-permute-start.3 = (bf16[512,256]{1,0:T(8,128)(2,1)S(1)}, bf16[512,256]{1,0:T(8,128)(2,1)S(1)}, u32[]{:S(2)}, u32[]{:S(2)}) collective-permute-start(bf16[512,256]{1,0:T(8,128)(2,1)S(1)} %shard_map.101.refs_0_), channel_id=1, source_target_pairs={{0,2},{1,5},{2,0},{3,7},{4,6},{5,1},{6,4},{7,3},{8,10},{9,13},{10,... | collective-permute-start | bytes 786440 | tf_op jit(solution)/shard_map/ppermute | solution.py:242
  16.3 0.0 collective-permute-start.4
  16.3 0.7 %collective-permute-start.8 = (bf16[512,256]{1,0:T(8,128)(2,1)S(1)}, bf16[512,256]{1,0:T(8,128)(2,1)S(1)}, u32[]{:S(2)}, u32[]{:S(2)}) collective-permute-start(bf16[512,256]{1,0:T(8,128)(2,1)S(1)} %shard_map.101.refs_0_), channel_id=1, source_target_pairs={{0,1},{1,0},{2,3},{3,2},{4,5},{5,4},{6,7},{7,6},{8,9},{9,8},{10,11... | collective-permute-start | bytes 786440 | tf_op jit(solution)/shard_map/ppermute | solution.py:194
  17.0 3.8 %all-to-all-done.right_ref = bf16[32,8,128]{2,1,0:T(8,128)(2,1)S(1)} async-done(((bf16[32,8,128]{2,1,0:T(8,128)(2,1)}), bf16[32,8,128]{2,1,0:T(8,128)(2,1)S(1)}, u32[]{:S(2)}, u32[]{:S(2)}) %all-to-all-start) | async-done | bytes 65568 | tf_op jit(solution)/shard_map/all_to_all | solution.py:228
  20.8 2.8 %shard_map.102.refs_2_.refs_1_ = bf16[8,1,256,2048]{3,2,1,0:T(8,128)(2,1)S(1)} custom-call(bf16[32,8,128]{2,1,0:T(8,128)(2,1)S(1)} %all-to-all-done.right_ref, bf16[1024,128]{1,0:T(8,128)(2,1)S(1)} %get-tuple-element.18.final_ref), custom_call_target="tpu_custom_call" | custom-call | flops 2147483648 | bytes 8388608 | tf_op jit(solution)/shard_map/pallas_call | solution.py:262
  23.6 0.0 collective-permute-done.3.refs_0_
  23.6 0.7 %collective-permute-done.4.refs_1_ = bf16[512,256]{1,0:T(8,128)(2,1)S(1)} collective-permute-done((bf16[512,256]{1,0:T(8,128)(2,1)S(1)}, bf16[512,256]{1,0:T(8,128)(2,1)S(1)}, u32[]{:S(2)}, u32[]{:S(2)}) %collective-permute-start.4) | collective-permute-done | bytes 262176 | tf_op jit(solution)/shard_map/ppermute | solution.py:242
  24.3 0.0 collective-permute-start.6
  24.3 0.5 %collective-permute-start.7 = (bf16[512,256]{1,0:T(8,128)(2,1)S(1)}, bf16[512,256]{1,0:T(8,128)(2,1)S(1)}, u32[]{:S(2)}, u32[]{:S(2)}) collective-permute-start(bf16[512,256]{1,0:T(8,128)(2,1)S(1)} %collective-permute-done.3.refs_0_), channel_id=1, source_target_pairs={{0,1},{1,0},{2,3},{3,2},{4,5},{5,4},{6,7},{7,6},{8,9},{9,8},{10,11... | collective-permute-start | bytes 786440 | tf_op jit(solution)/shard_map/ppermute | solution.py:194
  24.8 1.5 %collective-permute-start.5 = (bf16[512,256]{1,0:T(8,128)(2,1)S(1)}, bf16[512,256]{1,0:T(8,128)(2,1)S(1)}, u32[]{:S(2)}, u32[]{:S(2)}) collective-permute-start(bf16[512,256]{1,0:T(8,128)(2,1)S(1)} %collective-permute-done.3.refs_0_), channel_id=1, source_target_pairs={{0,4},{1,3},{2,6},{3,1},{4,0},{5,7},{6,2},{7,5},{8,12},{9,11},{10,... | collective-permute-start | bytes 786440 | tf_op jit(solution)/shard_map/ppermute | solution.py:242
  26.3 0.0 collective-permute-done.8.refs_1_
  26.3 1.3 %shard_map.103.refs_3_ = f32[512,2048]{1,0:T(8,128)S(1)} custom-call(bf16[512,256]{1,0:T(8,128)(2,1)S(1)} %shard_map.101.refs_0_, bf16[512,256]{1,0:T(8,128)(2,1)S(1)} %collective-permute-done.8.refs_1_, bf16[8,1,256,2048]{3,2,1,0:T(8,128)(2,1)S(1)} %shard_map.102.refs_2_.refs_1_), custom_call_target="tpu_custom_call" | custom-call | flops 1048576 | bytes 8192 | tf_op jit(solution)/shard_map/pallas_call | solution.py:299
  27.6 1.6 %shard_map.104 = (f32[512,2048]{1,0:T(8,128)S(1)}, bf16[512,16,128]{2,1,0:T(8,128)(2,1)S(1)}) custom-call(bf16[512,256]{1,0:T(8,128)(2,1)S(1)} %collective-permute-done.3.refs_0_, bf16[512,256]{1,0:T(8,128)(2,1)S(1)} %collective-permute-done.4.refs_1_, bf16[8,1,256,2048]{3,2,1,0:T(8,128)(2,1)S(1)} %shard_map.102.refs_2_.refs_1_, ...), custom_call_target="tpu_custom_call" | custom-call | flops 1048576 | bytes 8192 | tf_op jit(solution)/shard_map/pallas_call | solution.py:299
  29.2 0.0 collective-permute-done.6.refs_0_
  29.2 0.0 collective-permute-done.7.refs_1_
  29.2 0.0 copy-start
  29.2 1.3 %shard_map.105.refs_2_ = f32[512,2048]{1,0:T(8,128)S(1)} custom-call(bf16[512,256]{1,0:T(8,128)(2,1)S(1)} %collective-permute-done.6.refs_0_, bf16[512,256]{1,0:T(8,128)(2,1)S(1)} %collective-permute-done.7.refs_1_, bf16[8,1,256,2048]{3,2,1,0:T(8,128)(2,1)S(1)} %shard_map.102.refs_2_.refs_1_, f32[512,2048]{1,0:T(8,128)S(1)} %get-tuple-element.21.refs_3_), custom_call_target="tpu_custom_call" | custom-call | flops 1048576 | bytes 8192 | tf_op jit(solution)/shard_map/pallas_call | solution.py:299
  30.5 0.6 %collective-permute-done.5.refs_0_ = bf16[512,256]{1,0:T(8,128)(2,1)S(1)} collective-permute-done((bf16[512,256]{1,0:T(8,128)(2,1)S(1)}, bf16[512,256]{1,0:T(8,128)(2,1)S(1)}, u32[]{:S(2)}, u32[]{:S(2)}) %collective-permute-start.5) | collective-permute-done | bytes 262176 | tf_op jit(solution)/shard_map/ppermute | solution.py:242
  31.1 0.0 collective-permute-start.9
  31.2 0.0 copy-done
  31.2 0.7 %shard_map.106.refs_2_ = f32[512,2048]{1,0:T(8,128)S(1)} custom-call(bf16[512,256]{1,0:T(8,128)(2,1)S(1)} %collective-permute-done.5.refs_0_, bf16[8,1,256,2048]{3,2,1,0:T(8,128)(2,1)S(1)} %shard_map.102.refs_2_.refs_1_, f32[512,2048]{1,0:T(8,128)S(1)} %shard_map.105.refs_2_, f32[1,128]{1,0:T(1,128)S(1)} %bitcast.7), custom_call_target="tpu_custom_call" | custom-call | flops 1048576 | bytes 8192 | tf_op jit(solution)/shard_map/pallas_call | solution.py:299
  31.9 0.8 %collective-permute-done.9.refs_0_ = bf16[512,256]{1,0:T(8,128)(2,1)S(1)} collective-permute-done((bf16[512,256]{1,0:T(8,128)(2,1)S(1)}, bf16[512,256]{1,0:T(8,128)(2,1)S(1)}, u32[]{:S(2)}, u32[]{:S(2)}) %collective-permute-start.9) | collective-permute-done | bytes 262176 | tf_op jit(solution)/shard_map/ppermute | solution.py:194
  32.7 2.2 %shard_map.107 = bf16[512,16,128]{2,1,0:T(8,128)(2,1)} custom-call(bf16[512,256]{1,0:T(8,128)(2,1)S(1)} %collective-permute-done.9.refs_0_, bf16[8,1,256,2048]{3,2,1,0:T(8,128)(2,1)S(1)} %shard_map.102.refs_2_.refs_1_, f32[512,2048]{1,0:T(8,128)S(1)} %shard_map.106.refs_2_, bf16[512,16,128]{2,1,0:T(8,128)(2,1)S(1)} %get-tuple-element.24.refs_3_), custom_call_target="tpu_custom_call" | custom-call | flops 1048576 | bytes 8192 | tf_op jit(solution)/shard_map/pallas_call | solution.py:299
Async XLA Ops:
  2.4 10.9 %collective-permute-start = (bf16[256,128]{1,0:T(8,128)(2,1)S(1)}, bf16[256,128]{1,0:T(8,128)(2,1)S(1)}, u32[]{:S(2)}, u32[]{:S(2)}) collective-permute-start(bf16[256,128]{1,0:T(8,128)(2,1)S(1)} %get-tuple-element.15.refs_0_), channel_id=1, source_target_pairs={{0,8},{1,9},{2,10},{3,11},{4,12},{5,13},{6,14},{7,15},{8,0},{9,1},... | collective-permute-start | bytes 196616 | tf_op jit(solution)/shard_map/ppermute | solution.py:194
  5.5 7.8 %collective-permute-start.1 = (bf16[256,128]{1,0:T(8,128)(2,1)S(1)}, bf16[256,128]{1,0:T(8,128)(2,1)S(1)}, u32[]{:S(2)}, u32[]{:S(2)}) collective-permute-start(bf16[256,128]{1,0:T(8,128)(2,1)S(1)} %get-tuple-element.15.refs_0_), channel_id=1, source_target_pairs={{0,24},{1,25},{2,26},{3,27},{4,28},{5,29},{6,30},{7,31},{8,16},{9,... | collective-permute-start | bytes 196616 | tf_op jit(solution)/shard_map/ppermute | solution.py:194
  8.0 6.4 %collective-permute-start.2 = (bf16[256,128]{1,0:T(8,128)(2,1)S(1)}, bf16[256,128]{1,0:T(8,128)(2,1)S(1)}, u32[]{:S(2)}, u32[]{:S(2)}) collective-permute-start(bf16[256,128]{1,0:T(8,128)(2,1)S(1)} %get-tuple-element.15.refs_0_), channel_id=1, source_target_pairs={{0,16},{1,17},{2,18},{3,19},{4,20},{5,21},{6,22},{7,23},{8,24},{9,... | collective-permute-start | bytes 196616 | tf_op jit(solution)/shard_map/ppermute | solution.py:194
  8.1 12.7 %all-to-all-start = ((bf16[32,8,128]{2,1,0:T(8,128)(2,1)}), bf16[32,8,128]{2,1,0:T(8,128)(2,1)S(1)}, u32[]{:S(2)}, u32[]{:S(2)}) async-start(bf16[32,8,128]{2,1,0:T(8,128)(2,1)} %get-tuple-element.17), calls=%async_computation | async-start | bytes 131072 | tf_op jit(solution)/shard_map/all_to_all | solution.py:228
  14.8 8.8 %collective-permute-start.3 = (bf16[512,256]{1,0:T(8,128)(2,1)S(1)}, bf16[512,256]{1,0:T(8,128)(2,1)S(1)}, u32[]{:S(2)}, u32[]{:S(2)}) collective-permute-start(bf16[512,256]{1,0:T(8,128)(2,1)S(1)} %shard_map.101.refs_0_), channel_id=1, source_target_pairs={{0,2},{1,5},{2,0},{3,7},{4,6},{5,1},{6,4},{7,3},{8,10},{9,13},{10,... | collective-permute-start | bytes 786440 | tf_op jit(solution)/shard_map/ppermute | solution.py:242
  16.3 8.0 %collective-permute-start.4 = (bf16[512,256]{1,0:T(8,128)(2,1)S(1)}, bf16[512,256]{1,0:T(8,128)(2,1)S(1)}, u32[]{:S(2)}, u32[]{:S(2)}) collective-permute-start(bf16[512,256]{1,0:T(8,128)(2,1)S(1)} %shard_map.101.refs_0_), channel_id=1, source_target_pairs={{0,5},{1,2},{2,7},{3,0},{4,1},{5,6},{6,3},{7,4},{8,13},{9,10},{10,... | collective-permute-start | bytes 786440 | tf_op jit(solution)/shard_map/ppermute | solution.py:242
  16.3 10.0 %collective-permute-start.8 = (bf16[512,256]{1,0:T(8,128)(2,1)S(1)}, bf16[512,256]{1,0:T(8,128)(2,1)S(1)}, u32[]{:S(2)}, u32[]{:S(2)}) collective-permute-start(bf16[512,256]{1,0:T(8,128)(2,1)S(1)} %shard_map.101.refs_0_), channel_id=1, source_target_pairs={{0,1},{1,0},{2,3},{3,2},{4,5},{5,4},{6,7},{7,6},{8,9},{9,8},{10,11... | collective-permute-start | bytes 786440 | tf_op jit(solution)/shard_map/ppermute | solution.py:194
  24.3 4.9 %collective-permute-start.6 = (bf16[512,256]{1,0:T(8,128)(2,1)S(1)}, bf16[512,256]{1,0:T(8,128)(2,1)S(1)}, u32[]{:S(2)}, u32[]{:S(2)}) collective-permute-start(bf16[512,256]{1,0:T(8,128)(2,1)S(1)} %collective-permute-done.4.refs_1_), channel_id=1, source_target_pairs={{0,1},{1,0},{2,3},{3,2},{4,5},{5,4},{6,7},{7,6},{8,9},{9,8},{10,11... | collective-permute-start | bytes 786440 | tf_op jit(solution)/shard_map/ppermute | solution.py:194
  24.3 4.9 %collective-permute-start.7 = (bf16[512,256]{1,0:T(8,128)(2,1)S(1)}, bf16[512,256]{1,0:T(8,128)(2,1)S(1)}, u32[]{:S(2)}, u32[]{:S(2)}) collective-permute-start(bf16[512,256]{1,0:T(8,128)(2,1)S(1)} %collective-permute-done.3.refs_0_), channel_id=1, source_target_pairs={{0,1},{1,0},{2,3},{3,2},{4,5},{5,4},{6,7},{7,6},{8,9},{9,8},{10,11... | collective-permute-start | bytes 786440 | tf_op jit(solution)/shard_map/ppermute | solution.py:194
  24.8 6.4 %collective-permute-start.5 = (bf16[512,256]{1,0:T(8,128)(2,1)S(1)}, bf16[512,256]{1,0:T(8,128)(2,1)S(1)}, u32[]{:S(2)}, u32[]{:S(2)}) collective-permute-start(bf16[512,256]{1,0:T(8,128)(2,1)S(1)} %collective-permute-done.3.refs_0_), channel_id=1, source_target_pairs={{0,4},{1,3},{2,6},{3,1},{4,0},{5,7},{6,2},{7,5},{8,12},{9,11},{10,... | collective-permute-start | bytes 786440 | tf_op jit(solution)/shard_map/ppermute | solution.py:242
  29.2 1.9 %copy-start = (f32[128]{0:T(128)S(1)}, f32[128]{0:T(128)}, u32[]{:S(2)}) copy-start(f32[128]{0:T(128)} %param.19) | copy-start | bytes 1540
  31.1 1.5 %collective-permute-start.9 = (bf16[512,256]{1,0:T(8,128)(2,1)S(1)}, bf16[512,256]{1,0:T(8,128)(2,1)S(1)}, u32[]{:S(2)}, u32[]{:S(2)}) collective-permute-start(bf16[512,256]{1,0:T(8,128)(2,1)S(1)} %collective-permute-done.5.refs_0_), channel_id=1, source_target_pairs={{0,1},{1,0},{2,3},{3,2},{4,5},{5,4},{6,7},{7,6},{8,9},{9,8},{10,11... | collective-permute-start | bytes 786440 | tf_op jit(solution)/shard_map/ppermute | solution.py:194
